TPU v7x, 32 devices: a whole 2x2x4 slice. The times are simulated.
32 devices in a mesh: tile: 16 (over z, y, core), head: 2 (over x).
Axes of the slice: x: 2, y: 2, z: 4, core: 2. Of those that a mesh axis runs over, the one named last changes fastest.
Arguments:
- query_rows: bfloat16 [6144, 5120], P('tile', 'head'), may hold values from -60 to 60
- key_rows: bfloat16 [6144, 5120], P('tile', 'head'), may hold values from -60 to 60
- value_rows: bfloat16 [6144, 5120], P('tile', 'head'), may hold values from -6 to 6
- gain_q: float32 [5120], P('head'), may hold values from 0.1 to 1.9
- gain_k: float32 [5120], P('head'), may hold values from 0.1 to 1.9
- mem_keys: bfloat16 [256, 8, 5120], P('tile', None, 'head'), may hold values from -6 to 6
- mem_values: bfloat16 [256, 8, 5120], P('tile', None, 'head'), may hold values from -6 to 6
- tile_len: int32 [16], P('tile'), may hold values from 1 to 384, 4608 in all
- session: int32 [16], P('tile'), may hold values from 0 to 5, never falling along the last dimension, each value on 1 to 5 neighbouring positions
- req_owner: int32 [1024, 1], P('tile'), may hold values from 0 to 15; in each aligned block of 64 rows (0 to 63, 64 to 127, ...) at most 8 rows name the same one
- requested_block_index: int32 [1024], P('tile'), may hold values from 0 to 15
Outputs:
- attended: bfloat16 [6144, 5120], P('tile', 'head')
Inputs may be any that keep to these rules, and one draw needn't show every extreme that they name: Each session's tiles stand in a row, the session numbers never falling along tiles; a session has 1 to 5 tiles. `req_owner`: among the 64 requests of one tile at most 8 name the same owner, and exactly 8 do for some owner and tile.
All inputs are finite; a program needn't handle non-finite values. No bound on the sum of `tile_len` on one device may be relied on, other than what follows from the above.
Results may differ from a plain program's by a relative error of at most 0.011.
Values may be sent and summed in bfloat16 or wider, within the bound.
No kernel may reach another device: no remote copies, remote signals or barrier semaphores. Data moves between devices by JAX's collectives and lax.ppermute only.
A program may use at most 64 MiB of HBM per device.

v0:
```python
import jax
import jax.numpy as jnp
from jax import lax
from jax.sharding import PartitionSpec as P

HEAD_DIM = 128
WIDTH = 5120
EDGE = 64


EPSILON = 1e-06


def passed_along(value, axis, steps):
    count = lax.axis_size(axis)
    first, last = (max(0, -steps), min(count, count - steps))
    return lax.ppermute(value, axis, [(source, source + steps) for source in range(first, last)])


def row_squares(raw_rows):
    rows32 = raw_rows.astype(jnp.float32)
    return jnp.sum(rows32 * rows32, axis=1)


def normalize(raw_rows, totals, gain):
    rows32 = raw_rows.astype(jnp.float32)
    factor = lax.rsqrt(totals / WIDTH + EPSILON)
    return (rows32 * factor[:, None] * gain).astype(jnp.bfloat16)


def per_device(
    query_rows,
    key_rows,
    value_rows,
    gain_q,
    gain_k,
    mem_keys,
    mem_values,
    tile_len,
    session,
    req_owner,
    requested_block_index,
):
    capacity, tile_local_width = query_rows.shape
    my_length = tile_len[0]
    own_label = (session[0] + 1).astype(jnp.bfloat16)
    edge_index = jnp.arange(EDGE, dtype=jnp.int32)
    tail_labels = jnp.where(edge_index >= EDGE - my_length, own_label, jnp.bfloat16(0))
    front_labels = jnp.where(edge_index < my_length, own_label, jnp.bfloat16(0))
    totals_q, totals_k = lax.psum((row_squares(query_rows), row_squares(key_rows)), "head")
    query_norm = normalize(query_rows, totals_q, gain_q)
    key_norm = normalize(key_rows, totals_k, gain_k)
    blank = jnp.zeros((EDGE, tile_local_width), jnp.bfloat16)
    tail_keys = lax.dynamic_slice_in_dim(jnp.concatenate([blank, key_norm], 0), my_length, EDGE, 0)
    tail_values = lax.dynamic_slice_in_dim(
        jnp.concatenate([blank, value_rows], 0), my_length, EDGE, 0
    )
    from_left = passed_along((tail_keys, tail_values, tail_labels), "tile", 1)
    from_right = passed_along((key_norm[:EDGE], value_rows[:EDGE], front_labels), "tile", -1)
    from_left, from_right = (from_left, from_right)
    left_keys = from_left[0]
    right_keys = from_right[0]
    retrieved_count = requested_block_index.shape[0]
    owners = req_owner[:, 0]
    rows_per_block = mem_keys.shape[1]
    owner_blocks = mem_keys.shape[0]
    global_block = owners * owner_blocks + requested_block_index
    empty_rows = jnp.zeros((retrieved_count, rows_per_block, tile_local_width), jnp.bfloat16)
    piece_keys = lax.all_gather(mem_keys, "tile", axis=0, tiled=True)
    piece_values = lax.all_gather(mem_values, "tile", axis=0, tiled=True)
    count = piece_keys.shape[0]
    inside = ((global_block >= 0) & (global_block < count))[:, None, None]
    safe_block = jnp.clip(global_block, 0, count - 1)
    picked_keys = jnp.take(piece_keys, safe_block, axis=0)
    picked_values = jnp.take(piece_values, safe_block, axis=0)
    found_keys = jnp.where(inside, picked_keys, empty_rows)
    found_values = jnp.where(inside, picked_values, empty_rows)
    memory_keys = found_keys.reshape(retrieved_count * rows_per_block, tile_local_width)
    memory_values = found_values.reshape(retrieved_count * rows_per_block, tile_local_width)
    live_rows = jnp.arange(capacity, dtype=jnp.int32) < my_length
    all_keys = jnp.concatenate([key_norm, left_keys, right_keys, memory_keys], 0)
    all_values = jnp.concatenate([value_rows, from_left[1], from_right[1], memory_values], 0)
    visible = jnp.concatenate(
        [
            live_rows,
            from_left[2] == own_label,
            from_right[2] == own_label,
            jnp.ones((retrieved_count * rows_per_block,), bool),
        ],
        0,
    )
    heads_here = tile_local_width // HEAD_DIM
    score_scale = 1.0 / HEAD_DIM**0.5

    def one_head(head_number):
        first = head_number * HEAD_DIM
        head_query = lax.dynamic_slice_in_dim(query_norm, first, HEAD_DIM, 1)
        head_keys = lax.dynamic_slice_in_dim(all_keys, first, HEAD_DIM, 1)
        head_values = lax.dynamic_slice_in_dim(all_values, first, HEAD_DIM, 1)
        scores = (
            lax.dot_general(
                head_query, head_keys, (((1,), (1,)), ((), ())), preferred_element_type=jnp.float32
            )
            * score_scale
        )
        scores = jnp.where(visible[None, :], scores, jnp.float32(-1e30))
        top = jnp.max(scores, axis=1, keepdims=True)
        expo = jnp.exp(scores - top)
        weights = (expo / jnp.sum(expo, axis=1, keepdims=True)).astype(jnp.bfloat16)
        return jnp.dot(weights, head_values, preferred_element_type=jnp.float32)

    outputs = lax.map(one_head, jnp.arange(heads_here, dtype=jnp.int32))
    attended = jnp.transpose(outputs, (1, 0, 2)).reshape(capacity, tile_local_width)
    return jnp.where(live_rows[:, None], attended, jnp.float32(0.0)).astype(jnp.bfloat16)


def solution(mesh):
    in_specs = (
        P("tile", "head"),
        P("tile", "head"),
        P("tile", "head"),
        P("head"),
        P("head"),
        P("tile", None, "head"),
        P("tile", None, "head"),
        P("tile"),
        P("tile"),
        P("tile", None),
        P("tile"),
    )
    out_specs = P("tile", "head")
    return jax.shard_map(
        per_device, mesh=mesh, in_specs=in_specs, out_specs=out_specs, check_vma=False
    )
```

profile of v0, /device:TPU:0, one launch (start us, length us, event | category | flops | bytes accessed | tf_op | source)
XLA Modules:
  0.0 324.7 jit_solution(12113159523385854752)
XLA Ops:
  8.7 3.0 fusion.8
  11.6 5.8 %all-reduce.2 = (f32[384]{0:T(512)S(1)}, f32[384]{0:T(512)S(1)}) all-reduce(f32[384]{0:T(512)S(1)} %get-tuple-element.71, f32[384]{0:T(512)S(1)} %get-tuple-element.72), channel_id=1, replica_groups=mesh['tile'=16,'head'=2] {'head'}, use_global_device_ids=true, to_apply=%region_1.2 | all-reduce | flops 768 | bytes 6144 | tf_op jit(solution)/shard_map/psum | solution.py:50
  17.5 2.2 fusion.13
  24.3 5.3 %collective-permute-start.4 = (bf16[64,2560]{1,0:T(8,128)(2,1)}, bf16[64,2560]{1,0:T(8,128)(2,1)S(1)}, u32[]{:S(2)}, u32[]{:S(2)}) collective-permute-start(bf16[64,2560]{1,0:T(8,128)(2,1)} %get-tuple-element.64), channel_id=1, source_target_pairs={{0,2},{2,4},{4,6},{6,8},{8,10},{10,12},{12,14},{14,16},{16,18},{18... | collective-permute-start | bytes 983048 | tf_op jit(solution)/shard_map/ppermute | solution.py:17
  31.6 4.3 %collective-permute-start = (bf16[64]{0:T(256)(128)(2,1)S(1)}, bf16[64]{0:T(256)(128)(2,1)S(1)}, u32[]{:S(2)}, u32[]{:S(2)}) collective-permute-start(bf16[64]{0:T(256)(128)(2,1)S(1)} %compare_select_fusion.2), channel_id=1, source_target_pairs={{0,2},{2,4},{4,6},{6,8},{8,10},{10,12},{12,14},{14,16},{16,18},{18... | collective-permute-start | bytes 392 | tf_op jit(solution)/shard_map/ppermute | solution.py:17
  36.0 3.4 %fusion.10 = bf16[384,2560]{1,0:T(8,128)(2,1)} fusion(bf16[384,2560]{1,0:T(8,128)(2,1)} %param.15, f32[2560]{0:T(1024)S(1)} %copy-done.5, f32[384]{0:T(512)S(1)} %add_rsqrt_fusion.1), kind=kLoop, calls=%fused_computation.22 | loop fusion | flops 3932160 | bytes 3943936 | tf_op jit(solution)/shard_map/convert_element_type | solution.py:28
  40.7 2.9 collective-permute-done.1
  43.7 62.4 %all-gather.3.cloned.1.call-done = bf16[256,8,2560]{2,1,0:T(8,128)(2,1)} async-done(((bf16[16,8,2560]{2,1,0:T(8,128)(2,1)}), bf16[256,8,2560]{2,1,0:T(8,128)(2,1)}) %all-gather.3.cloned.1.call-update) | async-done | bytes 10485776 | tf_op jit(solution)/shard_map/all_gather | solution.py:69
  106.1 6.2 %gather_fusion = bf16[64,8,2560]{2,1,0:T(8,128)(2,1)} fusion(bf16[256,8,2560]{2,1,0:T(8,128)(2,1)} %all-gather.3.cloned.1.call-done, s32[1024]{0:T(1024)S(1)} %pad_clamp_fusion), kind=kCustom, calls=%fused_computation.clone | custom fusion | bytes 5243136 | tf_op jit(solution)/shard_map/jit(_take)/gather | solution.py:74
  112.4 82.1 %all-gather.5.cloned.1.call-done = bf16[256,8,2560]{2,1,0:T(8,128)(2,1)} async-done(((bf16[16,8,2560]{2,1,0:T(8,128)(2,1)}), bf16[256,8,2560]{2,1,0:T(8,128)(2,1)}) %all-gather.5.cloned.1.call-update) | async-done | bytes 10485776 | tf_op jit(solution)/shard_map/all_gather | solution.py:70
  194.5 6.2 %gather_fusion.1 = bf16[64,8,2560]{2,1,0:T(8,128)(2,1)} fusion(bf16[256,8,2560]{2,1,0:T(8,128)(2,1)} %all-gather.5.cloned.1.call-done, s32[1024]{0:T(1024)S(1)} %pad_clamp_fusion), kind=kCustom, calls=%fused_computation.1.clone | custom fusion | bytes 5243136 | tf_op jit(solution)/shard_map/jit(_take)/gather | solution.py:75
  200.8 3.0 fusion.15
  203.8 8.0 %pad_maximum_fusion = bf16[1024,2560]{1,0:T(8,128)(2,1)} fusion(bf16[512,2560]{1,0:T(8,128)(2,1)S(1)} %get-tuple-element.69, bf16[64,2560]{1,0:T(8,128)(2,1)S(1)} %collective-permute-done.3, bf16[64,2560]{1,0:T(8,128)(2,1)S(1)} %collective-permute-done.2, bf16[384,2560]{1,0:T(8,128)(2,1)S(1)} %fusion.13), kind=kLoop, calls=%fused_computation.14 | loop fusion | flops 20971520 | bytes 10485760 | tf_op jit(solution)/shard_map/concatenate | solution.py:81
  211.9 8.1 %pad_maximum_fusion.1 = bf16[1024,2560]{1,0:T(8,128)(2,1)} fusion(bf16[512,2560]{1,0:T(8,128)(2,1)S(1)} %get-tuple-element.68, bf16[64,2560]{1,0:T(8,128)(2,1)S(1)} %collective-permute-done.5, bf16[64,2560]{1,0:T(8,128)(2,1)S(1)} %collective-permute-done.4, bf16[384,2560]{1,0:T(8,128)(2,1)S(1)} %copy-done.1), kind=kLoop, calls=%fused_computation.15 | loop fusion | flops 20971520 | bytes 10485760 | tf_op jit(solution)/shard_map/concatenate | solution.py:82
  219.9 92.3 %while.10 = (s32[]{:T(128)}, bf16[20,384,128]{1,2,0:T(8,128)(2,1)S(1)}, pred[1024]{0:T(1024)(128)(4,1)S(1)}, s32[20]{0:T(128)S(1)}, bf16[384,2560]{1,0:T(8,128)(...) while((s32[]{:T(128)}, ...), condition=%wide.region_7.9_spmd, body=%wide.region_4.0_spmd.sunk | while | flops 204471552 | bytes 5549227 | solution.py:112
  223.0 1.5 fusion.25
  227.6 1.5 fusion.25
  232.3 1.5 fusion.25
  241.5 1.5 fusion.25
  250.7 1.5 fusion.25
  255.3 1.5 fusion.25
  259.9 1.5 fusion.25
  264.5 1.6 fusion.25
  269.2 1.5 fusion.25
  273.8 1.5 fusion.25
  278.4 1.5 fusion.25
  283.1 1.5 fusion.25
  287.7 1.5 fusion.25
  306.1 1.5 fusion.25
  310.7 1.5 fusion.25
  313.5 1.9 fusion.14
  315.4 2.4 copy.16
  (109 shorter events, 66.3 us)
Async XLA Ops:
  6.5 11.0 %copy-start.4 = (f32[2560]{0:T(1024)S(1)}, f32[2560]{0:T(1024)}, u32[]{:S(2)}) copy-start(f32[2560]{0:T(1024)} %param.19) | copy-start | bytes 30724
  6.5 99.6 %all-gather.3.cloned.1.call-start = ((), (), s32[]{:S(2)}) async-start(), calls=%async_computation | async-start | bytes 11141120 | tf_op jit(solution)/shard_map/all_gather | solution.py:69
  7.3 187.3 %all-gather.5.cloned.1.call-start = ((), (), s32[]{:S(2)}) async-start(), calls=%async_computation.1 | async-start | bytes 11141120 | tf_op jit(solution)/shard_map/all_gather | solution.py:70
  17.5 5.8 %copy-start = (bf16[384,2560]{1,0:T(8,128)(2,1)S(1)}, bf16[384,2560]{1,0:T(8,128)(2,1)}, u32[]{:S(2)}) copy-start(bf16[384,2560]{1,0:T(8,128)(2,1)} %param.17) | copy-start | bytes 5898244
  19.7 16.2 %copy-start.6 = (s32[64]{0:T(128)S(1)}, s32[64]{0:T(128)}, u32[]{:S(2)}) copy-start(s32[64]{0:T(128)} %param.25) | copy-start | bytes 772
  19.7 16.2 %copy-start.7 = (s32[64,1]{0,1:T(1,128)S(1)}, s32[64,1]{0,1:T(1,128)}, u32[]{:S(2)}) copy-start(s32[64,1]{0,1:T(1,128)} %param.24) | copy-start | bytes 772
  19.7 16.2 %copy-start.5 = (f32[2560]{0:T(1024)S(1)}, f32[2560]{0:T(1024)}, u32[]{:S(2)}) copy-start(f32[2560]{0:T(1024)} %param.18) | copy-start | bytes 30724
  20.7 183.1 %collective-permute-start.2 = (bf16[64,2560]{1,0:T(8,128)(2,1)}, bf16[64,2560]{1,0:T(8,128)(2,1)S(1)}, u32[]{:S(2)}, u32[]{:S(2)}) collective-permute-start(bf16[64,2560]{1,0:T(8,128)(2,1)} %get-tuple-element.66), channel_id=1, source_target_pairs={{0,2},{2,4},{4,6},{6,8},{8,10},{10,12},{12,14},{14,16},{16,18},{18... | collective-permute-start | bytes 983048 | tf_op jit(solution)/shard_map/ppermute | solution.py:17
  22.0 181.8 %collective-permute-start.3 = (bf16[64,2560]{1,0:T(8,128)(2,1)}, bf16[64,2560]{1,0:T(8,128)(2,1)S(1)}, u32[]{:S(2)}, u32[]{:S(2)}) collective-permute-start(bf16[64,2560]{1,0:T(8,128)(2,1)} %get-tuple-element.67), channel_id=1, source_target_pairs={{2,0},{4,2},{6,4},{8,6},{10,8},{12,10},{14,12},{16,14},{18,16},{20... | collective-permute-start | bytes 983048 | tf_op jit(solution)/shard_map/ppermute | solution.py:17
  24.3 187.6 %collective-permute-start.4 = (bf16[64,2560]{1,0:T(8,128)(2,1)}, bf16[64,2560]{1,0:T(8,128)(2,1)S(1)}, u32[]{:S(2)}, u32[]{:S(2)}) collective-permute-start(bf16[64,2560]{1,0:T(8,128)(2,1)} %get-tuple-element.64), channel_id=1, source_target_pairs={{0,2},{2,4},{4,6},{6,8},{8,10},{10,12},{12,14},{14,16},{16,18},{18... | collective-permute-start | bytes 983048 | tf_op jit(solution)/shard_map/ppermute | solution.py:17
  29.6 182.2 %collective-permute-start.5 = (bf16[64,2560]{1,0:T(8,128)(2,1)}, bf16[64,2560]{1,0:T(8,128)(2,1)S(1)}, u32[]{:S(2)}, u32[]{:S(2)}) collective-permute-start(bf16[64,2560]{1,0:T(8,128)(2,1)} %get-tuple-element.65), channel_id=1, source_target_pairs={{2,0},{4,2},{6,4},{8,6},{10,8},{12,10},{14,12},{16,14},{18,16},{20... | collective-permute-start | bytes 983048 | tf_op jit(solution)/shard_map/ppermute | solution.py:17
  31.6 7.8 %collective-permute-start = (bf16[64]{0:T(256)(128)(2,1)S(1)}, bf16[64]{0:T(256)(128)(2,1)S(1)}, u32[]{:S(2)}, u32[]{:S(2)}) collective-permute-start(bf16[64]{0:T(256)(128)(2,1)S(1)} %compare_select_fusion.2), channel_id=1, source_target_pairs={{0,2},{2,4},{4,6},{6,8},{8,10},{10,12},{12,14},{14,16},{16,18},{18... | collective-permute-start | bytes 392 | tf_op jit(solution)/shard_map/ppermute | solution.py:17
  39.4 4.2 %collective-permute-start.1 = (bf16[64]{0:T(256)(128)(2,1)S(1)}, bf16[64]{0:T(256)(128)(2,1)S(1)}, u32[]{:S(2)}, u32[]{:S(2)}) collective-permute-start(bf16[64]{0:T(256)(128)(2,1)S(1)} %compare_select_fusion.1), channel_id=1, source_target_pairs={{2,0},{4,2},{6,4},{8,6},{10,8},{12,10},{14,12},{16,14},{18,16},{20... | collective-permute-start | bytes 392 | tf_op jit(solution)/shard_map/ppermute | solution.py:17
  203.8 8.0 %copy-start.1 = (bf16[384,2560]{1,0:T(8,128)(2,1)S(1)}, bf16[384,2560]{1,0:T(8,128)(2,1)}, u32[]{:S(2)}) copy-start(bf16[384,2560]{1,0:T(8,128)(2,1)} %param.17) | copy-start | bytes 5898244
  211.9 8.1 %copy-start.2 = (bf16[20,384,128]{1,2,0:T(8,128)(2,1)S(1)}, bf16[20,384,128]{1,2,0:T(8,128)(2,1)}, u32[]{:S(2)}) copy-start(bf16[20,384,128]{1,2,0:T(8,128)(2,1)} %custom-call.4) | copy-start | bytes 5898244
  312.3 1.3 copy-start.3
Sparse Core Ops, SparseCore 0:
  9.6 96.4 all-gather.2
  108.4 86.0 all-gather.4
where the time goes:
time: 326 us; the launch traced here: 325 us
  waiting for transfers between devices  149 us (46%)
  matrix products  59.3 us (18%)
  other arithmetic  37.6 us (12%)
  local copies, waits for them, and re-layouts  29.8 us (9%)
  between operations  14.9 us (5%)
  starting transfers between devices  14.8 us (5%)
  loops' own time  13.5 us (4%)
  blocking collectives  5.84 us (2%)
    all_gather x1, waiting for transfers between devices, per_device(): piece_values = lax.all_gather(mem_values, 'tile', axis=0, tiled=True)  82.1 us
    all_gather x1, waiting for transfers between devices, per_device(): piece_keys = lax.all_gather(mem_keys, 'tile', axis=0, tiled=True)  62.4 us
    dot_general x20, matrix products, one_head(): return jnp.dot(weights, head_values, preferred_element_type=jnp.float32)  30 us
    dot_general x20, matrix products, one_head(): lax.dot_general(head_query, head_keys, (((1,), (1,)), ((), ())), preferre...  29.3 us
    ppermute x6, starting transfers between devices, passed_along(): lax.ppermute(value, axis, [(source, source + steps) for source in range(f...  14.8 us
    another operation x1, loops' own time, per_device(): outputs = lax.map(one_head, jnp.arange(heads_here, dtype=jnp.int32))  13.5 us
    dynamic_slice x20, local copies, waits for them, and re-layouts, per_device(): outputs = lax.map(one_head, jnp.arange(heads_here, dtype=jnp.int32))  11.7 us
    concatenate x1, other arithmetic, per_device(): jnp.concatenate([value_rows, from_left[1], from_right[1], memory_values], 0)  8.06 us
  transfers between devices with their start and end apart: 8, of which 3 were waited for; matrix products, arithmetic and copies ran while one was open for 11% of the time, Pallas kernels for 0%

commit v1 on v0

v1 whole, which is shorter than its diff:
```python
import functools
import math

import jax
import jax.numpy as jnp
from jax import lax
from jax.experimental import pallas as pl
from jax.experimental.pallas import tpu as pltpu
from jax.sharding import PartitionSpec as P

HEAD_DIM = 128
WIDTH = 5120
EDGE = 64
EPSILON = 1e-06
HIDDEN = -1e30
VMEM_BYTES = 48 * 1024 * 1024


def passed_along(value, axis, steps):
    count = lax.axis_size(axis)
    first, last = (max(0, -steps), min(count, count - steps))
    return lax.ppermute(value, axis, [(source, source + steps) for source in range(first, last)])


def row_squares(raw_rows):
    rows32 = raw_rows.astype(jnp.float32)
    return jnp.sum(rows32 * rows32, axis=1)


def normalize(raw_rows, totals, gain):
    rows32 = raw_rows.astype(jnp.float32)
    factor = lax.rsqrt(totals / WIDTH + EPSILON)
    return (rows32 * factor[:, None] * gain).astype(jnp.bfloat16)


def chip_position(tile, levels):
    level, row = tile // 4, (tile // 2) % 2
    return level + row * (2 * levels - 1 - 2 * level)


def ring_pairs(count, step):
    levels = count // 4
    at = {(chip_position(t, levels), t % 2): t for t in range(count)}
    places = 2 * levels
    return [(at[p, c], at[(p + step) % places, c]) for p in range(places) for c in range(2)]


def across_t(first, second):
    return lax.dot_general(first, second, (((1,), (1,)), ((), ())), preferred_element_type=jnp.float32)


def across(first, second):
    return jnp.dot(first, second, preferred_element_type=jnp.float32)


def with_ones(values):
    return jnp.concatenate([values, jnp.ones(values.shape, values.dtype)], axis=1)


def near_kernel(heads_per_step, bias_ref, q_ref, k_ref, v_ref, ek_ref, ev_ref, acc_ref, top_ref, sum_ref):
    step = pl.program_id(0)
    lane = lax.broadcasted_iota(jnp.int32, top_ref.shape, 1)

    @pl.when(step == 0)
    def _():
        top_ref[...] = jnp.zeros_like(top_ref)
        sum_ref[...] = jnp.zeros_like(sum_ref)

    own = k_ref.shape[0]
    for j in range(heads_per_step):
        columns = slice(j * HEAD_DIM, (j + 1) * HEAD_DIM)
        query = q_ref[:, columns]
        near = across_t(query, k_ref[:, columns]) + bias_ref[:, :own]
        edge = across_t(query, ek_ref[:, columns]) + bias_ref[:, own:]
        top = jnp.maximum(jnp.max(near, axis=1, keepdims=True), jnp.max(edge, axis=1, keepdims=True))
        near = jnp.exp2(near - top).astype(jnp.bfloat16)
        edge = jnp.exp2(edge - top).astype(jnp.bfloat16)
        both = across(near, with_ones(v_ref[:, columns])) + across(edge, with_ones(ev_ref[:, columns]))
        acc_ref[:, columns] = both[:, :HEAD_DIM]
        here = lane == step * heads_per_step + j
        top_ref[...] = jnp.where(here, top, top_ref[...])
        sum_ref[...] = jnp.where(here, both[:, HEAD_DIM:], sum_ref[...])


def near_part(bias, query, keys, values, edge_keys, edge_values):
    rows, width = query.shape
    heads = width // HEAD_DIM
    per_step = 2 if heads % 2 == 0 else 1
    wide = per_step * HEAD_DIM
    keys_seen = keys.shape[0] + edge_keys.shape[0]

    def columns(array):
        return pl.BlockSpec((array.shape[0], wide), lambda i: (0, i))

    stat = jax.ShapeDtypeStruct((rows, 128), jnp.float32)
    stat_spec = pl.BlockSpec((rows, 128), lambda i: (0, 0))
    return pl.pallas_call(
        functools.partial(near_kernel, per_step),
        grid=(heads // per_step,),
        in_specs=[pl.BlockSpec(bias.shape, lambda i: (0, 0))]
        + [columns(array) for array in (query, keys, values, edge_keys, edge_values)],
        out_specs=[pl.BlockSpec((rows, wide), lambda i: (0, i)), stat_spec, stat_spec],
        out_shape=[jax.ShapeDtypeStruct((rows, width), jnp.float32), stat, stat],
        compiler_params=pltpu.CompilerParams(vmem_limit_bytes=VMEM_BYTES),
        cost_estimate=pl.CostEstimate(
            flops=4 * rows * keys_seen * width,
            bytes_accessed=10 * rows * width,
            transcendentals=rows * keys_seen * heads,
        ),
        name="near_part",
    )(bias, query, keys, values, edge_keys, edge_values)


def far_kernel(groups, heads_per_step, *refs):
    first_ref, block_ref, live_ref, q_ref, acc_ref, top_ref, sum_ref = refs[:7]
    key_pieces = refs[7 : 7 + groups]
    value_pieces = refs[7 + groups : 7 + 2 * groups]
    out_ref, keys, values, sems = refs[7 + 2 * groups :]
    step = pl.program_id(0)
    wanted = keys.shape[0]

    def copies(key_piece, value_piece, block, slot):
        return (
            pltpu.make_async_copy(key_piece.at[block], keys.at[slot], sems.at[0]),
            pltpu.make_async_copy(value_piece.at[block], values.at[slot], sems.at[1]),
        )

    @pl.when(step == 0)
    def _():
        for g in range(groups):

            def fetch(slot, carry, g=g):
                for copy in copies(key_pieces[g], value_pieces[g], block_ref[slot], slot):
                    copy.start()
                return carry

            lax.fori_loop(first_ref[g], first_ref[g + 1], fetch, 0)
        for array, sem in ((keys, sems.at[0]), (values, sems.at[1])):
            pltpu.make_async_copy(array, array, sem).wait()

    lane = lax.broadcasted_iota(jnp.int32, top_ref.shape, 1)
    for j in range(heads_per_step):
        columns = slice(j * HEAD_DIM, (j + 1) * HEAD_DIM)
        head = step * heads_per_step + j
        place = pl.ds(pl.multiple_of(head * HEAD_DIM, HEAD_DIM), HEAD_DIM)

        def flat(array):
            block = array[:, :, place].astype(jnp.float32)
            return block.reshape(wanted * array.shape[1], HEAD_DIM).astype(jnp.bfloat16)

        scores = across_t(q_ref[:, columns], flat(keys))
        here = lane == head
        top_near = jnp.sum(jnp.where(here, top_ref[...], 0.0), axis=1, keepdims=True)
        sum_near = jnp.sum(jnp.where(here, sum_ref[...], 0.0), axis=1, keepdims=True)
        top = jnp.maximum(top_near, jnp.max(scores, axis=1, keepdims=True))
        weights = jnp.exp2(scores - top).astype(jnp.bfloat16)
        kept = jnp.exp2(top_near - top)
        both = across(weights, with_ones(flat(values)))
        total = both[:, HEAD_DIM:] + kept * sum_near
        result = (both[:, :HEAD_DIM] + kept * acc_ref[:, columns]) / total
        out_ref[:, columns] = jnp.where(live_ref[...] > 0.0, result, 0.0).astype(out_ref.dtype)


def far_part(first, block, live, query, acc, top, total, key_pieces, value_pieces):
    rows, width = query.shape
    heads = width // HEAD_DIM
    per_step = 2 if heads % 2 == 0 else 1
    wide = per_step * HEAD_DIM
    groups, wanted = len(key_pieces), block.shape[0]
    tokens = key_pieces[0].shape[1]

    def columns(array):
        return pl.BlockSpec((array.shape[0], wide), lambda i: (0, i))

    def whole(array):
        return pl.BlockSpec(array.shape, lambda i: (0, 0))

    return pl.pallas_call(
        functools.partial(far_kernel, groups, per_step),
        grid=(heads // per_step,),
        in_specs=[pl.BlockSpec(memory_space=pltpu.SMEM)] * 2
        + [whole(live), columns(query), columns(acc), whole(top), whole(total)]
        + [pl.BlockSpec(memory_space=pl.ANY)] * (2 * groups),
        out_specs=pl.BlockSpec((rows, wide), lambda i: (0, i)),
        out_shape=jax.ShapeDtypeStruct((rows, width), jnp.bfloat16),
        scratch_shapes=[
            pltpu.VMEM((wanted, tokens, width), jnp.bfloat16),
            pltpu.VMEM((wanted, tokens, width), jnp.bfloat16),
            pltpu.SemaphoreType.DMA((2,)),
        ],
        compiler_params=pltpu.CompilerParams(vmem_limit_bytes=VMEM_BYTES),
        cost_estimate=pl.CostEstimate(
            flops=4 * rows * wanted * tokens * width,
            bytes_accessed=8 * rows * width + 4 * wanted * tokens * width,
            transcendentals=rows * wanted * tokens * heads,
        ),
        name="far_part",
    )(first, block, live, query, acc, top, total, *key_pieces, *value_pieces)


def per_device(
    query_rows,
    key_rows,
    value_rows,
    gain_q,
    gain_k,
    mem_keys,
    mem_values,
    tile_len,
    session,
    req_owner,
    requested_block_index,
):
    capacity, width_here = query_rows.shape
    count = lax.axis_size("tile")
    levels = count // 4
    places = 2 * levels
    me = lax.axis_index("tile")

    up, down = ring_pairs(count, 1), ring_pairs(count, -1)
    swap = [(t, t ^ 1) for t in range(count)]
    lane_keys, lane_values = [mem_keys], [mem_values]
    for _ in range(places - 1):
        lane_keys.append(lax.ppermute(lane_keys[-1], "tile", up))
        lane_values.append(lax.ppermute(lane_values[-1], "tile", down))
    other_keys = [lax.ppermute(piece, "tile", swap) for piece in lane_keys]
    other_values = [lax.ppermute(piece, "tile", swap) for piece in lane_values]
    key_pieces, value_pieces = [], []
    for d in range(places):
        key_pieces += [lane_keys[d], other_keys[d]]
        value_pieces += [lane_values[-d], other_values[-d]] if d else [lane_values[0], other_values[0]]

    owners = req_owner[:, 0]
    distance = (chip_position(me, levels) - chip_position(owners, levels)) % places
    group = distance * 2 + ((owners % 2) != (me % 2)).astype(jnp.int32)
    number = jnp.arange(group.shape[0], dtype=jnp.int32)
    rank_key = group * group.shape[0] + number
    rank = jnp.sum((rank_key[None, :] < rank_key[:, None]).astype(jnp.int32), axis=1)
    block = jnp.sum(jnp.where(rank[None, :] == number[:, None], requested_block_index[None, :], 0), axis=1)
    first = jnp.sum(
        (group[None, :] < jnp.arange(count + 1, dtype=jnp.int32)[:, None]).astype(jnp.int32), axis=1
    )

    my_length = tile_len[0]
    totals_q, totals_k = lax.psum((row_squares(query_rows), row_squares(key_rows)), "head")
    query_norm = normalize(query_rows, totals_q, gain_q * (math.log2(math.e) / HEAD_DIM**0.5))
    key_norm = normalize(key_rows, totals_k, gain_k)
    blank = jnp.zeros((EDGE, width_here), jnp.bfloat16)

    def tail(rows):
        return lax.dynamic_slice_in_dim(jnp.concatenate([blank, rows], 0), my_length, EDGE, 0)

    about = jnp.stack([session[0] + 1, my_length])
    left_keys, left_values, left = passed_along((tail(key_norm), tail(value_rows), about), "tile", 1)
    right_keys, right_values, right = passed_along(
        (key_norm[:EDGE], value_rows[:EDGE], about), "tile", -1
    )
    edge_index = jnp.arange(EDGE, dtype=jnp.int32)
    live_rows = jnp.arange(capacity, dtype=jnp.int32) < my_length
    visible = jnp.concatenate(
        [
            live_rows,
            (left[0] == about[0]) & (edge_index >= EDGE - left[1]),
            (right[0] == about[0]) & (edge_index < right[1]),
        ]
    )
    bias = jnp.where(visible, 0.0, jnp.float32(HIDDEN))[None, :]
    live = jnp.broadcast_to(live_rows[:, None], (capacity, HEAD_DIM)).astype(jnp.float32)
    edge_keys = jnp.concatenate([left_keys, right_keys], 0)
    edge_values = jnp.concatenate([left_values, right_values], 0)
    acc, top, total = near_part(bias, query_norm, key_norm, value_rows, edge_keys, edge_values)
    return far_part(first, block, live, query_norm, acc, top, total, key_pieces, value_pieces)


def solution(mesh):
    in_specs = (
        P("tile", "head"),
        P("tile", "head"),
        P("tile", "head"),
        P("head"),
        P("head"),
        P("tile", None, "head"),
        P("tile", None, "head"),
        P("tile"),
        P("tile"),
        P("tile", None),
        P("tile"),
    )
    out_specs = P("tile", "head")
    return jax.shard_map(
        per_device, mesh=mesh, in_specs=in_specs, out_specs=out_specs, check_vma=False
    )
```

time: 326 us -> 168 us (0.52)
  waiting for transfers between devices: 149 us -> 56.2 us
  matrix products: 59.3 us -> 0 us
  starting transfers between devices: 14.8 us -> 58.9 us
  Pallas kernels: 0 us -> 30.4 us
  other arithmetic: 37.6 us -> 9.48 us
  local copies, waits for them, and re-layouts: 29.8 us -> 3.29 us
  loops' own time: 13.5 us -> 0 us
  between operations: 14.9 us -> 3.75 us
    all_gather x2 -> x0, waiting for transfers between devices: 145 us -> none  [the longest x1 82.1 us: per_device(): piece_values = lax.all_gather(mem_values, 'tile', axis=0, tiled=True)]
    dot_general x40 -> x0, matrix products: 59.3 us -> none  [the longest x20 30 us: one_head(): return jnp.dot(weights, head_values, preferred_element_type=jnp.float32)]
    ppermute x0 -> x30, waiting for transfers between devices: none -> 51.5 us  [the longest x7 49.6 us: per_device(): lane_keys.append(lax.ppermute(lane_keys[-1], 'tile', up))]
    ppermute x0 -> x30, starting transfers between devices: none -> 36.8 us  [the longest x8 15.7 us: per_device(): other_values = [lax.ppermute(piece, 'tile', swap) for piece in lane_values]]
    pallas_call x0 -> x2, Pallas kernels: none -> 30.4 us  [the longest x1 15.4 us: far_part(): pl.pallas_call(functools.partial(far_kernel, groups, per_step), grid=(hea...]
    concatenate x3, other arithmetic: 16.2 us -> 1.75 us  [the longest x1 1.02 us: per_device(): edge_values = jnp.concatenate([left_values, right_values], 0)]
    another operation x1 -> x0, loops' own time: 13.5 us -> none  [per_device(): outputs = lax.map(one_head, jnp.arange(heads_here, dtype=jnp.int32))]
    dynamic_slice x22 -> x2, local copies, waits for them, and re-layouts: 13.7 us -> 1.04 us  [tail(): lax.dynamic_slice_in_dim(jnp.concatenate([blank, rows], 0), my_length, ED...]
  transfers between devices with their start and end apart: 8 -> 36, of which waited for: 3 -> 13; matrix products, arithmetic and copies ran while one was open for 11% -> 7% of each run, Pallas kernels for 0% -> 9%
where the time goes in v1:
time: 168 us; the launch traced here: 167 us
  starting transfers between devices  58.9 us (35%)
  waiting for transfers between devices  56.2 us (33%)
  Pallas kernels  30.4 us (18%)
  other arithmetic  9.48 us (6%)
  blocking collectives  4.94 us (3%)
  between operations  3.75 us (2%)
  local copies, waits for them, and re-layouts  3.29 us (2%)
    ppermute x7, waiting for transfers between devices, per_device(): lane_keys.append(lax.ppermute(lane_keys[-1], 'tile', up))  49.6 us
    ppermute x6, starting transfers between devices, passed_along(): lax.ppermute(value, axis, [(source, source + steps) for source in range(f...  22.2 us
    ppermute x8, starting transfers between devices, per_device(): other_values = [lax.ppermute(piece, 'tile', swap) for piece in lane_values]  15.7 us
    pallas_call x1, Pallas kernels, far_part(): pl.pallas_call(functools.partial(far_kernel, groups, per_step), grid=(hea...  15.4 us
    pallas_call x1, Pallas kernels, near_part(): pl.pallas_call(functools.partial(near_kernel, per_step), grid=(heads // p...  15 us
    ppermute x7, starting transfers between devices, per_device(): lane_keys.append(lax.ppermute(lane_keys[-1], 'tile', up))  11.5 us
    ppermute x7, starting transfers between devices, per_device(): lane_values.append(lax.ppermute(lane_values[-1], 'tile', down))  7.68 us
    psum x1, blocking collectives, per_device(): lax.psum((row_squares(query_rows), row_squares(key_rows)), 'head')  4.94 us
  transfers between devices with their start and end apart: 36, of which 13 were waited for; matrix products, arithmetic and copies ran while one was open for 7% of the time, Pallas kernels for 9%

profile of v1, /device:TPU:0, one launch (start us, length us, event | category | flops | bytes accessed | tf_op | source)
XLA Modules:
  0.0 166.9 jit_solution(5852628028888926140)
XLA Ops:
  1.4 2.5 %collective-permute-start = (s32[2]{0:T(128)S(1)}, s32[2]{0:T(128)S(1)}, u32[]{:S(2)}, u32[]{:S(2)}) collective-permute-start(s32[2]{0:T(128)S(1)} %pad_add_fusion), channel_id=1, source_target_pairs={{0,2},{2,4},{4,6},{6,8},{8,10},{10,12},{12,14},{14,16},{16,18},{18... | collective-permute-start | bytes 32 | tf_op jit(solution)/shard_map/ppermute | solution.py:22
  3.9 2.6 %collective-permute-start.7 = (bf16[16,8,2560]{2,1,0:T(8,128)(2,1)}, bf16[16,8,2560]{2,1,0:T(8,128)(2,1)S(1)}, u32[]{:S(2)}, u32[]{:S(2)}) collective-permute-start(bf16[16,8,2560]{2,1,0:T(8,128)(2,1)} %refs_7_.1), channel_id=1, source_target_pairs={{0,8},{2,10},{8,16},{10,18},{16,24},{18,26},{24,28},{26,30},{28,20... | collective-permute-start | bytes 1966088 | tf_op jit(solution)/shard_map/ppermute | solution.py:224
  6.5 3.0 %fusion = (f32[384]{0:T(512)S(1)}, f32[384]{0:T(512)S(1)}) fusion(bf16[384,2560]{1,0:T(8,128)(2,1)} %param.11, bf16[384,2560]{1,0:T(8,128)(2,1)} %param.12), kind=kLoop, calls=%fused_computation.4 | loop fusion | flops 5897472 | bytes 3935232 | tf_op jit(solution)/shard_map/reduce_sum | solution.py:27
  9.5 4.9 %all-reduce.2 = (f32[384]{0:T(512)S(1)}, f32[384]{0:T(512)S(1)}) all-reduce(f32[384]{0:T(512)S(1)} %get-tuple-element.23, f32[384]{0:T(512)S(1)} %get-tuple-element.24), channel_id=1, replica_groups=mesh['tile'=16,'head'=2] {'head'}, use_global_device_ids=true, to_apply=%region_4.5 | all-reduce | flops 768 | bytes 6144 | tf_op jit(solution)/shard_map/psum | solution.py:245
  14.4 2.1 %fusion.5.k_ref = bf16[384,2560]{1,0:T(8,128)(2,1)S(1)} fusion(bf16[384,2560]{1,0:T(8,128)(2,1)} %param.12, f32[2560]{0:T(1024)S(1)} %copy-done.23, f32[384]{0:T(512)S(1)} %add_rsqrt_fusion), kind=kLoop, calls=%fused_computation.9 | loop fusion | flops 3932160 | bytes 3943936 | tf_op jit(solution)/shard_map/convert_element_type | solution.py:33
  16.5 4.8 %collective-permute-done.7.refs_9_ = bf16[16,8,2560]{2,1,0:T(8,128)(2,1)S(1)} collective-permute-done((bf16[16,8,2560]{2,1,0:T(8,128)(2,1)}, bf16[16,8,2560]{2,1,0:T(8,128)(2,1)S(1)}, u32[]{:S(2)}, u32[]{:S(2)}) %collective-permute-start.7) | collective-permute-done | bytes 655392 | tf_op jit(solution)/shard_map/ppermute | solution.py:224
  21.3 2.4 %collective-permute-start.9 = (bf16[16,8,2560]{2,1,0:T(8,128)(2,1)S(1)}, bf16[16,8,2560]{2,1,0:T(8,128)(2,1)S(1)}, u32[]{:S(2)}, u32[]{:S(2)}) collective-permute-start(bf16[16,8,2560]{2,1,0:T(8,128)(2,1)S(1)} %collective-permute-done.7.refs_9_), channel_id=1, source_target_pairs={{0,8},{2,10},{8,16},{10,18},{16,24},{18,26},{24,28},{26,30},{28,20... | collective-permute-start | bytes 1966088 | tf_op jit(solution)/shard_map/ppermute | solution.py:224
  24.3 2.2 %collective-permute-start.2 = (bf16[64,2560]{1,0:T(8,128)(2,1)S(1)}, bf16[64,2560]{1,0:T(8,128)(2,1)S(1)}, u32[]{:S(2)}, u32[]{:S(2)}) collective-permute-start(bf16[64,2560]{1,0:T(8,128)(2,1)S(1)} %get-tuple-element.17), channel_id=1, source_target_pairs={{0,2},{2,4},{4,6},{6,8},{8,10},{10,12},{12,14},{14,16},{16,18},{18... | collective-permute-start | bytes 983048 | tf_op jit(solution)/shard_map/ppermute | solution.py:22
  26.5 1.3 collective-permute-start.3
  27.8 11.3 %collective-permute-done.9.refs_11_ = bf16[16,8,2560]{2,1,0:T(8,128)(2,1)S(1)} collective-permute-done((bf16[16,8,2560]{2,1,0:T(8,128)(2,1)S(1)}, bf16[16,8,2560]{2,1,0:T(8,128)(2,1)S(1)}, u32[]{:S(2)}, u32[]{:S(2)}) %collective-permute-start.9) | collective-permute-done | bytes 655392 | tf_op jit(solution)/shard_map/ppermute | solution.py:224
  39.1 2.1 %collective-permute-start.11 = (bf16[16,8,2560]{2,1,0:T(8,128)(2,1)S(1)}, bf16[16,8,2560]{2,1,0:T(8,128)(2,1)}, u32[]{:S(2)}, u32[]{:S(2)}) collective-permute-start(bf16[16,8,2560]{2,1,0:T(8,128)(2,1)S(1)} %collective-permute-done.9.refs_11_), channel_id=1, source_target_pairs={{0,8},{2,10},{8,16},{10,18},{16,24},{18,26},{24,28},{26,30},{28,20... | collective-permute-start | bytes 1966088 | tf_op jit(solution)/shard_map/ppermute | solution.py:224
  41.2 0.7 collective-permute-start.24
  41.9 0.9 pad_dynamic-slice_fusion
  42.8 1.3 collective-permute-start.1
  44.1 1.7 %collective-permute-done.1 = s32[2]{0:T(128)S(1)} collective-permute-done((s32[2]{0:T(128)S(1)}, s32[2]{0:T(128)S(1)}, u32[]{:S(2)}, u32[]{:S(2)}) %collective-permute-start.1) | collective-permute-done | bytes 40 | tf_op jit(solution)/shard_map/ppermute | solution.py:22
  45.8 13.6 %collective-permute-start.4 = (bf16[64,2560]{1,0:T(8,128)(2,1)}, bf16[64,2560]{1,0:T(8,128)(2,1)}, u32[]{:S(2)}, u32[]{:S(2)}) collective-permute-start(bf16[64,2560]{1,0:T(8,128)(2,1)} %get-tuple-element.15), channel_id=1, source_target_pairs={{0,2},{2,4},{4,6},{6,8},{8,10},{10,12},{12,14},{14,16},{16,18},{18... | collective-permute-start | bytes 983048 | tf_op jit(solution)/shard_map/ppermute | solution.py:22
  60.1 0.8 collective-permute-start.13
  60.9 1.7 %collective-permute-start.25 = (bf16[16,8,2560]{2,1,0:T(8,128)(2,1)}, bf16[16,8,2560]{2,1,0:T(8,128)(2,1)}, u32[]{:S(2)}, u32[]{:S(2)}) collective-permute-start(bf16[16,8,2560]{2,1,0:T(8,128)(2,1)} %collective-permute-done.24.refs_33_), channel_id=1, source_target_pairs={{0,4},{2,6},{8,0},{10,2},{16,8},{18,10},{24,16},{26,18},{28,24},{3... | collective-permute-start | bytes 1966088 | tf_op jit(solution)/shard_map/ppermute | solution.py:225
  62.7 1.3 collective-permute-start.5
  64.0 2.9 %collective-permute-done.5 = bf16[64,2560]{1,0:T(8,128)(2,1)S(1)} collective-permute-done((bf16[64,2560]{1,0:T(8,128)(2,1)}, bf16[64,2560]{1,0:T(8,128)(2,1)S(1)}, u32[]{:S(2)}, u32[]{:S(2)}) %collective-permute-start.5) | collective-permute-done | bytes 327712 | tf_op jit(solution)/shard_map/ppermute | solution.py:22
  66.9 14.1 %collective-permute-start.35 = (bf16[16,8,2560]{2,1,0:T(8,128)(2,1)}, bf16[16,8,2560]{2,1,0:T(8,128)(2,1)S(1)}, u32[]{:S(2)}, u32[]{:S(2)}) collective-permute-start(bf16[16,8,2560]{2,1,0:T(8,128)(2,1)} %collective-permute-done.22.refs_37_), channel_id=1, source_target_pairs={{0,2},{2,0},{4,6},{6,4},{8,10},{10,8},{12,14},{14,12},{16,18},{18,... | collective-permute-start | bytes 1966088 | tf_op jit(solution)/shard_map/ppermute | solution.py:227
  81.6 2.0 %collective-permute-start.26 = (bf16[16,8,2560]{2,1,0:T(8,128)(2,1)}, bf16[16,8,2560]{2,1,0:T(8,128)(2,1)S(1)}, u32[]{:S(2)}, u32[]{:S(2)}) collective-permute-start(bf16[16,8,2560]{2,1,0:T(8,128)(2,1)} %collective-permute-done.25.refs_31_), channel_id=1, source_target_pairs={{0,4},{2,6},{8,0},{10,2},{16,8},{18,10},{24,16},{26,18},{28,24},{3... | collective-permute-start | bytes 1966088 | tf_op jit(solution)/shard_map/ppermute | solution.py:225
  85.3 13.3 %collective-permute-done.15.refs_17_ = bf16[16,8,2560]{2,1,0:T(8,128)(2,1)S(1)} collective-permute-done((bf16[16,8,2560]{2,1,0:T(8,128)(2,1)}, bf16[16,8,2560]{2,1,0:T(8,128)(2,1)S(1)}, u32[]{:S(2)}, u32[]{:S(2)}) %collective-permute-start.15) | collective-permute-done | bytes 655392 | tf_op jit(solution)/shard_map/ppermute | solution.py:224
  98.5 3.6 %collective-permute-start.17 = (bf16[16,8,2560]{2,1,0:T(8,128)(2,1)S(1)}, bf16[16,8,2560]{2,1,0:T(8,128)(2,1)S(1)}, u32[]{:S(2)}, u32[]{:S(2)}) collective-permute-start(bf16[16,8,2560]{2,1,0:T(8,128)(2,1)S(1)} %collective-permute-done.15.refs_17_), channel_id=1, source_target_pairs={{0,8},{2,10},{8,16},{10,18},{16,24},{18,26},{24,28},{26,30},{28,20... | collective-permute-start | bytes 1966088 | tf_op jit(solution)/shard_map/ppermute | solution.py:224
  102.5 1.5 collective-permute-start.27
  104.0 2.1 %fusion.2.q_ref.refs_3_ = bf16[384,2560]{1,0:T(8,128)(2,1)S(1)} fusion(bf16[384,2560]{1,0:T(8,128)(2,1)} %param.11, f32[2560]{0:T(1024)S(1)} %broadcast_multiply_fusion, f32[384]{0:T(512)S(1)} %add_rsqrt_fusion.1), kind=kLoop, calls=%fused_computation.6 | loop fusion | flops 3932160 | bytes 3943936 | tf_op jit(solution)/shard_map/convert_element_type | solution.py:33
  106.9 11.5 %collective-permute-done.17.refs_19_ = bf16[16,8,2560]{2,1,0:T(8,128)(2,1)S(1)} collective-permute-done((bf16[16,8,2560]{2,1,0:T(8,128)(2,1)S(1)}, bf16[16,8,2560]{2,1,0:T(8,128)(2,1)S(1)}, u32[]{:S(2)}, u32[]{:S(2)}) %collective-permute-start.17) | collective-permute-done | bytes 655392 | tf_op jit(solution)/shard_map/ppermute | solution.py:224
  118.8 1.7 collective-permute-start.28
  125.3 8.7 %collective-permute-done.19.refs_21_ = bf16[16,8,2560]{2,1,0:T(8,128)(2,1)S(1)} collective-permute-done((bf16[16,8,2560]{2,1,0:T(8,128)(2,1)S(1)}, bf16[16,8,2560]{2,1,0:T(8,128)(2,1)S(1)}, u32[]{:S(2)}, u32[]{:S(2)}) %collective-permute-start.19) | collective-permute-done | bytes 655392 | tf_op jit(solution)/shard_map/ppermute | solution.py:224
  134.6 1.0 pad_maximum_fusion.1.ev_ref
  135.6 15.0 %near_part.1 = (f32[384,2560]{1,0:T(8,128)}, f32[384,128]{1,0:T(8,128)S(1)}, f32[384,128]{1,0:T(8,128)S(1)}) custom-call(f32[1,512]{1,0:T(1,128)S(1)} %add_select_fusion.bias_ref, bf16[384,2560]{1,0:T(8,128)(2,1)S(1)} %fusion.2.q_ref.refs_3_, bf16[384,2560]{1,0:T(8,128)(2,1)S(1)} %fusion.5.k_ref, bf16[384,2560]{1,0:T(8,128)(2,1)} %v_ref.1, ...), custom_call_target="tpu_custom_call" | custom-call | flops 2013265920 | bytes 9830400 | tf_op jit(solution)/shard_map/near_part/pallas_call | solution.py:97
  151.5 15.4 %far_part.1 = bf16[384,2560]{1,0:T(8,128)(2,1)} custom-call(s32[17]{0:T(128)S(1)} %convert_reduce_fusion.1.refs_0_, s32[64]{0:T(128)S(1)} %select_reduce_fusion.refs_1_, f32[384,128]{1,0:T(8,128)S(1)} %broadcast_in_dim.24.refs_2_, bf16[384,2560]{1,0:T(8,128)(2,1)} %copy-done, f32[384,2560]{1,0:T(8,128)} %get-tuple-element.8.refs_4_, ...), custom_call_target="tpu_custom_call" | custom-call | flops 2013265920 | bytes 13107200 | tf_op jit(solution)/shard_map/far_part/pallas_call | solution.py:178
  (119 shorter events, 9.1 us)
Async XLA Ops:
  1.4 41.5 %collective-permute-start = (s32[2]{0:T(128)S(1)}, s32[2]{0:T(128)S(1)}, u32[]{:S(2)}, u32[]{:S(2)}) collective-permute-start(s32[2]{0:T(128)S(1)} %pad_add_fusion), channel_id=1, source_target_pairs={{0,2},{2,4},{4,6},{6,8},{8,10},{10,12},{12,14},{14,16},{16,18},{18... | collective-permute-start | bytes 32 | tf_op jit(solution)/shard_map/ppermute | solution.py:22
  3.9 17.5 %collective-permute-start.7 = (bf16[16,8,2560]{2,1,0:T(8,128)(2,1)}, bf16[16,8,2560]{2,1,0:T(8,128)(2,1)S(1)}, u32[]{:S(2)}, u32[]{:S(2)}) collective-permute-start(bf16[16,8,2560]{2,1,0:T(8,128)(2,1)} %refs_7_.1), channel_id=1, source_target_pairs={{0,8},{2,10},{8,16},{10,18},{16,24},{18,26},{24,28},{26,30},{28,20... | collective-permute-start | bytes 1966088 | tf_op jit(solution)/shard_map/ppermute | solution.py:224
  6.5 17.6 %collective-permute-start.22 = (bf16[16,8,2560]{2,1,0:T(8,128)(2,1)}, bf16[16,8,2560]{2,1,0:T(8,128)(2,1)}, u32[]{:S(2)}, u32[]{:S(2)}) collective-permute-start(bf16[16,8,2560]{2,1,0:T(8,128)(2,1)} %refs_23_.1), channel_id=1, source_target_pairs={{0,4},{2,6},{8,0},{10,2},{16,8},{18,10},{24,16},{26,18},{28,24},{3... | collective-permute-start | bytes 1966088 | tf_op jit(solution)/shard_map/ppermute | solution.py:225
  21.3 17.8 %collective-permute-start.9 = (bf16[16,8,2560]{2,1,0:T(8,128)(2,1)S(1)}, bf16[16,8,2560]{2,1,0:T(8,128)(2,1)S(1)}, u32[]{:S(2)}, u32[]{:S(2)}) collective-permute-start(bf16[16,8,2560]{2,1,0:T(8,128)(2,1)S(1)} %collective-permute-done.7.refs_9_), channel_id=1, source_target_pairs={{0,8},{2,10},{8,16},{10,18},{16,24},{18,26},{24,28},{26,30},{28,20... | collective-permute-start | bytes 1966088 | tf_op jit(solution)/shard_map/ppermute | solution.py:224
  24.1 17.0 %collective-permute-start.23 = (bf16[16,8,2560]{2,1,0:T(8,128)(2,1)}, bf16[16,8,2560]{2,1,0:T(8,128)(2,1)S(1)}, u32[]{:S(2)}, u32[]{:S(2)}) collective-permute-start(bf16[16,8,2560]{2,1,0:T(8,128)(2,1)} %collective-permute-done.22.refs_37_), channel_id=1, source_target_pairs={{0,4},{2,6},{8,0},{10,2},{16,8},{18,10},{24,16},{26,18},{28,24},{3... | collective-permute-start | bytes 1966088 | tf_op jit(solution)/shard_map/ppermute | solution.py:225
  24.3 35.2 %collective-permute-start.2 = (bf16[64,2560]{1,0:T(8,128)(2,1)S(1)}, bf16[64,2560]{1,0:T(8,128)(2,1)S(1)}, u32[]{:S(2)}, u32[]{:S(2)}) collective-permute-start(bf16[64,2560]{1,0:T(8,128)(2,1)S(1)} %get-tuple-element.17), channel_id=1, source_target_pairs={{0,2},{2,4},{4,6},{6,8},{8,10},{10,12},{12,14},{14,16},{16,18},{18... | collective-permute-start | bytes 983048 | tf_op jit(solution)/shard_map/ppermute | solution.py:22
  26.5 33.0 %collective-permute-start.3 = (bf16[64,2560]{1,0:T(8,128)(2,1)S(1)}, bf16[64,2560]{1,0:T(8,128)(2,1)S(1)}, u32[]{:S(2)}, u32[]{:S(2)}) collective-permute-start(bf16[64,2560]{1,0:T(8,128)(2,1)S(1)} %get-tuple-element.18), channel_id=1, source_target_pairs={{2,0},{4,2},{6,4},{8,6},{10,8},{12,10},{14,12},{16,14},{18,16},{20... | collective-permute-start | bytes 983048 | tf_op jit(solution)/shard_map/ppermute | solution.py:22
  39.1 21.0 %collective-permute-start.11 = (bf16[16,8,2560]{2,1,0:T(8,128)(2,1)S(1)}, bf16[16,8,2560]{2,1,0:T(8,128)(2,1)}, u32[]{:S(2)}, u32[]{:S(2)}) collective-permute-start(bf16[16,8,2560]{2,1,0:T(8,128)(2,1)S(1)} %collective-permute-done.9.refs_11_), channel_id=1, source_target_pairs={{0,8},{2,10},{8,16},{10,18},{16,24},{18,26},{24,28},{26,30},{28,20... | collective-permute-start | bytes 1966088 | tf_op jit(solution)/shard_map/ppermute | solution.py:224
  41.2 19.7 %collective-permute-start.24 = (bf16[16,8,2560]{2,1,0:T(8,128)(2,1)S(1)}, bf16[16,8,2560]{2,1,0:T(8,128)(2,1)}, u32[]{:S(2)}, u32[]{:S(2)}) collective-permute-start(bf16[16,8,2560]{2,1,0:T(8,128)(2,1)S(1)} %collective-permute-done.23.refs_35_), channel_id=1, source_target_pairs={{0,4},{2,6},{8,0},{10,2},{16,8},{18,10},{24,16},{26,18},{28,24},{3... | collective-permute-start | bytes 1966088 | tf_op jit(solution)/shard_map/ppermute | solution.py:225
  45.8 16.8 %collective-permute-start.4 = (bf16[64,2560]{1,0:T(8,128)(2,1)}, bf16[64,2560]{1,0:T(8,128)(2,1)}, u32[]{:S(2)}, u32[]{:S(2)}) collective-permute-start(bf16[64,2560]{1,0:T(8,128)(2,1)} %get-tuple-element.15), channel_id=1, source_target_pairs={{0,2},{2,4},{4,6},{6,8},{8,10},{10,12},{12,14},{14,16},{16,18},{18... | collective-permute-start | bytes 983048 | tf_op jit(solution)/shard_map/ppermute | solution.py:22
  59.5 21.6 %collective-permute-start.21 = (bf16[16,8,2560]{2,1,0:T(8,128)(2,1)}, bf16[16,8,2560]{2,1,0:T(8,128)(2,1)}, u32[]{:S(2)}, u32[]{:S(2)}) collective-permute-start(bf16[16,8,2560]{2,1,0:T(8,128)(2,1)} %refs_23_.1), channel_id=1, source_target_pairs={{0,2},{2,0},{4,6},{6,4},{8,10},{10,8},{12,14},{14,12},{16,18},{18,... | collective-permute-start | bytes 1966088 | tf_op jit(solution)/shard_map/ppermute | solution.py:227
  59.5 21.6 %collective-permute-start.6 = (bf16[16,8,2560]{2,1,0:T(8,128)(2,1)S(1)}, bf16[16,8,2560]{2,1,0:T(8,128)(2,1)}, u32[]{:S(2)}, u32[]{:S(2)}) collective-permute-start(bf16[16,8,2560]{2,1,0:T(8,128)(2,1)S(1)} %copy-done.1), channel_id=1, source_target_pairs={{0,2},{2,0},{4,6},{6,4},{8,10},{10,8},{12,14},{14,12},{16,18},{18,... | collective-permute-start | bytes 1966088 | tf_op jit(solution)/shard_map/ppermute | solution.py:226
  60.1 21.5 %collective-permute-start.13 = (bf16[16,8,2560]{2,1,0:T(8,128)(2,1)}, bf16[16,8,2560]{2,1,0:T(8,128)(2,1)}, u32[]{:S(2)}, u32[]{:S(2)}) collective-permute-start(bf16[16,8,2560]{2,1,0:T(8,128)(2,1)} %collective-permute-done.11.refs_13_), channel_id=1, source_target_pairs={{0,8},{2,10},{8,16},{10,18},{16,24},{18,26},{24,28},{26,30},{28,20... | collective-permute-start | bytes 1966088 | tf_op jit(solution)/shard_map/ppermute | solution.py:224
  60.9 20.7 %collective-permute-start.25 = (bf16[16,8,2560]{2,1,0:T(8,128)(2,1)}, bf16[16,8,2560]{2,1,0:T(8,128)(2,1)}, u32[]{:S(2)}, u32[]{:S(2)}) collective-permute-start(bf16[16,8,2560]{2,1,0:T(8,128)(2,1)} %collective-permute-done.24.refs_33_), channel_id=1, source_target_pairs={{0,4},{2,6},{8,0},{10,2},{16,8},{18,10},{24,16},{26,18},{28,24},{3... | collective-permute-start | bytes 1966088 | tf_op jit(solution)/shard_map/ppermute | solution.py:225
  66.9 17.1 %collective-permute-start.35 = (bf16[16,8,2560]{2,1,0:T(8,128)(2,1)}, bf16[16,8,2560]{2,1,0:T(8,128)(2,1)S(1)}, u32[]{:S(2)}, u32[]{:S(2)}) collective-permute-start(bf16[16,8,2560]{2,1,0:T(8,128)(2,1)} %collective-permute-done.22.refs_37_), channel_id=1, source_target_pairs={{0,2},{2,0},{4,6},{6,4},{8,10},{10,8},{12,14},{14,12},{16,18},{18,... | collective-permute-start | bytes 1966088 | tf_op jit(solution)/shard_map/ppermute | solution.py:227
  81.6 16.9 %collective-permute-start.15 = (bf16[16,8,2560]{2,1,0:T(8,128)(2,1)}, bf16[16,8,2560]{2,1,0:T(8,128)(2,1)S(1)}, u32[]{:S(2)}, u32[]{:S(2)}) collective-permute-start(bf16[16,8,2560]{2,1,0:T(8,128)(2,1)} %collective-permute-done.13.refs_15_), channel_id=1, source_target_pairs={{0,8},{2,10},{8,16},{10,18},{16,24},{18,26},{24,28},{26,30},{28,20... | collective-permute-start | bytes 1966088 | tf_op jit(solution)/shard_map/ppermute | solution.py:224
  81.6 20.9 %collective-permute-start.26 = (bf16[16,8,2560]{2,1,0:T(8,128)(2,1)}, bf16[16,8,2560]{2,1,0:T(8,128)(2,1)S(1)}, u32[]{:S(2)}, u32[]{:S(2)}) collective-permute-start(bf16[16,8,2560]{2,1,0:T(8,128)(2,1)} %collective-permute-done.25.refs_31_), channel_id=1, source_target_pairs={{0,4},{2,6},{8,0},{10,2},{16,8},{18,10},{24,16},{26,18},{28,24},{3... | collective-permute-start | bytes 1966088 | tf_op jit(solution)/shard_map/ppermute | solution.py:225
  84.0 22.1 %collective-permute-start.34 = (bf16[16,8,2560]{2,1,0:T(8,128)(2,1)}, bf16[16,8,2560]{2,1,0:T(8,128)(2,1)S(1)}, u32[]{:S(2)}, u32[]{:S(2)}) collective-permute-start(bf16[16,8,2560]{2,1,0:T(8,128)(2,1)} %copy-done.5), channel_id=1, source_target_pairs={{0,2},{2,0},{4,6},{6,4},{8,10},{10,8},{12,14},{14,12},{16,18},{18,... | collective-permute-start | bytes 1966088 | tf_op jit(solution)/shard_map/ppermute | solution.py:227
  84.6 21.7 %collective-permute-start.12 = (bf16[16,8,2560]{2,1,0:T(8,128)(2,1)}, bf16[16,8,2560]{2,1,0:T(8,128)(2,1)S(1)}, u32[]{:S(2)}, u32[]{:S(2)}) collective-permute-start(bf16[16,8,2560]{2,1,0:T(8,128)(2,1)} %collective-permute-done.11.refs_13_), channel_id=1, source_target_pairs={{0,2},{2,0},{4,6},{6,4},{8,10},{10,8},{12,14},{14,12},{16,18},{18,... | collective-permute-start | bytes 1966088 | tf_op jit(solution)/shard_map/ppermute | solution.py:226
  84.9 21.8 %collective-permute-start.33 = (bf16[16,8,2560]{2,1,0:T(8,128)(2,1)}, bf16[16,8,2560]{2,1,0:T(8,128)(2,1)S(1)}, u32[]{:S(2)}, u32[]{:S(2)}) collective-permute-start(bf16[16,8,2560]{2,1,0:T(8,128)(2,1)} %collective-permute-done.24.refs_33_), channel_id=1, source_target_pairs={{0,2},{2,0},{4,6},{6,4},{8,10},{10,8},{12,14},{14,12},{16,18},{18,... | collective-permute-start | bytes 1966088 | tf_op jit(solution)/shard_map/ppermute | solution.py:227
  98.5 19.9 %collective-permute-start.17 = (bf16[16,8,2560]{2,1,0:T(8,128)(2,1)S(1)}, bf16[16,8,2560]{2,1,0:T(8,128)(2,1)S(1)}, u32[]{:S(2)}, u32[]{:S(2)}) collective-permute-start(bf16[16,8,2560]{2,1,0:T(8,128)(2,1)S(1)} %collective-permute-done.15.refs_17_), channel_id=1, source_target_pairs={{0,8},{2,10},{8,16},{10,18},{16,24},{18,26},{24,28},{26,30},{28,20... | collective-permute-start | bytes 1966088 | tf_op jit(solution)/shard_map/ppermute | solution.py:224
  102.5 16.3 %collective-permute-start.27 = (bf16[16,8,2560]{2,1,0:T(8,128)(2,1)S(1)}, bf16[16,8,2560]{2,1,0:T(8,128)(2,1)S(1)}, u32[]{:S(2)}, u32[]{:S(2)}) collective-permute-start(bf16[16,8,2560]{2,1,0:T(8,128)(2,1)S(1)} %collective-permute-done.26.refs_29_), channel_id=1, source_target_pairs={{0,4},{2,6},{8,0},{10,2},{16,8},{18,10},{24,16},{26,18},{28,24},{3... | collective-permute-start | bytes 1966088 | tf_op jit(solution)/shard_map/ppermute | solution.py:225
  106.1 18.5 %collective-permute-start.14 = (bf16[16,8,2560]{2,1,0:T(8,128)(2,1)}, bf16[16,8,2560]{2,1,0:T(8,128)(2,1)S(1)}, u32[]{:S(2)}, u32[]{:S(2)}) collective-permute-start(bf16[16,8,2560]{2,1,0:T(8,128)(2,1)} %collective-permute-done.13.refs_15_), channel_id=1, source_target_pairs={{0,2},{2,0},{4,6},{6,4},{8,10},{10,8},{12,14},{14,12},{16,18},{18,... | collective-permute-start | bytes 1966088 | tf_op jit(solution)/shard_map/ppermute | solution.py:226
  106.2 18.5 %collective-permute-start.32 = (bf16[16,8,2560]{2,1,0:T(8,128)(2,1)}, bf16[16,8,2560]{2,1,0:T(8,128)(2,1)S(1)}, u32[]{:S(2)}, u32[]{:S(2)}) collective-permute-start(bf16[16,8,2560]{2,1,0:T(8,128)(2,1)} %collective-permute-done.25.refs_31_), channel_id=1, source_target_pairs={{0,2},{2,0},{4,6},{6,4},{8,10},{10,8},{12,14},{14,12},{16,18},{18,... | collective-permute-start | bytes 1966088 | tf_op jit(solution)/shard_map/ppermute | solution.py:227
  106.7 18.5 %collective-permute-start.16 = (bf16[16,8,2560]{2,1,0:T(8,128)(2,1)S(1)}, bf16[16,8,2560]{2,1,0:T(8,128)(2,1)S(1)}, u32[]{:S(2)}, u32[]{:S(2)}) collective-permute-start(bf16[16,8,2560]{2,1,0:T(8,128)(2,1)S(1)} %collective-permute-done.15.refs_17_), channel_id=1, source_target_pairs={{0,2},{2,0},{4,6},{6,4},{8,10},{10,8},{12,14},{14,12},{16,18},{18,... | collective-permute-start | bytes 1966088 | tf_op jit(solution)/shard_map/ppermute | solution.py:226
  118.4 15.6 %collective-permute-start.19 = (bf16[16,8,2560]{2,1,0:T(8,128)(2,1)S(1)}, bf16[16,8,2560]{2,1,0:T(8,128)(2,1)S(1)}, u32[]{:S(2)}, u32[]{:S(2)}) collective-permute-start(bf16[16,8,2560]{2,1,0:T(8,128)(2,1)S(1)} %collective-permute-done.17.refs_19_), channel_id=1, source_target_pairs={{0,8},{2,10},{8,16},{10,18},{16,24},{18,26},{24,28},{26,30},{28,20... | collective-permute-start | bytes 1966088 | tf_op jit(solution)/shard_map/ppermute | solution.py:224
  118.8 15.5 %collective-permute-start.28 = (bf16[16,8,2560]{2,1,0:T(8,128)(2,1)S(1)}, bf16[16,8,2560]{2,1,0:T(8,128)(2,1)}, u32[]{:S(2)}, u32[]{:S(2)}) collective-permute-start(bf16[16,8,2560]{2,1,0:T(8,128)(2,1)S(1)} %collective-permute-done.27.refs_27_), channel_id=1, source_target_pairs={{0,4},{2,6},{8,0},{10,2},{16,8},{18,10},{24,16},{26,18},{28,24},{3... | collective-permute-start | bytes 1966088 | tf_op jit(solution)/shard_map/ppermute | solution.py:225
  124.6 26.0 %collective-permute-start.31 = (bf16[16,8,2560]{2,1,0:T(8,128)(2,1)S(1)}, bf16[16,8,2560]{2,1,0:T(8,128)(2,1)}, u32[]{:S(2)}, u32[]{:S(2)}) collective-permute-start(bf16[16,8,2560]{2,1,0:T(8,128)(2,1)S(1)} %collective-permute-done.26.refs_29_), channel_id=1, source_target_pairs={{0,2},{2,0},{4,6},{6,4},{8,10},{10,8},{12,14},{14,12},{16,18},{18,... | collective-permute-start | bytes 1966088 | tf_op jit(solution)/shard_map/ppermute | solution.py:227
  124.7 25.9 %collective-permute-start.18 = (bf16[16,8,2560]{2,1,0:T(8,128)(2,1)S(1)}, bf16[16,8,2560]{2,1,0:T(8,128)(2,1)}, u32[]{:S(2)}, u32[]{:S(2)}) collective-permute-start(bf16[16,8,2560]{2,1,0:T(8,128)(2,1)S(1)} %collective-permute-done.17.refs_19_), channel_id=1, source_target_pairs={{0,2},{2,0},{4,6},{6,4},{8,10},{10,8},{12,14},{14,12},{16,18},{18,... | collective-permute-start | bytes 1966088 | tf_op jit(solution)/shard_map/ppermute | solution.py:226
  125.2 25.4 %collective-permute-start.30 = (bf16[16,8,2560]{2,1,0:T(8,128)(2,1)S(1)}, bf16[16,8,2560]{2,1,0:T(8,128)(2,1)S(1)}, u32[]{:S(2)}, u32[]{:S(2)}) collective-permute-start(bf16[16,8,2560]{2,1,0:T(8,128)(2,1)S(1)} %collective-permute-done.27.refs_27_), channel_id=1, source_target_pairs={{0,2},{2,0},{4,6},{6,4},{8,10},{10,8},{12,14},{14,12},{16,18},{18,... | collective-permute-start | bytes 1966088 | tf_op jit(solution)/shard_map/ppermute | solution.py:227
  134.0 16.7 %collective-permute-start.20 = (bf16[16,8,2560]{2,1,0:T(8,128)(2,1)S(1)}, bf16[16,8,2560]{2,1,0:T(8,128)(2,1)}, u32[]{:S(2)}, u32[]{:S(2)}) collective-permute-start(bf16[16,8,2560]{2,1,0:T(8,128)(2,1)S(1)} %collective-permute-done.19.refs_21_), channel_id=1, source_target_pairs={{0,2},{2,0},{4,6},{6,4},{8,10},{10,8},{12,14},{14,12},{16,18},{18,... | collective-permute-start | bytes 1966088 | tf_op jit(solution)/shard_map/ppermute | solution.py:226
  134.3 16.4 %collective-permute-start.29 = (bf16[16,8,2560]{2,1,0:T(8,128)(2,1)}, bf16[16,8,2560]{2,1,0:T(8,128)(2,1)}, u32[]{:S(2)}, u32[]{:S(2)}) collective-permute-start(bf16[16,8,2560]{2,1,0:T(8,128)(2,1)} %collective-permute-done.28.refs_25_), channel_id=1, source_target_pairs={{0,2},{2,0},{4,6},{6,4},{8,10},{10,8},{12,14},{14,12},{16,18},{18,... | collective-permute-start | bytes 1966088 | tf_op jit(solution)/shard_map/ppermute | solution.py:227
  (30 other events, 727.4 us)

commit v2 on v0

v2 whole, which is shorter than its diff:
```python
import functools
import math

import jax
import jax.numpy as jnp
from jax import lax
from jax.experimental import pallas as pl
from jax.experimental.pallas import tpu as pltpu
from jax.sharding import PartitionSpec as P

HEAD_DIM = 128
WIDTH = 5120
EDGE = 64
EPSILON = 1e-06
HIDDEN = -1e30
VMEM_BYTES = 48 * 1024 * 1024


def passed_along(value, axis, steps):
    count = lax.axis_size(axis)
    first, last = (max(0, -steps), min(count, count - steps))
    return lax.ppermute(value, axis, [(source, source + steps) for source in range(first, last)])


def row_squares(raw_rows):
    rows32 = raw_rows.astype(jnp.float32)
    return jnp.sum(rows32 * rows32, axis=1)


def normalize(raw_rows, totals, gain):
    rows32 = raw_rows.astype(jnp.float32)
    factor = lax.rsqrt(totals / WIDTH + EPSILON)
    return (rows32 * factor[:, None] * gain).astype(jnp.bfloat16)


def chip_position(tile, levels):
    level, row = tile // 4, (tile // 2) % 2
    return level + row * (2 * levels - 1 - 2 * level)


def ring_pairs(count, step):
    levels = count // 4
    at = {(chip_position(t, levels), t % 2): t for t in range(count)}
    places = 2 * levels
    return [(at[p, c], at[(p + step) % places, c]) for p in range(places) for c in range(2)]


def across_t(first, second):
    return lax.dot_general(first, second, (((1,), (1,)), ((), ())), preferred_element_type=jnp.float32)


def down_rows(first, second):
    return lax.dot_general(first, second, (((0,), (0,)), ((), ())), preferred_element_type=jnp.float32)


def attend(query, parts, before):
    scores = []
    for keys, _, bias in parts:
        wide = jnp.concatenate([bias] * (query.shape[0] // bias.shape[1]), axis=1)
        scores.append(across_t(keys, query) + wide)
    top = functools.reduce(jnp.maximum, [jnp.max(part, axis=0, keepdims=True) for part in scores])
    if before is not None:
        top = jnp.maximum(top, before[0])
    total, acc = jnp.float32(0.0), jnp.float32(0.0)
    for part, (_, values, _) in zip(scores, parts):
        weights = jnp.exp2(part - top)
        total = total + jnp.sum(weights, axis=0, keepdims=True)
        acc = acc + down_rows(values, weights.astype(jnp.bfloat16))
    if before is not None:
        kept = jnp.exp2(before[0] - top)
        total = total + kept * before[1]
        acc = acc + kept * before[2]
    return top, total, acc


def store_sums(sums, j, columns, top_ref, sum_ref, acc_ref):
    top, total, acc = sums
    top_ref[j] = jnp.broadcast_to(top, top_ref.shape[1:])
    sum_ref[j] = jnp.broadcast_to(total, sum_ref.shape[1:])
    acc_ref[columns, :] = acc


def near_kernel(per_step, bias_ref, q_ref, k_ref, v_ref, ek_ref, ev_ref, top_ref, sum_ref, acc_ref):
    own = k_ref.shape[0]
    for j in range(per_step):
        columns = slice(j * HEAD_DIM, (j + 1) * HEAD_DIM)
        parts = [
            (k_ref[:, columns], v_ref[:, columns], bias_ref[:own, :]),
            (ek_ref[:, columns], ev_ref[:, columns], bias_ref[own:, :]),
        ]
        sums = attend(q_ref[:, columns], parts, None)
        store_sums(sums, j, columns, top_ref, sum_ref, acc_ref)


def specs(width, rows):
    heads = width // HEAD_DIM
    per_step = 2 if heads % 2 == 0 else 1
    wide = per_step * HEAD_DIM
    stat = jax.ShapeDtypeStruct((heads, 8, rows), jnp.float32)
    stat_spec = pl.BlockSpec((per_step, 8, rows), lambda i: (i, 0, 0))
    acc = jax.ShapeDtypeStruct((width, rows), jnp.float32)
    acc_spec = pl.BlockSpec((wide, rows), lambda i: (i, 0))
    return heads, per_step, [stat, stat, acc], [stat_spec, stat_spec, acc_spec]


def columns_of(array, per_step):
    return pl.BlockSpec((array.shape[0], per_step * HEAD_DIM), lambda i: (0, i))


def whole(array):
    return pl.BlockSpec(array.shape, lambda i: (0, 0))


def cost(rows, seen, width):
    return pl.CostEstimate(
        flops=4 * rows * seen * width,
        bytes_accessed=10 * rows * width,
        transcendentals=rows * seen * width // HEAD_DIM,
    )


def near_part(bias, query, keys, values, edge_keys, edge_values):
    rows, width = query.shape
    heads, per_step, shapes, out_specs = specs(width, rows)
    arrays = (query, keys, values, edge_keys, edge_values)
    return pl.pallas_call(
        functools.partial(near_kernel, per_step),
        grid=(heads // per_step,),
        in_specs=[whole(bias)] + [columns_of(array, per_step) for array in arrays],
        out_specs=out_specs,
        out_shape=shapes,
        compiler_params=pltpu.CompilerParams(vmem_limit_bytes=VMEM_BYTES),
        cost_estimate=cost(rows, bias.shape[0], width),
        name="near_part",
    )(bias, *arrays)


def far_kernel(groups, per_step, last, *refs):
    first_ref, block_ref, bias_ref, q_ref, before_top, before_sum, before_acc = refs[:7]
    refs = refs[7:]
    if last:
        live_ref, refs = refs[0], refs[1:]
    *out_refs, keys, values, sems = refs[len(refs) - (4 if last else 6) :]
    pieces = refs[: len(refs) - len(out_refs) - 3]
    joined = len(pieces) == groups
    key_pieces, value_pieces = pieces[:groups], pieces if joined else pieces[groups:]
    offset = pieces[0].shape[0] // 2 if joined else 0
    step = pl.program_id(0)
    slots, tokens = keys.shape[:2]

    @pl.when(step == 0)
    def _():
        start = first_ref[0]

        def fetch_from(g):
            def fetch(slot, carry):
                block = block_ref[slot]
                to = slot - start
                pltpu.make_async_copy(key_pieces[g].at[block], keys.at[to], sems.at[0]).start()
                pltpu.make_async_copy(value_pieces[g].at[block + offset], values.at[to], sems.at[1]).start()
                return carry

            return fetch

        for g in range(groups):
            lax.fori_loop(first_ref[g], first_ref[g + 1], fetch_from(g), 0)
        lax.fori_loop(first_ref[groups], start + slots, fetch_from(0), 0)
        pltpu.make_async_copy(keys, keys, sems.at[0]).wait()
        pltpu.make_async_copy(values, values, sems.at[1]).wait()

    for j in range(per_step):
        columns = slice(j * HEAD_DIM, (j + 1) * HEAD_DIM)
        place = pl.ds(pl.multiple_of((step * per_step + j) * HEAD_DIM, HEAD_DIM), HEAD_DIM)

        def flat(array):
            block = array[:, :, place].astype(jnp.float32)
            return block.reshape(slots * tokens, HEAD_DIM).astype(jnp.bfloat16)

        before = (before_top[j, :1, :], before_sum[j, :1, :], before_acc[columns, :])
        sums = attend(q_ref[:, columns], [(flat(keys), flat(values), bias_ref[...])], before)
        if last:
            result = jnp.where(live_ref[...] > 0.0, sums[2] / sums[1], 0.0)
            out_refs[0][:, columns] = result.T.astype(out_refs[0].dtype)
        else:
            store_sums(sums, j, columns, *out_refs)


def far_part(name, first, block, slots, query, before, pieces, live=None):
    rows, width = query.shape
    heads, per_step, shapes, out_specs = specs(width, rows)
    in_specs = list(out_specs)
    groups, tokens = first.shape[0] - 1, pieces[0].shape[1]
    seen = slots * tokens
    token = jnp.arange(seen, dtype=jnp.int32)[:, None]
    bias = jnp.where(token < (first[-1] - first[0]) * tokens, 0.0, jnp.float32(HIDDEN))
    bias = jnp.broadcast_to(bias, (seen, 128))
    block = jnp.concatenate([block, jnp.zeros((slots,), jnp.int32)])
    if live is not None:
        shapes, out_specs = jax.ShapeDtypeStruct((rows, width), jnp.bfloat16), columns_of(query, per_step)
    extra = [] if live is None else [live]
    return pl.pallas_call(
        functools.partial(far_kernel, groups, per_step, live is not None),
        grid=(heads // per_step,),
        in_specs=[pl.BlockSpec(memory_space=pltpu.SMEM)] * 2
        + [whole(bias), columns_of(query, per_step)]
        + in_specs
        + [whole(array) for array in extra]
        + [pl.BlockSpec(memory_space=pl.ANY)] * len(pieces),
        out_specs=out_specs,
        out_shape=shapes,
        scratch_shapes=[
            pltpu.VMEM((slots, tokens, width), jnp.bfloat16),
            pltpu.VMEM((slots, tokens, width), jnp.bfloat16),
            pltpu.SemaphoreType.DMA((2,)),
        ],
        compiler_params=pltpu.CompilerParams(vmem_limit_bytes=VMEM_BYTES),
        cost_estimate=cost(rows, seen, width),
        name=name,
    )(first, block, bias, query, *before, *extra, *pieces)


def per_device(
    query_rows,
    key_rows,
    value_rows,
    gain_q,
    gain_k,
    mem_keys,
    mem_values,
    tile_len,
    session,
    req_owner,
    requested_block_index,
):
    capacity, width_here = query_rows.shape
    count = lax.axis_size("tile")
    levels = count // 4
    places = 2 * levels
    half = places // 2
    me = lax.axis_index("tile")

    owners = req_owner[:, 0]
    ahead = (chip_position(owners, levels) - chip_position(me, levels)) % places
    distance = jnp.minimum(ahead, places - ahead)
    side = 2 * (ahead > half).astype(jnp.int32)
    other = ((owners % 2) != (me % 2)).astype(jnp.int32)
    group = jnp.where(distance == 0, other, 4 * distance - 2 + side + other)
    number = jnp.arange(group.shape[0], dtype=jnp.int32)
    rank_key = group * group.shape[0] + number
    rank = jnp.sum((rank_key[None, :] < rank_key[:, None]).astype(jnp.int32), axis=1)
    block = jnp.sum(jnp.where(rank[None, :] == number[:, None], requested_block_index[None, :], 0), axis=1)
    first = jnp.sum(
        (group[None, :] < jnp.arange(count + 1, dtype=jnp.int32)[:, None]).astype(jnp.int32), axis=1
    )

    my_length = tile_len[0]
    blank = jnp.zeros((EDGE, width_here), jnp.bfloat16)

    def tail(rows):
        return lax.dynamic_slice_in_dim(jnp.concatenate([blank, rows], 0), my_length, EDGE, 0)

    about = jnp.stack([session[0] + 1, my_length])
    tails = jnp.concatenate([tail(key_rows), tail(value_rows)], 0)
    fronts = jnp.concatenate([key_rows[:EDGE], value_rows[:EDGE]], 0)
    from_left, left = passed_along((tails, about), "tile", 1)
    from_right, right = passed_along((fronts, about), "tile", -1)
    edge_keys = jnp.concatenate([from_left[:EDGE], from_right[:EDGE]], 0)
    edge_values = jnp.concatenate([from_left[EDGE:], from_right[EDGE:]], 0)
    totals_q, totals_k, totals_e = lax.psum(
        (row_squares(query_rows), row_squares(key_rows), row_squares(edge_keys)), "head"
    )
    query_norm = normalize(query_rows, totals_q, gain_q * (math.log2(math.e) / HEAD_DIM**0.5))
    key_norm = normalize(key_rows, totals_k, gain_k)
    edge_norm = normalize(edge_keys, totals_e, gain_k)
    edge_index = jnp.arange(EDGE, dtype=jnp.int32)
    live_rows = jnp.arange(capacity, dtype=jnp.int32) < my_length
    visible = jnp.concatenate(
        [
            live_rows,
            (left[0] == about[0]) & (edge_index >= EDGE - left[1]),
            (right[0] == about[0]) & (edge_index < right[1]),
        ]
    )
    bias = jnp.where(visible, 0.0, jnp.float32(HIDDEN))
    bias = jnp.broadcast_to(bias[:, None], (bias.shape[0], 128))
    live = live_rows[None, :].astype(jnp.float32)
    sums = near_part(bias, query_norm, key_norm, value_rows, edge_norm, edge_values)

    up, down = ring_pairs(count, 1), ring_pairs(count, -1)
    swap = [(t, t ^ 1) for t in range(count)]

    def moved(piece, pairs):
        return lax.ppermute(piece, "tile", pairs)

    def after(pieces, results):
        *pieces, top = lax.optimization_barrier((*pieces, results[0]))
        return pieces, [top, *results[1:]]

    own = jnp.concatenate([mem_keys, mem_values], 0)
    blocks = mem_keys.shape[0]
    below, above = own, own
    pieces = [own, moved(own, swap)]
    for step in range(1, half):
        below, above = moved(below, up), moved(above, down)
        if step == half - 2:
            (below, above), sums = after([below, above], sums)
        if step == half - 1:
            sums = far_part("far_part", first[: 4 * half - 5], block, number.shape[0], query_norm, sums, pieces)
            (below, above), sums = after([below, above], sums)
            pieces = []
        pieces += [above, moved(above, swap), below, moved(below, swap)]
    keys, values = moved(below[:blocks], up), moved(above[blocks:], down)
    most = 2 * number.shape[0] // count
    sums = far_part("far_next", first[4 * half - 6 : 4 * half - 1], block, 4 * most, query_norm, sums, pieces)
    (keys, values), sums = after([keys, values], sums)
    pieces = [keys, moved(keys, swap), values, moved(values, swap)]
    return far_part("far_last", first[4 * half - 2 :], block, 2 * most, query_norm, sums, pieces, live)


def solution(mesh):
    in_specs = (
        P("tile", "head"),
        P("tile", "head"),
        P("tile", "head"),
        P("head"),
        P("head"),
        P("tile", None, "head"),
        P("tile", None, "head"),
        P("tile"),
        P("tile"),
        P("tile", None),
        P("tile"),
    )
    out_specs = P("tile", "head")
    return jax.shard_map(
        per_device, mesh=mesh, in_specs=in_specs, out_specs=out_specs, check_vma=False
    )
```

time: 326 us -> 164 us (0.50)
  waiting for transfers between devices: 149 us -> 32.5 us
  matrix products: 59.3 us -> 0 us
  Pallas kernels: 0 us -> 56.4 us
  other arithmetic: 37.6 us -> 4.91 us
  starting transfers between devices: 14.8 us -> 45.6 us
  local copies, waits for them, and re-layouts: 29.8 us -> 11.3 us
  loops' own time: 13.5 us -> 0 us
  between operations: 14.9 us -> 7.25 us
    all_gather x2 -> x0, waiting for transfers between devices: 145 us -> none  [the longest x1 82.1 us: per_device(): piece_values = lax.all_gather(mem_values, 'tile', axis=0, tiled=True)]
    dot_general x40 -> x0, matrix products: 59.3 us -> none  [the longest x20 30 us: one_head(): return jnp.dot(weights, head_values, preferred_element_type=jnp.float32)]
    pallas_call x0 -> x4, Pallas kernels: none -> 56.4 us  [the longest x3 43.5 us: far_part(): pl.pallas_call(functools.partial(far_kernel, groups, per_step, live is no...]
    ppermute x0 -> x17, starting transfers between devices: none -> 39.1 us  [moved(): return lax.ppermute(piece, 'tile', pairs)]
    ppermute x0 -> x17, waiting for transfers between devices: none -> 32.5 us  [moved(): return lax.ppermute(piece, 'tile', pairs)]
    concatenate x3, other arithmetic: 16.2 us -> 0.13 us  [the longest x1 0.04 us: per_device(): tails = jnp.concatenate([tail(key_rows), tail(value_rows)], 0)]
    another operation x1 -> x0, loops' own time: 13.5 us -> none  [per_device(): outputs = lax.map(one_head, jnp.arange(heads_here, dtype=jnp.int32))]
    gather x2 -> x0, local copies, waits for them, and re-layouts: 12.5 us -> none  [the longest x1 6.24 us: per_device(): picked_values = jnp.take(piece_values, safe_block, axis=0)]
  transfers between devices with their start and end apart: 8 -> 21, of which waited for: 3 -> 7; matrix products, arithmetic and copies ran while one was open for 11% -> 8% of each run, Pallas kernels for 0% -> 27%
where the time goes in v2:
time: 164 us; the launch traced here: 163 us
  Pallas kernels  56.4 us (34%)
  starting transfers between devices  45.6 us (28%)
  waiting for transfers between devices  32.5 us (20%)
  local copies, waits for them, and re-layouts  11.3 us (7%)
  between operations  7.25 us (4%)
  blocking collectives  4.99 us (3%)
  other arithmetic  4.91 us (3%)
    pallas_call x3, Pallas kernels, far_part(): pl.pallas_call(functools.partial(far_kernel, groups, per_step, live is no...  43.5 us
    ppermute x17, starting transfers between devices, moved(): return lax.ppermute(piece, 'tile', pairs)  39.1 us
    ppermute x17, waiting for transfers between devices, moved(): return lax.ppermute(piece, 'tile', pairs)  32.5 us
    pallas_call x1, Pallas kernels, near_part(): pl.pallas_call(functools.partial(near_kernel, per_step), grid=(heads // p...  13 us
    ppermute x4, starting transfers between devices, passed_along(): lax.ppermute(value, axis, [(source, source + steps) for source in range(f...  6.52 us
    psum x1, blocking collectives, per_device(): lax.psum((row_squares(query_rows), row_squares(key_rows), row_squares(edg...  4.99 us
    unnamed x35, local copies, waits for them, and re-layouts  4.81 us
  transfers between devices with their start and end apart: 21, of which 7 were waited for; matrix products, arithmetic and copies ran while one was open for 8% of the time, Pallas kernels for 27%

profile of v2, /device:TPU:0, one launch (start us, length us, event | category | flops | bytes accessed | tf_op | source)
XLA Modules:
  0.0 163.1 jit_solution(626685271044406869)
XLA Ops:
  1.4 2.5 %collective-permute-start.4 = (s32[2]{0:T(128)S(1)}, s32[2]{0:T(128)S(1)}, u32[]{:S(2)}, u32[]{:S(2)}) collective-permute-start(s32[2]{0:T(128)S(1)} %pad_add_fusion), channel_id=1, source_target_pairs={{0,2},{2,4},{4,6},{6,8},{8,10},{10,12},{12,14},{14,16},{16,18},{18... | collective-permute-start | bytes 32 | tf_op jit(solution)/shard_map/ppermute | solution.py:22
  3.9 1.3 collective-permute-start.5
  5.2 1.1 constant_dynamic-update-slice_fusion.1
  6.4 5.9 %collective-permute-start = (bf16[32,8,2560]{2,1,0:T(8,128)(2,1)S(1)}, bf16[32,8,2560]{2,1,0:T(8,128)(2,1)}, u32[]{:S(2)}, u32[]{:S(2)}) collective-permute-start(bf16[32,8,2560]{2,1,0:T(8,128)(2,1)S(1)} %constant_dynamic-update-slice_fusion.refs_7_), channel_id=1, source_target_pairs={{0,8},{2,10},{8,16},{10,18},{16,24},{18,26},{24,28},{26,30},{28,20... | collective-permute-start | bytes 3932168 | tf_op jit(solution)/shard_map/ppermute | solution.py:293
  12.3 1.3 pad_dynamic-slice_fusion
  13.7 1.5 collective-permute-start.6
  16.3 1.7 %collective-permute-start.10 = (bf16[32,8,2560]{2,1,0:T(8,128)(2,1)S(1)}, bf16[32,8,2560]{2,1,0:T(8,128)(2,1)}, u32[]{:S(2)}, u32[]{:S(2)}) collective-permute-start(bf16[32,8,2560]{2,1,0:T(8,128)(2,1)S(1)} %constant_dynamic-update-slice_fusion.refs_7_), channel_id=1, source_target_pairs={{0,2},{2,0},{4,6},{6,4},{8,10},{10,8},{12,14},{14,12},{16,18},{18,... | collective-permute-start | bytes 3932168 | tf_op jit(solution)/shard_map/ppermute | solution.py:293
  19.4 1.3 collective-permute-start.7
  22.4 0.7 compare_and_fusion
  23.2 0.8 fusion.20
  24.0 0.8 fusion.21
  24.8 0.7 copy-done.8
  25.7 5.0 %all-reduce.5 = (f32[384]{0:T(512)S(1)}, f32[384]{0:T(512)S(1)}, f32[128]{0:T(128)S(1)}) all-reduce(f32[384]{0:T(512)S(1)} %fusion, f32[384]{0:T(512)S(1)} %fusion.3, f32[128]{0:T(128)S(1)} %fusion.6), channel_id=1, replica_groups=mesh['tile'=16,'head'=2] {'head'}, use_global_device_ids=true, to_apply=%region_4.5 | all-reduce | flops 896 | bytes 7168 | tf_op jit(solution)/shard_map/psum | solution.py:269
  30.7 1.3 fusion.8.ek_ref
  32.6 7.9 %collective-permute-done.refs_11_ = bf16[32,8,2560]{2,1,0:T(8,128)(2,1)} collective-permute-done((bf16[32,8,2560]{2,1,0:T(8,128)(2,1)S(1)}, bf16[32,8,2560]{2,1,0:T(8,128)(2,1)}, u32[]{:S(2)}, u32[]{:S(2)}) %collective-permute-start) | collective-permute-done | bytes 1310752 | tf_op jit(solution)/shard_map/ppermute | solution.py:293
  40.5 19.1 %collective-permute-start.1 = (bf16[32,8,2560]{2,1,0:T(8,128)(2,1)}, bf16[32,8,2560]{2,1,0:T(8,128)(2,1)}, u32[]{:S(2)}, u32[]{:S(2)}) collective-permute-start(bf16[32,8,2560]{2,1,0:T(8,128)(2,1)} %collective-permute-done.refs_11_), channel_id=1, source_target_pairs={{0,8},{2,10},{8,16},{10,18},{16,24},{18,26},{24,28},{26,30},{28,20... | collective-permute-start | bytes 3932168 | tf_op jit(solution)/shard_map/ppermute | solution.py:293
  59.6 6.1 %collective-permute-start.3 = (bf16[32,8,2560]{2,1,0:T(8,128)(2,1)}, bf16[32,8,2560]{2,1,0:T(8,128)(2,1)}, u32[]{:S(2)}, u32[]{:S(2)}) collective-permute-start(bf16[32,8,2560]{2,1,0:T(8,128)(2,1)} %collective-permute-done.2.refs_9_), channel_id=1, source_target_pairs={{0,4},{2,6},{8,0},{10,2},{16,8},{18,10},{24,16},{26,18},{28,24},{3... | collective-permute-start | bytes 3932168 | tf_op jit(solution)/shard_map/ppermute | solution.py:293
  66.6 13.0 %near_part.1 = (f32[20,8,384]{2,1,0:T(8,128)S(1)}, f32[20,8,384]{2,1,0:T(8,128)S(1)}, f32[2560,384]{1,0:T(8,128)}) custom-call(f32[512,128]{1,0:T(8,128)S(1)} %broadcast_in_dim.55.bias_ref, bf16[384,2560]{1,0:T(8,128)(2,1)S(1)} %fusion.2.q_ref.refs_3_, bf16[384,2560]{1,0:T(8,128)(2,1)S(1)} %fusion.5.k_ref, bf16[384,2560]{1,0:T(8,128)(2,1)} %v_ref.1, ...), custom_call_target="tpu_custom_call" | custom-call | flops 2013265920 | bytes 9830400 | tf_op jit(solution)/shard_map/near_part/pallas_call | solution.py:126
  79.6 0.7 copy-done.2
  80.8 12.4 %collective-permute-done.1.refs_15_ = bf16[32,8,2560]{2,1,0:T(8,128)(2,1)} collective-permute-done((bf16[32,8,2560]{2,1,0:T(8,128)(2,1)}, bf16[32,8,2560]{2,1,0:T(8,128)(2,1)}, u32[]{:S(2)}, u32[]{:S(2)}) %collective-permute-start.1) | collective-permute-done | bytes 1310752 | tf_op jit(solution)/shard_map/ppermute | solution.py:293
  93.7 2.0 %collective-permute-start.9 = (bf16[32,8,2560]{2,1,0:T(8,128)(2,1)}, bf16[32,8,2560]{2,1,0:T(8,128)(2,1)}, u32[]{:S(2)}, u32[]{:S(2)}) collective-permute-start(bf16[32,8,2560]{2,1,0:T(8,128)(2,1)} %collective-permute-done.3.refs_13_), channel_id=1, source_target_pairs={{0,4},{2,6},{8,0},{10,2},{16,8},{18,10},{24,16},{26,18},{28,24},{3... | collective-permute-start | bytes 3932168 | tf_op jit(solution)/shard_map/ppermute | solution.py:293
  96.2 0.7 fusion.22
  98.6 0.9 copy-done.3
  99.5 16.7 %far_part.1 = (f32[20,8,384]{2,1,0:T(8,128)S(1)}, f32[20,8,384]{2,1,0:T(8,128)S(1)}, f32[2560,384]{1,0:T(8,128)}) custom-call(s32[11]{0:T(128)S(1)} %bitcast.33, s32[128]{0:T(128)S(1)} %concatenate.46.refs_1_, f32[512,128]{1,0:T(8,128)S(1)} %broadcast_in_dim.88.refs_2_, bf16[384,2560]{1,0:T(8,128)(2,1)} %copy-done, ...), custom_call_target="tpu_custom_call" | custom-call | flops 2013265920 | bytes 9830400 | tf_op jit(solution)/shard_map/far_part/pallas_call | solution.py:201
  116.2 8.4 %collective-permute-done.8.refs_9_ = bf16[32,8,2560]{2,1,0:T(8,128)(2,1)S(1)} collective-permute-done((bf16[32,8,2560]{2,1,0:T(8,128)(2,1)}, bf16[32,8,2560]{2,1,0:T(8,128)(2,1)S(1)}, u32[]{:S(2)}, u32[]{:S(2)}) %collective-permute-start.8) | collective-permute-done | bytes 1310752 | tf_op jit(solution)/shard_map/ppermute | solution.py:293
  124.6 2.3 %collective-permute-done.9.refs_7_ = bf16[32,8,2560]{2,1,0:T(8,128)(2,1)} collective-permute-done((bf16[32,8,2560]{2,1,0:T(8,128)(2,1)}, bf16[32,8,2560]{2,1,0:T(8,128)(2,1)}, u32[]{:S(2)}, u32[]{:S(2)}) %collective-permute-start.9) | collective-permute-done | bytes 1310752 | tf_op jit(solution)/shard_map/ppermute | solution.py:293
  127.4 1.1 slice.82
  128.5 1.8 %collective-permute-start.15 = (bf16[16,8,2560]{2,1,0:T(8,128)(2,1)S(1)}, bf16[16,8,2560]{2,1,0:T(8,128)(2,1)S(1)}, u32[]{:S(2)}, u32[]{:S(2)}) collective-permute-start(bf16[16,8,2560]{2,1,0:T(8,128)(2,1)S(1)} %slice.81), channel_id=1, source_target_pairs={{0,8},{2,10},{8,16},{10,18},{16,24},{18,26},{24,28},{26,30},{28,20... | collective-permute-start | bytes 1966088 | tf_op jit(solution)/shard_map/ppermute | solution.py:293
  132.0 1.1 copy-done.9
  133.1 14.4 %far_next.1 = (f32[20,8,384]{2,1,0:T(8,128)S(1)}, f32[20,8,384]{2,1,0:T(8,128)S(1)}, f32[2560,384]{1,0:T(8,128)}) custom-call(s32[5]{0:T(128)S(1)} %slice.83.refs_0_, s32[96]{0:T(128)S(1)} %concatenate.47.refs_1_, f32[256,128]{1,0:T(8,128)S(1)} %broadcast_in_dim.91.refs_2_, bf16[384,2560]{1,0:T(8,128)(2,1)} %copy-done, ...), custom_call_target="tpu_custom_call" | custom-call | flops 1006632960 | bytes 9830400 | tf_op jit(solution)/shard_map/far_next/pallas_call | solution.py:201
  149.7 0.9 collective-permute-done.20.refs_11_
  150.7 12.4 %far_last.1 = bf16[384,2560]{1,0:T(8,128)(2,1)} custom-call(s32[3]{0:T(128)S(1)} %slice.65.refs_0_, s32[80]{0:T(128)S(1)} %concatenate.37.refs_1_, f32[128,128]{1,0:T(8,128)S(1)} %broadcast_in_dim.50.refs_2_, bf16[384,2560]{1,0:T(8,128)(2,1)S(1)} %copy-done.1, f32[20,8,384]{2,1,0:T(8,128)S(1)} %get-tuple-element.36.refs_4_, ...), custom_call_target="tpu_custom_call" | custom-call | flops 503316480 | bytes 9830400 | tf_op jit(solution)/shard_map/far_last/pallas_call | solution.py:201
  (94 shorter events, 8.1 us)
Async XLA Ops:
  0.0 6.4 %copy-start.12 = (bf16[16,8,2560]{2,1,0:T(8,128)(2,1)S(1)}, bf16[16,8,2560]{2,1,0:T(8,128)(2,1)}, u32[]{:S(2)}) copy-start(bf16[16,8,2560]{2,1,0:T(8,128)(2,1)} %param.17) | copy-start | bytes 1966084
  1.4 10.9 %copy-start.4 = (bf16[384,2560]{1,0:T(8,128)(2,1)S(1)}, bf16[384,2560]{1,0:T(8,128)(2,1)}, u32[]{:S(2)}) copy-start(bf16[384,2560]{1,0:T(8,128)(2,1)} %param.12) | copy-start | bytes 5898244
  1.4 14.9 %collective-permute-start.4 = (s32[2]{0:T(128)S(1)}, s32[2]{0:T(128)S(1)}, u32[]{:S(2)}, u32[]{:S(2)}) collective-permute-start(s32[2]{0:T(128)S(1)} %pad_add_fusion), channel_id=1, source_target_pairs={{0,2},{2,4},{4,6},{6,8},{8,10},{10,12},{12,14},{14,16},{16,18},{18... | collective-permute-start | bytes 32 | tf_op jit(solution)/shard_map/ppermute | solution.py:22
  3.9 15.4 %collective-permute-start.5 = (s32[2]{0:T(128)S(1)}, s32[2]{0:T(128)S(1)}, u32[]{:S(2)}, u32[]{:S(2)}) collective-permute-start(s32[2]{0:T(128)S(1)} %pad_add_fusion), channel_id=1, source_target_pairs={{2,0},{4,2},{6,4},{8,6},{10,8},{12,10},{14,12},{16,14},{18,16},{20... | collective-permute-start | bytes 32 | tf_op jit(solution)/shard_map/ppermute | solution.py:22
  6.4 34.1 %collective-permute-start = (bf16[32,8,2560]{2,1,0:T(8,128)(2,1)S(1)}, bf16[32,8,2560]{2,1,0:T(8,128)(2,1)}, u32[]{:S(2)}, u32[]{:S(2)}) collective-permute-start(bf16[32,8,2560]{2,1,0:T(8,128)(2,1)S(1)} %constant_dynamic-update-slice_fusion.refs_7_), channel_id=1, source_target_pairs={{0,8},{2,10},{8,16},{10,18},{16,24},{18,26},{24,28},{26,30},{28,20... | collective-permute-start | bytes 3932168 | tf_op jit(solution)/shard_map/ppermute | solution.py:293
  12.3 47.3 %collective-permute-start.2 = (bf16[32,8,2560]{2,1,0:T(8,128)(2,1)S(1)}, bf16[32,8,2560]{2,1,0:T(8,128)(2,1)}, u32[]{:S(2)}, u32[]{:S(2)}) collective-permute-start(bf16[32,8,2560]{2,1,0:T(8,128)(2,1)S(1)} %constant_dynamic-update-slice_fusion.refs_7_), channel_id=1, source_target_pairs={{0,4},{2,6},{8,0},{10,2},{16,8},{18,10},{24,16},{26,18},{28,24},{3... | collective-permute-start | bytes 3932168 | tf_op jit(solution)/shard_map/ppermute | solution.py:293
  13.7 1.9 %copy-start.5 = (bf16[384,2560]{1,0:T(8,128)(2,1)S(1)}, bf16[384,2560]{1,0:T(8,128)(2,1)}, u32[]{:S(2)}) copy-start(bf16[384,2560]{1,0:T(8,128)(2,1)} %param.11) | copy-start | bytes 5898244
  13.7 9.5 %collective-permute-start.6 = (bf16[128,2560]{1,0:T(8,128)(2,1)S(1)}, bf16[128,2560]{1,0:T(8,128)(2,1)S(1)}, u32[]{:S(2)}, u32[]{:S(2)}) collective-permute-start(bf16[128,2560]{1,0:T(8,128)(2,1)S(1)} %pad_maximum_fusion), channel_id=1, source_target_pairs={{0,2},{2,4},{4,6},{6,8},{8,10},{10,12},{12,14},{14,16},{16,18},{18... | collective-permute-start | bytes 1966088 | tf_op jit(solution)/shard_map/ppermute | solution.py:22
  16.3 77.3 %collective-permute-start.10 = (bf16[32,8,2560]{2,1,0:T(8,128)(2,1)S(1)}, bf16[32,8,2560]{2,1,0:T(8,128)(2,1)}, u32[]{:S(2)}, u32[]{:S(2)}) collective-permute-start(bf16[32,8,2560]{2,1,0:T(8,128)(2,1)S(1)} %constant_dynamic-update-slice_fusion.refs_7_), channel_id=1, source_target_pairs={{0,2},{2,0},{4,6},{6,4},{8,10},{10,8},{12,14},{14,12},{16,18},{18,... | collective-permute-start | bytes 3932168 | tf_op jit(solution)/shard_map/ppermute | solution.py:293
  19.4 4.6 %collective-permute-start.7 = (bf16[128,2560]{1,0:T(8,128)(2,1)S(1)}, bf16[128,2560]{1,0:T(8,128)(2,1)S(1)}, u32[]{:S(2)}, u32[]{:S(2)}) collective-permute-start(bf16[128,2560]{1,0:T(8,128)(2,1)S(1)} %pad_maximum_fusion.1), channel_id=1, source_target_pairs={{2,0},{4,2},{6,4},{8,6},{10,8},{12,10},{14,12},{16,14},{18,16},{20... | collective-permute-start | bytes 1966088 | tf_op jit(solution)/shard_map/ppermute | solution.py:22
  24.0 6.8 %copy-start.13 = (f32[2560]{0:T(1024)S(1)}, f32[2560]{0:T(1024)}, u32[]{:S(2)}) copy-start(f32[2560]{0:T(1024)} %param.15) | copy-start | bytes 30724
  32.0 33.7 %copy-start.10 = (bf16[64,2560]{1,0:T(8,128)(2,1)S(1)}, bf16[64,2560]{1,0:T(8,128)(2,1)}, u32[]{:S(2)}) copy-start(bf16[64,2560]{1,0:T(8,128)(2,1)} %get-tuple-element.50) | copy-start | bytes 983044
  32.0 33.7 %copy-start.11 = (bf16[64,2560]{1,0:T(8,128)(2,1)S(1)}, bf16[64,2560]{1,0:T(8,128)(2,1)}, u32[]{:S(2)}) copy-start(bf16[64,2560]{1,0:T(8,128)(2,1)} %get-tuple-element.52) | copy-start | bytes 983044
  32.1 33.8 %copy-start.6 = (bf16[384,2560]{1,0:T(8,128)(2,1)S(1)}, bf16[384,2560]{1,0:T(8,128)(2,1)}, u32[]{:S(2)}) copy-start(bf16[384,2560]{1,0:T(8,128)(2,1)} %param.11) | copy-start | bytes 5898244
  40.5 52.6 %collective-permute-start.1 = (bf16[32,8,2560]{2,1,0:T(8,128)(2,1)}, bf16[32,8,2560]{2,1,0:T(8,128)(2,1)}, u32[]{:S(2)}, u32[]{:S(2)}) collective-permute-start(bf16[32,8,2560]{2,1,0:T(8,128)(2,1)} %collective-permute-done.refs_11_), channel_id=1, source_target_pairs={{0,8},{2,10},{8,16},{10,18},{16,24},{18,26},{24,28},{26,30},{28,20... | collective-permute-start | bytes 3932168 | tf_op jit(solution)/shard_map/ppermute | solution.py:293
  59.6 33.5 %collective-permute-start.3 = (bf16[32,8,2560]{2,1,0:T(8,128)(2,1)}, bf16[32,8,2560]{2,1,0:T(8,128)(2,1)}, u32[]{:S(2)}, u32[]{:S(2)}) collective-permute-start(bf16[32,8,2560]{2,1,0:T(8,128)(2,1)} %collective-permute-done.2.refs_9_), channel_id=1, source_target_pairs={{0,4},{2,6},{8,0},{10,2},{16,8},{18,10},{24,16},{26,18},{28,24},{3... | collective-permute-start | bytes 3932168 | tf_op jit(solution)/shard_map/ppermute | solution.py:293
  65.8 27.9 %collective-permute-start.11 = (bf16[32,8,2560]{2,1,0:T(8,128)(2,1)}, bf16[32,8,2560]{2,1,0:T(8,128)(2,1)}, u32[]{:S(2)}, u32[]{:S(2)}) collective-permute-start(bf16[32,8,2560]{2,1,0:T(8,128)(2,1)} %collective-permute-done.2.refs_9_), channel_id=1, source_target_pairs={{0,2},{2,0},{4,6},{6,4},{8,10},{10,8},{12,14},{14,12},{16,18},{18,... | collective-permute-start | bytes 3932168 | tf_op jit(solution)/shard_map/ppermute | solution.py:293
  66.4 13.2 %copy-start = (bf16[384,2560]{1,0:T(8,128)(2,1)}, bf16[384,2560]{1,0:T(8,128)(2,1)S(1)}, u32[]{:S(2)}) copy-start(bf16[384,2560]{1,0:T(8,128)(2,1)S(1)} %fusion.2.q_ref.refs_3_) | copy-start | bytes 5898244
  66.6 29.1 %copy-start.15 = (s32[64,1]{0,1:T(1,128)S(1)}, s32[64,1]{0,1:T(1,128)}, u32[]{:S(2)}) copy-start(s32[64,1]{0,1:T(1,128)} %param.20) | copy-start | bytes 772
  66.6 29.4 %copy-start.16 = (s32[64]{0:T(128)S(1)}, s32[64]{0:T(128)}, u32[]{:S(2)}) copy-start(s32[64]{0:T(128)} %param.21) | copy-start | bytes 772
  80.3 17.8 %collective-permute-start.12 = (bf16[32,8,2560]{2,1,0:T(8,128)(2,1)}, bf16[32,8,2560]{2,1,0:T(8,128)(2,1)}, u32[]{:S(2)}, u32[]{:S(2)}) collective-permute-start(bf16[32,8,2560]{2,1,0:T(8,128)(2,1)} %collective-permute-done.refs_11_), channel_id=1, source_target_pairs={{0,2},{2,0},{4,6},{6,4},{8,10},{10,8},{12,14},{14,12},{16,18},{18,... | collective-permute-start | bytes 3932168 | tf_op jit(solution)/shard_map/ppermute | solution.py:293
  93.2 4.9 %collective-permute-start.13 = (bf16[32,8,2560]{2,1,0:T(8,128)(2,1)}, bf16[32,8,2560]{2,1,0:T(8,128)(2,1)}, u32[]{:S(2)}, u32[]{:S(2)}) collective-permute-start(bf16[32,8,2560]{2,1,0:T(8,128)(2,1)} %collective-permute-done.3.refs_13_), channel_id=1, source_target_pairs={{0,2},{2,0},{4,6},{6,4},{8,10},{10,8},{12,14},{14,12},{16,18},{18,... | collective-permute-start | bytes 3932168 | tf_op jit(solution)/shard_map/ppermute | solution.py:293
  93.2 5.2 %collective-permute-start.14 = (bf16[32,8,2560]{2,1,0:T(8,128)(2,1)}, bf16[32,8,2560]{2,1,0:T(8,128)(2,1)}, u32[]{:S(2)}, u32[]{:S(2)}) collective-permute-start(bf16[32,8,2560]{2,1,0:T(8,128)(2,1)} %collective-permute-done.1.refs_15_), channel_id=1, source_target_pairs={{0,2},{2,0},{4,6},{6,4},{8,10},{10,8},{12,14},{14,12},{16,18},{18,... | collective-permute-start | bytes 3932168 | tf_op jit(solution)/shard_map/ppermute | solution.py:293
  93.7 30.9 %collective-permute-start.8 = (bf16[32,8,2560]{2,1,0:T(8,128)(2,1)}, bf16[32,8,2560]{2,1,0:T(8,128)(2,1)S(1)}, u32[]{:S(2)}, u32[]{:S(2)}) collective-permute-start(bf16[32,8,2560]{2,1,0:T(8,128)(2,1)} %collective-permute-done.1.refs_15_), channel_id=1, source_target_pairs={{0,8},{2,10},{8,16},{10,18},{16,24},{18,26},{24,28},{26,30},{28,20... | collective-permute-start | bytes 3932168 | tf_op jit(solution)/shard_map/ppermute | solution.py:293
  93.7 33.2 %collective-permute-start.9 = (bf16[32,8,2560]{2,1,0:T(8,128)(2,1)}, bf16[32,8,2560]{2,1,0:T(8,128)(2,1)}, u32[]{:S(2)}, u32[]{:S(2)}) collective-permute-start(bf16[32,8,2560]{2,1,0:T(8,128)(2,1)} %collective-permute-done.3.refs_13_), channel_id=1, source_target_pairs={{0,4},{2,6},{8,0},{10,2},{16,8},{18,10},{24,16},{26,18},{28,24},{3... | collective-permute-start | bytes 3932168 | tf_op jit(solution)/shard_map/ppermute | solution.py:293
  126.8 5.1 %collective-permute-start.17 = (bf16[32,8,2560]{2,1,0:T(8,128)(2,1)}, bf16[32,8,2560]{2,1,0:T(8,128)(2,1)S(1)}, u32[]{:S(2)}, u32[]{:S(2)}) collective-permute-start(bf16[32,8,2560]{2,1,0:T(8,128)(2,1)} %collective-permute-done.9.refs_7_), channel_id=1, source_target_pairs={{0,2},{2,0},{4,6},{6,4},{8,10},{10,8},{12,14},{14,12},{16,18},{18,... | collective-permute-start | bytes 3932168 | tf_op jit(solution)/shard_map/ppermute | solution.py:293
  126.8 5.1 %collective-permute-start.18 = (bf16[32,8,2560]{2,1,0:T(8,128)(2,1)S(1)}, bf16[32,8,2560]{2,1,0:T(8,128)(2,1)S(1)}, u32[]{:S(2)}, u32[]{:S(2)}) collective-permute-start(bf16[32,8,2560]{2,1,0:T(8,128)(2,1)S(1)} %collective-permute-done.8.refs_9_), channel_id=1, source_target_pairs={{0,2},{2,0},{4,6},{6,4},{8,10},{10,8},{12,14},{14,12},{16,18},{18,... | collective-permute-start | bytes 3932168 | tf_op jit(solution)/shard_map/ppermute | solution.py:293
  128.5 19.0 %collective-permute-start.15 = (bf16[16,8,2560]{2,1,0:T(8,128)(2,1)S(1)}, bf16[16,8,2560]{2,1,0:T(8,128)(2,1)S(1)}, u32[]{:S(2)}, u32[]{:S(2)}) collective-permute-start(bf16[16,8,2560]{2,1,0:T(8,128)(2,1)S(1)} %slice.81), channel_id=1, source_target_pairs={{0,8},{2,10},{8,16},{10,18},{16,24},{18,26},{24,28},{26,30},{28,20... | collective-permute-start | bytes 1966088 | tf_op jit(solution)/shard_map/ppermute | solution.py:293
  130.3 17.2 %collective-permute-start.16 = (bf16[16,8,2560]{2,1,0:T(8,128)(2,1)S(1)}, bf16[16,8,2560]{2,1,0:T(8,128)(2,1)S(1)}, u32[]{:S(2)}, u32[]{:S(2)}) collective-permute-start(bf16[16,8,2560]{2,1,0:T(8,128)(2,1)S(1)} %slice.82), channel_id=1, source_target_pairs={{0,4},{2,6},{8,0},{10,2},{16,8},{18,10},{24,16},{26,18},{28,24},{3... | collective-permute-start | bytes 1966088 | tf_op jit(solution)/shard_map/ppermute | solution.py:293
  133.1 17.6 %copy-start.1 = (bf16[384,2560]{1,0:T(8,128)(2,1)S(1)}, bf16[384,2560]{1,0:T(8,128)(2,1)}, u32[]{:S(2)}) copy-start(bf16[384,2560]{1,0:T(8,128)(2,1)} %copy-done) | copy-start | bytes 5898244
  147.5 2.2 %collective-permute-start.19 = (bf16[16,8,2560]{2,1,0:T(8,128)(2,1)S(1)}, bf16[16,8,2560]{2,1,0:T(8,128)(2,1)S(1)}, u32[]{:S(2)}, u32[]{:S(2)}) collective-permute-start(bf16[16,8,2560]{2,1,0:T(8,128)(2,1)S(1)} %collective-permute-done.15.refs_8_), channel_id=1, source_target_pairs={{0,2},{2,0},{4,6},{6,4},{8,10},{10,8},{12,14},{14,12},{16,18},{18,... | collective-permute-start | bytes 1966088 | tf_op jit(solution)/shard_map/ppermute | solution.py:293
  147.6 3.0 %collective-permute-start.20 = (bf16[16,8,2560]{2,1,0:T(8,128)(2,1)S(1)}, bf16[16,8,2560]{2,1,0:T(8,128)(2,1)S(1)}, u32[]{:S(2)}, u32[]{:S(2)}) collective-permute-start(bf16[16,8,2560]{2,1,0:T(8,128)(2,1)S(1)} %collective-permute-done.16.refs_10_), channel_id=1, source_target_pairs={{0,2},{2,0},{4,6},{6,4},{8,10},{10,8},{12,14},{14,12},{16,18},{18,... | collective-permute-start | bytes 1966088 | tf_op jit(solution)/shard_map/ppermute | solution.py:293
  (6 other events, 5.1 us)

commit v3 on v2

v3 whole, which is shorter than its diff:
```python
import functools
import math

import jax
import jax.numpy as jnp
from jax import lax
from jax.experimental import pallas as pl
from jax.experimental.pallas import tpu as pltpu
from jax.sharding import PartitionSpec as P

HEAD_DIM = 128
WIDTH = 5120
EDGE = 64
EPSILON = 1e-06
HIDDEN = -1e30
VMEM_BYTES = 32 * 1024 * 1024


def passed_along(value, axis, steps):
    count = lax.axis_size(axis)
    first, last = (max(0, -steps), min(count, count - steps))
    return lax.ppermute(value, axis, [(source, source + steps) for source in range(first, last)])


def row_squares(raw_rows):
    rows32 = raw_rows.astype(jnp.float32)
    return jnp.sum(rows32 * rows32, axis=1)


def normalize(raw_rows, totals, gain):
    rows32 = raw_rows.astype(jnp.float32)
    factor = lax.rsqrt(totals / WIDTH + EPSILON)
    return (rows32 * factor[:, None] * gain).astype(jnp.bfloat16)


def chip_position(tile, levels):
    level, row = tile // 4, (tile // 2) % 2
    return level + row * (2 * levels - 1 - 2 * level)


def ring_pairs(count, step):
    levels = count // 4
    at = {(chip_position(t, levels), t % 2): t for t in range(count)}
    places = 2 * levels
    return [(at[p, c], at[(p + step) % places, c]) for p in range(places) for c in range(2)]


def across_t(first, second):
    return lax.dot_general(first, second, (((1,), (1,)), ((), ())), preferred_element_type=jnp.float32)


def down_rows(first, second):
    return lax.dot_general(first, second, (((0,), (0,)), ((), ())), preferred_element_type=jnp.float32)


def attend(heads):
    scores = []
    for query, parts, _ in heads:
        wide = [jnp.concatenate([bias] * (query.shape[0] // bias.shape[1]), axis=1) for _, _, bias in parts]
        scores.append([across_t(keys, query) + add for (keys, _, _), add in zip(parts, wide)])
    tops = []
    for group, (_, _, before) in zip(scores, heads):
        found = [jnp.max(part, axis=0, keepdims=True) for part in group]
        tops.append(functools.reduce(jnp.maximum, found if before is None else found + [before[0]]))
    weights = [[jnp.exp2(part - top) for part in group] for group, top in zip(scores, tops)]
    results = []
    for group, top, (_, parts, before) in zip(weights, tops, heads):
        total = sum(jnp.sum(part, axis=0, keepdims=True) for part in group)
        acc = sum(down_rows(values, part.astype(jnp.bfloat16)) for part, (_, values, _) in zip(group, parts))
        if before is not None:
            kept = jnp.exp2(before[0] - top)
            total = total + kept * before[1]
            acc = acc + kept * before[2]
        results.append((top, total, acc))
    return results


def store_sums(sums, head, place, top_ref, sum_ref, acc_ref):
    top, total, acc = sums
    top_ref[head] = jnp.broadcast_to(top, top_ref.shape[1:])
    sum_ref[head] = jnp.broadcast_to(total, sum_ref.shape[1:])
    acc_ref[place, :] = acc


def over_heads(width, body):
    heads = width // HEAD_DIM
    together = max(n for n in (1, 2, 4, 5) if heads % n == 0 and (n < 5 or heads < 10))

    def some(i, carry):
        numbers = [i * together + j for j in range(together)]
        body([(head, pl.ds(pl.multiple_of(head * HEAD_DIM, HEAD_DIM), HEAD_DIM)) for head in numbers])
        return carry

    lax.fori_loop(0, heads // together, some, 0)


def near_kernel(bias_ref, q_ref, k_ref, v_ref, ek_ref, ev_ref, top_ref, sum_ref, acc_ref):
    own = k_ref.shape[0]

    def body(places):
        heads = []
        for _, place in places:
            parts = [
                (k_ref[:, place], v_ref[:, place], bias_ref[:own, :]),
                (ek_ref[:, place], ev_ref[:, place], bias_ref[own:, :]),
            ]
            heads.append((q_ref[:, place], parts, None))
        for (head, place), sums in zip(places, attend(heads)):
            store_sums(sums, head, place, top_ref, sum_ref, acc_ref)

    over_heads(q_ref.shape[1], body)


def sum_shapes(rows, width):
    stat = jax.ShapeDtypeStruct((width // HEAD_DIM, 8, rows), jnp.float32)
    return [stat, stat, jax.ShapeDtypeStruct((width, rows), jnp.float32)]


IN_VMEM = pl.BlockSpec(memory_space=pltpu.VMEM)


def cost(rows, seen, width):
    return pl.CostEstimate(
        flops=4 * rows * seen * width,
        bytes_accessed=10 * rows * width,
        transcendentals=rows * seen * width // HEAD_DIM,
    )


def near_part(bias, query, keys, values, edge_keys, edge_values):
    rows, width = query.shape
    return pl.pallas_call(
        near_kernel,
        in_specs=[IN_VMEM] * 6,
        out_specs=[IN_VMEM] * 3,
        out_shape=sum_shapes(rows, width),
        compiler_params=pltpu.CompilerParams(vmem_limit_bytes=VMEM_BYTES),
        cost_estimate=cost(rows, bias.shape[0], width),
        name="near_part",
    )(bias, query, keys, values, edge_keys, edge_values)


def far_kernel(groups, last, *refs):
    first_ref, block_ref, bias_ref, q_ref, before_top, before_sum, before_acc = refs[:7]
    refs = refs[7:]
    if last:
        live_ref, refs = refs[0], refs[1:]
    *out_refs, keys, values, sems = refs[len(refs) - (4 if last else 6) :]
    pieces = refs[: len(refs) - len(out_refs) - 3]
    joined = len(pieces) == groups
    key_pieces, value_pieces = pieces[:groups], pieces if joined else pieces[groups:]
    offset = pieces[0].shape[0] // 2 if joined else 0
    slots, tokens = keys.shape[:2]
    start = first_ref[0]

    def fetch_from(g):
        def fetch(slot, carry):
            block = block_ref[slot]
            to = slot - start
            pltpu.make_async_copy(key_pieces[g].at[block], keys.at[to], sems.at[0]).start()
            pltpu.make_async_copy(value_pieces[g].at[block + offset], values.at[to], sems.at[1]).start()
            return carry

        return fetch

    for g in range(groups):
        lax.fori_loop(first_ref[g], first_ref[g + 1], fetch_from(g), 0)
    lax.fori_loop(first_ref[groups], start + slots, fetch_from(0), 0)
    pltpu.make_async_copy(keys, keys, sems.at[0]).wait()
    pltpu.make_async_copy(values, values, sems.at[1]).wait()

    def flat(array, place):
        block = array[:, :, place].astype(jnp.float32)
        return block.reshape(slots * tokens, HEAD_DIM).astype(jnp.bfloat16)

    def body(places):
        heads = []
        for head, place in places:
            before = (before_top[head][:1, :], before_sum[head][:1, :], before_acc[place, :])
            heads.append((q_ref[:, place], [(flat(keys, place), flat(values, place), bias_ref[...])], before))
        for (head, place), sums in zip(places, attend(heads)):
            if last:
                result = jnp.where(live_ref[...] > 0.0, sums[2] / sums[1], 0.0)
                out_refs[0][:, place] = result.T.astype(out_refs[0].dtype)
            else:
                store_sums(sums, head, place, *out_refs)

    over_heads(q_ref.shape[1], body)


def far_part(name, first, block, slots, query, before, pieces, live=None):
    rows, width = query.shape
    groups, tokens = first.shape[0] - 1, pieces[0].shape[1]
    seen = slots * tokens
    token = jnp.arange(seen, dtype=jnp.int32)[:, None]
    bias = jnp.where(token < (first[-1] - first[0]) * tokens, 0.0, jnp.float32(HIDDEN))
    bias = jnp.broadcast_to(bias, (seen, 128))
    block = jnp.concatenate([block, jnp.zeros((slots,), jnp.int32)])
    extra = [] if live is None else [live]
    final = jax.ShapeDtypeStruct((rows, width), jnp.bfloat16)
    return pl.pallas_call(
        functools.partial(far_kernel, groups, live is not None),
        in_specs=[pl.BlockSpec(memory_space=pltpu.SMEM)] * 2
        + [IN_VMEM] * (5 + len(extra))
        + [pl.BlockSpec(memory_space=pl.ANY)] * len(pieces),
        out_specs=[IN_VMEM] * 3 if live is None else IN_VMEM,
        out_shape=sum_shapes(rows, width) if live is None else final,
        input_output_aliases={4: 0, 5: 1, 6: 2} if live is None else {},
        scratch_shapes=[
            pltpu.VMEM((slots, tokens, width), jnp.bfloat16),
            pltpu.VMEM((slots, tokens, width), jnp.bfloat16),
            pltpu.SemaphoreType.DMA((2,)),
        ],
        compiler_params=pltpu.CompilerParams(vmem_limit_bytes=VMEM_BYTES),
        cost_estimate=cost(rows, seen, width),
        name=name,
    )(first, block, bias, query, *before, *extra, *pieces)


def per_device(
    query_rows,
    key_rows,
    value_rows,
    gain_q,
    gain_k,
    mem_keys,
    mem_values,
    tile_len,
    session,
    req_owner,
    requested_block_index,
):
    capacity, width_here = query_rows.shape
    count = lax.axis_size("tile")
    levels = count // 4
    places = 2 * levels
    half = places // 2
    me = lax.axis_index("tile")

    owners = req_owner[:, 0]
    ahead = (chip_position(owners, levels) - chip_position(me, levels)) % places
    distance = jnp.minimum(ahead, places - ahead)
    side = 2 * (ahead > half).astype(jnp.int32)
    other = ((owners % 2) != (me % 2)).astype(jnp.int32)
    group = jnp.where(distance == 0, other, 4 * distance - 2 + side + other)
    number = jnp.arange(group.shape[0], dtype=jnp.int32)
    rank_key = group * group.shape[0] + number
    rank = jnp.sum((rank_key[None, :] < rank_key[:, None]).astype(jnp.int32), axis=1)
    block = jnp.sum(jnp.where(rank[None, :] == number[:, None], requested_block_index[None, :], 0), axis=1)
    first = jnp.sum(
        (group[None, :] < jnp.arange(count + 1, dtype=jnp.int32)[:, None]).astype(jnp.int32), axis=1
    )

    my_length = tile_len[0]
    totals_q, totals_k = lax.psum((row_squares(query_rows), row_squares(key_rows)), "head")
    query_norm = normalize(query_rows, totals_q, gain_q * (math.log2(math.e) / HEAD_DIM**0.5))
    key_norm = normalize(key_rows, totals_k, gain_k)
    live_rows = jnp.arange(capacity, dtype=jnp.int32) < my_length
    live = live_rows[None, :].astype(jnp.float32)
    own_label = (session[0] + 1).astype(jnp.bfloat16)
    edge_index = jnp.arange(EDGE, dtype=jnp.int32)
    blank = jnp.zeros((EDGE, width_here), jnp.bfloat16)

    def tail(rows):
        return lax.dynamic_slice_in_dim(jnp.concatenate([blank, rows], 0), my_length, EDGE, 0)

    def edge(keys, values, is_live):
        labels = jnp.where(is_live, own_label, jnp.bfloat16(0))
        return jnp.concatenate([keys, values, jnp.pad(labels[None, :], ((0, 15), (0, width_here - EDGE)))], 0)

    tails = edge(tail(key_norm), tail(value_rows), edge_index >= EDGE - my_length)
    fronts = edge(key_norm[:EDGE], value_rows[:EDGE], edge_index < my_length)
    from_left, from_right = passed_along(tails, "tile", 1), passed_along(fronts, "tile", -1)

    def near_sums(from_left, from_right):
        edge_keys = jnp.concatenate([from_left[:EDGE], from_right[:EDGE]], 0)
        edge_values = jnp.concatenate([from_left[EDGE : 2 * EDGE], from_right[EDGE : 2 * EDGE]], 0)
        labels = jnp.concatenate([from_left[2 * EDGE, :EDGE], from_right[2 * EDGE, :EDGE]])
        bias = jnp.where(jnp.concatenate([live_rows, labels == own_label]), 0.0, jnp.float32(HIDDEN))
        bias = jnp.broadcast_to(bias[:, None], (bias.shape[0], 128))
        return near_part(bias, query_norm, key_norm, value_rows, edge_keys, edge_values)

    up, down = ring_pairs(count, 1), ring_pairs(count, -1)
    swap = [(t, t ^ 1) for t in range(count)]

    def moved(piece, pairs):
        return lax.ppermute(piece, "tile", pairs)

    def after(pieces, results):
        *pieces, top = lax.optimization_barrier((*pieces, results[0]))
        return pieces, [top, *results[1:]]

    own = jnp.concatenate([mem_keys, mem_values], 0)
    blocks = mem_keys.shape[0]
    below, above = own, own
    pieces, unswapped = [], [own]
    for step in range(1, half):
        below, above = moved(below, up), moved(above, down)
        if step == 1:
            late, _, _ = lax.optimization_barrier((own, below, above))
            pieces, unswapped = [own, moved(late, swap)], []
            from_left, from_right, pieces[1] = lax.optimization_barrier((from_left, from_right, pieces[1]))
            sums = near_sums(from_left, from_right)
        unswapped += [above, below]
        if step == half - 2:
            unswapped, sums = after(unswapped, sums)
            below, above = unswapped[-1], unswapped[-2]
            for piece in unswapped:
                pieces += [piece, moved(piece, swap)]
            unswapped = []
        if step == half - 1:
            sums = far_part("far_part", first[: 4 * half - 5], block, number.shape[0], query_norm, sums, pieces)
            (below, above), sums = after([below, above], sums)
            below, above, keys, values = lax.optimization_barrier((below, above, below[:blocks], above[blocks:]))
            pieces = [above, moved(above, swap), below, moved(below, swap)]
    keys, values = moved(keys, up), moved(values, down)
    most = 2 * number.shape[0] // count
    sums = far_part("far_next", first[4 * half - 6 : 4 * half - 1], block, 4 * most, query_norm, sums, pieces)
    (keys, values), sums = after([keys, values], sums)
    pieces = [keys, moved(keys, swap), values, moved(values, swap)]
    return far_part("far_last", first[4 * half - 2 :], block, 2 * most, query_norm, sums, pieces, live)


def solution(mesh):
    in_specs = (
        P("tile", "head"),
        P("tile", "head"),
        P("tile", "head"),
        P("head"),
        P("head"),
        P("tile", None, "head"),
        P("tile", None, "head"),
        P("tile"),
        P("tile"),
        P("tile", None),
        P("tile"),
    )
    out_specs = P("tile", "head")
    return jax.shard_map(
        per_device, mesh=mesh, in_specs=in_specs, out_specs=out_specs, check_vma=False
    )
```

time: 164 us -> 146 us (0.89)
  waiting for transfers between devices: 32.5 us -> 63.1 us
  starting transfers between devices: 45.6 us -> 15.3 us
  Pallas kernels: 56.4 us -> 33.8 us
  local copies, waits for them, and re-layouts: 11.3 us -> 18.2 us
  between operations: 7.25 us -> 5.54 us
    ppermute x17, waiting for transfers between devices: 32.5 us -> 63.1 us  [moved(): return lax.ppermute(piece, 'tile', pairs)]
    ppermute x17, starting transfers between devices: 39.1 us -> 12.6 us  [moved(): return lax.ppermute(piece, 'tile', pairs)]
    pallas_call x4, Pallas kernels: 56.4 us -> 33.8 us  [the longest x3 26.7 us: far_part(): pl.pallas_call(functools.partial(far_kernel, groups, live is not None), i...]
    unnamed x35 -> x39, local copies, waits for them, and re-layouts: 4.81 us -> 12.8 us
    ppermute x4 -> x2, starting transfers between devices: 6.52 us -> 2.76 us  [passed_along(): lax.ppermute(value, axis, [(source, source + steps) for source in range(f...]
    slice x6 -> x5, local copies, waits for them, and re-layouts: 3.95 us -> 4.2 us  [the longest x1 1.85 us: per_device(): fronts = edge(key_norm[:EDGE], value_rows[:EDGE], edge_index < my_length)]
  transfers between devices with their start and end apart: 21 -> 19, of which waited for: 7 -> 11; matrix products, arithmetic and copies ran while one was open for 8% -> 5% of each run, Pallas kernels for 27% -> 19%
where the time goes in v3:
time: 146 us; the launch traced here: 145 us
  waiting for transfers between devices  63.1 us (43%)
  Pallas kernels  33.8 us (23%)
  local copies, waits for them, and re-layouts  18.2 us (12%)
  starting transfers between devices  15.3 us (10%)
  between operations  5.54 us (4%)
  blocking collectives  4.93 us (3%)
  other arithmetic  4.3 us (3%)
    ppermute x17, waiting for transfers between devices, moved(): return lax.ppermute(piece, 'tile', pairs)  63.1 us
    pallas_call x3, Pallas kernels, far_part(): pl.pallas_call(functools.partial(far_kernel, groups, live is not None), i...  26.7 us
    unnamed x39, local copies, waits for them, and re-layouts  12.8 us
    ppermute x17, starting transfers between devices, moved(): return lax.ppermute(piece, 'tile', pairs)  12.6 us
    pallas_call x1, Pallas kernels, near_part(): pl.pallas_call(near_kernel, in_specs=[IN_VMEM] * 6, out_specs=[IN_VMEM] *...  7.06 us
    psum x1, blocking collectives, per_device(): lax.psum((row_squares(query_rows), row_squares(key_rows)), 'head')  4.93 us
  transfers between devices with their start and end apart: 19, of which 11 were waited for; matrix products, arithmetic and copies ran while one was open for 5% of the time, Pallas kernels for 19%

profile of v3, /device:TPU:0, one launch (start us, length us, event | category | flops | bytes accessed | tf_op | source)
XLA Modules:
  0.0 145.2 jit_solution(8060842956755962606)
XLA Ops:
  0.0 1.3 constant_dynamic-update-slice_fusion.1
  1.4 3.0 %collective-permute-start = (bf16[32,8,2560]{2,1,0:T(8,128)(2,1)S(1)}, bf16[32,8,2560]{2,1,0:T(8,128)(2,1)}, u32[]{:S(2)}, u32[]{:S(2)}) collective-permute-start(bf16[32,8,2560]{2,1,0:T(8,128)(2,1)S(1)} %constant_dynamic-update-slice_fusion.refs_7_), channel_id=1, source_target_pairs={{0,4},{2,6},{8,0},{10,2},{16,8},{18,10},{24,16},{26,18},{28,24},{3... | collective-permute-start | bytes 3932168 | tf_op jit(solution)/shard_map/ppermute | solution.py:287
  6.1 4.9 %all-reduce.7 = (f32[384]{0:T(512)S(1)}, f32[384]{0:T(512)S(1)}) all-reduce(f32[384]{0:T(512)S(1)} %fusion, f32[384]{0:T(512)S(1)} %fusion.3), channel_id=1, replica_groups=mesh['tile'=16,'head'=2] {'head'}, use_global_device_ids=true, to_apply=%region_4.5 | all-reduce | flops 768 | bytes 6144 | tf_op jit(solution)/shard_map/psum | solution.py:255
  11.7 2.1 %fusion.5.k_ref = bf16[384,2560]{1,0:T(8,128)(2,1)S(1)} fusion(bf16[384,2560]{1,0:T(8,128)(2,1)} %param.12, f32[2560]{0:T(1024)S(1)} %copy-done.16, f32[384]{0:T(512)S(1)} %add_rsqrt_fusion), kind=kLoop, calls=%fused_computation.9 | loop fusion | flops 3932160 | bytes 3943936 | tf_op jit(solution)/shard_map/convert_element_type | solution.py:33
  13.8 1.9 %fusion.21 = (bf16[64,2560]{1,0:T(8,128)(2,1)S(1)}, bf16[64,2560]{1,0:T(8,128)(2,1)S(1)}, bf16[64,2560]{1,0:T(8,128)(2,1)S(1)}, bf16[64,2560]{1,0:T(8,128)(2,1)S(1)}) fusion(bf16[384,2560]{1,0:T(8,128)(2,1)S(1)} %fusion.5.k_ref, s32[]{:T(128)S(6)} %select_n.185, bf16[384,2560]{1,0:T(8,128)(2,1)} %v_ref.1), kind=kLoop, calls=%fused_computation.91 | loop fusion | bytes 5898244 | tf_op jit(solution)/shard_map/slice | solution.py:272
  15.8 1.5 %collective-permute-start.4 = (bf16[144,2560]{1,0:T(8,128)(2,1)S(1)}, bf16[144,2560]{1,0:T(8,128)(2,1)S(1)}, u32[]{:S(2)}, u32[]{:S(2)}) collective-permute-start(bf16[144,2560]{1,0:T(8,128)(2,1)S(1)} %fusion.8), channel_id=1, source_target_pairs={{0,2},{2,4},{4,6},{6,8},{8,10},{10,12},{12,14},{14,16},{16,18},{18... | collective-permute-start | bytes 2211848 | tf_op jit(solution)/shard_map/ppermute | solution.py:22
  17.3 1.3 collective-permute-start.5
  18.6 22.8 %collective-permute-done.refs_9_ = bf16[32,8,2560]{2,1,0:T(8,128)(2,1)} collective-permute-done((bf16[32,8,2560]{2,1,0:T(8,128)(2,1)S(1)}, bf16[32,8,2560]{2,1,0:T(8,128)(2,1)}, u32[]{:S(2)}, u32[]{:S(2)}) %collective-permute-start) | collective-permute-done | bytes 1310752 | tf_op jit(solution)/shard_map/ppermute | solution.py:287
  42.1 2.6 %collective-permute-start.2 = (bf16[32,8,2560]{2,1,0:T(8,128)(2,1)}, bf16[32,8,2560]{2,1,0:T(8,128)(2,1)}, u32[]{:S(2)}, u32[]{:S(2)}) collective-permute-start(bf16[32,8,2560]{2,1,0:T(8,128)(2,1)} %collective-permute-done.refs_9_), channel_id=1, source_target_pairs={{0,4},{2,6},{8,0},{10,2},{16,8},{18,10},{24,16},{26,18},{28,24},{3... | collective-permute-start | bytes 3932168 | tf_op jit(solution)/shard_map/ppermute | solution.py:287
  47.3 7.1 %near_part.1 = (f32[20,8,384]{2,1,0:T(8,128)S(1)}, f32[20,8,384]{2,1,0:T(8,128)S(1)}, f32[2560,384]{1,0:T(8,128)S(1)}) custom-call(f32[512,128]{1,0:T(8,128)S(1)} %broadcast_in_dim.99.bias_ref, bf16[384,2560]{1,0:T(8,128)(2,1)S(1)} %fusion.2.q_ref.refs_3_, bf16[384,2560]{1,0:T(8,128)(2,1)S(1)} %copy-done.3, bf16[384,2560]{1,0:T(8,128)(2,1)S(1)} %copy-done.4, ...), custom_call_target="tpu_custom_call" | custom-call | flops 2013265920 | bytes 9830400 | tf_op jit(solution)/shard_map/near_part/pallas_call | solution.py:132
  54.4 1.9 %copy-done = f32[2560,384]{1,0:T(8,128)} copy-done((f32[2560,384]{1,0:T(8,128)}, f32[2560,384]{1,0:T(8,128)S(1)}, u32[]{:S(2)}) %copy-start) | copy-done | bytes 3932184
  57.0 17.3 %collective-permute-done.2.refs_13_ = bf16[32,8,2560]{2,1,0:T(8,128)(2,1)} collective-permute-done((bf16[32,8,2560]{2,1,0:T(8,128)(2,1)}, bf16[32,8,2560]{2,1,0:T(8,128)(2,1)}, u32[]{:S(2)}, u32[]{:S(2)}) %collective-permute-start.2) | collective-permute-done | bytes 1310752 | tf_op jit(solution)/shard_map/ppermute | solution.py:287
  74.2 1.7 %collective-permute-done.3.refs_15_ = bf16[32,8,2560]{2,1,0:T(8,128)(2,1)} collective-permute-done((bf16[32,8,2560]{2,1,0:T(8,128)(2,1)}, bf16[32,8,2560]{2,1,0:T(8,128)(2,1)}, u32[]{:S(2)}, u32[]{:S(2)}) %collective-permute-start.3) | collective-permute-done | bytes 1310752 | tf_op jit(solution)/shard_map/ppermute | solution.py:287
  77.2 4.0 %collective-permute-done.10.refs_12_ = bf16[32,8,2560]{2,1,0:T(8,128)(2,1)S(1)} collective-permute-done((bf16[32,8,2560]{2,1,0:T(8,128)(2,1)}, bf16[32,8,2560]{2,1,0:T(8,128)(2,1)S(1)}, u32[]{:S(2)}, u32[]{:S(2)}) %collective-permute-start.10) | collective-permute-done | bytes 1310752 | tf_op jit(solution)/shard_map/ppermute | solution.py:287
  81.2 1.1 copy-done.9
  82.3 2.2 %collective-permute-start.8 = (bf16[32,8,2560]{2,1,0:T(8,128)(2,1)}, bf16[32,8,2560]{2,1,0:T(8,128)(2,1)}, u32[]{:S(2)}, u32[]{:S(2)}) collective-permute-start(bf16[32,8,2560]{2,1,0:T(8,128)(2,1)} %collective-permute-done.2.refs_13_), channel_id=1, source_target_pairs={{0,4},{2,6},{8,0},{10,2},{16,8},{18,10},{24,16},{26,18},{28,24},{3... | collective-permute-start | bytes 3932168 | tf_op jit(solution)/shard_map/ppermute | solution.py:287
  87.1 2.1 %copy-done.1 = f32[2560,384]{1,0:T(8,128)S(1)} copy-done((f32[2560,384]{1,0:T(8,128)S(1)}, f32[2560,384]{1,0:T(8,128)}, u32[]{:S(2)}) %copy-start.1) | copy-done | bytes 3932184
  89.2 0.9 copy-done.6
  90.2 1.3 copy-done.8
  91.5 1.3 copy-done.10
  92.8 12.3 %far_part.1 = (f32[20,8,384]{2,1,0:T(8,128)S(1)}, f32[20,8,384]{2,1,0:T(8,128)S(1)}, f32[2560,384]{1,0:T(8,128)S(1)}) custom-call(s32[11]{0:T(128)S(1)} %bitcast.36, s32[128]{0:T(128)S(1)} %concatenate.58.refs_1_, f32[512,128]{1,0:T(8,128)S(1)} %broadcast_in_dim.100.refs_2_, ...), custom_call_target="tpu_custom_call", output_to_operand_aliasing={{0}: (4, {}), {1}: (5, {}), {2}: (6, {})} | custom-call | flops 2013265920 | bytes 9830400 | tf_op jit(solution)/shard_map/far_part/pallas_call | solution.py:201
  105.1 3.9 %collective-permute-done.7.refs_9_ = bf16[32,8,2560]{2,1,0:T(8,128)(2,1)} collective-permute-done((bf16[32,8,2560]{2,1,0:T(8,128)(2,1)}, bf16[32,8,2560]{2,1,0:T(8,128)(2,1)}, u32[]{:S(2)}, u32[]{:S(2)}) %collective-permute-start.7) | collective-permute-done | bytes 1310752 | tf_op jit(solution)/shard_map/ppermute | solution.py:287
  109.0 4.7 %collective-permute-done.8.refs_7_ = bf16[32,8,2560]{2,1,0:T(8,128)(2,1)} collective-permute-done((bf16[32,8,2560]{2,1,0:T(8,128)(2,1)}, bf16[32,8,2560]{2,1,0:T(8,128)(2,1)}, u32[]{:S(2)}, u32[]{:S(2)}) %collective-permute-start.8) | collective-permute-done | bytes 1310752 | tf_op jit(solution)/shard_map/ppermute | solution.py:287
  113.7 1.1 slice.73
  114.8 1.1 slice.74
  116.5 2.2 %collective-permute-start.14 = (bf16[16,8,2560]{2,1,0:T(8,128)(2,1)S(1)}, bf16[16,8,2560]{2,1,0:T(8,128)(2,1)S(1)}, u32[]{:S(2)}, u32[]{:S(2)}) collective-permute-start(bf16[16,8,2560]{2,1,0:T(8,128)(2,1)S(1)} %slice.74), channel_id=1, source_target_pairs={{0,4},{2,6},{8,0},{10,2},{16,8},{18,10},{24,16},{26,18},{28,24},{3... | collective-permute-start | bytes 1966088 | tf_op jit(solution)/shard_map/ppermute | solution.py:287
  120.1 1.1 collective-permute-done.16.refs_10_
  121.2 7.5 %far_next.1 = (f32[20,8,384]{2,1,0:T(8,128)S(1)}, f32[20,8,384]{2,1,0:T(8,128)S(1)}, f32[2560,384]{1,0:T(8,128)S(1)}) custom-call(s32[5]{0:T(128)S(1)} %slice.75.refs_0_, s32[96]{0:T(128)S(1)} %concatenate.59.refs_1_, f32[256,128]{1,0:T(8,128)S(1)} %broadcast_in_dim.103.refs_2_, ...), custom_call_target="tpu_custom_call", output_to_operand_aliasing={{0}: (4, {}), {1}: (5, {}), {2}: (6, {})} | custom-call | flops 1006632960 | bytes 9830400 | tf_op jit(solution)/shard_map/far_next/pallas_call | solution.py:201
  128.8 4.9 %collective-permute-done.13.refs_8_ = bf16[16,8,2560]{2,1,0:T(8,128)(2,1)S(1)} collective-permute-done((bf16[16,8,2560]{2,1,0:T(8,128)(2,1)S(1)}, bf16[16,8,2560]{2,1,0:T(8,128)(2,1)S(1)}, u32[]{:S(2)}, u32[]{:S(2)}) %collective-permute-start.13) | collective-permute-done | bytes 655392 | tf_op jit(solution)/shard_map/ppermute | solution.py:287
  133.7 1.5 %collective-permute-done.14.refs_10_ = bf16[16,8,2560]{2,1,0:T(8,128)(2,1)S(1)} collective-permute-done((bf16[16,8,2560]{2,1,0:T(8,128)(2,1)S(1)}, bf16[16,8,2560]{2,1,0:T(8,128)(2,1)S(1)}, u32[]{:S(2)}, u32[]{:S(2)}) %collective-permute-start.14) | collective-permute-done | bytes 655392 | tf_op jit(solution)/shard_map/ppermute | solution.py:287
  137.3 0.9 collective-permute-done.18.refs_11_
  138.3 6.9 %far_last.1 = bf16[384,2560]{1,0:T(8,128)(2,1)} custom-call(s32[3]{0:T(128)S(1)} %slice.59.refs_0_, s32[80]{0:T(128)S(1)} %concatenate.46.refs_1_, f32[128,128]{1,0:T(8,128)S(1)} %broadcast_in_dim.94.refs_2_, bf16[384,2560]{1,0:T(8,128)(2,1)S(1)} %fusion.2.q_ref.refs_3_, f32[20,8,384]{2,1,0:T(8,128)S(1)} %get-tuple-element.56.refs_4_, ...), custom_call_target="tpu_custom_call" | custom-call | flops 503316480 | bytes 9830400 | tf_op jit(solution)/shard_map/far_last/pallas_call | solution.py:201
  (93 shorter events, 9.3 us)
Async XLA Ops:
  0.0 5.2 %copy-start.12 = (bf16[384,2560]{1,0:T(8,128)(2,1)S(1)}, bf16[384,2560]{1,0:T(8,128)(2,1)}, u32[]{:S(2)}) copy-start(bf16[384,2560]{1,0:T(8,128)(2,1)} %param.11) | copy-start | bytes 5898244
  1.3 4.3 %copy-start.11 = (bf16[384,2560]{1,0:T(8,128)(2,1)S(1)}, bf16[384,2560]{1,0:T(8,128)(2,1)}, u32[]{:S(2)}) copy-start(bf16[384,2560]{1,0:T(8,128)(2,1)} %param.12) | copy-start | bytes 5898244
  1.4 40.1 %collective-permute-start = (bf16[32,8,2560]{2,1,0:T(8,128)(2,1)S(1)}, bf16[32,8,2560]{2,1,0:T(8,128)(2,1)}, u32[]{:S(2)}, u32[]{:S(2)}) collective-permute-start(bf16[32,8,2560]{2,1,0:T(8,128)(2,1)S(1)} %constant_dynamic-update-slice_fusion.refs_7_), channel_id=1, source_target_pairs={{0,4},{2,6},{8,0},{10,2},{16,8},{18,10},{24,16},{26,18},{28,24},{3... | collective-permute-start | bytes 3932168 | tf_op jit(solution)/shard_map/ppermute | solution.py:287
  4.4 37.1 %collective-permute-start.1 = (bf16[32,8,2560]{2,1,0:T(8,128)(2,1)S(1)}, bf16[32,8,2560]{2,1,0:T(8,128)(2,1)}, u32[]{:S(2)}, u32[]{:S(2)}) collective-permute-start(bf16[32,8,2560]{2,1,0:T(8,128)(2,1)S(1)} %constant_dynamic-update-slice_fusion.refs_7_), channel_id=1, source_target_pairs={{0,8},{2,10},{8,16},{10,18},{16,24},{18,26},{24,28},{26,30},{28,20... | collective-permute-start | bytes 3932168 | tf_op jit(solution)/shard_map/ppermute | solution.py:287
  5.6 6.1 %copy-start.16 = (f32[2560]{0:T(1024)S(1)}, f32[2560]{0:T(1024)}, u32[]{:S(2)}) copy-start(f32[2560]{0:T(1024)} %param.15) | copy-start | bytes 30724
  13.8 1.9 %copy-start.2 = (bf16[384,2560]{1,0:T(8,128)(2,1)}, bf16[384,2560]{1,0:T(8,128)(2,1)S(1)}, u32[]{:S(2)}) copy-start(bf16[384,2560]{1,0:T(8,128)(2,1)S(1)} %fusion.5.k_ref) | copy-start | bytes 5898244
  15.7 25.8 %copy-start.15 = (f32[2560]{0:T(1024)S(1)}, f32[2560]{0:T(1024)}, u32[]{:S(2)}) copy-start(f32[2560]{0:T(1024)} %param.14) | copy-start | bytes 30724
  15.7 25.8 %copy-start.13 = (bf16[384,2560]{1,0:T(8,128)(2,1)S(1)}, bf16[384,2560]{1,0:T(8,128)(2,1)}, u32[]{:S(2)}) copy-start(bf16[384,2560]{1,0:T(8,128)(2,1)} %param.11) | copy-start | bytes 5898244
  15.8 28.9 %collective-permute-start.4 = (bf16[144,2560]{1,0:T(8,128)(2,1)S(1)}, bf16[144,2560]{1,0:T(8,128)(2,1)S(1)}, u32[]{:S(2)}, u32[]{:S(2)}) collective-permute-start(bf16[144,2560]{1,0:T(8,128)(2,1)S(1)} %fusion.8), channel_id=1, source_target_pairs={{0,2},{2,4},{4,6},{6,8},{8,10},{10,12},{12,14},{14,16},{16,18},{18... | collective-permute-start | bytes 2211848 | tf_op jit(solution)/shard_map/ppermute | solution.py:22
  17.3 27.4 %collective-permute-start.5 = (bf16[144,2560]{1,0:T(8,128)(2,1)S(1)}, bf16[144,2560]{1,0:T(8,128)(2,1)S(1)}, u32[]{:S(2)}, u32[]{:S(2)}) collective-permute-start(bf16[144,2560]{1,0:T(8,128)(2,1)S(1)} %fusion.9), channel_id=1, source_target_pairs={{2,0},{4,2},{6,4},{8,6},{10,8},{12,10},{14,12},{16,14},{18,16},{20... | collective-permute-start | bytes 2211848 | tf_op jit(solution)/shard_map/ppermute | solution.py:22
  41.5 3.2 %collective-permute-start.6 = (bf16[32,8,2560]{2,1,0:T(8,128)(2,1)S(1)}, bf16[32,8,2560]{2,1,0:T(8,128)(2,1)S(1)}, u32[]{:S(2)}, u32[]{:S(2)}) collective-permute-start(bf16[32,8,2560]{2,1,0:T(8,128)(2,1)S(1)} %constant_dynamic-update-slice_fusion.refs_7_), channel_id=1, source_target_pairs={{0,2},{2,0},{4,6},{6,4},{8,10},{10,8},{12,14},{14,12},{16,18},{18,... | collective-permute-start | bytes 3932168 | tf_op jit(solution)/shard_map/ppermute | solution.py:287
  42.1 32.2 %collective-permute-start.2 = (bf16[32,8,2560]{2,1,0:T(8,128)(2,1)}, bf16[32,8,2560]{2,1,0:T(8,128)(2,1)}, u32[]{:S(2)}, u32[]{:S(2)}) collective-permute-start(bf16[32,8,2560]{2,1,0:T(8,128)(2,1)} %collective-permute-done.refs_9_), channel_id=1, source_target_pairs={{0,4},{2,6},{8,0},{10,2},{16,8},{18,10},{24,16},{26,18},{28,24},{3... | collective-permute-start | bytes 3932168 | tf_op jit(solution)/shard_map/ppermute | solution.py:287
  44.7 31.2 %collective-permute-start.3 = (bf16[32,8,2560]{2,1,0:T(8,128)(2,1)}, bf16[32,8,2560]{2,1,0:T(8,128)(2,1)}, u32[]{:S(2)}, u32[]{:S(2)}) collective-permute-start(bf16[32,8,2560]{2,1,0:T(8,128)(2,1)} %collective-permute-done.1.refs_11_), channel_id=1, source_target_pairs={{0,8},{2,10},{8,16},{10,18},{16,24},{18,26},{24,28},{26,30},{28,20... | collective-permute-start | bytes 3932168 | tf_op jit(solution)/shard_map/ppermute | solution.py:287
  44.9 1.9 %copy-start.4 = (bf16[384,2560]{1,0:T(8,128)(2,1)S(1)}, bf16[384,2560]{1,0:T(8,128)(2,1)}, u32[]{:S(2)}) copy-start(bf16[384,2560]{1,0:T(8,128)(2,1)} %v_ref.1) | copy-start | bytes 5898244
  45.0 2.4 %copy-start.3 = (bf16[384,2560]{1,0:T(8,128)(2,1)S(1)}, bf16[384,2560]{1,0:T(8,128)(2,1)}, u32[]{:S(2)}) copy-start(bf16[384,2560]{1,0:T(8,128)(2,1)} %copy-done.2) | copy-start | bytes 5898244
  47.3 37.2 %copy-start.17 = (s32[64,1]{0,1:T(1,128)S(1)}, s32[64,1]{0,1:T(1,128)}, u32[]{:S(2)}) copy-start(s32[64,1]{0,1:T(1,128)} %param.20) | copy-start | bytes 772
  47.3 37.4 %copy-start.18 = (s32[64]{0:T(128)S(1)}, s32[64]{0:T(128)}, u32[]{:S(2)}) copy-start(s32[64]{0:T(128)} %param.21) | copy-start | bytes 772
  54.4 1.9 %copy-start = (f32[2560,384]{1,0:T(8,128)}, f32[2560,384]{1,0:T(8,128)S(1)}, u32[]{:S(2)}) copy-start(f32[2560,384]{1,0:T(8,128)S(1)} %get-tuple-element.41.refs_6_) | copy-start | bytes 11796484
  75.9 5.3 %collective-permute-start.10 = (bf16[32,8,2560]{2,1,0:T(8,128)(2,1)}, bf16[32,8,2560]{2,1,0:T(8,128)(2,1)S(1)}, u32[]{:S(2)}, u32[]{:S(2)}) collective-permute-start(bf16[32,8,2560]{2,1,0:T(8,128)(2,1)} %collective-permute-done.1.refs_11_), channel_id=1, source_target_pairs={{0,2},{2,0},{4,6},{6,4},{8,10},{10,8},{12,14},{14,12},{16,18},{18,... | collective-permute-start | bytes 3932168 | tf_op jit(solution)/shard_map/ppermute | solution.py:287
  76.5 10.4 %collective-permute-start.11 = (bf16[32,8,2560]{2,1,0:T(8,128)(2,1)}, bf16[32,8,2560]{2,1,0:T(8,128)(2,1)}, u32[]{:S(2)}, u32[]{:S(2)}) collective-permute-start(bf16[32,8,2560]{2,1,0:T(8,128)(2,1)} %collective-permute-done.2.refs_13_), channel_id=1, source_target_pairs={{0,2},{2,0},{4,6},{6,4},{8,10},{10,8},{12,14},{14,12},{16,18},{18,... | collective-permute-start | bytes 3932168 | tf_op jit(solution)/shard_map/ppermute | solution.py:287
  76.5 10.4 %collective-permute-start.12 = (bf16[32,8,2560]{2,1,0:T(8,128)(2,1)}, bf16[32,8,2560]{2,1,0:T(8,128)(2,1)}, u32[]{:S(2)}, u32[]{:S(2)}) collective-permute-start(bf16[32,8,2560]{2,1,0:T(8,128)(2,1)} %collective-permute-done.3.refs_15_), channel_id=1, source_target_pairs={{0,2},{2,0},{4,6},{6,4},{8,10},{10,8},{12,14},{14,12},{16,18},{18,... | collective-permute-start | bytes 3932168 | tf_op jit(solution)/shard_map/ppermute | solution.py:287
  77.0 9.9 %collective-permute-start.9 = (bf16[32,8,2560]{2,1,0:T(8,128)(2,1)}, bf16[32,8,2560]{2,1,0:T(8,128)(2,1)}, u32[]{:S(2)}, u32[]{:S(2)}) collective-permute-start(bf16[32,8,2560]{2,1,0:T(8,128)(2,1)} %collective-permute-done.refs_9_), channel_id=1, source_target_pairs={{0,2},{2,0},{4,6},{6,4},{8,10},{10,8},{12,14},{14,12},{16,18},{18,... | collective-permute-start | bytes 3932168 | tf_op jit(solution)/shard_map/ppermute | solution.py:287
  77.0 31.9 %collective-permute-start.7 = (bf16[32,8,2560]{2,1,0:T(8,128)(2,1)}, bf16[32,8,2560]{2,1,0:T(8,128)(2,1)}, u32[]{:S(2)}, u32[]{:S(2)}) collective-permute-start(bf16[32,8,2560]{2,1,0:T(8,128)(2,1)} %collective-permute-done.3.refs_15_), channel_id=1, source_target_pairs={{0,8},{2,10},{8,16},{10,18},{16,24},{18,26},{24,28},{26,30},{28,20... | collective-permute-start | bytes 3932168 | tf_op jit(solution)/shard_map/ppermute | solution.py:287
  82.3 31.4 %collective-permute-start.8 = (bf16[32,8,2560]{2,1,0:T(8,128)(2,1)}, bf16[32,8,2560]{2,1,0:T(8,128)(2,1)}, u32[]{:S(2)}, u32[]{:S(2)}) collective-permute-start(bf16[32,8,2560]{2,1,0:T(8,128)(2,1)} %collective-permute-done.2.refs_13_), channel_id=1, source_target_pairs={{0,4},{2,6},{8,0},{10,2},{16,8},{18,10},{24,16},{26,18},{28,24},{3... | collective-permute-start | bytes 3932168 | tf_op jit(solution)/shard_map/ppermute | solution.py:287
  87.1 2.1 %copy-start.1 = (f32[2560,384]{1,0:T(8,128)S(1)}, f32[2560,384]{1,0:T(8,128)}, u32[]{:S(2)}) copy-start(f32[2560,384]{1,0:T(8,128)} %copy-done) | copy-start | bytes 11796484
  90.2 1.3 copy-start.8
  115.9 4.1 %collective-permute-start.15 = (bf16[32,8,2560]{2,1,0:T(8,128)(2,1)}, bf16[32,8,2560]{2,1,0:T(8,128)(2,1)S(1)}, u32[]{:S(2)}, u32[]{:S(2)}) collective-permute-start(bf16[32,8,2560]{2,1,0:T(8,128)(2,1)} %collective-permute-done.8.refs_7_), channel_id=1, source_target_pairs={{0,2},{2,0},{4,6},{6,4},{8,10},{10,8},{12,14},{14,12},{16,18},{18,... | collective-permute-start | bytes 3932168 | tf_op jit(solution)/shard_map/ppermute | solution.py:287
  116.0 5.1 %collective-permute-start.16 = (bf16[32,8,2560]{2,1,0:T(8,128)(2,1)}, bf16[32,8,2560]{2,1,0:T(8,128)(2,1)S(1)}, u32[]{:S(2)}, u32[]{:S(2)}) collective-permute-start(bf16[32,8,2560]{2,1,0:T(8,128)(2,1)} %collective-permute-done.7.refs_9_), channel_id=1, source_target_pairs={{0,2},{2,0},{4,6},{6,4},{8,10},{10,8},{12,14},{14,12},{16,18},{18,... | collective-permute-start | bytes 3932168 | tf_op jit(solution)/shard_map/ppermute | solution.py:287
  116.5 17.2 %collective-permute-start.13 = (bf16[16,8,2560]{2,1,0:T(8,128)(2,1)S(1)}, bf16[16,8,2560]{2,1,0:T(8,128)(2,1)S(1)}, u32[]{:S(2)}, u32[]{:S(2)}) collective-permute-start(bf16[16,8,2560]{2,1,0:T(8,128)(2,1)S(1)} %slice.73), channel_id=1, source_target_pairs={{0,8},{2,10},{8,16},{10,18},{16,24},{18,26},{24,28},{26,30},{28,20... | collective-permute-start | bytes 1966088 | tf_op jit(solution)/shard_map/ppermute | solution.py:287
  116.5 18.7 %collective-permute-start.14 = (bf16[16,8,2560]{2,1,0:T(8,128)(2,1)S(1)}, bf16[16,8,2560]{2,1,0:T(8,128)(2,1)S(1)}, u32[]{:S(2)}, u32[]{:S(2)}) collective-permute-start(bf16[16,8,2560]{2,1,0:T(8,128)(2,1)S(1)} %slice.74), channel_id=1, source_target_pairs={{0,4},{2,6},{8,0},{10,2},{16,8},{18,10},{24,16},{26,18},{28,24},{3... | collective-permute-start | bytes 1966088 | tf_op jit(solution)/shard_map/ppermute | solution.py:287
  135.2 2.1 %collective-permute-start.17 = (bf16[16,8,2560]{2,1,0:T(8,128)(2,1)S(1)}, bf16[16,8,2560]{2,1,0:T(8,128)(2,1)S(1)}, u32[]{:S(2)}, u32[]{:S(2)}) collective-permute-start(bf16[16,8,2560]{2,1,0:T(8,128)(2,1)S(1)} %collective-permute-done.13.refs_8_), channel_id=1, source_target_pairs={{0,2},{2,0},{4,6},{6,4},{8,10},{10,8},{12,14},{14,12},{16,18},{18,... | collective-permute-start | bytes 1966088 | tf_op jit(solution)/shard_map/ppermute | solution.py:287
  135.2 3.0 %collective-permute-start.18 = (bf16[16,8,2560]{2,1,0:T(8,128)(2,1)S(1)}, bf16[16,8,2560]{2,1,0:T(8,128)(2,1)S(1)}, u32[]{:S(2)}, u32[]{:S(2)}) collective-permute-start(bf16[16,8,2560]{2,1,0:T(8,128)(2,1)S(1)} %collective-permute-done.14.refs_10_), channel_id=1, source_target_pairs={{0,2},{2,0},{4,6},{6,4},{8,10},{10,8},{12,14},{14,12},{16,18},{18,... | collective-permute-start | bytes 1966088 | tf_op jit(solution)/shard_map/ppermute | solution.py:287
  (6 other events, 6.4 us)

commit v4 on v3

--- a/solution.py
+++ b/solution.py
@@ -140,32 +140,73 @@
     )(bias, query, keys, values, edge_keys, edge_values)
 
 
+def pick_kernel(groups, slots, first_ref, block_ref, *refs):
+    key_pieces, value_pieces = refs[:groups], refs[groups : 2 * groups]
+    picked, sem = refs[2 * groups :]
+    start = first_ref[0]
+
+    def fetch_from(g):
+        def fetch(slot, carry):
+            block = block_ref[slot]
+            to = slot - start
+            pltpu.make_async_copy(key_pieces[g].at[block], picked.at[to], sem).start()
+            pltpu.make_async_copy(value_pieces[g].at[block], picked.at[slots + to], sem).start()
+            return carry
+
+        return fetch
+
+    for g in range(groups):
+        lax.fori_loop(first_ref[g], first_ref[g + 1], fetch_from(g), 0)
+    lax.fori_loop(first_ref[groups], start + slots, fetch_from(0), 0)
+    pltpu.make_async_copy(picked, picked, sem).wait()
+
+
+def pick_part(name, first, block, slots, key_pieces, value_pieces):
+    groups, (_, tokens, width) = len(key_pieces), key_pieces[0].shape
+    block = jnp.concatenate([block, jnp.zeros((slots,), jnp.int32)])
+    return pl.pallas_call(
+        functools.partial(pick_kernel, groups, slots),
+        in_specs=[pl.BlockSpec(memory_space=pltpu.SMEM)] * 2 + [pl.BlockSpec(memory_space=pl.ANY)] * (2 * groups),
+        out_specs=pl.BlockSpec(memory_space=pl.ANY),
+        out_shape=jax.ShapeDtypeStruct((2 * slots, tokens, width), jnp.bfloat16),
+        scratch_shapes=[pltpu.SemaphoreType.DMA],
+        cost_estimate=pl.CostEstimate(flops=0, bytes_accessed=8 * slots * tokens * width, transcendentals=0),
+        name=name,
+    )(first, block, *key_pieces, *value_pieces)
+
+
 def far_kernel(groups, last, *refs):
     first_ref, block_ref, bias_ref, q_ref, before_top, before_sum, before_acc = refs[:7]
     refs = refs[7:]
     if last:
         live_ref, refs = refs[0], refs[1:]
-    *out_refs, keys, values, sems = refs[len(refs) - (4 if last else 6) :]
-    pieces = refs[: len(refs) - len(out_refs) - 3]
-    joined = len(pieces) == groups
-    key_pieces, value_pieces = pieces[:groups], pieces if joined else pieces[groups:]
-    offset = pieces[0].shape[0] // 2 if joined else 0
+    key_pieces, value_pieces, received = refs[:groups], refs[groups : 2 * groups], refs[2 * groups]
+    *out_refs, keys, values, sems = refs[2 * groups + 1 :]
     slots, tokens = keys.shape[:2]
+    offset = received.shape[0] // 2
     start = first_ref[0]
+
+    def fetch_one(key_block, value_block, to):
+        pltpu.make_async_copy(key_block, keys.at[to], sems.at[0]).start()
+        pltpu.make_async_copy(value_block, values.at[to], sems.at[1]).start()
 
     def fetch_from(g):
         def fetch(slot, carry):
             block = block_ref[slot]
-            to = slot - start
-            pltpu.make_async_copy(key_pieces[g].at[block], keys.at[to], sems.at[0]).start()
-            pltpu.make_async_copy(value_pieces[g].at[block + offset], values.at[to], sems.at[1]).start()
+            fetch_one(key_pieces[g].at[block], value_pieces[g].at[block], slot - start)
             return carry
 
         return fetch
+
+    def fetch_received(slot, carry):
+        block = slot - first_ref[groups]
+        fetch_one(received.at[block], received.at[offset + block], slot - start)
+        return carry
 
     for g in range(groups):
         lax.fori_loop(first_ref[g], first_ref[g + 1], fetch_from(g), 0)
-    lax.fori_loop(first_ref[groups], start + slots, fetch_from(0), 0)
+    lax.fori_loop(first_ref[groups], first_ref[groups + 1], fetch_received, 0)
+    lax.fori_loop(first_ref[groups + 1], start + slots, fetch_from(0), 0)
     pltpu.make_async_copy(keys, keys, sems.at[0]).wait()
     pltpu.make_async_copy(values, values, sems.at[1]).wait()
 
@@ -188,9 +229,9 @@
     over_heads(q_ref.shape[1], body)
 
 
-def far_part(name, first, block, slots, query, before, pieces, live=None):
+def far_part(name, first, block, slots, query, before, key_pieces, value_pieces, received, live=None):
     rows, width = query.shape
-    groups, tokens = first.shape[0] - 1, pieces[0].shape[1]
+    groups, tokens = len(key_pieces), key_pieces[0].shape[1]
     seen = slots * tokens
     token = jnp.arange(seen, dtype=jnp.int32)[:, None]
     bias = jnp.where(token < (first[-1] - first[0]) * tokens, 0.0, jnp.float32(HIDDEN))
@@ -202,7 +243,7 @@
         functools.partial(far_kernel, groups, live is not None),
         in_specs=[pl.BlockSpec(memory_space=pltpu.SMEM)] * 2
         + [IN_VMEM] * (5 + len(extra))
-        + [pl.BlockSpec(memory_space=pl.ANY)] * len(pieces),
+        + [pl.BlockSpec(memory_space=pl.ANY)] * (2 * groups + 1),
         out_specs=[IN_VMEM] * 3 if live is None else IN_VMEM,
         out_shape=sum_shapes(rows, width) if live is None else final,
         input_output_aliases={4: 0, 5: 1, 6: 2} if live is None else {},
@@ -214,7 +255,34 @@
         compiler_params=pltpu.CompilerParams(vmem_limit_bytes=VMEM_BYTES),
         cost_estimate=cost(rows, seen, width),
         name=name,
-    )(first, block, bias, query, *before, *extra, *pieces)
+    )(first, block, bias, query, *before, *extra, *key_pieces, *value_pieces, received)
+
+
+def in_order(request, lane, owner_blocks, count, me):
+    levels = count // 4
+    places = 2 * levels
+    half = places // 2
+    owners, index = request // owner_blocks, request % owner_blocks
+    ahead = (chip_position(owners, levels) - chip_position(me, levels)) % places
+    distance = jnp.minimum(ahead, places - ahead)
+    piece = jnp.where(distance == 0, 0, 2 * distance - 1 + (ahead > half).astype(jnp.int32))
+    other = ((owners % 2) != lane).astype(jnp.int32)
+    low, size = jnp.zeros_like(piece), jnp.zeros_like(piece)
+    for first, stop in stages(half):
+        inside = (piece >= first) & (piece < stop)
+        low, size = jnp.where(inside, first, low), jnp.where(inside, stop - first, size)
+    group = low + other * size + piece
+    number = jnp.arange(group.shape[0], dtype=jnp.int32)
+    rank_key = group * group.shape[0] + number
+    rank = jnp.sum((rank_key[None, :] < rank_key[:, None]).astype(jnp.int32), axis=1)
+    block = jnp.sum(jnp.where(rank[None, :] == number[:, None], index[None, :], 0), axis=1)
+    groups = jnp.arange(2 * places + 1, dtype=jnp.int32)
+    first = jnp.sum((group[None, :] < groups[:, None]).astype(jnp.int32), axis=1)
+    return block, first
+
+
+def stages(half):
+    return (0, 2 * half - 3), (2 * half - 3, 2 * half - 1), (2 * half - 1, 2 * half)
 
 
 def per_device(
@@ -237,19 +305,11 @@
     half = places // 2
     me = lax.axis_index("tile")
 
-    owners = req_owner[:, 0]
-    ahead = (chip_position(owners, levels) - chip_position(me, levels)) % places
-    distance = jnp.minimum(ahead, places - ahead)
-    side = 2 * (ahead > half).astype(jnp.int32)
-    other = ((owners % 2) != (me % 2)).astype(jnp.int32)
-    group = jnp.where(distance == 0, other, 4 * distance - 2 + side + other)
-    number = jnp.arange(group.shape[0], dtype=jnp.int32)
-    rank_key = group * group.shape[0] + number
-    rank = jnp.sum((rank_key[None, :] < rank_key[:, None]).astype(jnp.int32), axis=1)
-    block = jnp.sum(jnp.where(rank[None, :] == number[:, None], requested_block_index[None, :], 0), axis=1)
-    first = jnp.sum(
-        (group[None, :] < jnp.arange(count + 1, dtype=jnp.int32)[:, None]).astype(jnp.int32), axis=1
-    )
+    swap = [(t, t ^ 1) for t in range(count)]
+    owner_blocks = mem_keys.shape[0]
+    request = req_owner[:, 0] * owner_blocks + requested_block_index
+    my_block, my_first = in_order(request, me % 2, owner_blocks, count, me)
+    my_plan = jnp.concatenate([my_first, my_block])
 
     my_length = tile_len[0]
     totals_q, totals_k = lax.psum((row_squares(query_rows), row_squares(key_rows)), "head")
@@ -281,7 +341,6 @@
         return near_part(bias, query_norm, key_norm, value_rows, edge_keys, edge_values)
 
     up, down = ring_pairs(count, 1), ring_pairs(count, -1)
-    swap = [(t, t ^ 1) for t in range(count)]
 
     def moved(piece, pairs):
         return lax.ppermute(piece, "tile", pairs)
@@ -290,35 +349,42 @@
         *pieces, top = lax.optimization_barrier((*pieces, results[0]))
         return pieces, [top, *results[1:]]
 
-    own = jnp.concatenate([mem_keys, mem_values], 0)
-    blocks = mem_keys.shape[0]
-    below, above = own, own
-    pieces, unswapped = [], [own]
+    keys, values = [mem_keys], [mem_values]
     for step in range(1, half):
-        below, above = moved(below, up), moved(above, down)
+        for pieces in (keys, values):
+            pieces += [moved(pieces[-2 if step > 1 else -1], down), moved(pieces[-1], up)]
         if step == 1:
-            late, _, _ = lax.optimization_barrier((own, below, above))
-            pieces, unswapped = [own, moved(late, swap)], []
-            from_left, from_right, pieces[1] = lax.optimization_barrier((from_left, from_right, pieces[1]))
+            from_left, from_right, *_ = lax.optimization_barrier((from_left, from_right, *values[1:]))
             sums = near_sums(from_left, from_right)
-        unswapped += [above, below]
-        if step == half - 2:
-            unswapped, sums = after(unswapped, sums)
-            below, above = unswapped[-1], unswapped[-2]
-            for piece in unswapped:
-                pieces += [piece, moved(piece, swap)]
-            unswapped = []
-        if step == half - 1:
-            sums = far_part("far_part", first[: 4 * half - 5], block, number.shape[0], query_norm, sums, pieces)
-            (below, above), sums = after([below, above], sums)
-            below, above, keys, values = lax.optimization_barrier((below, above, below[:blocks], above[blocks:]))
-            pieces = [above, moved(above, swap), below, moved(below, swap)]
-    keys, values = moved(keys, up), moved(values, down)
-    most = 2 * number.shape[0] // count
-    sums = far_part("far_next", first[4 * half - 6 : 4 * half - 1], block, 4 * most, query_norm, sums, pieces)
-    (keys, values), sums = after([keys, values], sums)
-    pieces = [keys, moved(keys, swap), values, moved(values, swap)]
-    return far_part("far_last", first[4 * half - 2 :], block, 2 * most, query_norm, sums, pieces, live)
+    keys.append(moved(keys[-1], up))
+    values.append(moved(values[-2], down))
+
+    most = 2 * request.shape[0] // count
+    limits = (min(request.shape[0], count * most), 2 * most, most)
+    for stage, ((first, stop), limit) in enumerate(zip(stages(half), limits)):
+        name = ("first", "second", "third")[stage]
+        size = stop - first
+        (*pieces,), sums = after([*keys[first:stop], *values[first:stop]], sums)
+        plan, *pieces = lax.optimization_barrier((my_plan, *pieces))
+        plan = moved(plan, swap)
+        their_first, their_block = plan[: my_first.shape[0]], plan[my_first.shape[0] :]
+        key_pieces, value_pieces = pieces[:size], pieces[size:]
+        theirs = their_first[2 * first + size : 2 * stop + 1]
+        picked = pick_part("pick_" + name, theirs, their_block, limit, key_pieces, value_pieces)
+        mine = jnp.concatenate([my_first[2 * first : 2 * first + size + 1], my_first[2 * stop :][:1]])
+        sums = far_part(
+            "far_" + name,
+            mine,
+            my_block,
+            min(request.shape[0], 2 * limit),
+            query_norm,
+            sums,
+            key_pieces,
+            value_pieces,
+            moved(picked, swap),
+            live if stage == 2 else None,
+        )
+    return sums
 
 
 def solution(mesh):

time: 146 us -> 375 us (2.57)
  Pallas kernels: 33.8 us -> 260 us
  waiting for transfers between devices: 63.1 us -> 9.71 us
  starting transfers between devices: 15.3 us -> 48.6 us
  local copies, waits for them, and re-layouts: 18.2 us -> 34.6 us
  other arithmetic: 4.3 us -> 10.8 us
    pallas_call x0 -> x3, Pallas kernels: none -> 224 us  [pick_part(): pl.pallas_call(functools.partial(pick_kernel, groups, slots), in_specs=[p...]
    ppermute x17 -> x20, waiting for transfers between devices: 63.1 us -> 9.71 us  [moved(): return lax.ppermute(piece, 'tile', pairs)]
    ppermute x17 -> x20, starting transfers between devices: 12.6 us -> 45.1 us  [moved(): return lax.ppermute(piece, 'tile', pairs)]
    unnamed x39 -> x68, local copies, waits for them, and re-layouts: 12.8 us -> 25.3 us
  transfers between devices with their start and end apart: 19 -> 22, of which waited for: 11 -> 8; matrix products, arithmetic and copies ran while one was open for 5% -> 4% of each run, Pallas kernels for 19% -> 8%
where the time goes in v4:
time: 375 us; the launch traced here: 374 us
  Pallas kernels  260 us (69%)
  starting transfers between devices  48.6 us (13%)
  local copies, waits for them, and re-layouts  34.6 us (9%)
  other arithmetic  10.8 us (3%)
  waiting for transfers between devices  9.71 us (3%)
  between operations  5.51 us (1%)
  blocking collectives  4.94 us (1%)
    pallas_call x3, Pallas kernels, pick_part(): pl.pallas_call(functools.partial(pick_kernel, groups, slots), in_specs=[p...  224 us
    ppermute x20, starting transfers between devices, moved(): return lax.ppermute(piece, 'tile', pairs)  45.1 us
    pallas_call x3, Pallas kernels, far_part(): pl.pallas_call(functools.partial(far_kernel, groups, live is not None), i...  29.2 us
    unnamed x68, local copies, waits for them, and re-layouts  25.3 us
    ppermute x20, waiting for transfers between devices, moved(): return lax.ppermute(piece, 'tile', pairs)  9.71 us
  transfers between devices with their start and end apart: 22, of which 8 were waited for; matrix products, arithmetic and copies ran while one was open for 4% of the time, Pallas kernels for 8%

profile of v4, /device:TPU:0, one launch (start us, length us, event | category | flops | bytes accessed | tf_op | source)
XLA Modules:
  0.0 374.3 jit_solution(16865726418135699794)
XLA Ops:
  0.0 3.0 collective-permute-start.11
  3.0 2.0 collective-permute-start
  5.7 2.0 fusion
  8.2 4.9 %all-reduce.10 = (f32[384]{0:T(512)S(1)}, f32[384]{0:T(512)S(1)}) all-reduce(f32[384]{0:T(512)S(1)} %fusion, f32[384]{0:T(512)S(1)} %fusion.3), channel_id=1, replica_groups=mesh['tile'=16,'head'=2] {'head'}, use_global_device_ids=true, to_apply=%region_4.5 | all-reduce | flops 768 | bytes 6144 | tf_op jit(solution)/shard_map/psum | solution.py:315
  13.8 2.1 fusion.5.k_ref
  16.0 2.8 fusion.21
  19.6 2.2 collective-permute-start.14
  24.9 2.1 fusion.2.q_ref.refs_3_
  27.0 5.1 %collective-permute-start.12 = (bf16[16,8,2560]{2,1,0:T(8,128)(2,1)S(1)}, bf16[16,8,2560]{2,1,0:T(8,128)(2,1)S(1)}, u32[]{:S(2)}, u32[]{:S(2)}) collective-permute-start(bf16[16,8,2560]{2,1,0:T(8,128)(2,1)S(1)} %collective-permute-done.11.refs_7_.refs_14_), channel_id=1, source_target_pairs={{0,8},{2,10},{8,16},{10,18},{16,24},{18,26},{24,28},{26,30},{28,20... | collective-permute-start | bytes 1966088 | tf_op jit(solution)/shard_map/ppermute | solution.py:346
  32.1 1.7 collective-permute-start.5
  33.8 1.4 collective-permute-start.1
  35.2 20.3 %collective-permute-start.9 = (bf16[16,8,2560]{2,1,0:T(8,128)(2,1)}, bf16[16,8,2560]{2,1,0:T(8,128)(2,1)S(1)}, u32[]{:S(2)}, u32[]{:S(2)}) collective-permute-start(bf16[16,8,2560]{2,1,0:T(8,128)(2,1)} %collective-permute-done.8.refs_1_.refs_8_), channel_id=1, source_target_pairs={{0,4},{2,6},{8,0},{10,2},{16,8},{18,10},{24,16},{26,18},{28,24},{3... | collective-permute-start | bytes 1966088 | tf_op jit(solution)/shard_map/ppermute | solution.py:346
  59.4 7.1 %near_part.1 = (f32[20,8,384]{2,1,0:T(8,128)S(1)}, f32[20,8,384]{2,1,0:T(8,128)S(1)}, f32[2560,384]{1,0:T(8,128)S(1)}) custom-call(f32[512,128]{1,0:T(8,128)S(1)} %broadcast_in_dim.111.bias_ref, bf16[384,2560]{1,0:T(8,128)(2,1)S(1)} %fusion.2.q_ref.refs_3_, bf16[384,2560]{1,0:T(8,128)(2,1)S(1)} %copy-done.7, bf16[384,2560]{1,0:T(8,128)(2,1)S(1)} %copy-done.8, ...), custom_call_target="tpu_custom_call" | custom-call | flops 2013265920 | bytes 9830400 | tf_op jit(solution)/shard_map/near_part/pallas_call | solution.py:132
  66.5 1.9 copy-done
  69.1 1.8 collective-permute-done.9.refs_3_.refs_10_
  70.9 4.5 %collective-permute-start.16 = (s32[81]{0:T(128)S(1)}, s32[81]{0:T(128)S(1)}, u32[]{:S(2)}, u32[]{:S(2)}) collective-permute-start(s32[81]{0:T(128)S(1)} %pad_add_fusion.2), channel_id=1, source_target_pairs={{0,2},{2,0},{4,6},{6,4},{8,10},{10,8},{12,14},{14,12},{16,18},{18,... | collective-permute-start | bytes 980 | tf_op jit(solution)/shard_map/ppermute | solution.py:346
  77.5 160.8 %pick_first.1 = bf16[128,8,2560]{2,1,0:T(8,128)(2,1)} custom-call(s32[6]{0:T(128)} %slice.91.first_ref, s32[128]{0:T(128)} %concatenate.81.block_ref, bf16[16,8,2560]{2,1,0:T(8,128)(2,1)} %refs_7_, bf16[16,8,2560]{2,1,0:T(8,128)(2,1)} %collective-permute-done.8.refs_1_.refs_8_, bf16[16,8,2560]{2,1,0:T(8,128)(2,1)} %collective-permute-done.refs_2_.refs_9_, ...), custom_call_target="tpu_custom_call" | custom-call | bytes 10485760 | tf_op jit(solution)/shard_map/pick_first/pallas_call | solution.py:167
  238.7 2.1 collective-permute-start.6
  240.7 2.1 collective-permute-start.10
  245.3 1.9 collective-permute-done.17.refs_17_
  247.4 2.1 copy-done.1
  257.0 14.6 %far_first.1 = (f32[20,8,384]{2,1,0:T(8,128)S(1)}, f32[20,8,384]{2,1,0:T(8,128)S(1)}, f32[2560,384]{1,0:T(8,128)S(1)}) custom-call(s32[7]{0:T(128)S(1)} %pad_add_fusion.1.refs_0_, s32[128]{0:T(128)S(1)} %concatenate.69.refs_1_, f32[512,128]{1,0:T(8,128)S(1)} %broadcast_in_dim.108.refs_2_, ...), custom_call_target="tpu_custom_call", output_to_operand_aliasing={{0}: (4, {}), {1}: (5, {}), {2}: (6, {})} | custom-call | flops 2013265920 | bytes 9830400 | tf_op jit(solution)/shard_map/far_first/pallas_call | solution.py:242
  271.6 1.9 copy-done.2
  276.6 41.5 %pick_second.1 = bf16[32,8,2560]{2,1,0:T(8,128)(2,1)} custom-call(s32[3]{0:T(128)} %slice.93.first_ref, s32[80]{0:T(128)} %concatenate.82.block_ref, bf16[16,8,2560]{2,1,0:T(8,128)(2,1)} %collective-permute-done.10.refs_0_.refs_7_, bf16[16,8,2560]{2,1,0:T(8,128)(2,1)} %collective-permute-done.2.refs_1_.refs_8_, ...), custom_call_target="tpu_custom_call" | custom-call | bytes 2621440 | tf_op jit(solution)/shard_map/pick_second/pallas_call | solution.py:167
  318.4 2.0 collective-permute-start.7
  322.5 2.1 copy-done.3
  325.6 7.1 %far_second.1 = (f32[20,8,384]{2,1,0:T(8,128)S(1)}, f32[20,8,384]{2,1,0:T(8,128)S(1)}, f32[2560,384]{1,0:T(8,128)S(1)}) custom-call(s32[4]{0:T(128)S(1)} %pad_add_fusion.refs_0_, s32[96]{0:T(128)S(1)} %concatenate.67.refs_1_, f32[256,128]{1,0:T(8,128)S(1)} %broadcast_in_dim.105.refs_2_, ...), custom_call_target="tpu_custom_call", output_to_operand_aliasing={{0}: (4, {}), {1}: (5, {}), {2}: (6, {})} | custom-call | flops 1006632960 | bytes 9830400 | tf_op jit(solution)/shard_map/far_second/pallas_call | solution.py:242
  332.7 1.9 copy-done.4
  335.6 1.7 collective-permute-done.3.refs_0_.refs_8_
  339.7 21.6 %pick_third.1 = bf16[16,8,2560]{2,1,0:T(8,128)(2,1)} custom-call(s32[2]{0:T(128)} %slice.95.first_ref, s32[72]{0:T(128)} %concatenate.83.block_ref, bf16[16,8,2560]{2,1,0:T(8,128)(2,1)} %collective-permute-done.3.refs_0_.refs_8_, bf16[16,8,2560]{2,1,0:T(8,128)(2,1)} %collective-permute-done.7.refs_1_.refs_9_), custom_call_target="tpu_custom_call" | custom-call | bytes 1310720 | tf_op jit(solution)/shard_map/pick_third/pallas_call | solution.py:167
  363.8 2.1 copy-done.5
  366.9 7.5 %far_third.1 = bf16[384,2560]{1,0:T(8,128)(2,1)} custom-call(s32[3]{0:T(128)S(1)} %get-tuple-element.121.refs_0_, s32[80]{0:T(128)S(1)} %concatenate.65.refs_1_, f32[128,128]{1,0:T(8,128)S(1)} %broadcast_in_dim.102.refs_2_, bf16[384,2560]{1,0:T(8,128)(2,1)S(1)} %fusion.2.q_ref.refs_3_, f32[20,8,384]{2,1,0:T(8,128)S(1)} %get-tuple-element.95.refs_4_, ...), custom_call_target="tpu_custom_call" | custom-call | flops 503316480 | bytes 9830400 | tf_op jit(solution)/shard_map/far_third/pallas_call | solution.py:242
  (138 shorter events, 31.1 us)
Async XLA Ops:
  0.0 7.7 %copy-start.29 = (bf16[384,2560]{1,0:T(8,128)(2,1)S(1)}, bf16[384,2560]{1,0:T(8,128)(2,1)}, u32[]{:S(2)}) copy-start(bf16[384,2560]{1,0:T(8,128)(2,1)} %param.12) | copy-start | bytes 5898244
  0.0 23.6 %collective-permute-start.11 = (bf16[16,8,2560]{2,1,0:T(8,128)(2,1)}, bf16[16,8,2560]{2,1,0:T(8,128)(2,1)S(1)}, u32[]{:S(2)}, u32[]{:S(2)}) collective-permute-start(bf16[16,8,2560]{2,1,0:T(8,128)(2,1)} %refs_12_), channel_id=1, source_target_pairs={{0,8},{2,10},{8,16},{10,18},{16,24},{18,26},{24,28},{26,30},{28,20... | collective-permute-start | bytes 1966088 | tf_op jit(solution)/shard_map/ppermute | solution.py:346
  3.0 23.9 %collective-permute-start.4 = (bf16[16,8,2560]{2,1,0:T(8,128)(2,1)}, bf16[16,8,2560]{2,1,0:T(8,128)(2,1)S(1)}, u32[]{:S(2)}, u32[]{:S(2)}) collective-permute-start(bf16[16,8,2560]{2,1,0:T(8,128)(2,1)} %refs_12_), channel_id=1, source_target_pairs={{0,4},{2,6},{8,0},{10,2},{16,8},{18,10},{24,16},{26,18},{28,24},{3... | collective-permute-start | bytes 1966088 | tf_op jit(solution)/shard_map/ppermute | solution.py:346
  3.0 29.1 %collective-permute-start = (bf16[16,8,2560]{2,1,0:T(8,128)(2,1)}, bf16[16,8,2560]{2,1,0:T(8,128)(2,1)}, u32[]{:S(2)}, u32[]{:S(2)}) collective-permute-start(bf16[16,8,2560]{2,1,0:T(8,128)(2,1)} %refs_7_), channel_id=1, source_target_pairs={{0,8},{2,10},{8,16},{10,18},{16,24},{18,26},{24,28},{26,30},{28,20... | collective-permute-start | bytes 1966088 | tf_op jit(solution)/shard_map/ppermute | solution.py:346
  5.1 28.8 %collective-permute-start.8 = (bf16[16,8,2560]{2,1,0:T(8,128)(2,1)}, bf16[16,8,2560]{2,1,0:T(8,128)(2,1)}, u32[]{:S(2)}, u32[]{:S(2)}) collective-permute-start(bf16[16,8,2560]{2,1,0:T(8,128)(2,1)} %refs_7_), channel_id=1, source_target_pairs={{0,4},{2,6},{8,0},{10,2},{16,8},{18,10},{24,16},{26,18},{28,24},{3... | collective-permute-start | bytes 1966088 | tf_op jit(solution)/shard_map/ppermute | solution.py:346
  5.7 8.1 %copy-start.31 = (f32[2560]{0:T(1024)S(1)}, f32[2560]{0:T(1024)}, u32[]{:S(2)}) copy-start(f32[2560]{0:T(1024)} %param.15) | copy-start | bytes 30724
  15.9 5.9 %copy-start.32 = (s32[64]{0:T(128)S(1)}, s32[64]{0:T(128)}, u32[]{:S(2)}) copy-start(s32[64]{0:T(128)} %param.21) | copy-start | bytes 772
  15.9 6.5 %copy-start.30 = (f32[2560]{0:T(1024)S(1)}, f32[2560]{0:T(1024)}, u32[]{:S(2)}) copy-start(f32[2560]{0:T(1024)} %param.14) | copy-start | bytes 30724
  19.6 15.5 %collective-permute-start.14 = (bf16[144,2560]{1,0:T(8,128)(2,1)}, bf16[144,2560]{1,0:T(8,128)(2,1)}, u32[]{:S(2)}, u32[]{:S(2)}) collective-permute-start(bf16[144,2560]{1,0:T(8,128)(2,1)} %fusion.8), channel_id=1, source_target_pairs={{0,2},{2,4},{4,6},{6,8},{8,10},{10,12},{12,14},{14,16},{16,18},{18... | collective-permute-start | bytes 2211848 | tf_op jit(solution)/shard_map/ppermute | solution.py:22
  23.6 31.8 %collective-permute-start.15 = (bf16[144,2560]{1,0:T(8,128)(2,1)S(1)}, bf16[144,2560]{1,0:T(8,128)(2,1)S(1)}, u32[]{:S(2)}, u32[]{:S(2)}) collective-permute-start(bf16[144,2560]{1,0:T(8,128)(2,1)S(1)} %fusion.9), channel_id=1, source_target_pairs={{2,0},{4,2},{6,4},{8,6},{10,8},{12,10},{14,12},{16,14},{18,16},{20... | collective-permute-start | bytes 2211848 | tf_op jit(solution)/shard_map/ppermute | solution.py:22
  27.0 30.5 %copy-start.13 = (bf16[16,8,2560]{2,1,0:T(8,128)(2,1)}, bf16[16,8,2560]{2,1,0:T(8,128)(2,1)S(1)}, u32[]{:S(2)}) copy-start(bf16[16,8,2560]{2,1,0:T(8,128)(2,1)S(1)} %collective-permute-done.4.refs_6_.refs_13_) | copy-start | bytes 1966084
  27.0 42.1 %collective-permute-start.12 = (bf16[16,8,2560]{2,1,0:T(8,128)(2,1)S(1)}, bf16[16,8,2560]{2,1,0:T(8,128)(2,1)S(1)}, u32[]{:S(2)}, u32[]{:S(2)}) collective-permute-start(bf16[16,8,2560]{2,1,0:T(8,128)(2,1)S(1)} %collective-permute-done.11.refs_7_.refs_14_), channel_id=1, source_target_pairs={{0,8},{2,10},{8,16},{10,18},{16,24},{18,26},{24,28},{26,30},{28,20... | collective-permute-start | bytes 1966088 | tf_op jit(solution)/shard_map/ppermute | solution.py:346
  32.1 37.0 %collective-permute-start.5 = (bf16[16,8,2560]{2,1,0:T(8,128)(2,1)S(1)}, bf16[16,8,2560]{2,1,0:T(8,128)(2,1)S(1)}, u32[]{:S(2)}, u32[]{:S(2)}) collective-permute-start(bf16[16,8,2560]{2,1,0:T(8,128)(2,1)S(1)} %collective-permute-done.4.refs_6_.refs_13_), channel_id=1, source_target_pairs={{0,4},{2,6},{8,0},{10,2},{16,8},{18,10},{24,16},{26,18},{28,24},{3... | collective-permute-start | bytes 1966088 | tf_op jit(solution)/shard_map/ppermute | solution.py:346
  33.8 35.3 %collective-permute-start.1 = (bf16[16,8,2560]{2,1,0:T(8,128)(2,1)}, bf16[16,8,2560]{2,1,0:T(8,128)(2,1)S(1)}, u32[]{:S(2)}, u32[]{:S(2)}) collective-permute-start(bf16[16,8,2560]{2,1,0:T(8,128)(2,1)} %collective-permute-done.refs_2_.refs_9_), channel_id=1, source_target_pairs={{0,8},{2,10},{8,16},{10,18},{16,24},{18,26},{24,28},{26,30},{28,20... | collective-permute-start | bytes 1966088 | tf_op jit(solution)/shard_map/ppermute | solution.py:346
  35.2 35.8 %collective-permute-start.9 = (bf16[16,8,2560]{2,1,0:T(8,128)(2,1)}, bf16[16,8,2560]{2,1,0:T(8,128)(2,1)S(1)}, u32[]{:S(2)}, u32[]{:S(2)}) collective-permute-start(bf16[16,8,2560]{2,1,0:T(8,128)(2,1)} %collective-permute-done.8.refs_1_.refs_8_), channel_id=1, source_target_pairs={{0,4},{2,6},{8,0},{10,2},{16,8},{18,10},{24,16},{26,18},{28,24},{3... | collective-permute-start | bytes 1966088 | tf_op jit(solution)/shard_map/ppermute | solution.py:346
  69.1 7.7 %copy-start.15 = (bf16[16,8,2560]{2,1,0:T(8,128)(2,1)}, bf16[16,8,2560]{2,1,0:T(8,128)(2,1)S(1)}, u32[]{:S(2)}) copy-start(bf16[16,8,2560]{2,1,0:T(8,128)(2,1)S(1)} %collective-permute-done.12.refs_9_.refs_16_) | copy-start | bytes 1966084
  69.1 7.7 %copy-start.19 = (bf16[16,8,2560]{2,1,0:T(8,128)(2,1)}, bf16[16,8,2560]{2,1,0:T(8,128)(2,1)S(1)}, u32[]{:S(2)}) copy-start(bf16[16,8,2560]{2,1,0:T(8,128)(2,1)S(1)} %collective-permute-done.5.refs_8_.refs_15_) | copy-start | bytes 1966084
  69.1 7.7 %copy-start.17 = (bf16[16,8,2560]{2,1,0:T(8,128)(2,1)}, bf16[16,8,2560]{2,1,0:T(8,128)(2,1)S(1)}, u32[]{:S(2)}) copy-start(bf16[16,8,2560]{2,1,0:T(8,128)(2,1)S(1)} %collective-permute-done.1.refs_4_.refs_11_) | copy-start | bytes 1966084
  70.9 5.3 %collective-permute-start.16 = (s32[81]{0:T(128)S(1)}, s32[81]{0:T(128)S(1)}, u32[]{:S(2)}, u32[]{:S(2)}) collective-permute-start(s32[81]{0:T(128)S(1)} %pad_add_fusion.2), channel_id=1, source_target_pairs={{0,2},{2,0},{4,6},{6,4},{8,10},{10,8},{12,14},{14,12},{16,18},{18,... | collective-permute-start | bytes 980 | tf_op jit(solution)/shard_map/ppermute | solution.py:346
  77.5 169.9 %copy-start.9 = (bf16[16,8,2560]{2,1,0:T(8,128)(2,1)S(1)}, bf16[16,8,2560]{2,1,0:T(8,128)(2,1)}, u32[]{:S(2)}) copy-start(bf16[16,8,2560]{2,1,0:T(8,128)(2,1)} %refs_7_) | copy-start | bytes 1966084
  77.5 169.9 %copy-start.10 = (bf16[16,8,2560]{2,1,0:T(8,128)(2,1)S(1)}, bf16[16,8,2560]{2,1,0:T(8,128)(2,1)}, u32[]{:S(2)}) copy-start(bf16[16,8,2560]{2,1,0:T(8,128)(2,1)} %refs_12_) | copy-start | bytes 1966084
  238.3 8.9 %collective-permute-start.17 = (bf16[128,8,2560]{2,1,0:T(8,128)(2,1)}, bf16[128,8,2560]{2,1,0:T(8,128)(2,1)S(1)}, u32[]{:S(2)}, u32[]{:S(2)}) collective-permute-start(bf16[128,8,2560]{2,1,0:T(8,128)(2,1)} %pick_first.1), channel_id=1, source_target_pairs={{0,2},{2,0},{4,6},{6,4},{8,10},{10,8},{12,14},{14,12},{16,18},{18,... | collective-permute-start | bytes 15728648 | tf_op jit(solution)/shard_map/ppermute | solution.py:346
  238.7 35.5 %collective-permute-start.6 = (bf16[16,8,2560]{2,1,0:T(8,128)(2,1)}, bf16[16,8,2560]{2,1,0:T(8,128)(2,1)}, u32[]{:S(2)}, u32[]{:S(2)}) collective-permute-start(bf16[16,8,2560]{2,1,0:T(8,128)(2,1)} %copy-done.19), channel_id=1, source_target_pairs={{0,4},{2,6},{8,0},{10,2},{16,8},{18,10},{24,16},{26,18},{28,24},{3... | collective-permute-start | bytes 1966088 | tf_op jit(solution)/shard_map/ppermute | solution.py:346
  240.7 33.4 %collective-permute-start.13 = (bf16[16,8,2560]{2,1,0:T(8,128)(2,1)}, bf16[16,8,2560]{2,1,0:T(8,128)(2,1)}, u32[]{:S(2)}, u32[]{:S(2)}) collective-permute-start(bf16[16,8,2560]{2,1,0:T(8,128)(2,1)} %copy-done.15), channel_id=1, source_target_pairs={{0,8},{2,10},{8,16},{10,18},{16,24},{18,26},{24,28},{26,30},{28,20... | collective-permute-start | bytes 1966088 | tf_op jit(solution)/shard_map/ppermute | solution.py:346
  240.7 33.4 %collective-permute-start.2 = (bf16[16,8,2560]{2,1,0:T(8,128)(2,1)}, bf16[16,8,2560]{2,1,0:T(8,128)(2,1)}, u32[]{:S(2)}, u32[]{:S(2)}) collective-permute-start(bf16[16,8,2560]{2,1,0:T(8,128)(2,1)} %copy-done.17), channel_id=1, source_target_pairs={{0,8},{2,10},{8,16},{10,18},{16,24},{18,26},{24,28},{26,30},{28,20... | collective-permute-start | bytes 1966088 | tf_op jit(solution)/shard_map/ppermute | solution.py:346
  240.7 33.4 %collective-permute-start.10 = (bf16[16,8,2560]{2,1,0:T(8,128)(2,1)}, bf16[16,8,2560]{2,1,0:T(8,128)(2,1)}, u32[]{:S(2)}, u32[]{:S(2)}) collective-permute-start(bf16[16,8,2560]{2,1,0:T(8,128)(2,1)} %copy-done.21), channel_id=1, source_target_pairs={{0,4},{2,6},{8,0},{10,2},{16,8},{18,10},{24,16},{26,18},{28,24},{3... | collective-permute-start | bytes 1966088 | tf_op jit(solution)/shard_map/ppermute | solution.py:346
  274.2 1.2 collective-permute-start.18
  318.1 4.3 %collective-permute-start.19 = (bf16[32,8,2560]{2,1,0:T(8,128)(2,1)}, bf16[32,8,2560]{2,1,0:T(8,128)(2,1)S(1)}, u32[]{:S(2)}, u32[]{:S(2)}) collective-permute-start(bf16[32,8,2560]{2,1,0:T(8,128)(2,1)} %pick_second.1), channel_id=1, source_target_pairs={{0,2},{2,0},{4,6},{6,4},{8,10},{10,8},{12,14},{14,12},{16,18},{18,... | collective-permute-start | bytes 3932168 | tf_op jit(solution)/shard_map/ppermute | solution.py:346
  318.4 17.3 %collective-permute-start.7 = (bf16[16,8,2560]{2,1,0:T(8,128)(2,1)}, bf16[16,8,2560]{2,1,0:T(8,128)(2,1)}, u32[]{:S(2)}, u32[]{:S(2)}) collective-permute-start(bf16[16,8,2560]{2,1,0:T(8,128)(2,1)} %collective-permute-done.6.refs_2_.refs_9_), channel_id=1, source_target_pairs={{0,4},{2,6},{8,0},{10,2},{16,8},{18,10},{24,16},{26,18},{28,24},{3... | collective-permute-start | bytes 1966088 | tf_op jit(solution)/shard_map/ppermute | solution.py:346
  320.4 17.0 %collective-permute-start.3 = (bf16[16,8,2560]{2,1,0:T(8,128)(2,1)}, bf16[16,8,2560]{2,1,0:T(8,128)(2,1)}, u32[]{:S(2)}, u32[]{:S(2)}) collective-permute-start(bf16[16,8,2560]{2,1,0:T(8,128)(2,1)} %collective-permute-done.2.refs_1_.refs_8_), channel_id=1, source_target_pairs={{0,8},{2,10},{8,16},{10,18},{16,24},{18,26},{24,28},{26,30},{28,20... | collective-permute-start | bytes 1966088 | tf_op jit(solution)/shard_map/ppermute | solution.py:346
  337.4 1.1 collective-permute-start.20
  361.3 2.4 collective-permute-start.21
  (24 other events, 45.3 us)

commit v5 on v4

--- a/solution.py
+++ b/solution.py
@@ -13,7 +13,7 @@
 EDGE = 64
 EPSILON = 1e-06
 HIDDEN = -1e30
-VMEM_BYTES = 32 * 1024 * 1024
+VMEM_BYTES = 24 * 1024 * 1024
 
 
 def passed_along(value, axis, steps):
@@ -117,6 +117,7 @@
 
 
 IN_VMEM = pl.BlockSpec(memory_space=pltpu.VMEM)
+IN_HBM = pl.BlockSpec(memory_space=pltpu.HBM)
 
 
 def cost(rows, seen, width):
@@ -166,10 +167,11 @@
     block = jnp.concatenate([block, jnp.zeros((slots,), jnp.int32)])
     return pl.pallas_call(
         functools.partial(pick_kernel, groups, slots),
-        in_specs=[pl.BlockSpec(memory_space=pltpu.SMEM)] * 2 + [pl.BlockSpec(memory_space=pl.ANY)] * (2 * groups),
-        out_specs=pl.BlockSpec(memory_space=pl.ANY),
+        in_specs=[pl.BlockSpec(memory_space=pltpu.SMEM)] * 2 + [IN_HBM] * (2 * groups),
+        out_specs=IN_VMEM,
         out_shape=jax.ShapeDtypeStruct((2 * slots, tokens, width), jnp.bfloat16),
         scratch_shapes=[pltpu.SemaphoreType.DMA],
+        compiler_params=pltpu.CompilerParams(vmem_limit_bytes=VMEM_BYTES),
         cost_estimate=pl.CostEstimate(flops=0, bytes_accessed=8 * slots * tokens * width, transcendentals=0),
         name=name,
     )(first, block, *key_pieces, *value_pieces)
@@ -243,7 +245,7 @@
         functools.partial(far_kernel, groups, live is not None),
         in_specs=[pl.BlockSpec(memory_space=pltpu.SMEM)] * 2
         + [IN_VMEM] * (5 + len(extra))
-        + [pl.BlockSpec(memory_space=pl.ANY)] * (2 * groups + 1),
+        + [IN_HBM] * (2 * groups + 1),
         out_specs=[IN_VMEM] * 3 if live is None else IN_VMEM,
         out_shape=sum_shapes(rows, width) if live is None else final,
         input_output_aliases={4: 0, 5: 1, 6: 2} if live is None else {},
@@ -309,12 +311,10 @@
     owner_blocks = mem_keys.shape[0]
     request = req_owner[:, 0] * owner_blocks + requested_block_index
     my_block, my_first = in_order(request, me % 2, owner_blocks, count, me)
-    my_plan = jnp.concatenate([my_first, my_block])
+    plan = lax.ppermute(jnp.concatenate([my_first, my_block]), "tile", swap)
+    their_first, their_block = plan[: my_first.shape[0]], plan[my_first.shape[0] :]
 
     my_length = tile_len[0]
-    totals_q, totals_k = lax.psum((row_squares(query_rows), row_squares(key_rows)), "head")
-    query_norm = normalize(query_rows, totals_q, gain_q * (math.log2(math.e) / HEAD_DIM**0.5))
-    key_norm = normalize(key_rows, totals_k, gain_k)
     live_rows = jnp.arange(capacity, dtype=jnp.int32) < my_length
     live = live_rows[None, :].astype(jnp.float32)
     own_label = (session[0] + 1).astype(jnp.bfloat16)
@@ -328,17 +328,25 @@
         labels = jnp.where(is_live, own_label, jnp.bfloat16(0))
         return jnp.concatenate([keys, values, jnp.pad(labels[None, :], ((0, 15), (0, width_here - EDGE)))], 0)
 
-    tails = edge(tail(key_norm), tail(value_rows), edge_index >= EDGE - my_length)
-    fronts = edge(key_norm[:EDGE], value_rows[:EDGE], edge_index < my_length)
+    tails = edge(tail(key_rows), tail(value_rows), edge_index >= EDGE - my_length)
+    fronts = edge(key_rows[:EDGE], value_rows[:EDGE], edge_index < my_length)
     from_left, from_right = passed_along(tails, "tile", 1), passed_along(fronts, "tile", -1)
-
-    def near_sums(from_left, from_right):
-        edge_keys = jnp.concatenate([from_left[:EDGE], from_right[:EDGE]], 0)
-        edge_values = jnp.concatenate([from_left[EDGE : 2 * EDGE], from_right[EDGE : 2 * EDGE]], 0)
-        labels = jnp.concatenate([from_left[2 * EDGE, :EDGE], from_right[2 * EDGE, :EDGE]])
-        bias = jnp.where(jnp.concatenate([live_rows, labels == own_label]), 0.0, jnp.float32(HIDDEN))
-        bias = jnp.broadcast_to(bias[:, None], (bias.shape[0], 128))
-        return near_part(bias, query_norm, key_norm, value_rows, edge_keys, edge_values)
+    from_left, from_right, mem_keys, mem_values = lax.optimization_barrier(
+        (from_left, from_right, mem_keys, mem_values)
+    )
+
+    edge_keys = jnp.concatenate([from_left[:EDGE], from_right[:EDGE]], 0)
+    edge_values = jnp.concatenate([from_left[EDGE : 2 * EDGE], from_right[EDGE : 2 * EDGE]], 0)
+    labels = jnp.concatenate([from_left[2 * EDGE, :EDGE], from_right[2 * EDGE, :EDGE]])
+    totals_q, totals_k, totals_e = lax.psum(
+        (row_squares(query_rows), row_squares(key_rows), row_squares(edge_keys)), "head"
+    )
+    query_norm = normalize(query_rows, totals_q, gain_q * (math.log2(math.e) / HEAD_DIM**0.5))
+    key_norm = normalize(key_rows, totals_k, gain_k)
+    edge_norm = normalize(edge_keys, totals_e, gain_k)
+    bias = jnp.where(jnp.concatenate([live_rows, labels == own_label]), 0.0, jnp.float32(HIDDEN))
+    bias = jnp.broadcast_to(bias[:, None], (bias.shape[0], 128))
+    sums = near_part(bias, query_norm, key_norm, value_rows, edge_norm, edge_values)
 
     up, down = ring_pairs(count, 1), ring_pairs(count, -1)
 
@@ -353,9 +361,6 @@
     for step in range(1, half):
         for pieces in (keys, values):
             pieces += [moved(pieces[-2 if step > 1 else -1], down), moved(pieces[-1], up)]
-        if step == 1:
-            from_left, from_right, *_ = lax.optimization_barrier((from_left, from_right, *values[1:]))
-            sums = near_sums(from_left, from_right)
     keys.append(moved(keys[-1], up))
     values.append(moved(values[-2], down))
 
@@ -365,9 +370,6 @@
         name = ("first", "second", "third")[stage]
         size = stop - first
         (*pieces,), sums = after([*keys[first:stop], *values[first:stop]], sums)
-        plan, *pieces = lax.optimization_barrier((my_plan, *pieces))
-        plan = moved(plan, swap)
-        their_first, their_block = plan[: my_first.shape[0]], plan[my_first.shape[0] :]
         key_pieces, value_pieces = pieces[:size], pieces[size:]
         theirs = their_first[2 * first + size : 2 * stop + 1]
         picked = pick_part("pick_" + name, theirs, their_block, limit, key_pieces, value_pieces)

time: 375 us -> 161 us (0.43)
  Pallas kernels: 260 us -> 48.5 us
  waiting for transfers between devices: 9.71 us -> 50.2 us
  local copies, waits for them, and re-layouts: 34.6 us -> 6.78 us
  starting transfers between devices: 48.6 us -> 37.2 us
    pallas_call x3, Pallas kernels: 224 us -> 11.7 us  [pick_part(): pl.pallas_call(functools.partial(pick_kernel, groups, slots), in_specs=[p...]
    ppermute x20 -> x17, waiting for transfers between devices: 9.71 us -> 50.2 us  [moved(): return lax.ppermute(piece, 'tile', pairs)]
    unnamed x68 -> x32, local copies, waits for them, and re-layouts: 25.3 us -> 0.6 us
    ppermute x20 -> x17, starting transfers between devices: 45.1 us -> 30.3 us  [moved(): return lax.ppermute(piece, 'tile', pairs)]
  transfers between devices with their start and end apart: 22 -> 20, of which waited for: 8 -> 10; matrix products, arithmetic and copies ran while one was open for 4% -> 5% of each run, Pallas kernels for 8% -> 19%
where the time goes in v5:
time: 161 us
  waiting for transfers between devices  50.2 us (31%)
  Pallas kernels  48.5 us (30%)
  starting transfers between devices  37.2 us (23%)
  other arithmetic  8.06 us (5%)
  local copies, waits for them, and re-layouts  6.78 us (4%)
  between operations  5.51 us (3%)
  blocking collectives  4.99 us (3%)
    ppermute x17, waiting for transfers between devices, moved(): return lax.ppermute(piece, 'tile', pairs)  50.2 us
    ppermute x17, starting transfers between devices, moved(): return lax.ppermute(piece, 'tile', pairs)  30.3 us
    pallas_call x3, Pallas kernels, far_part(): pl.pallas_call(functools.partial(far_kernel, groups, live is not None), i...  29.8 us
    pallas_call x3, Pallas kernels, pick_part(): pl.pallas_call(functools.partial(pick_kernel, groups, slots), in_specs=[p...  11.7 us
    pallas_call x1, Pallas kernels, near_part(): pl.pallas_call(near_kernel, in_specs=[IN_VMEM] * 6, out_specs=[IN_VMEM] *...  7.06 us
    psum x1, blocking collectives, per_device(): lax.psum((row_squares(query_rows), row_squares(key_rows), row_squares(edg...  4.99 us
    ppermute x2, starting transfers between devices, passed_along(): lax.ppermute(value, axis, [(source, source + steps) for source in range(f...  4.35 us
  transfers between devices with their start and end apart: 20, of which 10 were waited for; matrix products, arithmetic and copies ran while one was open for 5% of the time, Pallas kernels for 19%

profile of v5, /device:TPU:0, one launch (start us, length us, event | category | flops | bytes accessed | tf_op | source)
XLA Modules:
  0.0 161.2 jit_solution(10269581920428268014)
XLA Ops:
  1.3 1.5 fusion.24
  3.8 1.3 collective-permute-start.1
  6.0 3.1 %collective-permute-start = (bf16[144,2560]{1,0:T(8,128)(2,1)}, bf16[144,2560]{1,0:T(8,128)(2,1)S(1)}, u32[]{:S(2)}, u32[]{:S(2)}) collective-permute-start(bf16[144,2560]{1,0:T(8,128)(2,1)} %fusion.11), channel_id=1, source_target_pairs={{0,2},{2,4},{4,6},{6,8},{8,10},{10,12},{12,14},{14,16},{16,18},{18... | collective-permute-start | bytes 2211848 | tf_op jit(solution)/shard_map/ppermute | solution.py:22
  9.7 2.6 %collective-permute-start.16 = (s32[81]{0:T(128)S(1)}, s32[81]{0:T(128)S(1)}, u32[]{:S(2)}, u32[]{:S(2)}) collective-permute-start(s32[81]{0:T(128)S(1)} %pad_add_fusion.2), channel_id=1, source_target_pairs={{0,2},{2,0},{4,6},{6,4},{8,10},{10,8},{12,14},{14,12},{16,18},{18,... | collective-permute-start | bytes 980 | tf_op jit(solution)/shard_map/ppermute | solution.py:314
  13.4 1.8 %fusion.27 = (bf16[64,2560]{1,0:T(8,128)(2,1)}, bf16[64,2560]{1,0:T(8,128)(2,1)S(1)}) fusion(bf16[144,2560]{1,0:T(8,128)(2,1)} %collective-permute-done.1), kind=kLoop, calls=%fused_computation.88 | loop fusion | bytes 1310720 | tf_op jit(solution)/shard_map/slice | solution.py:339
  16.7 15.1 %collective-permute-start.10 = (bf16[16,8,2560]{2,1,0:T(8,128)(2,1)S(1)}, bf16[16,8,2560]{2,1,0:T(8,128)(2,1)S(1)}, u32[]{:S(2)}, u32[]{:S(2)}) collective-permute-start(bf16[16,8,2560]{2,1,0:T(8,128)(2,1)S(1)} %copy-done.1), channel_id=1, source_target_pairs={{0,4},{2,6},{8,0},{10,2},{16,8},{18,10},{24,16},{26,18},{28,24},{3... | collective-permute-start | bytes 1966088 | tf_op jit(solution)/shard_map/ppermute | solution.py:354
  31.8 2.0 %collective-permute-start.6 = (bf16[16,8,2560]{2,1,0:T(8,128)(2,1)S(1)}, bf16[16,8,2560]{2,1,0:T(8,128)(2,1)}, u32[]{:S(2)}, u32[]{:S(2)}) collective-permute-start(bf16[16,8,2560]{2,1,0:T(8,128)(2,1)S(1)} %copy-done.2), channel_id=1, source_target_pairs={{0,4},{2,6},{8,0},{10,2},{16,8},{18,10},{24,16},{26,18},{28,24},{3... | collective-permute-start | bytes 1966088 | tf_op jit(solution)/shard_map/ppermute | solution.py:354
  34.1 5.0 %all-reduce.10 = (f32[384]{0:T(512)S(1)}, f32[384]{0:T(512)S(1)}, f32[128]{0:T(128)S(1)}) all-reduce(f32[384]{0:T(512)S(1)} %fusion, f32[384]{0:T(512)S(1)} %fusion.3, f32[128]{0:T(128)S(1)} %fusion.8), channel_id=1, replica_groups=mesh['tile'=16,'head'=2] {'head'}, use_global_device_ids=true, to_apply=%region_4.5 | all-reduce | flops 896 | bytes 7168 | tf_op jit(solution)/shard_map/psum | solution.py:341
  39.1 2.2 %fusion.2.q_ref.refs_3_ = bf16[384,2560]{1,0:T(8,128)(2,1)S(1)} fusion(bf16[384,2560]{1,0:T(8,128)(2,1)} %param.11, f32[2560]{0:T(1024)S(1)} %broadcast_multiply_fusion, f32[384]{0:T(512)S(1)} %add_rsqrt_fusion.1), kind=kLoop, calls=%fused_computation.6 | loop fusion | flops 3932160 | bytes 3943936 | tf_op jit(solution)/shard_map/convert_element_type | solution.py:33
  42.7 4.3 %collective-permute-done.10.refs_1_.refs_8_ = bf16[16,8,2560]{2,1,0:T(8,128)(2,1)S(1)} collective-permute-done((bf16[16,8,2560]{2,1,0:T(8,128)(2,1)S(1)}, bf16[16,8,2560]{2,1,0:T(8,128)(2,1)S(1)}, u32[]{:S(2)}, u32[]{:S(2)}) %collective-permute-start.10) | collective-permute-done | bytes 655392 | tf_op jit(solution)/shard_map/ppermute | solution.py:354
  47.0 2.5 %collective-permute-start.11 = (bf16[16,8,2560]{2,1,0:T(8,128)(2,1)S(1)}, bf16[16,8,2560]{2,1,0:T(8,128)(2,1)S(1)}, u32[]{:S(2)}, u32[]{:S(2)}) collective-permute-start(bf16[16,8,2560]{2,1,0:T(8,128)(2,1)S(1)} %collective-permute-done.10.refs_1_.refs_8_), channel_id=1, source_target_pairs={{0,4},{2,6},{8,0},{10,2},{16,8},{18,10},{24,16},{26,18},{28,24},{3... | collective-permute-start | bytes 1966088 | tf_op jit(solution)/shard_map/ppermute | solution.py:354
  49.5 10.8 %collective-permute-done.13.refs_7_.refs_14_ = bf16[16,8,2560]{2,1,0:T(8,128)(2,1)S(1)} collective-permute-done((bf16[16,8,2560]{2,1,0:T(8,128)(2,1)S(1)}, bf16[16,8,2560]{2,1,0:T(8,128)(2,1)S(1)}, u32[]{:S(2)}, u32[]{:S(2)}) %collective-permute-start.13) | collective-permute-done | bytes 655392 | tf_op jit(solution)/shard_map/ppermute | solution.py:354
  60.3 1.7 %collective-permute-start.14 = (bf16[16,8,2560]{2,1,0:T(8,128)(2,1)S(1)}, bf16[16,8,2560]{2,1,0:T(8,128)(2,1)S(1)}, u32[]{:S(2)}, u32[]{:S(2)}) collective-permute-start(bf16[16,8,2560]{2,1,0:T(8,128)(2,1)S(1)} %collective-permute-done.13.refs_7_.refs_14_), channel_id=1, source_target_pairs={{0,8},{2,10},{8,16},{10,18},{16,24},{18,26},{24,28},{26,30},{28,20... | collective-permute-start | bytes 1966088 | tf_op jit(solution)/shard_map/ppermute | solution.py:354
  62.0 2.0 %collective-permute-start.7 = (bf16[16,8,2560]{2,1,0:T(8,128)(2,1)}, bf16[16,8,2560]{2,1,0:T(8,128)(2,1)S(1)}, u32[]{:S(2)}, u32[]{:S(2)}) collective-permute-start(bf16[16,8,2560]{2,1,0:T(8,128)(2,1)} %collective-permute-done.6.refs_6_.refs_13_), channel_id=1, source_target_pairs={{0,4},{2,6},{8,0},{10,2},{16,8},{18,10},{24,16},{26,18},{28,24},{3... | collective-permute-start | bytes 1966088 | tf_op jit(solution)/shard_map/ppermute | solution.py:354
  64.2 7.1 %near_part.1 = (f32[20,8,384]{2,1,0:T(8,128)S(1)}, f32[20,8,384]{2,1,0:T(8,128)S(1)}, f32[2560,384]{1,0:T(8,128)S(1)}) custom-call(f32[512,128]{1,0:T(8,128)S(1)} %broadcast_in_dim.113.bias_ref, bf16[384,2560]{1,0:T(8,128)(2,1)S(1)} %fusion.2.q_ref.refs_3_, bf16[384,2560]{1,0:T(8,128)(2,1)S(1)} %fusion.5.k_ref, bf16[384,2560]{1,0:T(8,128)(2,1)S(1)} %copy-done, ...), custom_call_target="tpu_custom_call" | custom-call | flops 2013265920 | bytes 9830400 | tf_op jit(solution)/shard_map/near_part/pallas_call | solution.py:133
  71.3 3.8 %collective-permute-done.11.refs_3_.refs_10_ = bf16[16,8,2560]{2,1,0:T(8,128)(2,1)S(1)} collective-permute-done((bf16[16,8,2560]{2,1,0:T(8,128)(2,1)S(1)}, bf16[16,8,2560]{2,1,0:T(8,128)(2,1)S(1)}, u32[]{:S(2)}, u32[]{:S(2)}) %collective-permute-start.11) | collective-permute-done | bytes 655392 | tf_op jit(solution)/shard_map/ppermute | solution.py:354
  75.1 2.9 %collective-permute-done.14.refs_9_.refs_16_ = bf16[16,8,2560]{2,1,0:T(8,128)(2,1)S(1)} collective-permute-done((bf16[16,8,2560]{2,1,0:T(8,128)(2,1)S(1)}, bf16[16,8,2560]{2,1,0:T(8,128)(2,1)S(1)}, u32[]{:S(2)}, u32[]{:S(2)}) %collective-permute-start.14) | collective-permute-done | bytes 655392 | tf_op jit(solution)/shard_map/ppermute | solution.py:354
  78.0 10.8 %collective-permute-done.3.refs_4_.refs_11_ = bf16[16,8,2560]{2,1,0:T(8,128)(2,1)S(1)} collective-permute-done((bf16[16,8,2560]{2,1,0:T(8,128)(2,1)S(1)}, bf16[16,8,2560]{2,1,0:T(8,128)(2,1)S(1)}, u32[]{:S(2)}, u32[]{:S(2)}) %collective-permute-start.3) | collective-permute-done | bytes 655392 | tf_op jit(solution)/shard_map/ppermute | solution.py:354
  88.7 7.8 %pick_first.1 = bf16[128,8,2560]{2,1,0:T(8,128)(2,1)S(1)} custom-call(s32[6]{0:T(128)S(1)} %slice.83.first_ref, s32[128]{0:T(128)S(1)} %concatenate.81.block_ref, bf16[16,8,2560]{2,1,0:T(8,128)(2,1)S(1)} %copy-done.1, bf16[16,8,2560]{2,1,0:T(8,128)(2,1)S(1)} %collective-permute-done.10.refs_1_.refs_8_, ...), custom_call_target="tpu_custom_call" | custom-call | bytes 10485760 | tf_op jit(solution)/shard_map/pick_first/pallas_call | solution.py:168
  96.6 2.5 %collective-permute-start.4 = (bf16[16,8,2560]{2,1,0:T(8,128)(2,1)S(1)}, bf16[16,8,2560]{2,1,0:T(8,128)(2,1)S(1)}, u32[]{:S(2)}, u32[]{:S(2)}) collective-permute-start(bf16[16,8,2560]{2,1,0:T(8,128)(2,1)S(1)} %collective-permute-done.3.refs_4_.refs_11_), channel_id=1, source_target_pairs={{0,8},{2,10},{8,16},{10,18},{16,24},{18,26},{24,28},{26,30},{28,20... | collective-permute-start | bytes 1966088 | tf_op jit(solution)/shard_map/ppermute | solution.py:354
  100.1 1.1 collective-permute-start.15
  104.0 1.3 collective-permute-done.17.refs_17_
  105.4 14.8 %far_first.1 = (f32[20,8,384]{2,1,0:T(8,128)S(1)}, f32[20,8,384]{2,1,0:T(8,128)S(1)}, f32[2560,384]{1,0:T(8,128)S(1)}) custom-call(s32[7]{0:T(128)S(1)} %pad_add_fusion.1.refs_0_, s32[128]{0:T(128)S(1)} %concatenate.73.refs_1_, f32[512,128]{1,0:T(8,128)S(1)} %broadcast_in_dim.112.refs_2_, ...), custom_call_target="tpu_custom_call", output_to_operand_aliasing={{0}: (4, {}), {1}: (5, {}), {2}: (6, {})} | custom-call | flops 2013265920 | bytes 9830400 | tf_op jit(solution)/shard_map/far_first/pallas_call | solution.py:244
  120.2 9.8 %collective-permute-done.12.refs_0_.refs_7_ = bf16[16,8,2560]{2,1,0:T(8,128)(2,1)S(1)} collective-permute-done((bf16[16,8,2560]{2,1,0:T(8,128)(2,1)S(1)}, bf16[16,8,2560]{2,1,0:T(8,128)(2,1)S(1)}, u32[]{:S(2)}, u32[]{:S(2)}) %collective-permute-start.12) | collective-permute-done | bytes 655392 | tf_op jit(solution)/shard_map/ppermute | solution.py:354
  130.0 2.4 %pick_second.1 = bf16[32,8,2560]{2,1,0:T(8,128)(2,1)S(1)} custom-call(s32[3]{0:T(128)S(1)} %slice.85.first_ref, s32[80]{0:T(128)S(1)} %concatenate.82.block_ref, bf16[16,8,2560]{2,1,0:T(8,128)(2,1)S(1)} %collective-permute-done.12.refs_0_.refs_7_, bf16[16,8,2560]{2,1,0:T(8,128)(2,1)S(1)} %collective-permute-done.4.refs_1_.refs_8_, ...), custom_call_target="tpu_custom_call" | custom-call | bytes 2621440 | tf_op jit(solution)/shard_map/pick_second/pallas_call | solution.py:168
  132.5 1.0 collective-permute-start.5
  133.5 1.1 collective-permute-start.9
  136.8 8.1 %far_second.1 = (f32[20,8,384]{2,1,0:T(8,128)S(1)}, f32[20,8,384]{2,1,0:T(8,128)S(1)}, f32[2560,384]{1,0:T(8,128)S(1)}) custom-call(s32[4]{0:T(128)S(1)} %pad_add_fusion.refs_0_, s32[96]{0:T(128)S(1)} %concatenate.71.refs_1_, f32[256,128]{1,0:T(8,128)S(1)} %broadcast_in_dim.109.refs_2_, ...), custom_call_target="tpu_custom_call", output_to_operand_aliasing={{0}: (4, {}), {1}: (5, {}), {2}: (6, {})} | custom-call | flops 1006632960 | bytes 9830400 | tf_op jit(solution)/shard_map/far_second/pallas_call | solution.py:244
  144.9 4.7 %collective-permute-done.5.refs_0_.refs_8_ = bf16[16,8,2560]{2,1,0:T(8,128)(2,1)S(1)} collective-permute-done((bf16[16,8,2560]{2,1,0:T(8,128)(2,1)S(1)}, bf16[16,8,2560]{2,1,0:T(8,128)(2,1)S(1)}, u32[]{:S(2)}, u32[]{:S(2)}) %collective-permute-start.5) | collective-permute-done | bytes 655392 | tf_op jit(solution)/shard_map/ppermute | solution.py:354
  149.6 1.0 collective-permute-done.9.refs_1_.refs_9_
  150.6 1.5 pick_third.1
  154.3 6.9 %far_third.1 = bf16[384,2560]{1,0:T(8,128)(2,1)} custom-call(s32[3]{0:T(128)S(1)} %get-tuple-element.88.refs_0_, s32[80]{0:T(128)S(1)} %concatenate.65.refs_1_, f32[128,128]{1,0:T(8,128)S(1)} %broadcast_in_dim.104.refs_2_, bf16[384,2560]{1,0:T(8,128)(2,1)S(1)} %fusion.2.q_ref.refs_3_, f32[20,8,384]{2,1,0:T(8,128)S(1)} %get-tuple-element.64.refs_4_, ...), custom_call_target="tpu_custom_call" | custom-call | flops 503316480 | bytes 9830400 | tf_op jit(solution)/shard_map/far_third/pallas_call | solution.py:244
  (98 shorter events, 11.3 us)
Async XLA Ops:
  2.8 6.3 %copy-start.14 = (s32[64]{0:T(128)S(1)}, s32[64]{0:T(128)}, u32[]{:S(2)}) copy-start(s32[64]{0:T(128)} %param.21) | copy-start | bytes 772
  2.8 6.3 %copy-start.15 = (s32[64,1]{0,1:T(1,128)S(1)}, s32[64,1]{0,1:T(1,128)}, u32[]{:S(2)}) copy-start(s32[64,1]{0,1:T(1,128)} %param.20) | copy-start | bytes 772
  2.8 9.4 %copy-start.13 = (f32[2560]{0:T(1024)S(1)}, f32[2560]{0:T(1024)}, u32[]{:S(2)}) copy-start(f32[2560]{0:T(1024)} %param.14) | copy-start | bytes 30724
  2.9 9.4 %copy-start.3 = (bf16[384,2560]{1,0:T(8,128)(2,1)S(1)}, bf16[384,2560]{1,0:T(8,128)(2,1)}, u32[]{:S(2)}) copy-start(bf16[384,2560]{1,0:T(8,128)(2,1)} %param.12) | copy-start | bytes 5898244
  3.8 9.6 %collective-permute-start.1 = (bf16[144,2560]{1,0:T(8,128)(2,1)}, bf16[144,2560]{1,0:T(8,128)(2,1)}, u32[]{:S(2)}, u32[]{:S(2)}) collective-permute-start(bf16[144,2560]{1,0:T(8,128)(2,1)} %fusion.12), channel_id=1, source_target_pairs={{2,0},{4,2},{6,4},{8,6},{10,8},{12,10},{14,12},{16,14},{18,16},{20... | collective-permute-start | bytes 2211848 | tf_op jit(solution)/shard_map/ppermute | solution.py:22
  6.0 7.4 %collective-permute-start = (bf16[144,2560]{1,0:T(8,128)(2,1)}, bf16[144,2560]{1,0:T(8,128)(2,1)S(1)}, u32[]{:S(2)}, u32[]{:S(2)}) collective-permute-start(bf16[144,2560]{1,0:T(8,128)(2,1)} %fusion.11), channel_id=1, source_target_pairs={{0,2},{2,4},{4,6},{6,8},{8,10},{10,12},{12,14},{14,16},{16,18},{18... | collective-permute-start | bytes 2211848 | tf_op jit(solution)/shard_map/ppermute | solution.py:22
  9.2 3.6 %copy-start.5 = (bf16[384,2560]{1,0:T(8,128)(2,1)S(1)}, bf16[384,2560]{1,0:T(8,128)(2,1)}, u32[]{:S(2)}) copy-start(bf16[384,2560]{1,0:T(8,128)(2,1)} %param.11) | copy-start | bytes 5898244
  9.7 3.5 %collective-permute-start.16 = (s32[81]{0:T(128)S(1)}, s32[81]{0:T(128)S(1)}, u32[]{:S(2)}, u32[]{:S(2)}) collective-permute-start(s32[81]{0:T(128)S(1)} %pad_add_fusion.2), channel_id=1, source_target_pairs={{0,2},{2,0},{4,6},{6,4},{8,10},{10,8},{12,14},{14,12},{16,18},{18,... | collective-permute-start | bytes 980 | tf_op jit(solution)/shard_map/ppermute | solution.py:314
  12.7 3.9 %copy-start.1 = (bf16[16,8,2560]{2,1,0:T(8,128)(2,1)S(1)}, bf16[16,8,2560]{2,1,0:T(8,128)(2,1)}, u32[]{:S(2)}) copy-start(bf16[16,8,2560]{2,1,0:T(8,128)(2,1)} %refs_7_) | copy-start | bytes 1966084
  12.8 19.1 %copy-start.2 = (bf16[16,8,2560]{2,1,0:T(8,128)(2,1)S(1)}, bf16[16,8,2560]{2,1,0:T(8,128)(2,1)}, u32[]{:S(2)}) copy-start(bf16[16,8,2560]{2,1,0:T(8,128)(2,1)} %refs_12_) | copy-start | bytes 1966084
  15.2 18.6 %copy-start.6 = (bf16[64,2560]{1,0:T(8,128)(2,1)}, bf16[64,2560]{1,0:T(8,128)(2,1)S(1)}, u32[]{:S(2)}) copy-start(bf16[64,2560]{1,0:T(8,128)(2,1)S(1)} %get-tuple-element.81) | copy-start | bytes 983044
  16.7 17.2 %copy-start.8 = (bf16[64,2560]{1,0:T(8,128)(2,1)}, bf16[64,2560]{1,0:T(8,128)(2,1)S(1)}, u32[]{:S(2)}) copy-start(bf16[64,2560]{1,0:T(8,128)(2,1)S(1)} %get-tuple-element.79) | copy-start | bytes 983044
  16.7 30.3 %collective-permute-start.10 = (bf16[16,8,2560]{2,1,0:T(8,128)(2,1)S(1)}, bf16[16,8,2560]{2,1,0:T(8,128)(2,1)S(1)}, u32[]{:S(2)}, u32[]{:S(2)}) collective-permute-start(bf16[16,8,2560]{2,1,0:T(8,128)(2,1)S(1)} %copy-done.1), channel_id=1, source_target_pairs={{0,4},{2,6},{8,0},{10,2},{16,8},{18,10},{24,16},{26,18},{28,24},{3... | collective-permute-start | bytes 1966088 | tf_op jit(solution)/shard_map/ppermute | solution.py:354
  31.8 30.2 %collective-permute-start.2 = (bf16[16,8,2560]{2,1,0:T(8,128)(2,1)S(1)}, bf16[16,8,2560]{2,1,0:T(8,128)(2,1)S(1)}, u32[]{:S(2)}, u32[]{:S(2)}) collective-permute-start(bf16[16,8,2560]{2,1,0:T(8,128)(2,1)S(1)} %copy-done.1), channel_id=1, source_target_pairs={{0,8},{2,10},{8,16},{10,18},{16,24},{18,26},{24,28},{26,30},{28,20... | collective-permute-start | bytes 1966088 | tf_op jit(solution)/shard_map/ppermute | solution.py:354
  31.8 28.5 %collective-permute-start.13 = (bf16[16,8,2560]{2,1,0:T(8,128)(2,1)S(1)}, bf16[16,8,2560]{2,1,0:T(8,128)(2,1)S(1)}, u32[]{:S(2)}, u32[]{:S(2)}) collective-permute-start(bf16[16,8,2560]{2,1,0:T(8,128)(2,1)S(1)} %copy-done.2), channel_id=1, source_target_pairs={{0,8},{2,10},{8,16},{10,18},{16,24},{18,26},{24,28},{26,30},{28,20... | collective-permute-start | bytes 1966088 | tf_op jit(solution)/shard_map/ppermute | solution.py:354
  31.8 30.2 %collective-permute-start.6 = (bf16[16,8,2560]{2,1,0:T(8,128)(2,1)S(1)}, bf16[16,8,2560]{2,1,0:T(8,128)(2,1)}, u32[]{:S(2)}, u32[]{:S(2)}) collective-permute-start(bf16[16,8,2560]{2,1,0:T(8,128)(2,1)S(1)} %copy-done.2), channel_id=1, source_target_pairs={{0,4},{2,6},{8,0},{10,2},{16,8},{18,10},{24,16},{26,18},{28,24},{3... | collective-permute-start | bytes 1966088 | tf_op jit(solution)/shard_map/ppermute | solution.py:354
  41.4 22.6 %copy-start.10 = (bf16[64,2560]{1,0:T(8,128)(2,1)S(1)}, bf16[64,2560]{1,0:T(8,128)(2,1)}, u32[]{:S(2)}) copy-start(bf16[64,2560]{1,0:T(8,128)(2,1)} %get-tuple-element.80) | copy-start | bytes 983044
  41.4 22.6 %copy-start.11 = (bf16[64,2560]{1,0:T(8,128)(2,1)S(1)}, bf16[64,2560]{1,0:T(8,128)(2,1)}, u32[]{:S(2)}) copy-start(bf16[64,2560]{1,0:T(8,128)(2,1)} %get-tuple-element.78) | copy-start | bytes 983044
  42.5 21.7 %copy-start = (bf16[384,2560]{1,0:T(8,128)(2,1)S(1)}, bf16[384,2560]{1,0:T(8,128)(2,1)}, u32[]{:S(2)}) copy-start(bf16[384,2560]{1,0:T(8,128)(2,1)} %v_ref.1) | copy-start | bytes 5898244
  47.0 28.1 %collective-permute-start.11 = (bf16[16,8,2560]{2,1,0:T(8,128)(2,1)S(1)}, bf16[16,8,2560]{2,1,0:T(8,128)(2,1)S(1)}, u32[]{:S(2)}, u32[]{:S(2)}) collective-permute-start(bf16[16,8,2560]{2,1,0:T(8,128)(2,1)S(1)} %collective-permute-done.10.refs_1_.refs_8_), channel_id=1, source_target_pairs={{0,4},{2,6},{8,0},{10,2},{16,8},{18,10},{24,16},{26,18},{28,24},{3... | collective-permute-start | bytes 1966088 | tf_op jit(solution)/shard_map/ppermute | solution.py:354
  60.3 17.7 %collective-permute-start.14 = (bf16[16,8,2560]{2,1,0:T(8,128)(2,1)S(1)}, bf16[16,8,2560]{2,1,0:T(8,128)(2,1)S(1)}, u32[]{:S(2)}, u32[]{:S(2)}) collective-permute-start(bf16[16,8,2560]{2,1,0:T(8,128)(2,1)S(1)} %collective-permute-done.13.refs_7_.refs_14_), channel_id=1, source_target_pairs={{0,8},{2,10},{8,16},{10,18},{16,24},{18,26},{24,28},{26,30},{28,20... | collective-permute-start | bytes 1966088 | tf_op jit(solution)/shard_map/ppermute | solution.py:354
  62.0 26.8 %collective-permute-start.3 = (bf16[16,8,2560]{2,1,0:T(8,128)(2,1)S(1)}, bf16[16,8,2560]{2,1,0:T(8,128)(2,1)S(1)}, u32[]{:S(2)}, u32[]{:S(2)}) collective-permute-start(bf16[16,8,2560]{2,1,0:T(8,128)(2,1)S(1)} %collective-permute-done.2.refs_2_.refs_9_), channel_id=1, source_target_pairs={{0,8},{2,10},{8,16},{10,18},{16,24},{18,26},{24,28},{26,30},{28,20... | collective-permute-start | bytes 1966088 | tf_op jit(solution)/shard_map/ppermute | solution.py:354
  62.0 26.7 %collective-permute-start.7 = (bf16[16,8,2560]{2,1,0:T(8,128)(2,1)}, bf16[16,8,2560]{2,1,0:T(8,128)(2,1)S(1)}, u32[]{:S(2)}, u32[]{:S(2)}) collective-permute-start(bf16[16,8,2560]{2,1,0:T(8,128)(2,1)} %collective-permute-done.6.refs_6_.refs_13_), channel_id=1, source_target_pairs={{0,4},{2,6},{8,0},{10,2},{16,8},{18,10},{24,16},{26,18},{28,24},{3... | collective-permute-start | bytes 1966088 | tf_op jit(solution)/shard_map/ppermute | solution.py:354
  96.6 8.7 %collective-permute-start.17 = (bf16[128,8,2560]{2,1,0:T(8,128)(2,1)S(1)}, bf16[128,8,2560]{2,1,0:T(8,128)(2,1)S(1)}, u32[]{:S(2)}, u32[]{:S(2)}) collective-permute-start(bf16[128,8,2560]{2,1,0:T(8,128)(2,1)S(1)} %pick_first.1), channel_id=1, source_target_pairs={{0,2},{2,0},{4,6},{6,4},{8,10},{10,8},{12,14},{14,12},{16,18},{18,... | collective-permute-start | bytes 15728648 | tf_op jit(solution)/shard_map/ppermute | solution.py:354
  96.6 23.6 %collective-permute-start.4 = (bf16[16,8,2560]{2,1,0:T(8,128)(2,1)S(1)}, bf16[16,8,2560]{2,1,0:T(8,128)(2,1)S(1)}, u32[]{:S(2)}, u32[]{:S(2)}) collective-permute-start(bf16[16,8,2560]{2,1,0:T(8,128)(2,1)S(1)} %collective-permute-done.3.refs_4_.refs_11_), channel_id=1, source_target_pairs={{0,8},{2,10},{8,16},{10,18},{16,24},{18,26},{24,28},{26,30},{28,20... | collective-permute-start | bytes 1966088 | tf_op jit(solution)/shard_map/ppermute | solution.py:354
  99.2 21.0 %collective-permute-start.8 = (bf16[16,8,2560]{2,1,0:T(8,128)(2,1)S(1)}, bf16[16,8,2560]{2,1,0:T(8,128)(2,1)S(1)}, u32[]{:S(2)}, u32[]{:S(2)}) collective-permute-start(bf16[16,8,2560]{2,1,0:T(8,128)(2,1)S(1)} %collective-permute-done.7.refs_8_.refs_15_), channel_id=1, source_target_pairs={{0,4},{2,6},{8,0},{10,2},{16,8},{18,10},{24,16},{26,18},{28,24},{3... | collective-permute-start | bytes 1966088 | tf_op jit(solution)/shard_map/ppermute | solution.py:354
  99.2 30.8 %collective-permute-start.12 = (bf16[16,8,2560]{2,1,0:T(8,128)(2,1)S(1)}, bf16[16,8,2560]{2,1,0:T(8,128)(2,1)S(1)}, u32[]{:S(2)}, u32[]{:S(2)}) collective-permute-start(bf16[16,8,2560]{2,1,0:T(8,128)(2,1)S(1)} %collective-permute-done.11.refs_3_.refs_10_), channel_id=1, source_target_pairs={{0,4},{2,6},{8,0},{10,2},{16,8},{18,10},{24,16},{26,18},{28,24},{3... | collective-permute-start | bytes 1966088 | tf_op jit(solution)/shard_map/ppermute | solution.py:354
  100.1 29.9 %collective-permute-start.15 = (bf16[16,8,2560]{2,1,0:T(8,128)(2,1)S(1)}, bf16[16,8,2560]{2,1,0:T(8,128)(2,1)S(1)}, u32[]{:S(2)}, u32[]{:S(2)}) collective-permute-start(bf16[16,8,2560]{2,1,0:T(8,128)(2,1)S(1)} %collective-permute-done.14.refs_9_.refs_16_), channel_id=1, source_target_pairs={{0,8},{2,10},{8,16},{10,18},{16,24},{18,26},{24,28},{26,30},{28,20... | collective-permute-start | bytes 1966088 | tf_op jit(solution)/shard_map/ppermute | solution.py:354
  132.4 4.3 %collective-permute-start.18 = (bf16[32,8,2560]{2,1,0:T(8,128)(2,1)S(1)}, bf16[32,8,2560]{2,1,0:T(8,128)(2,1)S(1)}, u32[]{:S(2)}, u32[]{:S(2)}) collective-permute-start(bf16[32,8,2560]{2,1,0:T(8,128)(2,1)S(1)} %pick_second.1), channel_id=1, source_target_pairs={{0,2},{2,0},{4,6},{6,4},{8,10},{10,8},{12,14},{14,12},{16,18},{18,... | collective-permute-start | bytes 3932168 | tf_op jit(solution)/shard_map/ppermute | solution.py:354
  132.5 17.1 %collective-permute-start.5 = (bf16[16,8,2560]{2,1,0:T(8,128)(2,1)S(1)}, bf16[16,8,2560]{2,1,0:T(8,128)(2,1)S(1)}, u32[]{:S(2)}, u32[]{:S(2)}) collective-permute-start(bf16[16,8,2560]{2,1,0:T(8,128)(2,1)S(1)} %collective-permute-done.4.refs_1_.refs_8_), channel_id=1, source_target_pairs={{0,8},{2,10},{8,16},{10,18},{16,24},{18,26},{24,28},{26,30},{28,20... | collective-permute-start | bytes 1966088 | tf_op jit(solution)/shard_map/ppermute | solution.py:354
  133.5 17.1 %collective-permute-start.9 = (bf16[16,8,2560]{2,1,0:T(8,128)(2,1)S(1)}, bf16[16,8,2560]{2,1,0:T(8,128)(2,1)S(1)}, u32[]{:S(2)}, u32[]{:S(2)}) collective-permute-start(bf16[16,8,2560]{2,1,0:T(8,128)(2,1)S(1)} %collective-permute-done.8.refs_2_.refs_9_), channel_id=1, source_target_pairs={{0,4},{2,6},{8,0},{10,2},{16,8},{18,10},{24,16},{26,18},{28,24},{3... | collective-permute-start | bytes 1966088 | tf_op jit(solution)/shard_map/ppermute | solution.py:354
  152.1 2.2 %collective-permute-start.19 = (bf16[16,8,2560]{2,1,0:T(8,128)(2,1)S(1)}, bf16[16,8,2560]{2,1,0:T(8,128)(2,1)S(1)}, u32[]{:S(2)}, u32[]{:S(2)}) collective-permute-start(bf16[16,8,2560]{2,1,0:T(8,128)(2,1)S(1)} %pick_third.1), channel_id=1, source_target_pairs={{0,2},{2,0},{4,6},{6,4},{8,10},{10,8},{12,14},{14,12},{16,18},{18,... | collective-permute-start | bytes 1966088 | tf_op jit(solution)/shard_map/ppermute | solution.py:354
  (4 other events, 6.7 us)

commit v6 on v5

--- a/solution.py
+++ b/solution.py
@@ -177,38 +177,46 @@
     )(first, block, *key_pieces, *value_pieces)
 
 
-def far_kernel(groups, last, *refs):
+def far_kernel(segments, last, beside, *refs):
     first_ref, block_ref, bias_ref, q_ref, before_top, before_sum, before_acc = refs[:7]
     refs = refs[7:]
     if last:
         live_ref, refs = refs[0], refs[1:]
-    key_pieces, value_pieces, received = refs[:groups], refs[groups : 2 * groups], refs[2 * groups]
-    *out_refs, keys, values, sems = refs[2 * groups + 1 :]
+    if beside:
+        (beside_bias, beside_keys, beside_values), refs = refs[:3], refs[3:]
+    *out_refs, keys, values, sems = refs[sum(2 * size + 1 for size in segments) :]
     slots, tokens = keys.shape[:2]
-    offset = received.shape[0] // 2
     start = first_ref[0]
 
     def fetch_one(key_block, value_block, to):
         pltpu.make_async_copy(key_block, keys.at[to], sems.at[0]).start()
         pltpu.make_async_copy(value_block, values.at[to], sems.at[1]).start()
 
-    def fetch_from(g):
+    def fetch_from(key_piece, value_piece):
         def fetch(slot, carry):
             block = block_ref[slot]
-            fetch_one(key_pieces[g].at[block], value_pieces[g].at[block], slot - start)
+            fetch_one(key_piece.at[block], value_piece.at[block], slot - start)
             return carry
 
         return fetch
 
-    def fetch_received(slot, carry):
-        block = slot - first_ref[groups]
-        fetch_one(received.at[block], received.at[offset + block], slot - start)
-        return carry
-
-    for g in range(groups):
-        lax.fori_loop(first_ref[g], first_ref[g + 1], fetch_from(g), 0)
-    lax.fori_loop(first_ref[groups], first_ref[groups + 1], fetch_received, 0)
-    lax.fori_loop(first_ref[groups + 1], start + slots, fetch_from(0), 0)
+    def fetch_received(received, base):
+        def fetch(slot, carry):
+            block = slot - base
+            fetch_one(received.at[block], received.at[received.shape[0] // 2 + block], slot - start)
+            return carry
+
+        return fetch
+
+    at, pieces = 0, refs
+    for size in segments:
+        for g in range(size):
+            lax.fori_loop(first_ref[at], first_ref[at + 1], fetch_from(pieces[g], pieces[size + g]), 0)
+            at += 1
+        lax.fori_loop(first_ref[at], first_ref[at + 1], fetch_received(pieces[2 * size], first_ref[at]), 0)
+        at += 1
+        pieces = pieces[2 * size + 1 :]
+    lax.fori_loop(first_ref[at], start + slots, fetch_from(refs[0], refs[segments[0]]), 0)
     pltpu.make_async_copy(keys, keys, sems.at[0]).wait()
     pltpu.make_async_copy(values, values, sems.at[1]).wait()
 
@@ -220,7 +228,10 @@
         heads = []
         for head, place in places:
             before = (before_top[head][:1, :], before_sum[head][:1, :], before_acc[place, :])
-            heads.append((q_ref[:, place], [(flat(keys, place), flat(values, place), bias_ref[...])], before))
+            parts = [(flat(keys, place), flat(values, place), bias_ref[...])]
+            if beside:
+                parts.append((beside_keys[:, place], beside_values[:, place], beside_bias[...]))
+            heads.append((q_ref[:, place], parts, before))
         for (head, place), sums in zip(places, attend(heads)):
             if last:
                 result = jnp.where(live_ref[...] > 0.0, sums[2] / sums[1], 0.0)
@@ -231,21 +242,22 @@
     over_heads(q_ref.shape[1], body)
 
 
-def far_part(name, first, block, slots, query, before, key_pieces, value_pieces, received, live=None):
+def far_part(name, first, block, slots, query, before, segments, live=None, beside=()):
     rows, width = query.shape
-    groups, tokens = len(key_pieces), key_pieces[0].shape[1]
+    pieces = [array for segment in segments for array in segment]
+    tokens = pieces[0].shape[1]
     seen = slots * tokens
     token = jnp.arange(seen, dtype=jnp.int32)[:, None]
     bias = jnp.where(token < (first[-1] - first[0]) * tokens, 0.0, jnp.float32(HIDDEN))
     bias = jnp.broadcast_to(bias, (seen, 128))
     block = jnp.concatenate([block, jnp.zeros((slots,), jnp.int32)])
-    extra = [] if live is None else [live]
+    extra = ([] if live is None else [live]) + list(beside)
     final = jax.ShapeDtypeStruct((rows, width), jnp.bfloat16)
     return pl.pallas_call(
-        functools.partial(far_kernel, groups, live is not None),
+        functools.partial(far_kernel, [len(segment) // 2 for segment in segments], live is not None, len(beside) > 0),
         in_specs=[pl.BlockSpec(memory_space=pltpu.SMEM)] * 2
         + [IN_VMEM] * (5 + len(extra))
-        + [IN_HBM] * (2 * groups + 1),
+        + [IN_HBM] * len(pieces),
         out_specs=[IN_VMEM] * 3 if live is None else IN_VMEM,
         out_shape=sum_shapes(rows, width) if live is None else final,
         input_output_aliases={4: 0, 5: 1, 6: 2} if live is None else {},
@@ -257,7 +269,7 @@
         compiler_params=pltpu.CompilerParams(vmem_limit_bytes=VMEM_BYTES),
         cost_estimate=cost(rows, seen, width),
         name=name,
-    )(first, block, bias, query, *before, *extra, *key_pieces, *value_pieces, received)
+    )(first, block, bias, query, *before, *extra, *pieces)
 
 
 def in_order(request, lane, owner_blocks, count, me):
@@ -284,7 +296,7 @@
 
 
 def stages(half):
-    return (0, 2 * half - 3), (2 * half - 3, 2 * half - 1), (2 * half - 1, 2 * half)
+    return (0, 2 * half - 5), (2 * half - 5, 2 * half - 3), (2 * half - 3, 2 * half - 1), (2 * half - 1, 2 * half)
 
 
 def per_device(
@@ -315,6 +327,9 @@
     their_first, their_block = plan[: my_first.shape[0]], plan[my_first.shape[0] :]
 
     my_length = tile_len[0]
+    totals_q, totals_k = lax.psum((row_squares(query_rows), row_squares(key_rows)), "head")
+    query_norm = normalize(query_rows, totals_q, gain_q * (math.log2(math.e) / HEAD_DIM**0.5))
+    key_norm = normalize(key_rows, totals_k, gain_k)
     live_rows = jnp.arange(capacity, dtype=jnp.int32) < my_length
     live = live_rows[None, :].astype(jnp.float32)
     own_label = (session[0] + 1).astype(jnp.bfloat16)
@@ -328,25 +343,16 @@
         labels = jnp.where(is_live, own_label, jnp.bfloat16(0))
         return jnp.concatenate([keys, values, jnp.pad(labels[None, :], ((0, 15), (0, width_here - EDGE)))], 0)
 
-    tails = edge(tail(key_rows), tail(value_rows), edge_index >= EDGE - my_length)
-    fronts = edge(key_rows[:EDGE], value_rows[:EDGE], edge_index < my_length)
-    from_left, from_right = passed_along(tails, "tile", 1), passed_along(fronts, "tile", -1)
-    from_left, from_right, mem_keys, mem_values = lax.optimization_barrier(
-        (from_left, from_right, mem_keys, mem_values)
-    )
-
-    edge_keys = jnp.concatenate([from_left[:EDGE], from_right[:EDGE]], 0)
-    edge_values = jnp.concatenate([from_left[EDGE : 2 * EDGE], from_right[EDGE : 2 * EDGE]], 0)
-    labels = jnp.concatenate([from_left[2 * EDGE, :EDGE], from_right[2 * EDGE, :EDGE]])
-    totals_q, totals_k, totals_e = lax.psum(
-        (row_squares(query_rows), row_squares(key_rows), row_squares(edge_keys)), "head"
-    )
-    query_norm = normalize(query_rows, totals_q, gain_q * (math.log2(math.e) / HEAD_DIM**0.5))
-    key_norm = normalize(key_rows, totals_k, gain_k)
-    edge_norm = normalize(edge_keys, totals_e, gain_k)
-    bias = jnp.where(jnp.concatenate([live_rows, labels == own_label]), 0.0, jnp.float32(HIDDEN))
-    bias = jnp.broadcast_to(bias[:, None], (bias.shape[0], 128))
-    sums = near_part(bias, query_norm, key_norm, value_rows, edge_norm, edge_values)
+    tails = edge(tail(key_norm), tail(value_rows), edge_index >= EDGE - my_length)
+    fronts = edge(key_norm[:EDGE], value_rows[:EDGE], edge_index < my_length)
+    from_left = passed_along(tails, "tile", 1)
+
+    def spread(is_visible):
+        bias = jnp.where(is_visible, 0.0, jnp.float32(HIDDEN))
+        return jnp.broadcast_to(bias[:, None], (bias.shape[0], 128))
+
+    def arrived(edge):
+        return edge[2 * EDGE, :EDGE] == own_label, edge[:EDGE], edge[EDGE : 2 * EDGE]
 
     up, down = ring_pairs(count, 1), ring_pairs(count, -1)
 
@@ -361,31 +367,35 @@
     for step in range(1, half):
         for pieces in (keys, values):
             pieces += [moved(pieces[-2 if step > 1 else -1], down), moved(pieces[-1], up)]
+        if step == 1:
+            from_left, *_ = lax.optimization_barrier((from_left, *values[1:]))
+            seen, left_keys, left_values = arrived(from_left)
+            bias = spread(jnp.concatenate([live_rows, seen]))
+            sums = near_part(bias, query_norm, key_norm, value_rows, left_keys, left_values)
     keys.append(moved(keys[-1], up))
     values.append(moved(values[-2], down))
 
     most = 2 * request.shape[0] // count
-    limits = (min(request.shape[0], count * most), 2 * most, most)
-    for stage, ((first, stop), limit) in enumerate(zip(stages(half), limits)):
-        name = ("first", "second", "third")[stage]
+    segments, starts = [], []
+    for stage, (first, stop) in enumerate(stages(half)):
         size = stop - first
         (*pieces,), sums = after([*keys[first:stop], *values[first:stop]], sums)
-        key_pieces, value_pieces = pieces[:size], pieces[size:]
         theirs = their_first[2 * first + size : 2 * stop + 1]
-        picked = pick_part("pick_" + name, theirs, their_block, limit, key_pieces, value_pieces)
-        mine = jnp.concatenate([my_first[2 * first : 2 * first + size + 1], my_first[2 * stop :][:1]])
-        sums = far_part(
-            "far_" + name,
-            mine,
-            my_block,
-            min(request.shape[0], 2 * limit),
-            query_norm,
-            sums,
-            key_pieces,
-            value_pieces,
-            moved(picked, swap),
-            live if stage == 2 else None,
-        )
+        limit = min(request.shape[0], size * most)
+        picked = pick_part(f"pick_{stage}", theirs, their_block, limit, pieces[:size], pieces[size:])
+        received = moved(picked, swap)
+        if stage == 1:
+            fronts, received = lax.optimization_barrier((fronts, received))
+            seen, right_keys, right_values = arrived(passed_along(fronts, "tile", -1))
+        segments.append([*pieces, received])
+        starts.append(my_first[2 * first : 2 * first + size + 1])
+        if stage > 0:
+            bounds = jnp.concatenate([*starts, my_first[2 * stop :][:1]])
+            slots = min(request.shape[0], sum(len(segment) // 2 for segment in segments) * 2 * most)
+            final = live if first == 2 * half - 1 else None
+            beside = (spread(seen), right_keys, right_values) if stage == 2 else ()
+            sums = far_part(f"far_{stage}", bounds, my_block, slots, query_norm, sums, segments, final, beside)
+            segments, starts = [], []
     return sums
 
 

time: 161 us -> 143 us (0.89)
  waiting for transfers between devices: 50.2 us -> 38 us
  local copies, waits for them, and re-layouts: 6.78 us -> 3.11 us
    ppermute x17 -> x18, waiting for transfers between devices: 50.2 us -> 38 us  [moved(): return lax.ppermute(piece, 'tile', pairs)]
    ppermute x17 -> x18, starting transfers between devices: 30.3 us -> 33.1 us  [moved(): return lax.ppermute(piece, 'tile', pairs)]
    ppermute x1, starting transfers between devices: 2.55 us -> 0.01 us  [per_device(): plan = lax.ppermute(jnp.concatenate([my_first, my_block]), 'tile', swap)]
    slice x4, local copies, waits for them, and re-layouts: 4.16 us -> 1.63 us  [the longest x1 1.47 us: per_device(): fronts = edge(key_norm[:EDGE], value_rows[:EDGE], edge_index < my_length)]
    pallas_call x3 -> x4, Pallas kernels: 11.7 us -> 9.33 us  [pick_part(): pl.pallas_call(functools.partial(pick_kernel, groups, slots), in_specs=[p...]
    concatenate x2, other arithmetic: 1.85 us -> 0.1 us  [edge(): jnp.concatenate([keys, values, jnp.pad(labels[None, :], ((0, 15), (0, wid...]
  transfers between devices with their start and end apart: 20 -> 21, of which waited for: 10 -> 9; matrix products, arithmetic and copies ran while one was open for 5% -> 8% of each run, Pallas kernels for 19% -> 27%
where the time goes in v6:
time: 143 us
  Pallas kernels  47 us (33%)
  waiting for transfers between devices  38 us (27%)
  starting transfers between devices  36.3 us (25%)
  other arithmetic  7.89 us (6%)
  between operations  5.68 us (4%)
  blocking collectives  4.94 us (3%)
  local copies, waits for them, and re-layouts  3.11 us (2%)
    ppermute x18, waiting for transfers between devices, moved(): return lax.ppermute(piece, 'tile', pairs)  38 us
    ppermute x18, starting transfers between devices, moved(): return lax.ppermute(piece, 'tile', pairs)  33.1 us
    pallas_call x3, Pallas kernels, far_part(): pl.pallas_call(functools.partial(far_kernel, [len(segment) // 2 for segme...  31.2 us
    pallas_call x4, Pallas kernels, pick_part(): pl.pallas_call(functools.partial(pick_kernel, groups, slots), in_specs=[p...  9.33 us
    pallas_call x1, Pallas kernels, near_part(): pl.pallas_call(near_kernel, in_specs=[IN_VMEM] * 6, out_specs=[IN_VMEM] *...  6.44 us
    psum x1, blocking collectives, per_device(): lax.psum((row_squares(query_rows), row_squares(key_rows)), 'head')  4.94 us
    ppermute x2, starting transfers between devices, passed_along(): lax.ppermute(value, axis, [(source, source + steps) for source in range(f...  3.17 us
  transfers between devices with their start and end apart: 21, of which 9 were waited for; matrix products, arithmetic and copies ran while one was open for 8% of the time, Pallas kernels for 27%

profile of v6, /device:TPU:0, one launch (start us, length us, event | category | flops | bytes accessed | tf_op | source)
XLA Modules:
  0.0 142.8 jit_solution(14761241850375514414)
XLA Ops:
  0.0 3.0 %collective-permute-start.11 = (bf16[16,8,2560]{2,1,0:T(8,128)(2,1)}, bf16[16,8,2560]{2,1,0:T(8,128)(2,1)S(1)}, u32[]{:S(2)}, u32[]{:S(2)}) collective-permute-start(bf16[16,8,2560]{2,1,0:T(8,128)(2,1)} %refs_10_), channel_id=1, source_target_pairs={{0,8},{2,10},{8,16},{10,18},{16,24},{18,26},{24,28},{26,30},{28,20... | collective-permute-start | bytes 1966088 | tf_op jit(solution)/shard_map/ppermute | solution.py:360
  3.0 2.0 %collective-permute-start = (bf16[16,8,2560]{2,1,0:T(8,128)(2,1)}, bf16[16,8,2560]{2,1,0:T(8,128)(2,1)}, u32[]{:S(2)}, u32[]{:S(2)}) collective-permute-start(bf16[16,8,2560]{2,1,0:T(8,128)(2,1)} %refs_7_), channel_id=1, source_target_pairs={{0,8},{2,10},{8,16},{10,18},{16,24},{18,26},{24,28},{26,30},{28,20... | collective-permute-start | bytes 1966088 | tf_op jit(solution)/shard_map/ppermute | solution.py:360
  7.0 2.0 %fusion = f32[384]{0:T(512)S(1)} fusion(bf16[384,2560]{1,0:T(8,128)(2,1)} %param.11), kind=kLoop, calls=%fused_computation.4 | loop fusion | flops 2948736 | bytes 1967616 | tf_op jit(solution)/shard_map/reduce_sum | solution.py:27
  9.4 4.9 %all-reduce.10 = (f32[384]{0:T(512)S(1)}, f32[384]{0:T(512)S(1)}) all-reduce(f32[384]{0:T(512)S(1)} %fusion, f32[384]{0:T(512)S(1)} %fusion.3), channel_id=1, replica_groups=mesh['tile'=16,'head'=2] {'head'}, use_global_device_ids=true, to_apply=%region_4.5 | all-reduce | flops 768 | bytes 6144 | tf_op jit(solution)/shard_map/psum | solution.py:330
  15.1 2.1 %fusion.5.k_ref = bf16[384,2560]{1,0:T(8,128)(2,1)S(1)} fusion(bf16[384,2560]{1,0:T(8,128)(2,1)} %param.12, f32[2560]{0:T(1024)S(1)} %copy-done.6, f32[384]{0:T(512)S(1)} %add_rsqrt_fusion), kind=kLoop, calls=%fused_computation.9 | loop fusion | flops 3932160 | bytes 3943936 | tf_op jit(solution)/shard_map/convert_element_type | solution.py:33
  17.2 1.5 %fusion.22 = (bf16[64,2560]{1,0:T(8,128)(2,1)S(1)}, bf16[64,2560]{1,0:T(8,128)(2,1)S(1)}, bf16[64,2560]{1,0:T(8,128)(2,1)S(1)}, bf16[64,2560]{1,0:T(8,128)(2,1)S(1)}) fusion(bf16[384,2560]{1,0:T(8,128)(2,1)S(1)} %fusion.5.k_ref, s32[]{:T(128)S(6)} %select_n.171, bf16[384,2560]{1,0:T(8,128)(2,1)} %v_ref.1), kind=kLoop, calls=%fused_computation.78 | loop fusion | bytes 5898244 | tf_op jit(solution)/shard_map/slice | solution.py:347
  18.8 1.9 %collective-permute-start.14 = (bf16[144,2560]{1,0:T(8,128)(2,1)S(1)}, bf16[144,2560]{1,0:T(8,128)(2,1)S(1)}, u32[]{:S(2)}, u32[]{:S(2)}) collective-permute-start(bf16[144,2560]{1,0:T(8,128)(2,1)S(1)} %fusion.8), channel_id=1, source_target_pairs={{0,2},{2,4},{4,6},{6,8},{8,10},{10,12},{12,14},{14,16},{16,18},{18... | collective-permute-start | bytes 2211848 | tf_op jit(solution)/shard_map/ppermute | solution.py:22
  21.4 2.2 %collective-permute-start.12 = (bf16[16,8,2560]{2,1,0:T(8,128)(2,1)S(1)}, bf16[16,8,2560]{2,1,0:T(8,128)(2,1)S(1)}, u32[]{:S(2)}, u32[]{:S(2)}) collective-permute-start(bf16[16,8,2560]{2,1,0:T(8,128)(2,1)S(1)} %collective-permute-done.11.refs_5_.refs_12_), channel_id=1, source_target_pairs={{0,8},{2,10},{8,16},{10,18},{16,24},{18,26},{24,28},{26,30},{28,20... | collective-permute-start | bytes 1966088 | tf_op jit(solution)/shard_map/ppermute | solution.py:360
  23.5 9.4 %collective-permute-done.refs_2_.refs_9_ = bf16[16,8,2560]{2,1,0:T(8,128)(2,1)} collective-permute-done((bf16[16,8,2560]{2,1,0:T(8,128)(2,1)}, bf16[16,8,2560]{2,1,0:T(8,128)(2,1)}, u32[]{:S(2)}, u32[]{:S(2)}) %collective-permute-start) | collective-permute-done | bytes 655392 | tf_op jit(solution)/shard_map/ppermute | solution.py:360
  32.9 2.1 %collective-permute-start.1 = (bf16[16,8,2560]{2,1,0:T(8,128)(2,1)}, bf16[16,8,2560]{2,1,0:T(8,128)(2,1)S(1)}, u32[]{:S(2)}, u32[]{:S(2)}) collective-permute-start(bf16[16,8,2560]{2,1,0:T(8,128)(2,1)} %collective-permute-done.refs_2_.refs_9_), channel_id=1, source_target_pairs={{0,8},{2,10},{8,16},{10,18},{16,24},{18,26},{24,28},{26,30},{28,20... | collective-permute-start | bytes 1966088 | tf_op jit(solution)/shard_map/ppermute | solution.py:360
  35.3 6.4 %near_part.1 = (f32[20,8,384]{2,1,0:T(8,128)S(1)}, f32[20,8,384]{2,1,0:T(8,128)S(1)}, f32[2560,384]{1,0:T(8,128)S(1)}) custom-call(f32[448,128]{1,0:T(8,128)S(1)} %broadcast_in_dim.133.bias_ref, bf16[384,2560]{1,0:T(8,128)(2,1)S(1)} %fusion.2.q_ref.refs_3_, bf16[384,2560]{1,0:T(8,128)(2,1)S(1)} %fusion.5.k_ref, bf16[384,2560]{1,0:T(8,128)(2,1)S(1)} %copy-done, ...), custom_call_target="tpu_custom_call" | custom-call | flops 1761607680 | bytes 9830400 | tf_op jit(solution)/shard_map/near_part/pallas_call | solution.py:133
  41.7 3.1 %pick_0.1 = bf16[48,8,2560]{2,1,0:T(8,128)(2,1)S(1)} custom-call(s32[4]{0:T(128)S(1)} %slice.86.first_ref, s32[88]{0:T(128)S(1)} %concatenate.61.block_ref, bf16[16,8,2560]{2,1,0:T(8,128)(2,1)S(1)} %copy-done.1, bf16[16,8,2560]{2,1,0:T(8,128)(2,1)} %collective-permute-done.8.refs_1_.refs_8_, bf16[16,8,2560]{2,1,0:T(8,128)(2,1)} %collective-permute-done.refs_2_.refs_9_, ...), custom_call_target="tpu_custom_call" | custom-call | bytes 3932160 | tf_op jit(solution)/shard_map/pick_0/pallas_call | solution.py:168
  44.8 10.9 %collective-permute-start.16 = (bf16[48,8,2560]{2,1,0:T(8,128)(2,1)S(1)}, bf16[48,8,2560]{2,1,0:T(8,128)(2,1)S(1)}, u32[]{:S(2)}, u32[]{:S(2)}) collective-permute-start(bf16[48,8,2560]{2,1,0:T(8,128)(2,1)S(1)} %pick_0.1), channel_id=1, source_target_pairs={{0,2},{2,0},{4,6},{6,4},{8,10},{10,8},{12,14},{14,12},{16,18},{18,... | collective-permute-start | bytes 5898248 | tf_op jit(solution)/shard_map/ppermute | solution.py:360
  55.8 4.3 %collective-permute-done.1.refs_1_.refs_15_ = bf16[16,8,2560]{2,1,0:T(8,128)(2,1)S(1)} collective-permute-done((bf16[16,8,2560]{2,1,0:T(8,128)(2,1)}, bf16[16,8,2560]{2,1,0:T(8,128)(2,1)S(1)}, u32[]{:S(2)}, u32[]{:S(2)}) %collective-permute-start.1) | collective-permute-done | bytes 655392 | tf_op jit(solution)/shard_map/ppermute | solution.py:360
  60.0 1.5 %collective-permute-done.9.refs_0_.refs_14_ = bf16[16,8,2560]{2,1,0:T(8,128)(2,1)S(1)} collective-permute-done((bf16[16,8,2560]{2,1,0:T(8,128)(2,1)}, bf16[16,8,2560]{2,1,0:T(8,128)(2,1)S(1)}, u32[]{:S(2)}, u32[]{:S(2)}) %collective-permute-start.9) | collective-permute-done | bytes 655392 | tf_op jit(solution)/shard_map/ppermute | solution.py:360
  61.6 2.4 %pick_1.1 = bf16[32,8,2560]{2,1,0:T(8,128)(2,1)S(1)} custom-call(s32[3]{0:T(128)S(1)} %get-tuple-element.83.first_ref, s32[80]{0:T(128)S(1)} %concatenate.63.block_ref, bf16[16,8,2560]{2,1,0:T(8,128)(2,1)S(1)} %collective-permute-done.9.refs_0_.refs_14_, bf16[16,8,2560]{2,1,0:T(8,128)(2,1)S(1)} %collective-permute-done.1.refs_1_.refs_15_, ...), custom_call_target="tpu_custom_call" | custom-call | bytes 2621440 | tf_op jit(solution)/shard_map/pick_1/pallas_call | solution.py:168
  64.0 6.0 %collective-permute-start.17 = (bf16[32,8,2560]{2,1,0:T(8,128)(2,1)S(1)}, bf16[32,8,2560]{2,1,0:T(8,128)(2,1)S(1)}, u32[]{:S(2)}, u32[]{:S(2)}) collective-permute-start(bf16[32,8,2560]{2,1,0:T(8,128)(2,1)S(1)} %pick_1.1), channel_id=1, source_target_pairs={{0,2},{2,0},{4,6},{6,4},{8,10},{10,8},{12,14},{14,12},{16,18},{18,... | collective-permute-start | bytes 3932168 | tf_op jit(solution)/shard_map/ppermute | solution.py:360
  70.0 2.1 %collective-permute-start.6 = (bf16[16,8,2560]{2,1,0:T(8,128)(2,1)S(1)}, bf16[16,8,2560]{2,1,0:T(8,128)(2,1)S(1)}, u32[]{:S(2)}, u32[]{:S(2)}) collective-permute-start(bf16[16,8,2560]{2,1,0:T(8,128)(2,1)S(1)} %collective-permute-done.5.refs_2_.refs_16_), channel_id=1, source_target_pairs={{0,4},{2,6},{8,0},{10,2},{16,8},{18,10},{24,16},{26,18},{28,24},{3... | collective-permute-start | bytes 1966088 | tf_op jit(solution)/shard_map/ppermute | solution.py:360
  72.7 2.1 %collective-permute-start.10 = (bf16[16,8,2560]{2,1,0:T(8,128)(2,1)S(1)}, bf16[16,8,2560]{2,1,0:T(8,128)(2,1)S(1)}, u32[]{:S(2)}, u32[]{:S(2)}) collective-permute-start(bf16[16,8,2560]{2,1,0:T(8,128)(2,1)S(1)} %collective-permute-done.9.refs_0_.refs_14_), channel_id=1, source_target_pairs={{0,4},{2,6},{8,0},{10,2},{16,8},{18,10},{24,16},{26,18},{28,24},{3... | collective-permute-start | bytes 1966088 | tf_op jit(solution)/shard_map/ppermute | solution.py:360
  75.5 1.3 collective-permute-start.18
  76.8 0.7 pad_add_fusion.1.refs_0_
  79.0 14.9 %far_1.1 = (f32[20,8,384]{2,1,0:T(8,128)S(1)}, f32[20,8,384]{2,1,0:T(8,128)S(1)}, f32[2560,384]{1,0:T(8,128)S(1)}) custom-call(s32[8]{0:T(128)S(1)} %pad_add_fusion.1.refs_0_, s32[128]{0:T(128)S(1)} %concatenate.55.refs_1_, f32[512,128]{1,0:T(8,128)S(1)} %broadcast_in_dim.128.refs_2_, ...), custom_call_target="tpu_custom_call", output_to_operand_aliasing={{0}: (4, {}), {1}: (5, {}), {2}: (6, {})} | custom-call | flops 2013265920 | bytes 9830400 | tf_op jit(solution)/shard_map/far_1/pallas_call | solution.py:256
  93.9 8.7 %collective-permute-done.2.refs_1_.refs_11_ = bf16[16,8,2560]{2,1,0:T(8,128)(2,1)S(1)} collective-permute-done((bf16[16,8,2560]{2,1,0:T(8,128)(2,1)S(1)}, bf16[16,8,2560]{2,1,0:T(8,128)(2,1)S(1)}, u32[]{:S(2)}, u32[]{:S(2)}) %collective-permute-start.2) | collective-permute-done | bytes 655392 | tf_op jit(solution)/shard_map/ppermute | solution.py:360
  102.6 5.7 %collective-permute-done.10.refs_0_.refs_10_ = bf16[16,8,2560]{2,1,0:T(8,128)(2,1)S(1)} collective-permute-done((bf16[16,8,2560]{2,1,0:T(8,128)(2,1)S(1)}, bf16[16,8,2560]{2,1,0:T(8,128)(2,1)S(1)}, u32[]{:S(2)}, u32[]{:S(2)}) %collective-permute-start.10) | collective-permute-done | bytes 655392 | tf_op jit(solution)/shard_map/ppermute | solution.py:360
  108.3 2.4 %pick_2.1 = bf16[32,8,2560]{2,1,0:T(8,128)(2,1)S(1)} custom-call(s32[3]{0:T(128)S(1)} %get-tuple-element.82.first_ref, s32[80]{0:T(128)S(1)} %concatenate.63.block_ref, bf16[16,8,2560]{2,1,0:T(8,128)(2,1)S(1)} %collective-permute-done.10.refs_0_.refs_10_, bf16[16,8,2560]{2,1,0:T(8,128)(2,1)S(1)} %collective-permute-done.2.refs_1_.refs_11_, ...), custom_call_target="tpu_custom_call" | custom-call | bytes 2621440 | tf_op jit(solution)/shard_map/pick_2/pallas_call | solution.py:168
  112.9 2.4 %collective-permute-start.7 = (bf16[16,8,2560]{2,1,0:T(8,128)(2,1)S(1)}, bf16[16,8,2560]{2,1,0:T(8,128)(2,1)S(1)}, u32[]{:S(2)}, u32[]{:S(2)}) collective-permute-start(bf16[16,8,2560]{2,1,0:T(8,128)(2,1)S(1)} %collective-permute-done.6.refs_2_.refs_12_), channel_id=1, source_target_pairs={{0,4},{2,6},{8,0},{10,2},{16,8},{18,10},{24,16},{26,18},{28,24},{3... | collective-permute-start | bytes 1966088 | tf_op jit(solution)/shard_map/ppermute | solution.py:360
  115.6 9.5 %far_2.1 = (f32[20,8,384]{2,1,0:T(8,128)S(1)}, f32[20,8,384]{2,1,0:T(8,128)S(1)}, f32[2560,384]{1,0:T(8,128)S(1)}) custom-call(s32[4]{0:T(128)S(1)} %pad_add_fusion.refs_0_, s32[96]{0:T(128)S(1)} %concatenate.53.refs_1_, f32[256,128]{1,0:T(8,128)S(1)} %broadcast_in_dim.125.refs_2_, ...), custom_call_target="tpu_custom_call", output_to_operand_aliasing={{0}: (4, {}), {1}: (5, {}), {2}: (6, {})} | custom-call | flops 1006632960 | bytes 9830400 | tf_op jit(solution)/shard_map/far_2/pallas_call | solution.py:256
  125.1 5.0 %collective-permute-done.7.refs_1_.refs_9_ = bf16[16,8,2560]{2,1,0:T(8,128)(2,1)S(1)} collective-permute-done((bf16[16,8,2560]{2,1,0:T(8,128)(2,1)S(1)}, bf16[16,8,2560]{2,1,0:T(8,128)(2,1)S(1)}, u32[]{:S(2)}, u32[]{:S(2)}) %collective-permute-start.7) | collective-permute-done | bytes 655392 | tf_op jit(solution)/shard_map/ppermute | solution.py:360
  130.1 2.2 %collective-permute-done.3.refs_0_.refs_8_ = bf16[16,8,2560]{2,1,0:T(8,128)(2,1)S(1)} collective-permute-done((bf16[16,8,2560]{2,1,0:T(8,128)(2,1)S(1)}, bf16[16,8,2560]{2,1,0:T(8,128)(2,1)S(1)}, u32[]{:S(2)}, u32[]{:S(2)}) %collective-permute-start.3) | collective-permute-done | bytes 655392 | tf_op jit(solution)/shard_map/ppermute | solution.py:360
  132.2 1.5 %pick_3.1 = bf16[16,8,2560]{2,1,0:T(8,128)(2,1)S(1)} custom-call(s32[2]{0:T(128)S(1)} %slice.95.first_ref, s32[72]{0:T(128)S(1)} %concatenate.64.block_ref, bf16[16,8,2560]{2,1,0:T(8,128)(2,1)S(1)} %collective-permute-done.3.refs_0_.refs_8_, bf16[16,8,2560]{2,1,0:T(8,128)(2,1)S(1)} %collective-permute-done.7.refs_1_.refs_9_), custom_call_target="tpu_custom_call" | custom-call | bytes 1310720 | tf_op jit(solution)/shard_map/pick_3/pallas_call | solution.py:168
  135.1 0.7 collective-permute-done.20.refs_10_
  136.0 6.9 %far_3.1 = bf16[384,2560]{1,0:T(8,128)(2,1)} custom-call(s32[3]{0:T(128)S(1)} %get-tuple-element.90.refs_0_, s32[80]{0:T(128)S(1)} %concatenate.51.refs_1_, f32[128,128]{1,0:T(8,128)S(1)} %broadcast_in_dim.122.refs_2_, bf16[384,2560]{1,0:T(8,128)(2,1)S(1)} %fusion.2.q_ref.refs_3_, f32[20,8,384]{2,1,0:T(8,128)S(1)} %get-tuple-element.64.refs_4_, ...), custom_call_target="tpu_custom_call" | custom-call | flops 503316480 | bytes 9830400 | tf_op jit(solution)/shard_map/far_3/pallas_call | solution.py:256
  (79 shorter events, 5.4 us)
Async XLA Ops:
  0.0 9.0 %copy-start.3 = (bf16[384,2560]{1,0:T(8,128)(2,1)S(1)}, bf16[384,2560]{1,0:T(8,128)(2,1)}, u32[]{:S(2)}) copy-start(bf16[384,2560]{1,0:T(8,128)(2,1)} %param.12) | copy-start | bytes 5898244
  0.0 21.4 %collective-permute-start.11 = (bf16[16,8,2560]{2,1,0:T(8,128)(2,1)}, bf16[16,8,2560]{2,1,0:T(8,128)(2,1)S(1)}, u32[]{:S(2)}, u32[]{:S(2)}) collective-permute-start(bf16[16,8,2560]{2,1,0:T(8,128)(2,1)} %refs_10_), channel_id=1, source_target_pairs={{0,8},{2,10},{8,16},{10,18},{16,24},{18,26},{24,28},{26,30},{28,20... | collective-permute-start | bytes 1966088 | tf_op jit(solution)/shard_map/ppermute | solution.py:360
  3.0 20.5 %collective-permute-start.4 = (bf16[16,8,2560]{2,1,0:T(8,128)(2,1)}, bf16[16,8,2560]{2,1,0:T(8,128)(2,1)S(1)}, u32[]{:S(2)}, u32[]{:S(2)}) collective-permute-start(bf16[16,8,2560]{2,1,0:T(8,128)(2,1)} %refs_10_), channel_id=1, source_target_pairs={{0,4},{2,6},{8,0},{10,2},{16,8},{18,10},{24,16},{26,18},{28,24},{3... | collective-permute-start | bytes 1966088 | tf_op jit(solution)/shard_map/ppermute | solution.py:360
  3.0 29.9 %collective-permute-start = (bf16[16,8,2560]{2,1,0:T(8,128)(2,1)}, bf16[16,8,2560]{2,1,0:T(8,128)(2,1)}, u32[]{:S(2)}, u32[]{:S(2)}) collective-permute-start(bf16[16,8,2560]{2,1,0:T(8,128)(2,1)} %refs_7_), channel_id=1, source_target_pairs={{0,8},{2,10},{8,16},{10,18},{16,24},{18,26},{24,28},{26,30},{28,20... | collective-permute-start | bytes 1966088 | tf_op jit(solution)/shard_map/ppermute | solution.py:360
  5.1 30.0 %collective-permute-start.8 = (bf16[16,8,2560]{2,1,0:T(8,128)(2,1)}, bf16[16,8,2560]{2,1,0:T(8,128)(2,1)}, u32[]{:S(2)}, u32[]{:S(2)}) collective-permute-start(bf16[16,8,2560]{2,1,0:T(8,128)(2,1)} %refs_7_), channel_id=1, source_target_pairs={{0,4},{2,6},{8,0},{10,2},{16,8},{18,10},{24,16},{26,18},{28,24},{3... | collective-permute-start | bytes 1966088 | tf_op jit(solution)/shard_map/ppermute | solution.py:360
  6.3 12.5 %collective-permute-start.15 = (s32[81]{0:T(128)S(1)}, s32[81]{0:T(128)S(1)}, u32[]{:S(2)}, u32[]{:S(2)}) collective-permute-start(s32[81]{0:T(128)S(1)} %pad_add_fusion.2), channel_id=1, source_target_pairs={{0,2},{2,0},{4,6},{6,4},{8,10},{10,8},{12,14},{14,12},{16,18},{18,... | collective-permute-start | bytes 980 | tf_op jit(solution)/shard_map/ppermute | solution.py:326
  6.9 8.1 %copy-start.5 = (f32[2560]{0:T(1024)S(1)}, f32[2560]{0:T(1024)}, u32[]{:S(2)}) copy-start(f32[2560]{0:T(1024)} %param.14) | copy-start | bytes 30724
  6.9 8.1 %copy-start.6 = (f32[2560]{0:T(1024)S(1)}, f32[2560]{0:T(1024)}, u32[]{:S(2)}) copy-start(f32[2560]{0:T(1024)} %param.15) | copy-start | bytes 30724
  17.2 3.5 %copy-start.4 = (bf16[384,2560]{1,0:T(8,128)(2,1)S(1)}, bf16[384,2560]{1,0:T(8,128)(2,1)}, u32[]{:S(2)}) copy-start(bf16[384,2560]{1,0:T(8,128)(2,1)} %param.11) | copy-start | bytes 5898244
  18.7 16.5 %copy-start = (bf16[384,2560]{1,0:T(8,128)(2,1)S(1)}, bf16[384,2560]{1,0:T(8,128)(2,1)}, u32[]{:S(2)}) copy-start(bf16[384,2560]{1,0:T(8,128)(2,1)} %v_ref.1) | copy-start | bytes 5898244
  18.8 16.3 %collective-permute-start.14 = (bf16[144,2560]{1,0:T(8,128)(2,1)S(1)}, bf16[144,2560]{1,0:T(8,128)(2,1)S(1)}, u32[]{:S(2)}, u32[]{:S(2)}) collective-permute-start(bf16[144,2560]{1,0:T(8,128)(2,1)S(1)} %fusion.8), channel_id=1, source_target_pairs={{0,2},{2,4},{4,6},{6,8},{8,10},{10,12},{12,14},{14,16},{16,18},{18... | collective-permute-start | bytes 2211848 | tf_op jit(solution)/shard_map/ppermute | solution.py:22
  21.4 34.4 %collective-permute-start.12 = (bf16[16,8,2560]{2,1,0:T(8,128)(2,1)S(1)}, bf16[16,8,2560]{2,1,0:T(8,128)(2,1)S(1)}, u32[]{:S(2)}, u32[]{:S(2)}) collective-permute-start(bf16[16,8,2560]{2,1,0:T(8,128)(2,1)S(1)} %collective-permute-done.11.refs_5_.refs_12_), channel_id=1, source_target_pairs={{0,8},{2,10},{8,16},{10,18},{16,24},{18,26},{24,28},{26,30},{28,20... | collective-permute-start | bytes 1966088 | tf_op jit(solution)/shard_map/ppermute | solution.py:360
  23.5 32.3 %collective-permute-start.5 = (bf16[16,8,2560]{2,1,0:T(8,128)(2,1)S(1)}, bf16[16,8,2560]{2,1,0:T(8,128)(2,1)S(1)}, u32[]{:S(2)}, u32[]{:S(2)}) collective-permute-start(bf16[16,8,2560]{2,1,0:T(8,128)(2,1)S(1)} %collective-permute-done.4.refs_4_.refs_11_), channel_id=1, source_target_pairs={{0,4},{2,6},{8,0},{10,2},{16,8},{18,10},{24,16},{26,18},{28,24},{3... | collective-permute-start | bytes 1966088 | tf_op jit(solution)/shard_map/ppermute | solution.py:360
  32.9 27.2 %collective-permute-start.1 = (bf16[16,8,2560]{2,1,0:T(8,128)(2,1)}, bf16[16,8,2560]{2,1,0:T(8,128)(2,1)S(1)}, u32[]{:S(2)}, u32[]{:S(2)}) collective-permute-start(bf16[16,8,2560]{2,1,0:T(8,128)(2,1)} %collective-permute-done.refs_2_.refs_9_), channel_id=1, source_target_pairs={{0,8},{2,10},{8,16},{10,18},{16,24},{18,26},{24,28},{26,30},{28,20... | collective-permute-start | bytes 1966088 | tf_op jit(solution)/shard_map/ppermute | solution.py:360
  35.0 26.5 %collective-permute-start.9 = (bf16[16,8,2560]{2,1,0:T(8,128)(2,1)}, bf16[16,8,2560]{2,1,0:T(8,128)(2,1)S(1)}, u32[]{:S(2)}, u32[]{:S(2)}) collective-permute-start(bf16[16,8,2560]{2,1,0:T(8,128)(2,1)} %collective-permute-done.8.refs_1_.refs_8_), channel_id=1, source_target_pairs={{0,4},{2,6},{8,0},{10,2},{16,8},{18,10},{24,16},{26,18},{28,24},{3... | collective-permute-start | bytes 1966088 | tf_op jit(solution)/shard_map/ppermute | solution.py:360
  35.3 6.5 %copy-start.1 = (bf16[16,8,2560]{2,1,0:T(8,128)(2,1)S(1)}, bf16[16,8,2560]{2,1,0:T(8,128)(2,1)}, u32[]{:S(2)}) copy-start(bf16[16,8,2560]{2,1,0:T(8,128)(2,1)} %refs_7_) | copy-start | bytes 1966084
  35.3 6.5 %copy-start.2 = (bf16[16,8,2560]{2,1,0:T(8,128)(2,1)S(1)}, bf16[16,8,2560]{2,1,0:T(8,128)(2,1)}, u32[]{:S(2)}) copy-start(bf16[16,8,2560]{2,1,0:T(8,128)(2,1)} %refs_10_) | copy-start | bytes 1966084
  44.8 30.7 %collective-permute-start.16 = (bf16[48,8,2560]{2,1,0:T(8,128)(2,1)S(1)}, bf16[48,8,2560]{2,1,0:T(8,128)(2,1)S(1)}, u32[]{:S(2)}, u32[]{:S(2)}) collective-permute-start(bf16[48,8,2560]{2,1,0:T(8,128)(2,1)S(1)} %pick_0.1), channel_id=1, source_target_pairs={{0,2},{2,0},{4,6},{6,4},{8,10},{10,8},{12,14},{14,12},{16,18},{18,... | collective-permute-start | bytes 5898248 | tf_op jit(solution)/shard_map/ppermute | solution.py:360
  64.0 8.7 %collective-permute-start.17 = (bf16[32,8,2560]{2,1,0:T(8,128)(2,1)S(1)}, bf16[32,8,2560]{2,1,0:T(8,128)(2,1)S(1)}, u32[]{:S(2)}, u32[]{:S(2)}) collective-permute-start(bf16[32,8,2560]{2,1,0:T(8,128)(2,1)S(1)} %pick_1.1), channel_id=1, source_target_pairs={{0,2},{2,0},{4,6},{6,4},{8,10},{10,8},{12,14},{14,12},{16,18},{18,... | collective-permute-start | bytes 3932168 | tf_op jit(solution)/shard_map/ppermute | solution.py:360
  70.0 23.8 %collective-permute-start.6 = (bf16[16,8,2560]{2,1,0:T(8,128)(2,1)S(1)}, bf16[16,8,2560]{2,1,0:T(8,128)(2,1)S(1)}, u32[]{:S(2)}, u32[]{:S(2)}) collective-permute-start(bf16[16,8,2560]{2,1,0:T(8,128)(2,1)S(1)} %collective-permute-done.5.refs_2_.refs_16_), channel_id=1, source_target_pairs={{0,4},{2,6},{8,0},{10,2},{16,8},{18,10},{24,16},{26,18},{28,24},{3... | collective-permute-start | bytes 1966088 | tf_op jit(solution)/shard_map/ppermute | solution.py:360
  72.2 21.7 %collective-permute-start.13 = (bf16[16,8,2560]{2,1,0:T(8,128)(2,1)S(1)}, bf16[16,8,2560]{2,1,0:T(8,128)(2,1)S(1)}, u32[]{:S(2)}, u32[]{:S(2)}) collective-permute-start(bf16[16,8,2560]{2,1,0:T(8,128)(2,1)S(1)} %collective-permute-done.12.refs_3_.refs_17_), channel_id=1, source_target_pairs={{0,8},{2,10},{8,16},{10,18},{16,24},{18,26},{24,28},{26,30},{28,20... | collective-permute-start | bytes 1966088 | tf_op jit(solution)/shard_map/ppermute | solution.py:360
  72.2 30.4 %collective-permute-start.2 = (bf16[16,8,2560]{2,1,0:T(8,128)(2,1)S(1)}, bf16[16,8,2560]{2,1,0:T(8,128)(2,1)S(1)}, u32[]{:S(2)}, u32[]{:S(2)}) collective-permute-start(bf16[16,8,2560]{2,1,0:T(8,128)(2,1)S(1)} %collective-permute-done.1.refs_1_.refs_15_), channel_id=1, source_target_pairs={{0,8},{2,10},{8,16},{10,18},{16,24},{18,26},{24,28},{26,30},{28,20... | collective-permute-start | bytes 1966088 | tf_op jit(solution)/shard_map/ppermute | solution.py:360
  72.7 35.7 %collective-permute-start.10 = (bf16[16,8,2560]{2,1,0:T(8,128)(2,1)S(1)}, bf16[16,8,2560]{2,1,0:T(8,128)(2,1)S(1)}, u32[]{:S(2)}, u32[]{:S(2)}) collective-permute-start(bf16[16,8,2560]{2,1,0:T(8,128)(2,1)S(1)} %collective-permute-done.9.refs_0_.refs_14_), channel_id=1, source_target_pairs={{0,4},{2,6},{8,0},{10,2},{16,8},{18,10},{24,16},{26,18},{28,24},{3... | collective-permute-start | bytes 1966088 | tf_op jit(solution)/shard_map/ppermute | solution.py:360
  75.5 39.9 %collective-permute-start.18 = (bf16[144,2560]{1,0:T(8,128)(2,1)S(1)}, bf16[144,2560]{1,0:T(8,128)(2,1)S(1)}, u32[]{:S(2)}, u32[]{:S(2)}) collective-permute-start(bf16[144,2560]{1,0:T(8,128)(2,1)S(1)} %fusion.9), channel_id=1, source_target_pairs={{2,0},{4,2},{6,4},{8,6},{10,8},{12,10},{14,12},{16,14},{18,16},{20... | collective-permute-start | bytes 2211848 | tf_op jit(solution)/shard_map/ppermute | solution.py:22
  110.7 4.7 %collective-permute-start.19 = (bf16[32,8,2560]{2,1,0:T(8,128)(2,1)S(1)}, bf16[32,8,2560]{2,1,0:T(8,128)(2,1)S(1)}, u32[]{:S(2)}, u32[]{:S(2)}) collective-permute-start(bf16[32,8,2560]{2,1,0:T(8,128)(2,1)S(1)} %pick_2.1), channel_id=1, source_target_pairs={{0,2},{2,0},{4,6},{6,4},{8,10},{10,8},{12,14},{14,12},{16,18},{18,... | collective-permute-start | bytes 3932168 | tf_op jit(solution)/shard_map/ppermute | solution.py:360
  112.9 17.1 %collective-permute-start.7 = (bf16[16,8,2560]{2,1,0:T(8,128)(2,1)S(1)}, bf16[16,8,2560]{2,1,0:T(8,128)(2,1)S(1)}, u32[]{:S(2)}, u32[]{:S(2)}) collective-permute-start(bf16[16,8,2560]{2,1,0:T(8,128)(2,1)S(1)} %collective-permute-done.6.refs_2_.refs_12_), channel_id=1, source_target_pairs={{0,4},{2,6},{8,0},{10,2},{16,8},{18,10},{24,16},{26,18},{28,24},{3... | collective-permute-start | bytes 1966088 | tf_op jit(solution)/shard_map/ppermute | solution.py:360
  115.4 16.9 %collective-permute-start.3 = (bf16[16,8,2560]{2,1,0:T(8,128)(2,1)S(1)}, bf16[16,8,2560]{2,1,0:T(8,128)(2,1)S(1)}, u32[]{:S(2)}, u32[]{:S(2)}) collective-permute-start(bf16[16,8,2560]{2,1,0:T(8,128)(2,1)S(1)} %collective-permute-done.2.refs_1_.refs_11_), channel_id=1, source_target_pairs={{0,8},{2,10},{8,16},{10,18},{16,24},{18,26},{24,28},{26,30},{28,20... | collective-permute-start | bytes 1966088 | tf_op jit(solution)/shard_map/ppermute | solution.py:360
  133.7 2.2 %collective-permute-start.20 = (bf16[16,8,2560]{2,1,0:T(8,128)(2,1)S(1)}, bf16[16,8,2560]{2,1,0:T(8,128)(2,1)S(1)}, u32[]{:S(2)}, u32[]{:S(2)}) collective-permute-start(bf16[16,8,2560]{2,1,0:T(8,128)(2,1)S(1)} %pick_3.1), channel_id=1, source_target_pairs={{0,2},{2,0},{4,6},{6,4},{8,10},{10,8},{12,14},{14,12},{16,18},{18,... | collective-permute-start | bytes 1966088 | tf_op jit(solution)/shard_map/ppermute | solution.py:360

commit v7 on v6

--- a/solution.py
+++ b/solution.py
@@ -235,7 +235,7 @@
         for (head, place), sums in zip(places, attend(heads)):
             if last:
                 result = jnp.where(live_ref[...] > 0.0, sums[2] / sums[1], 0.0)
-                out_refs[0][:, place] = result.T.astype(out_refs[0].dtype)
+                out_refs[0][:, place] = result.astype(out_refs[0].dtype).T
             else:
                 store_sums(sums, head, place, *out_refs)
 
@@ -380,16 +380,22 @@
     for stage, (first, stop) in enumerate(stages(half)):
         size = stop - first
         (*pieces,), sums = after([*keys[first:stop], *values[first:stop]], sums)
+        if stage < 2:
+            *pieces, values[stop], values[stop + 1] = lax.optimization_barrier(
+                (*pieces, values[stop], values[stop + 1])
+            )
+        if stage == 2:
+            *pieces, segments[0][-1] = lax.optimization_barrier((*pieces, segments[0][-1]))
         theirs = their_first[2 * first + size : 2 * stop + 1]
         limit = min(request.shape[0], size * most)
         picked = pick_part(f"pick_{stage}", theirs, their_block, limit, pieces[:size], pieces[size:])
         received = moved(picked, swap)
-        if stage == 1:
+        if stage == 0:
             fronts, received = lax.optimization_barrier((fronts, received))
             seen, right_keys, right_values = arrived(passed_along(fronts, "tile", -1))
         segments.append([*pieces, received])
         starts.append(my_first[2 * first : 2 * first + size + 1])
-        if stage > 0:
+        if stage != 1:
             bounds = jnp.concatenate([*starts, my_first[2 * stop :][:1]])
             slots = min(request.shape[0], sum(len(segment) // 2 for segment in segments) * 2 * most)
             final = live if first == 2 * half - 1 else None

time: 143 us -> 153 us (1.070); the launches traced: 143 us -> 151 us
  waiting for transfers between devices: 38 us -> 50.8 us
  starting transfers between devices: 36.3 us -> 24.7 us
  Pallas kernels: 47 us -> 49.5 us
  other arithmetic: 7.89 us -> 10.3 us
  local copies, waits for them, and re-layouts: 3.11 us -> 4.91 us
    ppermute x18, starting transfers between devices: 33.1 us -> 19.9 us  [moved(): return lax.ppermute(piece, 'tile', pairs)]
    ppermute x18, waiting for transfers between devices: 38 us -> 50.8 us  [moved(): return lax.ppermute(piece, 'tile', pairs)]
    pallas_call x3, Pallas kernels: 31.2 us -> 33.9 us  [far_part(): pl.pallas_call(functools.partial(far_kernel, [len(segment) // 2 for segme...]
    convert_element_type x2, other arithmetic: 2.58 us -> 4.26 us  [normalize(): return (rows32 * factor[:, None] * gain).astype(jnp.bfloat16)]
  transfers between devices with their start and end apart: 21 -> 21, of which waited for: 9 -> 11; matrix products, arithmetic and copies ran while one was open for 8% -> 10% of each run, Pallas kernels for 27% -> 24%
where the time goes in v7:
time: 153 us; the launch traced here: 151 us
  waiting for transfers between devices  50.8 us (33%)
  Pallas kernels  49.5 us (32%)
  starting transfers between devices  24.7 us (16%)
  other arithmetic  10.3 us (7%)
  between operations  5.4 us (4%)
  blocking collectives  4.94 us (3%)
  local copies, waits for them, and re-layouts  4.91 us (3%)
    ppermute x18, waiting for transfers between devices, moved(): return lax.ppermute(piece, 'tile', pairs)  50.8 us
    pallas_call x3, Pallas kernels, far_part(): pl.pallas_call(functools.partial(far_kernel, [len(segment) // 2 for segme...  33.9 us
    ppermute x18, starting transfers between devices, moved(): return lax.ppermute(piece, 'tile', pairs)  19.9 us
    pallas_call x4, Pallas kernels, pick_part(): pl.pallas_call(functools.partial(pick_kernel, groups, slots), in_specs=[p...  9.23 us
    pallas_call x1, Pallas kernels, near_part(): pl.pallas_call(near_kernel, in_specs=[IN_VMEM] * 6, out_specs=[IN_VMEM] *...  6.4 us
    psum x1, blocking collectives, per_device(): lax.psum((row_squares(query_rows), row_squares(key_rows)), 'head')  4.94 us
    convert_element_type x2, other arithmetic, normalize(): return (rows32 * factor[:, None] * gain).astype(jnp.bfloat16)  4.26 us
    ppermute x2, starting transfers between devices, passed_along(): lax.ppermute(value, axis, [(source, source + steps) for source in range(f...  3.43 us
  transfers between devices with their start and end apart: 21, of which 11 were waited for; matrix products, arithmetic and copies ran while one was open for 10% of the time, Pallas kernels for 24%

profile of v7, /device:TPU:0, one launch (start us, length us, event | category | flops | bytes accessed | tf_op | source)
XLA Modules:
  0.0 150.5 jit_solution(2642705831832630715)
XLA Ops:
  0.0 3.0 %collective-permute-start.11 = (bf16[16,8,2560]{2,1,0:T(8,128)(2,1)}, bf16[16,8,2560]{2,1,0:T(8,128)(2,1)S(1)}, u32[]{:S(2)}, u32[]{:S(2)}) collective-permute-start(bf16[16,8,2560]{2,1,0:T(8,128)(2,1)} %refs_10_), channel_id=1, source_target_pairs={{0,8},{2,10},{8,16},{10,18},{16,24},{18,26},{24,28},{26,30},{28,20... | collective-permute-start | bytes 1966088 | tf_op jit(solution)/shard_map/ppermute | solution.py:360
  3.7 2.0 %fusion = f32[384]{0:T(512)S(1)} fusion(bf16[384,2560]{1,0:T(8,128)(2,1)} %param.11), kind=kLoop, calls=%fused_computation.4 | loop fusion | flops 2948736 | bytes 1967616 | tf_op jit(solution)/shard_map/reduce_sum | solution.py:27
  6.2 4.9 %all-reduce.10 = (f32[384]{0:T(512)S(1)}, f32[384]{0:T(512)S(1)}) all-reduce(f32[384]{0:T(512)S(1)} %fusion, f32[384]{0:T(512)S(1)} %fusion.3), channel_id=1, replica_groups=mesh['tile'=16,'head'=2] {'head'}, use_global_device_ids=true, to_apply=%region_4.5 | all-reduce | flops 768 | bytes 6144 | tf_op jit(solution)/shard_map/psum | solution.py:330
  11.8 2.1 %fusion.5.k_ref = bf16[384,2560]{1,0:T(8,128)(2,1)S(1)} fusion(bf16[384,2560]{1,0:T(8,128)(2,1)} %param.12, f32[2560]{0:T(1024)S(1)} %copy-done.7, f32[384]{0:T(512)S(1)} %add_rsqrt_fusion), kind=kLoop, calls=%fused_computation.9 | loop fusion | flops 3932160 | bytes 3943936 | tf_op jit(solution)/shard_map/convert_element_type | solution.py:33
  13.9 2.2 %fusion.23 = (bf16[64,2560]{1,0:T(8,128)(2,1)}, bf16[64,2560]{1,0:T(8,128)(2,1)S(1)}, bf16[64,2560]{1,0:T(8,128)(2,1)S(1)}, bf16[64,2560]{1,0:T(8,128)(2,1)}) fusion(bf16[384,2560]{1,0:T(8,128)(2,1)S(1)} %fusion.5.k_ref, s32[]{:T(128)S(6)} %select_n.170, bf16[384,2560]{1,0:T(8,128)(2,1)} %v_ref.1), kind=kLoop, calls=%fused_computation.79 | loop fusion | bytes 5898244 | tf_op jit(solution)/shard_map/slice | solution.py:347
  17.0 2.2 %collective-permute-start.12 = (bf16[144,2560]{1,0:T(8,128)(2,1)}, bf16[144,2560]{1,0:T(8,128)(2,1)}, u32[]{:S(2)}, u32[]{:S(2)}) collective-permute-start(bf16[144,2560]{1,0:T(8,128)(2,1)} %fusion.8), channel_id=1, source_target_pairs={{0,2},{2,4},{4,6},{6,8},{8,10},{10,12},{12,14},{14,16},{16,18},{18... | collective-permute-start | bytes 2211848 | tf_op jit(solution)/shard_map/ppermute | solution.py:22
  19.2 1.8 %collective-permute-start = (bf16[16,8,2560]{2,1,0:T(8,128)(2,1)S(1)}, bf16[16,8,2560]{2,1,0:T(8,128)(2,1)}, u32[]{:S(2)}, u32[]{:S(2)}) collective-permute-start(bf16[16,8,2560]{2,1,0:T(8,128)(2,1)S(1)} %copy-done.1), channel_id=1, source_target_pairs={{0,8},{2,10},{8,16},{10,18},{16,24},{18,26},{24,28},{26,30},{28,20... | collective-permute-start | bytes 1966088 | tf_op jit(solution)/shard_map/ppermute | solution.py:360
  21.5 1.4 collective-permute-start.14
  22.9 2.2 %fusion.2.q_ref.refs_3_ = bf16[384,2560]{1,0:T(8,128)(2,1)S(1)} fusion(bf16[384,2560]{1,0:T(8,128)(2,1)} %param.11, f32[2560]{0:T(1024)S(1)} %broadcast_multiply_fusion, f32[384]{0:T(512)S(1)} %add_rsqrt_fusion.1), kind=kLoop, calls=%fused_computation.6 | loop fusion | flops 3932160 | bytes 3943936 | tf_op jit(solution)/shard_map/convert_element_type | solution.py:33
  25.8 1.6 %collective-permute-start.13 = (bf16[16,8,2560]{2,1,0:T(8,128)(2,1)S(1)}, bf16[16,8,2560]{2,1,0:T(8,128)(2,1)S(1)}, u32[]{:S(2)}, u32[]{:S(2)}) collective-permute-start(bf16[16,8,2560]{2,1,0:T(8,128)(2,1)S(1)} %collective-permute-done.11.refs_5_.refs_12_), channel_id=1, source_target_pairs={{0,8},{2,10},{8,16},{10,18},{16,24},{18,26},{24,28},{26,30},{28,20... | collective-permute-start | bytes 1966088 | tf_op jit(solution)/shard_map/ppermute | solution.py:360
  28.5 1.1 fusion.26
  29.8 6.4 %near_part.1 = (f32[20,8,384]{2,1,0:T(8,128)S(1)}, f32[20,8,384]{2,1,0:T(8,128)S(1)}, f32[2560,384]{1,0:T(8,128)S(1)}) custom-call(f32[448,128]{1,0:T(8,128)S(1)} %broadcast_in_dim.130.bias_ref, bf16[384,2560]{1,0:T(8,128)(2,1)S(1)} %fusion.2.q_ref.refs_3_, bf16[384,2560]{1,0:T(8,128)(2,1)S(1)} %fusion.5.k_ref, bf16[384,2560]{1,0:T(8,128)(2,1)S(1)} %copy-done, ...), custom_call_target="tpu_custom_call" | custom-call | flops 1761607680 | bytes 9830400 | tf_op jit(solution)/shard_map/near_part/pallas_call | solution.py:133
  36.2 6.6 %collective-permute-done.8.refs_1_.refs_8_ = bf16[16,8,2560]{2,1,0:T(8,128)(2,1)S(1)} collective-permute-done((bf16[16,8,2560]{2,1,0:T(8,128)(2,1)S(1)}, bf16[16,8,2560]{2,1,0:T(8,128)(2,1)S(1)}, u32[]{:S(2)}, u32[]{:S(2)}) %collective-permute-start.8) | collective-permute-done | bytes 655392 | tf_op jit(solution)/shard_map/ppermute | solution.py:360
  42.8 7.1 %collective-permute-done.13.refs_3_.refs_13_ = bf16[16,8,2560]{2,1,0:T(8,128)(2,1)S(1)} collective-permute-done((bf16[16,8,2560]{2,1,0:T(8,128)(2,1)S(1)}, bf16[16,8,2560]{2,1,0:T(8,128)(2,1)S(1)}, u32[]{:S(2)}, u32[]{:S(2)}) %collective-permute-start.13) | collective-permute-done | bytes 655392 | tf_op jit(solution)/shard_map/ppermute | solution.py:360
  49.9 6.0 %collective-permute-done.5.refs_2_.refs_12_ = bf16[16,8,2560]{2,1,0:T(8,128)(2,1)S(1)} collective-permute-done((bf16[16,8,2560]{2,1,0:T(8,128)(2,1)}, bf16[16,8,2560]{2,1,0:T(8,128)(2,1)S(1)}, u32[]{:S(2)}, u32[]{:S(2)}) %collective-permute-start.5) | collective-permute-done | bytes 655392 | tf_op jit(solution)/shard_map/ppermute | solution.py:360
  55.9 3.0 %pick_0.1 = bf16[48,8,2560]{2,1,0:T(8,128)(2,1)S(1)} custom-call(s32[4]{0:T(128)S(1)} %slice.88.first_ref, s32[88]{0:T(128)S(1)} %concatenate.62.block_ref, bf16[16,8,2560]{2,1,0:T(8,128)(2,1)S(1)} %copy-done.1, bf16[16,8,2560]{2,1,0:T(8,128)(2,1)S(1)} %collective-permute-done.8.refs_1_.refs_8_, bf16[16,8,2560]{2,1,0:T(8,128)(2,1)} %collective-permute-done.refs_2_.refs_9_, ...), custom_call_target="tpu_custom_call" | custom-call | bytes 3932160 | tf_op jit(solution)/shard_map/pick_0/pallas_call | solution.py:168
  58.9 1.9 %collective-permute-start.15 = (bf16[48,8,2560]{2,1,0:T(8,128)(2,1)S(1)}, bf16[48,8,2560]{2,1,0:T(8,128)(2,1)S(1)}, u32[]{:S(2)}, u32[]{:S(2)}) collective-permute-start(bf16[48,8,2560]{2,1,0:T(8,128)(2,1)S(1)} %pick_0.1), channel_id=1, source_target_pairs={{0,2},{2,0},{4,6},{6,4},{8,10},{10,8},{12,14},{14,12},{16,18},{18,... | collective-permute-start | bytes 5898248 | tf_op jit(solution)/shard_map/ppermute | solution.py:360
  63.3 2.0 %collective-permute-start.9 = (bf16[16,8,2560]{2,1,0:T(8,128)(2,1)S(1)}, bf16[16,8,2560]{2,1,0:T(8,128)(2,1)S(1)}, u32[]{:S(2)}, u32[]{:S(2)}) collective-permute-start(bf16[16,8,2560]{2,1,0:T(8,128)(2,1)S(1)} %collective-permute-done.8.refs_1_.refs_8_), channel_id=1, source_target_pairs={{0,4},{2,6},{8,0},{10,2},{16,8},{18,10},{24,16},{26,18},{28,24},{3... | collective-permute-start | bytes 1966088 | tf_op jit(solution)/shard_map/ppermute | solution.py:360
  65.4 2.0 %collective-permute-start.6 = (bf16[16,8,2560]{2,1,0:T(8,128)(2,1)S(1)}, bf16[16,8,2560]{2,1,0:T(8,128)(2,1)S(1)}, u32[]{:S(2)}, u32[]{:S(2)}) collective-permute-start(bf16[16,8,2560]{2,1,0:T(8,128)(2,1)S(1)} %collective-permute-done.5.refs_2_.refs_12_), channel_id=1, source_target_pairs={{0,4},{2,6},{8,0},{10,2},{16,8},{18,10},{24,16},{26,18},{28,24},{3... | collective-permute-start | bytes 1966088 | tf_op jit(solution)/shard_map/ppermute | solution.py:360
  67.6 11.3 %far_0.1 = (f32[20,8,384]{2,1,0:T(8,128)S(1)}, f32[20,8,384]{2,1,0:T(8,128)S(1)}, f32[2560,384]{1,0:T(8,128)S(1)}) custom-call(s32[5]{0:T(128)S(1)} %pad_add_fusion.1.refs_0_, s32[112]{0:T(128)S(1)} %concatenate.59.refs_1_, f32[384,128]{1,0:T(8,128)S(1)} %broadcast_in_dim.133.refs_2_, ...), custom_call_target="tpu_custom_call", output_to_operand_aliasing={{0}: (4, {}), {1}: (5, {}), {2}: (6, {})} | custom-call | flops 1509949440 | bytes 9830400 | tf_op jit(solution)/shard_map/far_0/pallas_call | solution.py:256
  78.9 2.1 %collective-permute-done.1.refs_1_.refs_11_ = bf16[16,8,2560]{2,1,0:T(8,128)(2,1)S(1)} collective-permute-done((bf16[16,8,2560]{2,1,0:T(8,128)(2,1)}, bf16[16,8,2560]{2,1,0:T(8,128)(2,1)S(1)}, u32[]{:S(2)}, u32[]{:S(2)}) %collective-permute-start.1) | collective-permute-done | bytes 655392 | tf_op jit(solution)/shard_map/ppermute | solution.py:360
  81.1 13.0 %collective-permute-done.6.refs_2_.refs_17_ = bf16[16,8,2560]{2,1,0:T(8,128)(2,1)S(1)} collective-permute-done((bf16[16,8,2560]{2,1,0:T(8,128)(2,1)S(1)}, bf16[16,8,2560]{2,1,0:T(8,128)(2,1)S(1)}, u32[]{:S(2)}, u32[]{:S(2)}) %collective-permute-start.6) | collective-permute-done | bytes 655392 | tf_op jit(solution)/shard_map/ppermute | solution.py:360
  94.5 2.4 %pick_1.1 = bf16[32,8,2560]{2,1,0:T(8,128)(2,1)S(1)} custom-call(s32[3]{0:T(128)S(1)} %get-tuple-element.121.first_ref, s32[80]{0:T(128)S(1)} %concatenate.63.block_ref, bf16[16,8,2560]{2,1,0:T(8,128)(2,1)S(1)} %collective-permute-done.9.refs_0_.refs_10_, bf16[16,8,2560]{2,1,0:T(8,128)(2,1)S(1)} %collective-permute-done.1.refs_1_.refs_11_, ...), custom_call_target="tpu_custom_call" | custom-call | bytes 2621440 | tf_op jit(solution)/shard_map/pick_1/pallas_call | solution.py:168
  97.0 4.3 %collective-permute-start.2 = (bf16[16,8,2560]{2,1,0:T(8,128)(2,1)S(1)}, bf16[16,8,2560]{2,1,0:T(8,128)(2,1)S(1)}, u32[]{:S(2)}, u32[]{:S(2)}) collective-permute-start(bf16[16,8,2560]{2,1,0:T(8,128)(2,1)S(1)} %collective-permute-done.1.refs_1_.refs_11_), channel_id=1, source_target_pairs={{0,8},{2,10},{8,16},{10,18},{16,24},{18,26},{24,28},{26,30},{28,20... | collective-permute-start | bytes 1966088 | tf_op jit(solution)/shard_map/ppermute | solution.py:360
  101.3 1.3 collective-permute-start.17
  103.8 12.1 %collective-permute-done.2.refs_1_.refs_16_ = bf16[16,8,2560]{2,1,0:T(8,128)(2,1)S(1)} collective-permute-done((bf16[16,8,2560]{2,1,0:T(8,128)(2,1)S(1)}, bf16[16,8,2560]{2,1,0:T(8,128)(2,1)S(1)}, u32[]{:S(2)}, u32[]{:S(2)}) %collective-permute-start.2) | collective-permute-done | bytes 655392 | tf_op jit(solution)/shard_map/ppermute | solution.py:360
  115.9 2.2 %collective-permute-done.10.refs_0_.refs_15_ = bf16[16,8,2560]{2,1,0:T(8,128)(2,1)S(1)} collective-permute-done((bf16[16,8,2560]{2,1,0:T(8,128)(2,1)S(1)}, bf16[16,8,2560]{2,1,0:T(8,128)(2,1)S(1)}, u32[]{:S(2)}, u32[]{:S(2)}) %collective-permute-start.10) | collective-permute-done | bytes 655392 | tf_op jit(solution)/shard_map/ppermute | solution.py:360
  118.1 2.4 %pick_2.1 = bf16[32,8,2560]{2,1,0:T(8,128)(2,1)S(1)} custom-call(s32[3]{0:T(128)S(1)} %get-tuple-element.120.first_ref, s32[80]{0:T(128)S(1)} %concatenate.63.block_ref, bf16[16,8,2560]{2,1,0:T(8,128)(2,1)S(1)} %collective-permute-done.10.refs_0_.refs_15_, bf16[16,8,2560]{2,1,0:T(8,128)(2,1)S(1)} %collective-permute-done.2.refs_1_.refs_16_, ...), custom_call_target="tpu_custom_call" | custom-call | bytes 2621440 | tf_op jit(solution)/shard_map/pick_2/pallas_call | solution.py:168
  121.7 1.7 %collective-permute-start.3 = (bf16[16,8,2560]{2,1,0:T(8,128)(2,1)S(1)}, bf16[16,8,2560]{2,1,0:T(8,128)(2,1)S(1)}, u32[]{:S(2)}, u32[]{:S(2)}) collective-permute-start(bf16[16,8,2560]{2,1,0:T(8,128)(2,1)S(1)} %collective-permute-done.2.refs_1_.refs_16_), channel_id=1, source_target_pairs={{0,8},{2,10},{8,16},{10,18},{16,24},{18,26},{24,28},{26,30},{28,20... | collective-permute-start | bytes 1966088 | tf_op jit(solution)/shard_map/ppermute | solution.py:360
  123.8 15.8 %far_2.1 = (f32[20,8,384]{2,1,0:T(8,128)S(1)}, f32[20,8,384]{2,1,0:T(8,128)S(1)}, f32[2560,384]{1,0:T(8,128)S(1)}) custom-call(s32[7]{0:T(128)S(1)} %pad_add_fusion.refs_0_, s32[128]{0:T(128)S(1)} %concatenate.53.refs_1_, f32[512,128]{1,0:T(8,128)S(1)} %broadcast_in_dim.125.refs_2_, ...), custom_call_target="tpu_custom_call", output_to_operand_aliasing={{0}: (4, {}), {1}: (5, {}), {2}: (6, {})} | custom-call | flops 2013265920 | bytes 9830400 | tf_op jit(solution)/shard_map/far_2/pallas_call | solution.py:256
  140.0 1.5 pick_3.1
  143.7 6.8 %far_3.1 = bf16[384,2560]{1,0:T(8,128)(2,1)} custom-call(s32[3]{0:T(128)S(1)} %get-tuple-element.128.refs_0_, s32[80]{0:T(128)S(1)} %concatenate.51.refs_1_, f32[128,128]{1,0:T(8,128)S(1)} %broadcast_in_dim.122.refs_2_, bf16[384,2560]{1,0:T(8,128)(2,1)S(1)} %fusion.2.q_ref.refs_3_, f32[20,8,384]{2,1,0:T(8,128)S(1)} %get-tuple-element.102.refs_4_, ...), custom_call_target="tpu_custom_call" | custom-call | flops 503316480 | bytes 9830400 | tf_op jit(solution)/shard_map/far_3/pallas_call | solution.py:256
  (85 shorter events, 8.9 us)
Async XLA Ops:
  0.0 5.7 %copy-start.3 = (bf16[384,2560]{1,0:T(8,128)(2,1)S(1)}, bf16[384,2560]{1,0:T(8,128)(2,1)}, u32[]{:S(2)}) copy-start(bf16[384,2560]{1,0:T(8,128)(2,1)} %param.12) | copy-start | bytes 5898244
  0.0 25.8 %collective-permute-start.11 = (bf16[16,8,2560]{2,1,0:T(8,128)(2,1)}, bf16[16,8,2560]{2,1,0:T(8,128)(2,1)S(1)}, u32[]{:S(2)}, u32[]{:S(2)}) collective-permute-start(bf16[16,8,2560]{2,1,0:T(8,128)(2,1)} %refs_10_), channel_id=1, source_target_pairs={{0,8},{2,10},{8,16},{10,18},{16,24},{18,26},{24,28},{26,30},{28,20... | collective-permute-start | bytes 1966088 | tf_op jit(solution)/shard_map/ppermute | solution.py:360
  3.0 24.4 %collective-permute-start.4 = (bf16[16,8,2560]{2,1,0:T(8,128)(2,1)}, bf16[16,8,2560]{2,1,0:T(8,128)(2,1)}, u32[]{:S(2)}, u32[]{:S(2)}) collective-permute-start(bf16[16,8,2560]{2,1,0:T(8,128)(2,1)} %refs_10_), channel_id=1, source_target_pairs={{0,4},{2,6},{8,0},{10,2},{16,8},{18,10},{24,16},{26,18},{28,24},{3... | collective-permute-start | bytes 1966088 | tf_op jit(solution)/shard_map/ppermute | solution.py:360
  3.7 8.1 %copy-start.7 = (f32[2560]{0:T(1024)S(1)}, f32[2560]{0:T(1024)}, u32[]{:S(2)}) copy-start(f32[2560]{0:T(1024)} %param.15) | copy-start | bytes 30724
  13.9 5.3 %copy-start.1 = (bf16[16,8,2560]{2,1,0:T(8,128)(2,1)S(1)}, bf16[16,8,2560]{2,1,0:T(8,128)(2,1)}, u32[]{:S(2)}) copy-start(bf16[16,8,2560]{2,1,0:T(8,128)(2,1)} %refs_7_) | copy-start | bytes 1966084
  13.9 7.1 %copy-start.8 = (s32[64]{0:T(128)S(1)}, s32[64]{0:T(128)}, u32[]{:S(2)}) copy-start(s32[64]{0:T(128)} %param.21) | copy-start | bytes 772
  13.9 7.1 %copy-start.9 = (s32[64,1]{0,1:T(1,128)S(1)}, s32[64,1]{0,1:T(1,128)}, u32[]{:S(2)}) copy-start(s32[64,1]{0,1:T(1,128)} %param.20) | copy-start | bytes 772
  13.9 9.0 %copy-start.6 = (f32[2560]{0:T(1024)S(1)}, f32[2560]{0:T(1024)}, u32[]{:S(2)}) copy-start(f32[2560]{0:T(1024)} %param.14) | copy-start | bytes 30724
  17.0 10.9 %collective-permute-start.12 = (bf16[144,2560]{1,0:T(8,128)(2,1)}, bf16[144,2560]{1,0:T(8,128)(2,1)}, u32[]{:S(2)}, u32[]{:S(2)}) collective-permute-start(bf16[144,2560]{1,0:T(8,128)(2,1)} %fusion.8), channel_id=1, source_target_pairs={{0,2},{2,4},{4,6},{6,8},{8,10},{10,12},{12,14},{14,16},{16,18},{18... | collective-permute-start | bytes 2211848 | tf_op jit(solution)/shard_map/ppermute | solution.py:22
  19.2 17.1 %collective-permute-start = (bf16[16,8,2560]{2,1,0:T(8,128)(2,1)S(1)}, bf16[16,8,2560]{2,1,0:T(8,128)(2,1)}, u32[]{:S(2)}, u32[]{:S(2)}) collective-permute-start(bf16[16,8,2560]{2,1,0:T(8,128)(2,1)S(1)} %copy-done.1), channel_id=1, source_target_pairs={{0,8},{2,10},{8,16},{10,18},{16,24},{18,26},{24,28},{26,30},{28,20... | collective-permute-start | bytes 1966088 | tf_op jit(solution)/shard_map/ppermute | solution.py:360
  21.5 3.6 %collective-permute-start.14 = (s32[81]{0:T(128)S(1)}, s32[81]{0:T(128)S(1)}, u32[]{:S(2)}, u32[]{:S(2)}) collective-permute-start(s32[81]{0:T(128)S(1)} %pad_add_fusion.2), channel_id=1, source_target_pairs={{0,2},{2,0},{4,6},{6,4},{8,10},{10,8},{12,14},{14,12},{16,18},{18,... | collective-permute-start | bytes 980 | tf_op jit(solution)/shard_map/ppermute | solution.py:326
  22.9 6.9 %copy-start = (bf16[384,2560]{1,0:T(8,128)(2,1)S(1)}, bf16[384,2560]{1,0:T(8,128)(2,1)}, u32[]{:S(2)}) copy-start(bf16[384,2560]{1,0:T(8,128)(2,1)} %v_ref.1) | copy-start | bytes 5898244
  25.2 17.6 %collective-permute-start.8 = (bf16[16,8,2560]{2,1,0:T(8,128)(2,1)S(1)}, bf16[16,8,2560]{2,1,0:T(8,128)(2,1)S(1)}, u32[]{:S(2)}, u32[]{:S(2)}) collective-permute-start(bf16[16,8,2560]{2,1,0:T(8,128)(2,1)S(1)} %copy-done.1), channel_id=1, source_target_pairs={{0,4},{2,6},{8,0},{10,2},{16,8},{18,10},{24,16},{26,18},{28,24},{3... | collective-permute-start | bytes 1966088 | tf_op jit(solution)/shard_map/ppermute | solution.py:360
  25.8 24.1 %collective-permute-start.13 = (bf16[16,8,2560]{2,1,0:T(8,128)(2,1)S(1)}, bf16[16,8,2560]{2,1,0:T(8,128)(2,1)S(1)}, u32[]{:S(2)}, u32[]{:S(2)}) collective-permute-start(bf16[16,8,2560]{2,1,0:T(8,128)(2,1)S(1)} %collective-permute-done.11.refs_5_.refs_12_), channel_id=1, source_target_pairs={{0,8},{2,10},{8,16},{10,18},{16,24},{18,26},{24,28},{26,30},{28,20... | collective-permute-start | bytes 1966088 | tf_op jit(solution)/shard_map/ppermute | solution.py:360
  27.4 28.5 %collective-permute-start.5 = (bf16[16,8,2560]{2,1,0:T(8,128)(2,1)}, bf16[16,8,2560]{2,1,0:T(8,128)(2,1)S(1)}, u32[]{:S(2)}, u32[]{:S(2)}) collective-permute-start(bf16[16,8,2560]{2,1,0:T(8,128)(2,1)} %collective-permute-done.4.refs_4_.refs_11_), channel_id=1, source_target_pairs={{0,4},{2,6},{8,0},{10,2},{16,8},{18,10},{24,16},{26,18},{28,24},{3... | collective-permute-start | bytes 1966088 | tf_op jit(solution)/shard_map/ppermute | solution.py:360
  29.8 26.1 %copy-start.2 = (bf16[16,8,2560]{2,1,0:T(8,128)(2,1)S(1)}, bf16[16,8,2560]{2,1,0:T(8,128)(2,1)}, u32[]{:S(2)}) copy-start(bf16[16,8,2560]{2,1,0:T(8,128)(2,1)} %refs_10_) | copy-start | bytes 1966084
  42.8 24.6 %copy-start.4 = (bf16[64,2560]{1,0:T(8,128)(2,1)S(1)}, bf16[64,2560]{1,0:T(8,128)(2,1)}, u32[]{:S(2)}) copy-start(bf16[64,2560]{1,0:T(8,128)(2,1)} %get-tuple-element.111) | copy-start | bytes 983044
  42.8 24.6 %copy-start.5 = (bf16[64,2560]{1,0:T(8,128)(2,1)S(1)}, bf16[64,2560]{1,0:T(8,128)(2,1)}, u32[]{:S(2)}) copy-start(bf16[64,2560]{1,0:T(8,128)(2,1)} %get-tuple-element.130) | copy-start | bytes 983044
  58.9 8.6 %collective-permute-start.15 = (bf16[48,8,2560]{2,1,0:T(8,128)(2,1)S(1)}, bf16[48,8,2560]{2,1,0:T(8,128)(2,1)S(1)}, u32[]{:S(2)}, u32[]{:S(2)}) collective-permute-start(bf16[48,8,2560]{2,1,0:T(8,128)(2,1)S(1)} %pick_0.1), channel_id=1, source_target_pairs={{0,2},{2,0},{4,6},{6,4},{8,10},{10,8},{12,14},{14,12},{16,18},{18,... | collective-permute-start | bytes 5898248 | tf_op jit(solution)/shard_map/ppermute | solution.py:360
  63.3 17.8 %collective-permute-start.1 = (bf16[16,8,2560]{2,1,0:T(8,128)(2,1)}, bf16[16,8,2560]{2,1,0:T(8,128)(2,1)S(1)}, u32[]{:S(2)}, u32[]{:S(2)}) collective-permute-start(bf16[16,8,2560]{2,1,0:T(8,128)(2,1)} %collective-permute-done.refs_2_.refs_9_), channel_id=1, source_target_pairs={{0,8},{2,10},{8,16},{10,18},{16,24},{18,26},{24,28},{26,30},{28,20... | collective-permute-start | bytes 1966088 | tf_op jit(solution)/shard_map/ppermute | solution.py:360
  63.3 17.8 %collective-permute-start.9 = (bf16[16,8,2560]{2,1,0:T(8,128)(2,1)S(1)}, bf16[16,8,2560]{2,1,0:T(8,128)(2,1)S(1)}, u32[]{:S(2)}, u32[]{:S(2)}) collective-permute-start(bf16[16,8,2560]{2,1,0:T(8,128)(2,1)S(1)} %collective-permute-done.8.refs_1_.refs_8_), channel_id=1, source_target_pairs={{0,4},{2,6},{8,0},{10,2},{16,8},{18,10},{24,16},{26,18},{28,24},{3... | collective-permute-start | bytes 1966088 | tf_op jit(solution)/shard_map/ppermute | solution.py:360
  65.4 28.7 %collective-permute-start.6 = (bf16[16,8,2560]{2,1,0:T(8,128)(2,1)S(1)}, bf16[16,8,2560]{2,1,0:T(8,128)(2,1)S(1)}, u32[]{:S(2)}, u32[]{:S(2)}) collective-permute-start(bf16[16,8,2560]{2,1,0:T(8,128)(2,1)S(1)} %collective-permute-done.5.refs_2_.refs_12_), channel_id=1, source_target_pairs={{0,4},{2,6},{8,0},{10,2},{16,8},{18,10},{24,16},{26,18},{28,24},{3... | collective-permute-start | bytes 1966088 | tf_op jit(solution)/shard_map/ppermute | solution.py:360
  67.3 27.1 %collective-permute-start.16 = (bf16[16,8,2560]{2,1,0:T(8,128)(2,1)S(1)}, bf16[16,8,2560]{2,1,0:T(8,128)(2,1)S(1)}, u32[]{:S(2)}, u32[]{:S(2)}) collective-permute-start(bf16[16,8,2560]{2,1,0:T(8,128)(2,1)S(1)} %collective-permute-done.13.refs_3_.refs_13_), channel_id=1, source_target_pairs={{0,8},{2,10},{8,16},{10,18},{16,24},{18,26},{24,28},{26,30},{28,20... | collective-permute-start | bytes 1966088 | tf_op jit(solution)/shard_map/ppermute | solution.py:360
  96.9 21.2 %collective-permute-start.18 = (bf16[32,8,2560]{2,1,0:T(8,128)(2,1)S(1)}, bf16[32,8,2560]{2,1,0:T(8,128)(2,1)S(1)}, u32[]{:S(2)}, u32[]{:S(2)}) collective-permute-start(bf16[32,8,2560]{2,1,0:T(8,128)(2,1)S(1)} %pick_1.1), channel_id=1, source_target_pairs={{0,2},{2,0},{4,6},{6,4},{8,10},{10,8},{12,14},{14,12},{16,18},{18,... | collective-permute-start | bytes 3932168 | tf_op jit(solution)/shard_map/ppermute | solution.py:360
  97.0 18.9 %collective-permute-start.2 = (bf16[16,8,2560]{2,1,0:T(8,128)(2,1)S(1)}, bf16[16,8,2560]{2,1,0:T(8,128)(2,1)S(1)}, u32[]{:S(2)}, u32[]{:S(2)}) collective-permute-start(bf16[16,8,2560]{2,1,0:T(8,128)(2,1)S(1)} %collective-permute-done.1.refs_1_.refs_11_), channel_id=1, source_target_pairs={{0,8},{2,10},{8,16},{10,18},{16,24},{18,26},{24,28},{26,30},{28,20... | collective-permute-start | bytes 1966088 | tf_op jit(solution)/shard_map/ppermute | solution.py:360
  101.3 16.8 %collective-permute-start.10 = (bf16[16,8,2560]{2,1,0:T(8,128)(2,1)S(1)}, bf16[16,8,2560]{2,1,0:T(8,128)(2,1)S(1)}, u32[]{:S(2)}, u32[]{:S(2)}) collective-permute-start(bf16[16,8,2560]{2,1,0:T(8,128)(2,1)S(1)} %collective-permute-done.9.refs_0_.refs_10_), channel_id=1, source_target_pairs={{0,4},{2,6},{8,0},{10,2},{16,8},{18,10},{24,16},{26,18},{28,24},{3... | collective-permute-start | bytes 1966088 | tf_op jit(solution)/shard_map/ppermute | solution.py:360
  101.3 22.2 %collective-permute-start.17 = (bf16[144,2560]{1,0:T(8,128)(2,1)S(1)}, bf16[144,2560]{1,0:T(8,128)(2,1)S(1)}, u32[]{:S(2)}, u32[]{:S(2)}) collective-permute-start(bf16[144,2560]{1,0:T(8,128)(2,1)S(1)} %fusion.9), channel_id=1, source_target_pairs={{2,0},{4,2},{6,4},{8,6},{10,8},{12,10},{14,12},{16,14},{18,16},{20... | collective-permute-start | bytes 2211848 | tf_op jit(solution)/shard_map/ppermute | solution.py:22
  120.5 3.1 %collective-permute-start.19 = (bf16[32,8,2560]{2,1,0:T(8,128)(2,1)S(1)}, bf16[32,8,2560]{2,1,0:T(8,128)(2,1)S(1)}, u32[]{:S(2)}, u32[]{:S(2)}) collective-permute-start(bf16[32,8,2560]{2,1,0:T(8,128)(2,1)S(1)} %pick_2.1), channel_id=1, source_target_pairs={{0,2},{2,0},{4,6},{6,4},{8,10},{10,8},{12,14},{14,12},{16,18},{18,... | collective-permute-start | bytes 3932168 | tf_op jit(solution)/shard_map/ppermute | solution.py:360
  121.4 18.6 %collective-permute-start.7 = (bf16[16,8,2560]{2,1,0:T(8,128)(2,1)S(1)}, bf16[16,8,2560]{2,1,0:T(8,128)(2,1)S(1)}, u32[]{:S(2)}, u32[]{:S(2)}) collective-permute-start(bf16[16,8,2560]{2,1,0:T(8,128)(2,1)S(1)} %collective-permute-done.6.refs_2_.refs_17_), channel_id=1, source_target_pairs={{0,4},{2,6},{8,0},{10,2},{16,8},{18,10},{24,16},{26,18},{28,24},{3... | collective-permute-start | bytes 1966088 | tf_op jit(solution)/shard_map/ppermute | solution.py:360
  121.7 18.3 %collective-permute-start.3 = (bf16[16,8,2560]{2,1,0:T(8,128)(2,1)S(1)}, bf16[16,8,2560]{2,1,0:T(8,128)(2,1)S(1)}, u32[]{:S(2)}, u32[]{:S(2)}) collective-permute-start(bf16[16,8,2560]{2,1,0:T(8,128)(2,1)S(1)} %collective-permute-done.2.refs_1_.refs_16_), channel_id=1, source_target_pairs={{0,8},{2,10},{8,16},{10,18},{16,24},{18,26},{24,28},{26,30},{28,20... | collective-permute-start | bytes 1966088 | tf_op jit(solution)/shard_map/ppermute | solution.py:360
  141.5 2.2 %collective-permute-start.20 = (bf16[16,8,2560]{2,1,0:T(8,128)(2,1)S(1)}, bf16[16,8,2560]{2,1,0:T(8,128)(2,1)S(1)}, u32[]{:S(2)}, u32[]{:S(2)}) collective-permute-start(bf16[16,8,2560]{2,1,0:T(8,128)(2,1)S(1)} %pick_3.1), channel_id=1, source_target_pairs={{0,2},{2,0},{4,6},{6,4},{8,10},{10,8},{12,14},{14,12},{16,18},{18,... | collective-permute-start | bytes 1966088 | tf_op jit(solution)/shard_map/ppermute | solution.py:360

commit v8 on v7

--- a/solution.py
+++ b/solution.py
@@ -143,15 +143,15 @@
 
 def pick_kernel(groups, slots, first_ref, block_ref, *refs):
     key_pieces, value_pieces = refs[:groups], refs[groups : 2 * groups]
-    picked, sem = refs[2 * groups :]
+    picked_keys, picked_values, sems = refs[2 * groups :]
     start = first_ref[0]
 
     def fetch_from(g):
         def fetch(slot, carry):
             block = block_ref[slot]
             to = slot - start
-            pltpu.make_async_copy(key_pieces[g].at[block], picked.at[to], sem).start()
-            pltpu.make_async_copy(value_pieces[g].at[block], picked.at[slots + to], sem).start()
+            pltpu.make_async_copy(key_pieces[g].at[block], picked_keys.at[to], sems.at[0]).start()
+            pltpu.make_async_copy(value_pieces[g].at[block], picked_values.at[to], sems.at[1]).start()
             return carry
 
         return fetch
@@ -159,7 +159,8 @@
     for g in range(groups):
         lax.fori_loop(first_ref[g], first_ref[g + 1], fetch_from(g), 0)
     lax.fori_loop(first_ref[groups], start + slots, fetch_from(0), 0)
-    pltpu.make_async_copy(picked, picked, sem).wait()
+    pltpu.make_async_copy(picked_keys, picked_keys, sems.at[0]).wait()
+    pltpu.make_async_copy(picked_values, picked_values, sems.at[1]).wait()
 
 
 def pick_part(name, first, block, slots, key_pieces, value_pieces):
@@ -168,9 +169,9 @@
     return pl.pallas_call(
         functools.partial(pick_kernel, groups, slots),
         in_specs=[pl.BlockSpec(memory_space=pltpu.SMEM)] * 2 + [IN_HBM] * (2 * groups),
-        out_specs=IN_VMEM,
-        out_shape=jax.ShapeDtypeStruct((2 * slots, tokens, width), jnp.bfloat16),
-        scratch_shapes=[pltpu.SemaphoreType.DMA],
+        out_specs=[IN_VMEM] * 2,
+        out_shape=[jax.ShapeDtypeStruct((slots, tokens, width), jnp.bfloat16)] * 2,
+        scratch_shapes=[pltpu.SemaphoreType.DMA((2,))],
         compiler_params=pltpu.CompilerParams(vmem_limit_bytes=VMEM_BYTES),
         cost_estimate=pl.CostEstimate(flops=0, bytes_accessed=8 * slots * tokens * width, transcendentals=0),
         name=name,
@@ -184,7 +185,7 @@
         live_ref, refs = refs[0], refs[1:]
     if beside:
         (beside_bias, beside_keys, beside_values), refs = refs[:3], refs[3:]
-    *out_refs, keys, values, sems = refs[sum(2 * size + 1 for size in segments) :]
+    *out_refs, keys, values, sems = refs[sum(2 * (size + got) for size, got in segments) :]
     slots, tokens = keys.shape[:2]
     start = first_ref[0]
 
@@ -200,23 +201,24 @@
 
         return fetch
 
-    def fetch_received(received, base):
+    def fetch_received(received_keys, received_values, base):
         def fetch(slot, carry):
-            block = slot - base
-            fetch_one(received.at[block], received.at[received.shape[0] // 2 + block], slot - start)
+            fetch_one(received_keys.at[slot - base], received_values.at[slot - base], slot - start)
             return carry
 
         return fetch
 
-    at, pieces = 0, refs
-    for size in segments:
+    at, pieces, spare = 0, refs, None
+    for size, got in segments:
         for g in range(size):
-            lax.fori_loop(first_ref[at], first_ref[at + 1], fetch_from(pieces[g], pieces[size + g]), 0)
+            spare = (pieces[g], pieces[size + g])
+            lax.fori_loop(first_ref[at], first_ref[at + 1], fetch_from(*spare), 0)
             at += 1
-        lax.fori_loop(first_ref[at], first_ref[at + 1], fetch_received(pieces[2 * size], first_ref[at]), 0)
-        at += 1
-        pieces = pieces[2 * size + 1 :]
-    lax.fori_loop(first_ref[at], start + slots, fetch_from(refs[0], refs[segments[0]]), 0)
+        pieces = pieces[2 * size :]
+        if got:
+            lax.fori_loop(first_ref[at], first_ref[at + 1], fetch_received(pieces[0], pieces[1], first_ref[at]), 0)
+            at, pieces = at + 1, pieces[2:]
+    lax.fori_loop(first_ref[at], start + slots, fetch_from(*spare), 0)
     pltpu.make_async_copy(keys, keys, sems.at[0]).wait()
     pltpu.make_async_copy(values, values, sems.at[1]).wait()
 
@@ -244,7 +246,8 @@
 
 def far_part(name, first, block, slots, query, before, segments, live=None, beside=()):
     rows, width = query.shape
-    pieces = [array for segment in segments for array in segment]
+    pieces = [array for own, received in segments for array in (*own, *received)]
+    sizes = [(len(own) // 2, len(received) // 2) for own, received in segments]
     tokens = pieces[0].shape[1]
     seen = slots * tokens
     token = jnp.arange(seen, dtype=jnp.int32)[:, None]
@@ -254,7 +257,7 @@
     extra = ([] if live is None else [live]) + list(beside)
     final = jax.ShapeDtypeStruct((rows, width), jnp.bfloat16)
     return pl.pallas_call(
-        functools.partial(far_kernel, [len(segment) // 2 for segment in segments], live is not None, len(beside) > 0),
+        functools.partial(far_kernel, sizes, live is not None, len(beside) > 0),
         in_specs=[pl.BlockSpec(memory_space=pltpu.SMEM)] * 2
         + [IN_VMEM] * (5 + len(extra))
         + [IN_HBM] * len(pieces),
@@ -376,32 +379,38 @@
     values.append(moved(values[-2], down))
 
     most = 2 * request.shape[0] // count
-    segments, starts = [], []
+    segments, starts, slots = [], [], 0
     for stage, (first, stop) in enumerate(stages(half)):
         size = stop - first
+        limit = min(request.shape[0], size * most)
         (*pieces,), sums = after([*keys[first:stop], *values[first:stop]], sums)
-        if stage < 2:
-            *pieces, values[stop], values[stop + 1] = lax.optimization_barrier(
-                (*pieces, values[stop], values[stop + 1])
-            )
+        middle, end = 2 * first + size, 2 * stop
+        if stage == 1:
+            segments.append((pieces, ()))
+            bounds = jnp.concatenate([*starts, my_first[2 * first : middle + 1]])
+            slots = min(request.shape[0], slots + limit)
+            sums = far_part("far_1", bounds, my_block, slots, query_norm, sums, segments)
+            (*pieces,), sums = after(pieces, sums)
+            segments, starts, slots = [], [], 0
         if stage == 2:
-            *pieces, segments[0][-1] = lax.optimization_barrier((*pieces, segments[0][-1]))
-        theirs = their_first[2 * first + size : 2 * stop + 1]
-        limit = min(request.shape[0], size * most)
+            *pieces, late = lax.optimization_barrier((*pieces, segments[0][1][0]))
+            segments[0] = ((), [late, segments[0][1][1]])
+        theirs = their_first[middle : end + 1]
         picked = pick_part(f"pick_{stage}", theirs, their_block, limit, pieces[:size], pieces[size:])
-        received = moved(picked, swap)
+        received = [moved(array, swap) for array in picked]
         if stage == 0:
-            fronts, received = lax.optimization_barrier((fronts, received))
+            fronts, received[0] = lax.optimization_barrier((fronts, received[0]))
             seen, right_keys, right_values = arrived(passed_along(fronts, "tile", -1))
-        segments.append([*pieces, received])
-        starts.append(my_first[2 * first : 2 * first + size + 1])
-        if stage != 1:
-            bounds = jnp.concatenate([*starts, my_first[2 * stop :][:1]])
-            slots = min(request.shape[0], sum(len(segment) // 2 for segment in segments) * 2 * most)
-            final = live if first == 2 * half - 1 else None
+        segments.append((() if stage == 1 else pieces, received))
+        starts.append(my_first[middle if stage == 1 else 2 * first : middle + 1])
+        slots += limit if stage == 1 else 2 * limit
+        if stage > 1:
+            bounds = jnp.concatenate([*starts, my_first[end:][:1]])
+            slots = min(request.shape[0], slots)
+            final = live if stage == 3 else None
             beside = (spread(seen), right_keys, right_values) if stage == 2 else ()
             sums = far_part(f"far_{stage}", bounds, my_block, slots, query_norm, sums, segments, final, beside)
-            segments, starts = [], []
+            segments, starts, slots = [], [], 0
     return sums
 
 

time: 153 us -> 138 us (0.902); the launches traced: 151 us -> 138 us
  waiting for transfers between devices: 50.8 us -> 30.9 us
  starting transfers between devices: 24.7 us -> 34.7 us
  other arithmetic: 10.3 us -> 7.9 us
  local copies, waits for them, and re-layouts: 4.91 us -> 3.15 us
    ppermute x18 -> x22, waiting for transfers between devices: 50.8 us -> 30.9 us  [moved(): return lax.ppermute(piece, 'tile', pairs)]
    ppermute x18 -> x22, starting transfers between devices: 19.9 us -> 31.6 us  [moved(): return lax.ppermute(piece, 'tile', pairs)]
    convert_element_type x2, other arithmetic: 4.26 us -> 2.59 us  [normalize(): return (rows32 * factor[:, None] * gain).astype(jnp.bfloat16)]
  transfers between devices with their start and end apart: 21 -> 25, of which waited for: 11 -> 9; matrix products, arithmetic and copies ran while one was open for 10% -> 8% of each run, Pallas kernels for 24% -> 31%
where the time goes in v8:
time: 138 us
  Pallas kernels  50.7 us (37%)
  starting transfers between devices  34.7 us (25%)
  waiting for transfers between devices  30.9 us (22%)
  other arithmetic  7.9 us (6%)
  between operations  5.61 us (4%)
  blocking collectives  4.94 us (4%)
  local copies, waits for them, and re-layouts  3.15 us (2%)
    pallas_call x3, Pallas kernels, far_part(): pl.pallas_call(functools.partial(far_kernel, sizes, live is not None, len...  34.9 us
    ppermute x22, starting transfers between devices, moved(): return lax.ppermute(piece, 'tile', pairs)  31.6 us
    ppermute x22, waiting for transfers between devices, moved(): return lax.ppermute(piece, 'tile', pairs)  30.9 us
    pallas_call x4, Pallas kernels, pick_part(): pl.pallas_call(functools.partial(pick_kernel, groups, slots), in_specs=[p...  9.6 us
    pallas_call x1, Pallas kernels, near_part(): pl.pallas_call(near_kernel, in_specs=[IN_VMEM] * 6, out_specs=[IN_VMEM] *...  6.25 us
    psum x1, blocking collectives, per_device(): lax.psum((row_squares(query_rows), row_squares(key_rows)), 'head')  4.94 us
    ppermute x2, starting transfers between devices, passed_along(): lax.ppermute(value, axis, [(source, source + steps) for source in range(f...  3.04 us
  transfers between devices with their start and end apart: 25, of which 9 were waited for; matrix products, arithmetic and copies ran while one was open for 8% of the time, Pallas kernels for 31%

profile of v8, /device:TPU:0, one launch (start us, length us, event | category | flops | bytes accessed | tf_op | source)
XLA Modules:
  0.0 137.9 jit_solution(9411668896467997764)
XLA Ops:
  0.0 3.0 %collective-permute-start.11 = (bf16[16,8,2560]{2,1,0:T(8,128)(2,1)}, bf16[16,8,2560]{2,1,0:T(8,128)(2,1)S(1)}, u32[]{:S(2)}, u32[]{:S(2)}) collective-permute-start(bf16[16,8,2560]{2,1,0:T(8,128)(2,1)} %refs_10_), channel_id=1, source_target_pairs={{0,8},{2,10},{8,16},{10,18},{16,24},{18,26},{24,28},{26,30},{28,20... | collective-permute-start | bytes 1966088 | tf_op jit(solution)/shard_map/ppermute | solution.py:363
  4.9 2.0 %fusion = f32[384]{0:T(512)S(1)} fusion(bf16[384,2560]{1,0:T(8,128)(2,1)} %param.11), kind=kLoop, calls=%fused_computation.4 | loop fusion | flops 2948736 | bytes 1967616 | tf_op jit(solution)/shard_map/reduce_sum | solution.py:27
  7.4 4.9 %all-reduce.10 = (f32[384]{0:T(512)S(1)}, f32[384]{0:T(512)S(1)}) all-reduce(f32[384]{0:T(512)S(1)} %fusion, f32[384]{0:T(512)S(1)} %fusion.3), channel_id=1, replica_groups=mesh['tile'=16,'head'=2] {'head'}, use_global_device_ids=true, to_apply=%region_4.5 | all-reduce | flops 768 | bytes 6144 | tf_op jit(solution)/shard_map/psum | solution.py:333
  13.0 2.1 %fusion.5.k_ref = bf16[384,2560]{1,0:T(8,128)(2,1)S(1)} fusion(bf16[384,2560]{1,0:T(8,128)(2,1)} %param.12, f32[2560]{0:T(1024)S(1)} %copy-done.6, f32[384]{0:T(512)S(1)} %add_rsqrt_fusion), kind=kLoop, calls=%fused_computation.9 | loop fusion | flops 3932160 | bytes 3943936 | tf_op jit(solution)/shard_map/convert_element_type | solution.py:33
  15.1 1.5 %fusion.23 = (bf16[64,2560]{1,0:T(8,128)(2,1)S(1)}, bf16[64,2560]{1,0:T(8,128)(2,1)S(1)}, bf16[64,2560]{1,0:T(8,128)(2,1)S(1)}, bf16[64,2560]{1,0:T(8,128)(2,1)S(1)}) fusion(bf16[384,2560]{1,0:T(8,128)(2,1)S(1)} %fusion.5.k_ref, s32[]{:T(128)S(6)} %select_n.170, bf16[384,2560]{1,0:T(8,128)(2,1)} %v_ref.1), kind=kLoop, calls=%fused_computation.79 | loop fusion | bytes 5898244 | tf_op jit(solution)/shard_map/slice | solution.py:350
  16.7 1.7 %collective-permute-start.14 = (bf16[144,2560]{1,0:T(8,128)(2,1)S(1)}, bf16[144,2560]{1,0:T(8,128)(2,1)S(1)}, u32[]{:S(2)}, u32[]{:S(2)}) collective-permute-start(bf16[144,2560]{1,0:T(8,128)(2,1)S(1)} %fusion.8), channel_id=1, source_target_pairs={{0,2},{2,4},{4,6},{6,8},{8,10},{10,12},{12,14},{14,16},{16,18},{18... | collective-permute-start | bytes 2211848 | tf_op jit(solution)/shard_map/ppermute | solution.py:22
  18.5 2.2 %collective-permute-start = (bf16[16,8,2560]{2,1,0:T(8,128)(2,1)S(1)}, bf16[16,8,2560]{2,1,0:T(8,128)(2,1)S(1)}, u32[]{:S(2)}, u32[]{:S(2)}) collective-permute-start(bf16[16,8,2560]{2,1,0:T(8,128)(2,1)S(1)} %copy-done.1), channel_id=1, source_target_pairs={{0,8},{2,10},{8,16},{10,18},{16,24},{18,26},{24,28},{26,30},{28,20... | collective-permute-start | bytes 1966088 | tf_op jit(solution)/shard_map/ppermute | solution.py:363
  23.5 2.0 %collective-permute-start.12 = (bf16[16,8,2560]{2,1,0:T(8,128)(2,1)S(1)}, bf16[16,8,2560]{2,1,0:T(8,128)(2,1)S(1)}, u32[]{:S(2)}, u32[]{:S(2)}) collective-permute-start(bf16[16,8,2560]{2,1,0:T(8,128)(2,1)S(1)} %collective-permute-done.11.refs_5_.refs_12_), channel_id=1, source_target_pairs={{0,8},{2,10},{8,16},{10,18},{16,24},{18,26},{24,28},{26,30},{28,20... | collective-permute-start | bytes 1966088 | tf_op jit(solution)/shard_map/ppermute | solution.py:363
  25.8 6.2 %near_part.1 = (f32[20,8,384]{2,1,0:T(8,128)S(1)}, f32[20,8,384]{2,1,0:T(8,128)S(1)}, f32[2560,384]{1,0:T(8,128)S(1)}) custom-call(f32[448,128]{1,0:T(8,128)S(1)} %broadcast_in_dim.130.bias_ref, bf16[384,2560]{1,0:T(8,128)(2,1)S(1)} %fusion.2.q_ref.refs_3_, bf16[384,2560]{1,0:T(8,128)(2,1)S(1)} %fusion.5.k_ref, bf16[384,2560]{1,0:T(8,128)(2,1)S(1)} %copy-done, ...), custom_call_target="tpu_custom_call" | custom-call | flops 1761607680 | bytes 9830400 | tf_op jit(solution)/shard_map/near_part/pallas_call | solution.py:133
  32.0 3.3 %collective-permute-done.refs_2_.refs_9_ = bf16[16,8,2560]{2,1,0:T(8,128)(2,1)S(1)} collective-permute-done((bf16[16,8,2560]{2,1,0:T(8,128)(2,1)S(1)}, bf16[16,8,2560]{2,1,0:T(8,128)(2,1)S(1)}, u32[]{:S(2)}, u32[]{:S(2)}) %collective-permute-start) | collective-permute-done | bytes 655392 | tf_op jit(solution)/shard_map/ppermute | solution.py:363
  35.3 5.3 %collective-permute-done.8.refs_1_.refs_8_ = bf16[16,8,2560]{2,1,0:T(8,128)(2,1)S(1)} collective-permute-done((bf16[16,8,2560]{2,1,0:T(8,128)(2,1)S(1)}, bf16[16,8,2560]{2,1,0:T(8,128)(2,1)S(1)}, u32[]{:S(2)}, u32[]{:S(2)}) %collective-permute-start.8) | collective-permute-done | bytes 655392 | tf_op jit(solution)/shard_map/ppermute | solution.py:363
  40.6 3.3 %pick_0.1 = (bf16[24,8,2560]{2,1,0:T(8,128)(2,1)S(1)}, bf16[24,8,2560]{2,1,0:T(8,128)(2,1)S(1)}) custom-call(s32[4]{0:T(128)S(1)} %slice.86.first_ref, s32[88]{0:T(128)S(1)} %concatenate.62.block_ref, bf16[16,8,2560]{2,1,0:T(8,128)(2,1)S(1)} %copy-done.1, bf16[16,8,2560]{2,1,0:T(8,128)(2,1)S(1)} %collective-permute-done.8.refs_1_.refs_8_, ...), custom_call_target="tpu_custom_call" | custom-call | bytes 3932160 | tf_op jit(solution)/shard_map/pick_0/pallas_call | solution.py:169
  43.9 7.0 %collective-permute-start.16 = (bf16[24,8,2560]{2,1,0:T(8,128)(2,1)S(1)}, bf16[24,8,2560]{2,1,0:T(8,128)(2,1)S(1)}, u32[]{:S(2)}, u32[]{:S(2)}) collective-permute-start(bf16[24,8,2560]{2,1,0:T(8,128)(2,1)S(1)} %get-tuple-element.71), channel_id=1, source_target_pairs={{0,2},{2,0},{4,6},{6,4},{8,10},{10,8},{12,14},{14,12},{16,18},{18,... | collective-permute-start | bytes 2949128 | tf_op jit(solution)/shard_map/ppermute | solution.py:363
  51.1 2.5 %collective-permute-start.9 = (bf16[16,8,2560]{2,1,0:T(8,128)(2,1)S(1)}, bf16[16,8,2560]{2,1,0:T(8,128)(2,1)S(1)}, u32[]{:S(2)}, u32[]{:S(2)}) collective-permute-start(bf16[16,8,2560]{2,1,0:T(8,128)(2,1)S(1)} %collective-permute-done.8.refs_1_.refs_8_), channel_id=1, source_target_pairs={{0,4},{2,6},{8,0},{10,2},{16,8},{18,10},{24,16},{26,18},{28,24},{3... | collective-permute-start | bytes 1966088 | tf_op jit(solution)/shard_map/ppermute | solution.py:363
  54.6 1.0 collective-permute-start.6
  55.8 13.1 %collective-permute-done.1.refs_16_.refs_1_ = bf16[16,8,2560]{2,1,0:T(8,128)(2,1)S(1)} collective-permute-done((bf16[16,8,2560]{2,1,0:T(8,128)(2,1)S(1)}, bf16[16,8,2560]{2,1,0:T(8,128)(2,1)S(1)}, u32[]{:S(2)}, u32[]{:S(2)}) %collective-permute-start.1) | collective-permute-done | bytes 655392 | tf_op jit(solution)/shard_map/ppermute | solution.py:363
  68.9 5.0 %collective-permute-start.13 = (bf16[16,8,2560]{2,1,0:T(8,128)(2,1)S(1)}, bf16[16,8,2560]{2,1,0:T(8,128)(2,1)S(1)}, u32[]{:S(2)}, u32[]{:S(2)}) collective-permute-start(bf16[16,8,2560]{2,1,0:T(8,128)(2,1)S(1)} %collective-permute-done.12.refs_18_.refs_3_), channel_id=1, source_target_pairs={{0,8},{2,10},{8,16},{10,18},{16,24},{18,26},{24,28},{26,30},{28,20... | collective-permute-start | bytes 1966088 | tf_op jit(solution)/shard_map/ppermute | solution.py:363
  73.9 2.3 %collective-permute-start.2 = (bf16[16,8,2560]{2,1,0:T(8,128)(2,1)S(1)}, bf16[16,8,2560]{2,1,0:T(8,128)(2,1)S(1)}, u32[]{:S(2)}, u32[]{:S(2)}) collective-permute-start(bf16[16,8,2560]{2,1,0:T(8,128)(2,1)S(1)} %collective-permute-done.1.refs_16_.refs_1_), channel_id=1, source_target_pairs={{0,8},{2,10},{8,16},{10,18},{16,24},{18,26},{24,28},{26,30},{28,20... | collective-permute-start | bytes 1966088 | tf_op jit(solution)/shard_map/ppermute | solution.py:363
  76.2 1.3 collective-permute-start.18
  77.6 15.2 %far_1.1 = (f32[20,8,384]{2,1,0:T(8,128)S(1)}, f32[20,8,384]{2,1,0:T(8,128)S(1)}, f32[2560,384]{1,0:T(8,128)S(1)}) custom-call(s32[7]{0:T(128)S(1)} %pad_add_fusion.1.refs_0_, s32[128]{0:T(128)S(1)} %concatenate.59.refs_1_, f32[512,128]{1,0:T(8,128)S(1)} %broadcast_in_dim.133.refs_2_, ...), custom_call_target="tpu_custom_call", output_to_operand_aliasing={{0}: (4, {}), {1}: (5, {}), {2}: (6, {})} | custom-call | flops 2013265920 | bytes 9830400 | tf_op jit(solution)/shard_map/far_1/pallas_call | solution.py:259
  92.8 2.4 %pick_1.1 = (bf16[16,8,2560]{2,1,0:T(8,128)(2,1)S(1)}, bf16[16,8,2560]{2,1,0:T(8,128)(2,1)S(1)}) custom-call(s32[3]{0:T(128)S(1)} %get-tuple-element.119.first_ref, s32[80]{0:T(128)S(1)} %concatenate.63.block_ref, bf16[16,8,2560]{2,1,0:T(8,128)(2,1)S(1)} %collective-permute-done.9.refs_15_.refs_0_, ...), custom_call_target="tpu_custom_call" | custom-call | bytes 2621440 | tf_op jit(solution)/shard_map/pick_1/pallas_call | solution.py:169
  95.2 1.2 collective-permute-start.19
  97.7 1.4 %pad_add_fusion.refs_0_ = s32[5]{0:T(128)S(1)} fusion(s32[1]{0:T(128)} %get-tuple-element.122, s32[3]{0:T(128)S(1)} %get-tuple-element.125, s32[1]{0:T(128)} %get-tuple-element.121), kind=kLoop, calls=%fused_computation.73 | loop fusion | flops 10 | bytes 40 | tf_op jit(solution)/shard_map/concatenate | solution.py:408
  99.3 2.7 %collective-permute-done.2.refs_1_.refs_13_ = bf16[16,8,2560]{2,1,0:T(8,128)(2,1)S(1)} collective-permute-done((bf16[16,8,2560]{2,1,0:T(8,128)(2,1)S(1)}, bf16[16,8,2560]{2,1,0:T(8,128)(2,1)S(1)}, u32[]{:S(2)}, u32[]{:S(2)}) %collective-permute-start.2) | collective-permute-done | bytes 655392 | tf_op jit(solution)/shard_map/ppermute | solution.py:363
  101.9 2.8 %collective-permute-done.10.refs_0_.refs_12_ = bf16[16,8,2560]{2,1,0:T(8,128)(2,1)S(1)} collective-permute-done((bf16[16,8,2560]{2,1,0:T(8,128)(2,1)S(1)}, bf16[16,8,2560]{2,1,0:T(8,128)(2,1)S(1)}, u32[]{:S(2)}, u32[]{:S(2)}) %collective-permute-start.10) | collective-permute-done | bytes 655392 | tf_op jit(solution)/shard_map/ppermute | solution.py:363
  104.7 2.6 %collective-permute-start.7 = (bf16[16,8,2560]{2,1,0:T(8,128)(2,1)S(1)}, bf16[16,8,2560]{2,1,0:T(8,128)(2,1)S(1)}, u32[]{:S(2)}, u32[]{:S(2)}) collective-permute-start(bf16[16,8,2560]{2,1,0:T(8,128)(2,1)S(1)} %collective-permute-done.6.refs_2_.refs_14_), channel_id=1, source_target_pairs={{0,4},{2,6},{8,0},{10,2},{16,8},{18,10},{24,16},{26,18},{28,24},{3... | collective-permute-start | bytes 1966088 | tf_op jit(solution)/shard_map/ppermute | solution.py:363
  107.3 2.4 %pick_2.1 = (bf16[16,8,2560]{2,1,0:T(8,128)(2,1)S(1)}, bf16[16,8,2560]{2,1,0:T(8,128)(2,1)S(1)}) custom-call(s32[3]{0:T(128)S(1)} %get-tuple-element.118.first_ref, s32[80]{0:T(128)S(1)} %concatenate.63.block_ref, bf16[16,8,2560]{2,1,0:T(8,128)(2,1)S(1)} %collective-permute-done.10.refs_0_.refs_12_, ...), custom_call_target="tpu_custom_call" | custom-call | bytes 2621440 | tf_op jit(solution)/shard_map/pick_2/pallas_call | solution.py:169
  109.7 1.8 %collective-permute-start.21 = (bf16[16,8,2560]{2,1,0:T(8,128)(2,1)S(1)}, bf16[16,8,2560]{2,1,0:T(8,128)(2,1)S(1)}, u32[]{:S(2)}, u32[]{:S(2)}) collective-permute-start(bf16[16,8,2560]{2,1,0:T(8,128)(2,1)S(1)} %get-tuple-element.95), channel_id=1, source_target_pairs={{0,2},{2,0},{4,6},{6,4},{8,10},{10,8},{12,14},{14,12},{16,18},{18,... | collective-permute-start | bytes 1966088 | tf_op jit(solution)/shard_map/ppermute | solution.py:363
  111.7 1.6 %collective-permute-done.21.refs_16_ = bf16[16,8,2560]{2,1,0:T(8,128)(2,1)S(1)} collective-permute-done((bf16[16,8,2560]{2,1,0:T(8,128)(2,1)S(1)}, bf16[16,8,2560]{2,1,0:T(8,128)(2,1)S(1)}, u32[]{:S(2)}, u32[]{:S(2)}) %collective-permute-start.21) | collective-permute-done | bytes 655392 | tf_op jit(solution)/shard_map/ppermute | solution.py:363
  114.4 12.9 %far_2.1 = (f32[20,8,384]{2,1,0:T(8,128)S(1)}, f32[20,8,384]{2,1,0:T(8,128)S(1)}, f32[2560,384]{1,0:T(8,128)S(1)}) custom-call(s32[5]{0:T(128)S(1)} %pad_add_fusion.refs_0_, s32[112]{0:T(128)S(1)} %concatenate.53.refs_1_, f32[384,128]{1,0:T(8,128)S(1)} %broadcast_in_dim.125.refs_2_, ...), custom_call_target="tpu_custom_call", output_to_operand_aliasing={{0}: (4, {}), {1}: (5, {}), {2}: (6, {})} | custom-call | flops 1509949440 | bytes 9830400 | tf_op jit(solution)/shard_map/far_2/pallas_call | solution.py:259
  127.3 1.5 %pick_3.1 = (bf16[8,8,2560]{2,1,0:T(8,128)(2,1)S(1)}, bf16[8,8,2560]{2,1,0:T(8,128)(2,1)S(1)}) custom-call(s32[2]{0:T(128)S(1)} %slice.93.first_ref, s32[72]{0:T(128)S(1)} %concatenate.64.block_ref, bf16[16,8,2560]{2,1,0:T(8,128)(2,1)S(1)} %collective-permute-done.3.refs_0_.refs_8_, bf16[16,8,2560]{2,1,0:T(8,128)(2,1)S(1)} %collective-permute-done.7.refs_1_.refs_9_), custom_call_target="tpu_custom_call" | custom-call | bytes 1310720 | tf_op jit(solution)/shard_map/pick_3/pallas_call | solution.py:169
  131.0 6.8 %far_3.1 = bf16[384,2560]{1,0:T(8,128)(2,1)} custom-call(s32[3]{0:T(128)S(1)} %get-tuple-element.126.refs_0_, s32[80]{0:T(128)S(1)} %concatenate.51.refs_1_, f32[128,128]{1,0:T(8,128)S(1)} %broadcast_in_dim.122.refs_2_, bf16[384,2560]{1,0:T(8,128)(2,1)S(1)} %fusion.2.q_ref.refs_3_, f32[20,8,384]{2,1,0:T(8,128)S(1)} %get-tuple-element.98.refs_4_, ...), custom_call_target="tpu_custom_call" | custom-call | flops 503316480 | bytes 9830400 | tf_op jit(solution)/shard_map/far_3/pallas_call | solution.py:259
  (87 shorter events, 7.2 us)
Async XLA Ops:
  0.0 6.9 %copy-start.3 = (bf16[384,2560]{1,0:T(8,128)(2,1)S(1)}, bf16[384,2560]{1,0:T(8,128)(2,1)}, u32[]{:S(2)}) copy-start(bf16[384,2560]{1,0:T(8,128)(2,1)} %param.12) | copy-start | bytes 5898244
  0.0 23.5 %collective-permute-start.11 = (bf16[16,8,2560]{2,1,0:T(8,128)(2,1)}, bf16[16,8,2560]{2,1,0:T(8,128)(2,1)S(1)}, u32[]{:S(2)}, u32[]{:S(2)}) collective-permute-start(bf16[16,8,2560]{2,1,0:T(8,128)(2,1)} %refs_10_), channel_id=1, source_target_pairs={{0,8},{2,10},{8,16},{10,18},{16,24},{18,26},{24,28},{26,30},{28,20... | collective-permute-start | bytes 1966088 | tf_op jit(solution)/shard_map/ppermute | solution.py:363
  3.0 22.5 %collective-permute-start.4 = (bf16[16,8,2560]{2,1,0:T(8,128)(2,1)}, bf16[16,8,2560]{2,1,0:T(8,128)(2,1)S(1)}, u32[]{:S(2)}, u32[]{:S(2)}) collective-permute-start(bf16[16,8,2560]{2,1,0:T(8,128)(2,1)} %refs_10_), channel_id=1, source_target_pairs={{0,4},{2,6},{8,0},{10,2},{16,8},{18,10},{24,16},{26,18},{28,24},{3... | collective-permute-start | bytes 1966088 | tf_op jit(solution)/shard_map/ppermute | solution.py:363
  4.2 19.0 %collective-permute-start.15 = (s32[81]{0:T(128)S(1)}, s32[81]{0:T(128)S(1)}, u32[]{:S(2)}, u32[]{:S(2)}) collective-permute-start(s32[81]{0:T(128)S(1)} %pad_add_fusion.2), channel_id=1, source_target_pairs={{0,2},{2,0},{4,6},{6,4},{8,10},{10,8},{12,14},{14,12},{16,18},{18,... | collective-permute-start | bytes 980 | tf_op jit(solution)/shard_map/ppermute | solution.py:329
  4.9 8.1 %copy-start.6 = (f32[2560]{0:T(1024)S(1)}, f32[2560]{0:T(1024)}, u32[]{:S(2)}) copy-start(f32[2560]{0:T(1024)} %param.15) | copy-start | bytes 30724
  15.1 3.3 %copy-start.1 = (bf16[16,8,2560]{2,1,0:T(8,128)(2,1)S(1)}, bf16[16,8,2560]{2,1,0:T(8,128)(2,1)}, u32[]{:S(2)}) copy-start(bf16[16,8,2560]{2,1,0:T(8,128)(2,1)} %refs_7_) | copy-start | bytes 1966084
  15.1 6.3 %copy-start.5 = (f32[2560]{0:T(1024)S(1)}, f32[2560]{0:T(1024)}, u32[]{:S(2)}) copy-start(f32[2560]{0:T(1024)} %param.14) | copy-start | bytes 30724
  15.1 7.6 %copy-start.4 = (bf16[384,2560]{1,0:T(8,128)(2,1)S(1)}, bf16[384,2560]{1,0:T(8,128)(2,1)}, u32[]{:S(2)}) copy-start(bf16[384,2560]{1,0:T(8,128)(2,1)} %param.11) | copy-start | bytes 5898244
  16.7 8.8 %collective-permute-start.14 = (bf16[144,2560]{1,0:T(8,128)(2,1)S(1)}, bf16[144,2560]{1,0:T(8,128)(2,1)S(1)}, u32[]{:S(2)}, u32[]{:S(2)}) collective-permute-start(bf16[144,2560]{1,0:T(8,128)(2,1)S(1)} %fusion.8), channel_id=1, source_target_pairs={{0,2},{2,4},{4,6},{6,8},{8,10},{10,12},{12,14},{14,16},{16,18},{18... | collective-permute-start | bytes 2211848 | tf_op jit(solution)/shard_map/ppermute | solution.py:22
  18.5 16.8 %collective-permute-start = (bf16[16,8,2560]{2,1,0:T(8,128)(2,1)S(1)}, bf16[16,8,2560]{2,1,0:T(8,128)(2,1)S(1)}, u32[]{:S(2)}, u32[]{:S(2)}) collective-permute-start(bf16[16,8,2560]{2,1,0:T(8,128)(2,1)S(1)} %copy-done.1), channel_id=1, source_target_pairs={{0,8},{2,10},{8,16},{10,18},{16,24},{18,26},{24,28},{26,30},{28,20... | collective-permute-start | bytes 1966088 | tf_op jit(solution)/shard_map/ppermute | solution.py:363
  22.7 3.0 %copy-start = (bf16[384,2560]{1,0:T(8,128)(2,1)S(1)}, bf16[384,2560]{1,0:T(8,128)(2,1)}, u32[]{:S(2)}) copy-start(bf16[384,2560]{1,0:T(8,128)(2,1)} %v_ref.1) | copy-start | bytes 5898244
  23.3 17.3 %collective-permute-start.8 = (bf16[16,8,2560]{2,1,0:T(8,128)(2,1)S(1)}, bf16[16,8,2560]{2,1,0:T(8,128)(2,1)S(1)}, u32[]{:S(2)}, u32[]{:S(2)}) collective-permute-start(bf16[16,8,2560]{2,1,0:T(8,128)(2,1)S(1)} %copy-done.1), channel_id=1, source_target_pairs={{0,4},{2,6},{8,0},{10,2},{16,8},{18,10},{24,16},{26,18},{28,24},{3... | collective-permute-start | bytes 1966088 | tf_op jit(solution)/shard_map/ppermute | solution.py:363
  23.5 27.6 %collective-permute-start.12 = (bf16[16,8,2560]{2,1,0:T(8,128)(2,1)S(1)}, bf16[16,8,2560]{2,1,0:T(8,128)(2,1)S(1)}, u32[]{:S(2)}, u32[]{:S(2)}) collective-permute-start(bf16[16,8,2560]{2,1,0:T(8,128)(2,1)S(1)} %collective-permute-done.11.refs_5_.refs_12_), channel_id=1, source_target_pairs={{0,8},{2,10},{8,16},{10,18},{16,24},{18,26},{24,28},{26,30},{28,20... | collective-permute-start | bytes 1966088 | tf_op jit(solution)/shard_map/ppermute | solution.py:363
  25.5 29.1 %collective-permute-start.5 = (bf16[16,8,2560]{2,1,0:T(8,128)(2,1)S(1)}, bf16[16,8,2560]{2,1,0:T(8,128)(2,1)S(1)}, u32[]{:S(2)}, u32[]{:S(2)}) collective-permute-start(bf16[16,8,2560]{2,1,0:T(8,128)(2,1)S(1)} %collective-permute-done.4.refs_4_.refs_11_), channel_id=1, source_target_pairs={{0,4},{2,6},{8,0},{10,2},{16,8},{18,10},{24,16},{26,18},{28,24},{3... | collective-permute-start | bytes 1966088 | tf_op jit(solution)/shard_map/ppermute | solution.py:363
  25.7 14.9 %copy-start.2 = (bf16[16,8,2560]{2,1,0:T(8,128)(2,1)S(1)}, bf16[16,8,2560]{2,1,0:T(8,128)(2,1)}, u32[]{:S(2)}) copy-start(bf16[16,8,2560]{2,1,0:T(8,128)(2,1)} %refs_10_) | copy-start | bytes 1966084
  43.9 32.2 %collective-permute-start.16 = (bf16[24,8,2560]{2,1,0:T(8,128)(2,1)S(1)}, bf16[24,8,2560]{2,1,0:T(8,128)(2,1)S(1)}, u32[]{:S(2)}, u32[]{:S(2)}) collective-permute-start(bf16[24,8,2560]{2,1,0:T(8,128)(2,1)S(1)} %get-tuple-element.71), channel_id=1, source_target_pairs={{0,2},{2,0},{4,6},{6,4},{8,10},{10,8},{12,14},{14,12},{16,18},{18,... | collective-permute-start | bytes 2949128 | tf_op jit(solution)/shard_map/ppermute | solution.py:363
  50.9 25.2 %collective-permute-start.17 = (bf16[24,8,2560]{2,1,0:T(8,128)(2,1)S(1)}, bf16[24,8,2560]{2,1,0:T(8,128)(2,1)S(1)}, u32[]{:S(2)}, u32[]{:S(2)}) collective-permute-start(bf16[24,8,2560]{2,1,0:T(8,128)(2,1)S(1)} %get-tuple-element.73), channel_id=1, source_target_pairs={{0,2},{2,0},{4,6},{6,4},{8,10},{10,8},{12,14},{14,12},{16,18},{18,... | collective-permute-start | bytes 2949128 | tf_op jit(solution)/shard_map/ppermute | solution.py:363
  51.1 17.8 %collective-permute-start.1 = (bf16[16,8,2560]{2,1,0:T(8,128)(2,1)S(1)}, bf16[16,8,2560]{2,1,0:T(8,128)(2,1)S(1)}, u32[]{:S(2)}, u32[]{:S(2)}) collective-permute-start(bf16[16,8,2560]{2,1,0:T(8,128)(2,1)S(1)} %collective-permute-done.refs_2_.refs_9_), channel_id=1, source_target_pairs={{0,8},{2,10},{8,16},{10,18},{16,24},{18,26},{24,28},{26,30},{28,20... | collective-permute-start | bytes 1966088 | tf_op jit(solution)/shard_map/ppermute | solution.py:363
  51.1 17.8 %collective-permute-start.9 = (bf16[16,8,2560]{2,1,0:T(8,128)(2,1)S(1)}, bf16[16,8,2560]{2,1,0:T(8,128)(2,1)S(1)}, u32[]{:S(2)}, u32[]{:S(2)}) collective-permute-start(bf16[16,8,2560]{2,1,0:T(8,128)(2,1)S(1)} %collective-permute-done.8.refs_1_.refs_8_), channel_id=1, source_target_pairs={{0,4},{2,6},{8,0},{10,2},{16,8},{18,10},{24,16},{26,18},{28,24},{3... | collective-permute-start | bytes 1966088 | tf_op jit(solution)/shard_map/ppermute | solution.py:363
  54.6 40.6 %collective-permute-start.6 = (bf16[16,8,2560]{2,1,0:T(8,128)(2,1)S(1)}, bf16[16,8,2560]{2,1,0:T(8,128)(2,1)S(1)}, u32[]{:S(2)}, u32[]{:S(2)}) collective-permute-start(bf16[16,8,2560]{2,1,0:T(8,128)(2,1)S(1)} %collective-permute-done.5.refs_17_.refs_2_), channel_id=1, source_target_pairs={{0,4},{2,6},{8,0},{10,2},{16,8},{18,10},{24,16},{26,18},{28,24},{3... | collective-permute-start | bytes 1966088 | tf_op jit(solution)/shard_map/ppermute | solution.py:363
  68.9 30.3 %collective-permute-start.13 = (bf16[16,8,2560]{2,1,0:T(8,128)(2,1)S(1)}, bf16[16,8,2560]{2,1,0:T(8,128)(2,1)S(1)}, u32[]{:S(2)}, u32[]{:S(2)}) collective-permute-start(bf16[16,8,2560]{2,1,0:T(8,128)(2,1)S(1)} %collective-permute-done.12.refs_18_.refs_3_), channel_id=1, source_target_pairs={{0,8},{2,10},{8,16},{10,18},{16,24},{18,26},{24,28},{26,30},{28,20... | collective-permute-start | bytes 1966088 | tf_op jit(solution)/shard_map/ppermute | solution.py:363
  73.9 28.0 %collective-permute-start.2 = (bf16[16,8,2560]{2,1,0:T(8,128)(2,1)S(1)}, bf16[16,8,2560]{2,1,0:T(8,128)(2,1)S(1)}, u32[]{:S(2)}, u32[]{:S(2)}) collective-permute-start(bf16[16,8,2560]{2,1,0:T(8,128)(2,1)S(1)} %collective-permute-done.1.refs_16_.refs_1_), channel_id=1, source_target_pairs={{0,8},{2,10},{8,16},{10,18},{16,24},{18,26},{24,28},{26,30},{28,20... | collective-permute-start | bytes 1966088 | tf_op jit(solution)/shard_map/ppermute | solution.py:363
  76.2 28.5 %collective-permute-start.10 = (bf16[16,8,2560]{2,1,0:T(8,128)(2,1)S(1)}, bf16[16,8,2560]{2,1,0:T(8,128)(2,1)S(1)}, u32[]{:S(2)}, u32[]{:S(2)}) collective-permute-start(bf16[16,8,2560]{2,1,0:T(8,128)(2,1)S(1)} %collective-permute-done.9.refs_15_.refs_0_), channel_id=1, source_target_pairs={{0,4},{2,6},{8,0},{10,2},{16,8},{18,10},{24,16},{26,18},{28,24},{3... | collective-permute-start | bytes 1966088 | tf_op jit(solution)/shard_map/ppermute | solution.py:363
  76.2 35.4 %collective-permute-start.18 = (bf16[144,2560]{1,0:T(8,128)(2,1)S(1)}, bf16[144,2560]{1,0:T(8,128)(2,1)S(1)}, u32[]{:S(2)}, u32[]{:S(2)}) collective-permute-start(bf16[144,2560]{1,0:T(8,128)(2,1)S(1)} %fusion.9), channel_id=1, source_target_pairs={{2,0},{4,2},{6,4},{8,6},{10,8},{12,10},{14,12},{16,14},{18,16},{20... | collective-permute-start | bytes 2211848 | tf_op jit(solution)/shard_map/ppermute | solution.py:22
  95.2 12.1 %collective-permute-start.19 = (bf16[16,8,2560]{2,1,0:T(8,128)(2,1)S(1)}, bf16[16,8,2560]{2,1,0:T(8,128)(2,1)S(1)}, u32[]{:S(2)}, u32[]{:S(2)}) collective-permute-start(bf16[16,8,2560]{2,1,0:T(8,128)(2,1)S(1)} %get-tuple-element.88), channel_id=1, source_target_pairs={{0,2},{2,0},{4,6},{6,4},{8,10},{10,8},{12,14},{14,12},{16,18},{18,... | collective-permute-start | bytes 1966088 | tf_op jit(solution)/shard_map/ppermute | solution.py:363
  99.2 12.5 %collective-permute-start.20 = (bf16[16,8,2560]{2,1,0:T(8,128)(2,1)S(1)}, bf16[16,8,2560]{2,1,0:T(8,128)(2,1)S(1)}, u32[]{:S(2)}, u32[]{:S(2)}) collective-permute-start(bf16[16,8,2560]{2,1,0:T(8,128)(2,1)S(1)} %get-tuple-element.90), channel_id=1, source_target_pairs={{0,2},{2,0},{4,6},{6,4},{8,10},{10,8},{12,14},{14,12},{16,18},{18,... | collective-permute-start | bytes 1966088 | tf_op jit(solution)/shard_map/ppermute | solution.py:363
  104.7 22.6 %collective-permute-start.7 = (bf16[16,8,2560]{2,1,0:T(8,128)(2,1)S(1)}, bf16[16,8,2560]{2,1,0:T(8,128)(2,1)S(1)}, u32[]{:S(2)}, u32[]{:S(2)}) collective-permute-start(bf16[16,8,2560]{2,1,0:T(8,128)(2,1)S(1)} %collective-permute-done.6.refs_2_.refs_14_), channel_id=1, source_target_pairs={{0,4},{2,6},{8,0},{10,2},{16,8},{18,10},{24,16},{26,18},{28,24},{3... | collective-permute-start | bytes 1966088 | tf_op jit(solution)/shard_map/ppermute | solution.py:363
  107.3 20.0 %collective-permute-start.3 = (bf16[16,8,2560]{2,1,0:T(8,128)(2,1)S(1)}, bf16[16,8,2560]{2,1,0:T(8,128)(2,1)S(1)}, u32[]{:S(2)}, u32[]{:S(2)}) collective-permute-start(bf16[16,8,2560]{2,1,0:T(8,128)(2,1)S(1)} %collective-permute-done.2.refs_1_.refs_13_), channel_id=1, source_target_pairs={{0,8},{2,10},{8,16},{10,18},{16,24},{18,26},{24,28},{26,30},{28,20... | collective-permute-start | bytes 1966088 | tf_op jit(solution)/shard_map/ppermute | solution.py:363
  109.7 3.6 %collective-permute-start.21 = (bf16[16,8,2560]{2,1,0:T(8,128)(2,1)S(1)}, bf16[16,8,2560]{2,1,0:T(8,128)(2,1)S(1)}, u32[]{:S(2)}, u32[]{:S(2)}) collective-permute-start(bf16[16,8,2560]{2,1,0:T(8,128)(2,1)S(1)} %get-tuple-element.95), channel_id=1, source_target_pairs={{0,2},{2,0},{4,6},{6,4},{8,10},{10,8},{12,14},{14,12},{16,18},{18,... | collective-permute-start | bytes 1966088 | tf_op jit(solution)/shard_map/ppermute | solution.py:363
  111.6 2.7 %collective-permute-start.22 = (bf16[16,8,2560]{2,1,0:T(8,128)(2,1)S(1)}, bf16[16,8,2560]{2,1,0:T(8,128)(2,1)S(1)}, u32[]{:S(2)}, u32[]{:S(2)}) collective-permute-start(bf16[16,8,2560]{2,1,0:T(8,128)(2,1)S(1)} %get-tuple-element.96), channel_id=1, source_target_pairs={{0,2},{2,0},{4,6},{6,4},{8,10},{10,8},{12,14},{14,12},{16,18},{18,... | collective-permute-start | bytes 1966088 | tf_op jit(solution)/shard_map/ppermute | solution.py:363
  128.8 1.9 %collective-permute-start.23 = (bf16[8,8,2560]{2,1,0:T(8,128)(2,1)S(1)}, bf16[8,8,2560]{2,1,0:T(8,128)(2,1)S(1)}, u32[]{:S(2)}, u32[]{:S(2)}) collective-permute-start(bf16[8,8,2560]{2,1,0:T(8,128)(2,1)S(1)} %get-tuple-element.103), channel_id=1, source_target_pairs={{0,2},{2,0},{4,6},{6,4},{8,10},{10,8},{12,14},{14,12},{16,18},{18,... | collective-permute-start | bytes 983048 | tf_op jit(solution)/shard_map/ppermute | solution.py:363
  129.2 1.7 %collective-permute-start.24 = (bf16[8,8,2560]{2,1,0:T(8,128)(2,1)S(1)}, bf16[8,8,2560]{2,1,0:T(8,128)(2,1)S(1)}, u32[]{:S(2)}, u32[]{:S(2)}) collective-permute-start(bf16[8,8,2560]{2,1,0:T(8,128)(2,1)S(1)} %get-tuple-element.104), channel_id=1, source_target_pairs={{0,2},{2,0},{4,6},{6,4},{8,10},{10,8},{12,14},{14,12},{16,18},{18,... | collective-permute-start | bytes 983048 | tf_op jit(solution)/shard_map/ppermute | solution.py:363

commit v9 on v8

--- a/solution.py
+++ b/solution.py
@@ -371,7 +371,7 @@
         for pieces in (keys, values):
             pieces += [moved(pieces[-2 if step > 1 else -1], down), moved(pieces[-1], up)]
         if step == 1:
-            from_left, *_ = lax.optimization_barrier((from_left, *values[1:]))
+            from_left, *_ = lax.optimization_barrier((from_left, *keys[1:], *values[1:]))
             seen, left_keys, left_values = arrived(from_left)
             bias = spread(jnp.concatenate([live_rows, seen]))
             sums = near_part(bias, query_norm, key_norm, value_rows, left_keys, left_values)

time: 138 us -> 153 us (1.11)
  the two profiles are of different devices: /device:TPU:0 before, /device:TPU:27 now
where the time goes in v9:
time: 153 us; the launch traced here: 152 us
  waiting for transfers between devices  57.8 us (38%)
  Pallas kernels  49.6 us (32%)
  starting transfers between devices  24 us (16%)
  other arithmetic  7.96 us (5%)
  between operations  5.73 us (4%)
  blocking collectives  4.09 us (3%)
  local copies, waits for them, and re-layouts  3.11 us (2%)
    ppermute x22, waiting for transfers between devices, moved(): return lax.ppermute(piece, 'tile', pairs)  39.6 us
    pallas_call x3, Pallas kernels, far_part(): pl.pallas_call(functools.partial(far_kernel, sizes, live is not None, len...  34 us
    ppermute x2, waiting for transfers between devices, passed_along(): lax.ppermute(value, axis, [(source, source + steps) for source in range(f...  18.1 us
    ppermute x22, starting transfers between devices, moved(): return lax.ppermute(piece, 'tile', pairs)  14.7 us
    pallas_call x4, Pallas kernels, pick_part(): pl.pallas_call(functools.partial(pick_kernel, groups, slots), in_specs=[p...  9.1 us
    ppermute x2, starting transfers between devices, passed_along(): lax.ppermute(value, axis, [(source, source + steps) for source in range(f...  7.45 us
    pallas_call x1, Pallas kernels, near_part(): pl.pallas_call(near_kernel, in_specs=[IN_VMEM] * 6, out_specs=[IN_VMEM] *...  6.44 us
    psum x1, blocking collectives, per_device(): lax.psum((row_squares(query_rows), row_squares(key_rows)), 'head')  4.09 us
  transfers between devices with their start and end apart: 25, of which 9 were waited for; matrix products, arithmetic and copies ran while one was open for 7% of the time, Pallas kernels for 27%

profile of v9, /device:TPU:27, one launch (start us, length us, event | category | flops | bytes accessed | tf_op | source)
XLA Modules:
  0.0 152.2 jit_solution(6878337760773454593)
XLA Ops:
  0.0 1.2 collective-permute-start.11
  1.5 1.2 collective-permute-start
  4.1 1.8 %collective-permute-start.15 = (s32[81]{0:T(128)S(1)}, s32[81]{0:T(128)S(1)}, u32[]{:S(2)}, u32[]{:S(2)}) collective-permute-start(s32[81]{0:T(128)S(1)} %pad_add_fusion.2), channel_id=1, source_target_pairs={{0,2},{2,0},{4,6},{6,4},{8,10},{10,8},{12,14},{14,12},{16,18},{18,... | collective-permute-start | bytes 980 | tf_op jit(solution)/shard_map/ppermute | solution.py:329
  7.3 2.0 %fusion = f32[384]{0:T(512)S(1)} fusion(bf16[384,2560]{1,0:T(8,128)(2,1)} %param.11), kind=kLoop, calls=%fused_computation.4 | loop fusion | flops 2948736 | bytes 1967616 | tf_op jit(solution)/shard_map/reduce_sum | solution.py:27
  9.8 4.1 %all-reduce.10 = (f32[384]{0:T(512)S(1)}, f32[384]{0:T(512)S(1)}) all-reduce(f32[384]{0:T(512)S(1)} %fusion, f32[384]{0:T(512)S(1)} %fusion.3), channel_id=1, replica_groups=mesh['tile'=16,'head'=2] {'head'}, use_global_device_ids=true, to_apply=%region_4.5 | all-reduce | flops 768 | bytes 6144 | tf_op jit(solution)/shard_map/psum | solution.py:333
  15.9 2.1 %fusion.5.k_ref = bf16[384,2560]{1,0:T(8,128)(2,1)S(1)} fusion(bf16[384,2560]{1,0:T(8,128)(2,1)} %param.12, f32[2560]{0:T(1024)S(1)} %copy-done.6, f32[384]{0:T(512)S(1)} %add_rsqrt_fusion), kind=kLoop, calls=%fused_computation.9 | loop fusion | flops 3932160 | bytes 3943936 | tf_op jit(solution)/shard_map/convert_element_type | solution.py:33
  18.0 1.4 fusion.23
  19.6 4.0 %collective-permute-start.14 = (bf16[144,2560]{1,0:T(8,128)(2,1)S(1)}, bf16[144,2560]{1,0:T(8,128)(2,1)S(1)}, u32[]{:S(2)}, u32[]{:S(2)}) collective-permute-start(bf16[144,2560]{1,0:T(8,128)(2,1)S(1)} %fusion.8), channel_id=1, source_target_pairs={{0,2},{2,4},{4,6},{6,8},{8,10},{10,12},{12,14},{14,16},{16,18},{18... | collective-permute-start | bytes 2211848 | tf_op jit(solution)/shard_map/ppermute | solution.py:22
  24.3 5.6 %collective-permute-done.refs_2_.refs_9_ = bf16[16,8,2560]{2,1,0:T(8,128)(2,1)} collective-permute-done((bf16[16,8,2560]{2,1,0:T(8,128)(2,1)}, bf16[16,8,2560]{2,1,0:T(8,128)(2,1)}, u32[]{:S(2)}, u32[]{:S(2)}) %collective-permute-start) | collective-permute-done | bytes 655392 | tf_op jit(solution)/shard_map/ppermute | solution.py:363
  30.0 1.2 collective-permute-start.1
  31.4 9.4 %collective-permute-done.14 = bf16[144,2560]{1,0:T(8,128)(2,1)S(1)} collective-permute-done((bf16[144,2560]{1,0:T(8,128)(2,1)S(1)}, bf16[144,2560]{1,0:T(8,128)(2,1)S(1)}, u32[]{:S(2)}, u32[]{:S(2)}) %collective-permute-start.14) | collective-permute-done | bytes 737312 | tf_op jit(solution)/shard_map/ppermute | solution.py:22
  41.0 6.4 %near_part.1 = (f32[20,8,384]{2,1,0:T(8,128)S(1)}, f32[20,8,384]{2,1,0:T(8,128)S(1)}, f32[2560,384]{1,0:T(8,128)S(1)}) custom-call(f32[448,128]{1,0:T(8,128)S(1)} %broadcast_in_dim.130.bias_ref, bf16[384,2560]{1,0:T(8,128)(2,1)S(1)} %fusion.2.q_ref.refs_3_, bf16[384,2560]{1,0:T(8,128)(2,1)S(1)} %fusion.5.k_ref, bf16[384,2560]{1,0:T(8,128)(2,1)S(1)} %copy-done, ...), custom_call_target="tpu_custom_call" | custom-call | flops 1761607680 | bytes 9830400 | tf_op jit(solution)/shard_map/near_part/pallas_call | solution.py:133
  47.5 2.8 %pick_0.1 = (bf16[24,8,2560]{2,1,0:T(8,128)(2,1)S(1)}, bf16[24,8,2560]{2,1,0:T(8,128)(2,1)S(1)}) custom-call(s32[4]{0:T(128)S(1)} %slice.86.first_ref, s32[88]{0:T(128)S(1)} %concatenate.62.block_ref, bf16[16,8,2560]{2,1,0:T(8,128)(2,1)S(1)} %copy-done.1, bf16[16,8,2560]{2,1,0:T(8,128)(2,1)} %collective-permute-done.8.refs_1_.refs_8_, ...), custom_call_target="tpu_custom_call" | custom-call | bytes 3932160 | tf_op jit(solution)/shard_map/pick_0/pallas_call | solution.py:169
  50.9 4.0 %collective-permute-done.1.refs_16_.refs_1_ = bf16[16,8,2560]{2,1,0:T(8,128)(2,1)S(1)} collective-permute-done((bf16[16,8,2560]{2,1,0:T(8,128)(2,1)}, bf16[16,8,2560]{2,1,0:T(8,128)(2,1)S(1)}, u32[]{:S(2)}, u32[]{:S(2)}) %collective-permute-start.1) | collective-permute-done | bytes 655392 | tf_op jit(solution)/shard_map/ppermute | solution.py:363
  55.0 11.1 %collective-permute-done.12.refs_18_.refs_3_ = bf16[16,8,2560]{2,1,0:T(8,128)(2,1)S(1)} collective-permute-done((bf16[16,8,2560]{2,1,0:T(8,128)(2,1)S(1)}, bf16[16,8,2560]{2,1,0:T(8,128)(2,1)S(1)}, u32[]{:S(2)}, u32[]{:S(2)}) %collective-permute-start.12) | collective-permute-done | bytes 655392 | tf_op jit(solution)/shard_map/ppermute | solution.py:363
  66.0 2.2 %collective-permute-start.2 = (bf16[16,8,2560]{2,1,0:T(8,128)(2,1)S(1)}, bf16[16,8,2560]{2,1,0:T(8,128)(2,1)S(1)}, u32[]{:S(2)}, u32[]{:S(2)}) collective-permute-start(bf16[16,8,2560]{2,1,0:T(8,128)(2,1)S(1)} %collective-permute-done.1.refs_16_.refs_1_), channel_id=1, source_target_pairs={{0,8},{2,10},{8,16},{10,18},{16,24},{18,26},{24,28},{26,30},{28,20... | collective-permute-start | bytes 1966088 | tf_op jit(solution)/shard_map/ppermute | solution.py:363
  68.4 13.6 %collective-permute-done.9.refs_15_.refs_0_ = bf16[16,8,2560]{2,1,0:T(8,128)(2,1)S(1)} collective-permute-done((bf16[16,8,2560]{2,1,0:T(8,128)(2,1)}, bf16[16,8,2560]{2,1,0:T(8,128)(2,1)S(1)}, u32[]{:S(2)}, u32[]{:S(2)}) %collective-permute-start.9) | collective-permute-done | bytes 655392 | tf_op jit(solution)/shard_map/ppermute | solution.py:363
  82.0 1.5 collective-permute-start.13
  83.5 3.4 %collective-permute-start.18 = (bf16[144,2560]{1,0:T(8,128)(2,1)S(1)}, bf16[144,2560]{1,0:T(8,128)(2,1)S(1)}, u32[]{:S(2)}, u32[]{:S(2)}) collective-permute-start(bf16[144,2560]{1,0:T(8,128)(2,1)S(1)} %fusion.9), channel_id=1, source_target_pairs={{2,0},{4,2},{6,4},{8,6},{10,8},{12,10},{14,12},{16,14},{18,16},{20... | collective-permute-start | bytes 2211848 | tf_op jit(solution)/shard_map/ppermute | solution.py:22
  87.0 14.3 %far_1.1 = (f32[20,8,384]{2,1,0:T(8,128)S(1)}, f32[20,8,384]{2,1,0:T(8,128)S(1)}, f32[2560,384]{1,0:T(8,128)S(1)}) custom-call(s32[7]{0:T(128)S(1)} %pad_add_fusion.1.refs_0_, s32[128]{0:T(128)S(1)} %concatenate.59.refs_1_, f32[512,128]{1,0:T(8,128)S(1)} %broadcast_in_dim.133.refs_2_, ...), custom_call_target="tpu_custom_call", output_to_operand_aliasing={{0}: (4, {}), {1}: (5, {}), {2}: (6, {})} | custom-call | flops 2013265920 | bytes 9830400 | tf_op jit(solution)/shard_map/far_1/pallas_call | solution.py:259
  101.4 2.4 %pick_1.1 = (bf16[16,8,2560]{2,1,0:T(8,128)(2,1)S(1)}, bf16[16,8,2560]{2,1,0:T(8,128)(2,1)S(1)}) custom-call(s32[3]{0:T(128)S(1)} %get-tuple-element.119.first_ref, s32[80]{0:T(128)S(1)} %concatenate.63.block_ref, bf16[16,8,2560]{2,1,0:T(8,128)(2,1)S(1)} %collective-permute-done.9.refs_15_.refs_0_, ...), custom_call_target="tpu_custom_call" | custom-call | bytes 2621440 | tf_op jit(solution)/shard_map/pick_1/pallas_call | solution.py:169
  103.8 1.5 %collective-permute-start.19 = (bf16[16,8,2560]{2,1,0:T(8,128)(2,1)S(1)}, bf16[16,8,2560]{2,1,0:T(8,128)(2,1)S(1)}, u32[]{:S(2)}, u32[]{:S(2)}) collective-permute-start(bf16[16,8,2560]{2,1,0:T(8,128)(2,1)S(1)} %get-tuple-element.88), channel_id=1, source_target_pairs={{0,2},{2,0},{4,6},{6,4},{8,10},{10,8},{12,14},{14,12},{16,18},{18,... | collective-permute-start | bytes 1966088 | tf_op jit(solution)/shard_map/ppermute | solution.py:363
  106.7 1.5 pad_add_fusion.refs_0_
  108.3 3.0 %collective-permute-done.10.refs_0_.refs_12_ = bf16[16,8,2560]{2,1,0:T(8,128)(2,1)S(1)} collective-permute-done((bf16[16,8,2560]{2,1,0:T(8,128)(2,1)S(1)}, bf16[16,8,2560]{2,1,0:T(8,128)(2,1)S(1)}, u32[]{:S(2)}, u32[]{:S(2)}) %collective-permute-start.10) | collective-permute-done | bytes 655392 | tf_op jit(solution)/shard_map/ppermute | solution.py:363
  111.3 0.8 collective-permute-start.3
  112.8 2.4 %pick_2.1 = (bf16[16,8,2560]{2,1,0:T(8,128)(2,1)S(1)}, bf16[16,8,2560]{2,1,0:T(8,128)(2,1)S(1)}) custom-call(s32[3]{0:T(128)S(1)} %get-tuple-element.118.first_ref, s32[80]{0:T(128)S(1)} %concatenate.63.block_ref, bf16[16,8,2560]{2,1,0:T(8,128)(2,1)S(1)} %collective-permute-done.10.refs_0_.refs_12_, ...), custom_call_target="tpu_custom_call" | custom-call | bytes 2621440 | tf_op jit(solution)/shard_map/pick_2/pallas_call | solution.py:169
  115.2 2.5 %collective-permute-start.21 = (bf16[16,8,2560]{2,1,0:T(8,128)(2,1)S(1)}, bf16[16,8,2560]{2,1,0:T(8,128)(2,1)S(1)}, u32[]{:S(2)}, u32[]{:S(2)}) collective-permute-start(bf16[16,8,2560]{2,1,0:T(8,128)(2,1)S(1)} %get-tuple-element.95), channel_id=1, source_target_pairs={{0,2},{2,0},{4,6},{6,4},{8,10},{10,8},{12,14},{14,12},{16,18},{18,... | collective-permute-start | bytes 1966088 | tf_op jit(solution)/shard_map/ppermute | solution.py:363
  117.7 8.8 %collective-permute-done.18 = bf16[144,2560]{1,0:T(8,128)(2,1)S(1)} collective-permute-done((bf16[144,2560]{1,0:T(8,128)(2,1)S(1)}, bf16[144,2560]{1,0:T(8,128)(2,1)S(1)}, u32[]{:S(2)}, u32[]{:S(2)}) %collective-permute-start.18) | collective-permute-done | bytes 737312 | tf_op jit(solution)/shard_map/ppermute | solution.py:22
  126.5 2.0 %collective-permute-done.22.refs_17_ = bf16[16,8,2560]{2,1,0:T(8,128)(2,1)S(1)} collective-permute-done((bf16[16,8,2560]{2,1,0:T(8,128)(2,1)S(1)}, bf16[16,8,2560]{2,1,0:T(8,128)(2,1)S(1)}, u32[]{:S(2)}, u32[]{:S(2)}) %collective-permute-start.22) | collective-permute-done | bytes 655392 | tf_op jit(solution)/shard_map/ppermute | solution.py:363
  128.7 12.9 %far_2.1 = (f32[20,8,384]{2,1,0:T(8,128)S(1)}, f32[20,8,384]{2,1,0:T(8,128)S(1)}, f32[2560,384]{1,0:T(8,128)S(1)}) custom-call(s32[5]{0:T(128)S(1)} %pad_add_fusion.refs_0_, s32[112]{0:T(128)S(1)} %concatenate.53.refs_1_, f32[384,128]{1,0:T(8,128)S(1)} %broadcast_in_dim.125.refs_2_, ...), custom_call_target="tpu_custom_call", output_to_operand_aliasing={{0}: (4, {}), {1}: (5, {}), {2}: (6, {})} | custom-call | flops 1509949440 | bytes 9830400 | tf_op jit(solution)/shard_map/far_2/pallas_call | solution.py:259
  141.6 1.5 pick_3.1
  145.4 6.8 %far_3.1 = bf16[384,2560]{1,0:T(8,128)(2,1)} custom-call(s32[3]{0:T(128)S(1)} %get-tuple-element.126.refs_0_, s32[80]{0:T(128)S(1)} %concatenate.51.refs_1_, f32[128,128]{1,0:T(8,128)S(1)} %broadcast_in_dim.122.refs_2_, bf16[384,2560]{1,0:T(8,128)(2,1)S(1)} %fusion.2.q_ref.refs_3_, f32[20,8,384]{2,1,0:T(8,128)S(1)} %get-tuple-element.98.refs_4_, ...), custom_call_target="tpu_custom_call" | custom-call | flops 503316480 | bytes 9830400 | tf_op jit(solution)/shard_map/far_3/pallas_call | solution.py:259
  (87 shorter events, 6.9 us)
Async XLA Ops:
  0.0 9.3 %copy-start.3 = (bf16[384,2560]{1,0:T(8,128)(2,1)S(1)}, bf16[384,2560]{1,0:T(8,128)(2,1)}, u32[]{:S(2)}) copy-start(bf16[384,2560]{1,0:T(8,128)(2,1)} %param.12) | copy-start | bytes 5898244
  0.0 31.2 %collective-permute-start.11 = (bf16[16,8,2560]{2,1,0:T(8,128)(2,1)}, bf16[16,8,2560]{2,1,0:T(8,128)(2,1)S(1)}, u32[]{:S(2)}, u32[]{:S(2)}) collective-permute-start(bf16[16,8,2560]{2,1,0:T(8,128)(2,1)} %refs_10_), channel_id=1, source_target_pairs={{0,8},{2,10},{8,16},{10,18},{16,24},{18,26},{24,28},{26,30},{28,20... | collective-permute-start | bytes 1966088 | tf_op jit(solution)/shard_map/ppermute | solution.py:363
  1.2 30.1 %collective-permute-start.4 = (bf16[16,8,2560]{2,1,0:T(8,128)(2,1)}, bf16[16,8,2560]{2,1,0:T(8,128)(2,1)S(1)}, u32[]{:S(2)}, u32[]{:S(2)}) collective-permute-start(bf16[16,8,2560]{2,1,0:T(8,128)(2,1)} %refs_10_), channel_id=1, source_target_pairs={{0,4},{2,6},{8,0},{10,2},{16,8},{18,10},{24,16},{26,18},{28,24},{3... | collective-permute-start | bytes 1966088 | tf_op jit(solution)/shard_map/ppermute | solution.py:363
  1.5 28.5 %collective-permute-start = (bf16[16,8,2560]{2,1,0:T(8,128)(2,1)}, bf16[16,8,2560]{2,1,0:T(8,128)(2,1)}, u32[]{:S(2)}, u32[]{:S(2)}) collective-permute-start(bf16[16,8,2560]{2,1,0:T(8,128)(2,1)} %refs_7_), channel_id=1, source_target_pairs={{0,8},{2,10},{8,16},{10,18},{16,24},{18,26},{24,28},{26,30},{28,20... | collective-permute-start | bytes 1966088 | tf_op jit(solution)/shard_map/ppermute | solution.py:363
  2.7 28.7 %collective-permute-start.8 = (bf16[16,8,2560]{2,1,0:T(8,128)(2,1)}, bf16[16,8,2560]{2,1,0:T(8,128)(2,1)}, u32[]{:S(2)}, u32[]{:S(2)}) collective-permute-start(bf16[16,8,2560]{2,1,0:T(8,128)(2,1)} %refs_7_), channel_id=1, source_target_pairs={{0,4},{2,6},{8,0},{10,2},{16,8},{18,10},{24,16},{26,18},{28,24},{3... | collective-permute-start | bytes 1966088 | tf_op jit(solution)/shard_map/ppermute | solution.py:363
  4.1 15.4 %collective-permute-start.15 = (s32[81]{0:T(128)S(1)}, s32[81]{0:T(128)S(1)}, u32[]{:S(2)}, u32[]{:S(2)}) collective-permute-start(s32[81]{0:T(128)S(1)} %pad_add_fusion.2), channel_id=1, source_target_pairs={{0,2},{2,0},{4,6},{6,4},{8,10},{10,8},{12,14},{14,12},{16,18},{18,... | collective-permute-start | bytes 980 | tf_op jit(solution)/shard_map/ppermute | solution.py:329
  7.3 7.3 %copy-start.5 = (f32[2560]{0:T(1024)S(1)}, f32[2560]{0:T(1024)}, u32[]{:S(2)}) copy-start(f32[2560]{0:T(1024)} %param.14) | copy-start | bytes 30724
  7.3 8.6 %copy-start.6 = (f32[2560]{0:T(1024)S(1)}, f32[2560]{0:T(1024)}, u32[]{:S(2)}) copy-start(f32[2560]{0:T(1024)} %param.15) | copy-start | bytes 30724
  18.0 5.6 %copy-start.4 = (bf16[384,2560]{1,0:T(8,128)(2,1)S(1)}, bf16[384,2560]{1,0:T(8,128)(2,1)}, u32[]{:S(2)}) copy-start(bf16[384,2560]{1,0:T(8,128)(2,1)} %param.11) | copy-start | bytes 5898244
  19.6 21.4 %copy-start = (bf16[384,2560]{1,0:T(8,128)(2,1)S(1)}, bf16[384,2560]{1,0:T(8,128)(2,1)}, u32[]{:S(2)}) copy-start(bf16[384,2560]{1,0:T(8,128)(2,1)} %v_ref.1) | copy-start | bytes 5898244
  19.6 21.2 %collective-permute-start.14 = (bf16[144,2560]{1,0:T(8,128)(2,1)S(1)}, bf16[144,2560]{1,0:T(8,128)(2,1)S(1)}, u32[]{:S(2)}, u32[]{:S(2)}) collective-permute-start(bf16[144,2560]{1,0:T(8,128)(2,1)S(1)} %fusion.8), channel_id=1, source_target_pairs={{0,2},{2,4},{4,6},{6,8},{8,10},{10,12},{12,14},{14,16},{16,18},{18... | collective-permute-start | bytes 2211848 | tf_op jit(solution)/shard_map/ppermute | solution.py:22
  30.0 24.9 %collective-permute-start.1 = (bf16[16,8,2560]{2,1,0:T(8,128)(2,1)}, bf16[16,8,2560]{2,1,0:T(8,128)(2,1)S(1)}, u32[]{:S(2)}, u32[]{:S(2)}) collective-permute-start(bf16[16,8,2560]{2,1,0:T(8,128)(2,1)} %collective-permute-done.refs_2_.refs_9_), channel_id=1, source_target_pairs={{0,8},{2,10},{8,16},{10,18},{16,24},{18,26},{24,28},{26,30},{28,20... | collective-permute-start | bytes 1966088 | tf_op jit(solution)/shard_map/ppermute | solution.py:363
  31.2 34.8 %collective-permute-start.12 = (bf16[16,8,2560]{2,1,0:T(8,128)(2,1)S(1)}, bf16[16,8,2560]{2,1,0:T(8,128)(2,1)S(1)}, u32[]{:S(2)}, u32[]{:S(2)}) collective-permute-start(bf16[16,8,2560]{2,1,0:T(8,128)(2,1)S(1)} %collective-permute-done.11.refs_5_.refs_12_), channel_id=1, source_target_pairs={{0,8},{2,10},{8,16},{10,18},{16,24},{18,26},{24,28},{26,30},{28,20... | collective-permute-start | bytes 1966088 | tf_op jit(solution)/shard_map/ppermute | solution.py:363
  41.0 6.5 %copy-start.1 = (bf16[16,8,2560]{2,1,0:T(8,128)(2,1)S(1)}, bf16[16,8,2560]{2,1,0:T(8,128)(2,1)}, u32[]{:S(2)}) copy-start(bf16[16,8,2560]{2,1,0:T(8,128)(2,1)} %refs_7_) | copy-start | bytes 1966084
  41.0 6.5 %copy-start.2 = (bf16[16,8,2560]{2,1,0:T(8,128)(2,1)S(1)}, bf16[16,8,2560]{2,1,0:T(8,128)(2,1)}, u32[]{:S(2)}) copy-start(bf16[16,8,2560]{2,1,0:T(8,128)(2,1)} %refs_10_) | copy-start | bytes 1966084
  50.3 31.7 %collective-permute-start.16 = (bf16[24,8,2560]{2,1,0:T(8,128)(2,1)S(1)}, bf16[24,8,2560]{2,1,0:T(8,128)(2,1)S(1)}, u32[]{:S(2)}, u32[]{:S(2)}) collective-permute-start(bf16[24,8,2560]{2,1,0:T(8,128)(2,1)S(1)} %get-tuple-element.71), channel_id=1, source_target_pairs={{0,2},{2,0},{4,6},{6,4},{8,10},{10,8},{12,14},{14,12},{16,18},{18,... | collective-permute-start | bytes 2949128 | tf_op jit(solution)/shard_map/ppermute | solution.py:363
  50.5 33.0 %collective-permute-start.17 = (bf16[24,8,2560]{2,1,0:T(8,128)(2,1)S(1)}, bf16[24,8,2560]{2,1,0:T(8,128)(2,1)S(1)}, u32[]{:S(2)}, u32[]{:S(2)}) collective-permute-start(bf16[24,8,2560]{2,1,0:T(8,128)(2,1)S(1)} %get-tuple-element.73), channel_id=1, source_target_pairs={{0,2},{2,0},{4,6},{6,4},{8,10},{10,8},{12,14},{14,12},{16,18},{18,... | collective-permute-start | bytes 2949128 | tf_op jit(solution)/shard_map/ppermute | solution.py:363
  50.9 17.5 %collective-permute-start.5 = (bf16[16,8,2560]{2,1,0:T(8,128)(2,1)S(1)}, bf16[16,8,2560]{2,1,0:T(8,128)(2,1)S(1)}, u32[]{:S(2)}, u32[]{:S(2)}) collective-permute-start(bf16[16,8,2560]{2,1,0:T(8,128)(2,1)S(1)} %collective-permute-done.4.refs_4_.refs_11_), channel_id=1, source_target_pairs={{0,4},{2,6},{8,0},{10,2},{16,8},{18,10},{24,16},{26,18},{28,24},{3... | collective-permute-start | bytes 1966088 | tf_op jit(solution)/shard_map/ppermute | solution.py:363
  54.9 27.1 %collective-permute-start.9 = (bf16[16,8,2560]{2,1,0:T(8,128)(2,1)}, bf16[16,8,2560]{2,1,0:T(8,128)(2,1)S(1)}, u32[]{:S(2)}, u32[]{:S(2)}) collective-permute-start(bf16[16,8,2560]{2,1,0:T(8,128)(2,1)} %collective-permute-done.8.refs_1_.refs_8_), channel_id=1, source_target_pairs={{0,4},{2,6},{8,0},{10,2},{16,8},{18,10},{24,16},{26,18},{28,24},{3... | collective-permute-start | bytes 1966088 | tf_op jit(solution)/shard_map/ppermute | solution.py:363
  66.0 37.7 %collective-permute-start.2 = (bf16[16,8,2560]{2,1,0:T(8,128)(2,1)S(1)}, bf16[16,8,2560]{2,1,0:T(8,128)(2,1)S(1)}, u32[]{:S(2)}, u32[]{:S(2)}) collective-permute-start(bf16[16,8,2560]{2,1,0:T(8,128)(2,1)S(1)} %collective-permute-done.1.refs_16_.refs_1_), channel_id=1, source_target_pairs={{0,8},{2,10},{8,16},{10,18},{16,24},{18,26},{24,28},{26,30},{28,20... | collective-permute-start | bytes 1966088 | tf_op jit(solution)/shard_map/ppermute | solution.py:363
  82.0 26.3 %collective-permute-start.6 = (bf16[16,8,2560]{2,1,0:T(8,128)(2,1)S(1)}, bf16[16,8,2560]{2,1,0:T(8,128)(2,1)S(1)}, u32[]{:S(2)}, u32[]{:S(2)}) collective-permute-start(bf16[16,8,2560]{2,1,0:T(8,128)(2,1)S(1)} %collective-permute-done.5.refs_17_.refs_2_), channel_id=1, source_target_pairs={{0,4},{2,6},{8,0},{10,2},{16,8},{18,10},{24,16},{26,18},{28,24},{3... | collective-permute-start | bytes 1966088 | tf_op jit(solution)/shard_map/ppermute | solution.py:363
  82.0 29.3 %collective-permute-start.10 = (bf16[16,8,2560]{2,1,0:T(8,128)(2,1)S(1)}, bf16[16,8,2560]{2,1,0:T(8,128)(2,1)S(1)}, u32[]{:S(2)}, u32[]{:S(2)}) collective-permute-start(bf16[16,8,2560]{2,1,0:T(8,128)(2,1)S(1)} %collective-permute-done.9.refs_15_.refs_0_), channel_id=1, source_target_pairs={{0,4},{2,6},{8,0},{10,2},{16,8},{18,10},{24,16},{26,18},{28,24},{3... | collective-permute-start | bytes 1966088 | tf_op jit(solution)/shard_map/ppermute | solution.py:363
  82.0 29.3 %collective-permute-start.13 = (bf16[16,8,2560]{2,1,0:T(8,128)(2,1)S(1)}, bf16[16,8,2560]{2,1,0:T(8,128)(2,1)S(1)}, u32[]{:S(2)}, u32[]{:S(2)}) collective-permute-start(bf16[16,8,2560]{2,1,0:T(8,128)(2,1)S(1)} %collective-permute-done.12.refs_18_.refs_3_), channel_id=1, source_target_pairs={{0,8},{2,10},{8,16},{10,18},{16,24},{18,26},{24,28},{26,30},{28,20... | collective-permute-start | bytes 1966088 | tf_op jit(solution)/shard_map/ppermute | solution.py:363
  83.5 43.0 %collective-permute-start.18 = (bf16[144,2560]{1,0:T(8,128)(2,1)S(1)}, bf16[144,2560]{1,0:T(8,128)(2,1)S(1)}, u32[]{:S(2)}, u32[]{:S(2)}) collective-permute-start(bf16[144,2560]{1,0:T(8,128)(2,1)S(1)} %fusion.9), channel_id=1, source_target_pairs={{2,0},{4,2},{6,4},{8,6},{10,8},{12,10},{14,12},{16,14},{18,16},{20... | collective-permute-start | bytes 2211848 | tf_op jit(solution)/shard_map/ppermute | solution.py:22
  103.8 9.0 %collective-permute-start.19 = (bf16[16,8,2560]{2,1,0:T(8,128)(2,1)S(1)}, bf16[16,8,2560]{2,1,0:T(8,128)(2,1)S(1)}, u32[]{:S(2)}, u32[]{:S(2)}) collective-permute-start(bf16[16,8,2560]{2,1,0:T(8,128)(2,1)S(1)} %get-tuple-element.88), channel_id=1, source_target_pairs={{0,2},{2,0},{4,6},{6,4},{8,10},{10,8},{12,14},{14,12},{16,18},{18,... | collective-permute-start | bytes 1966088 | tf_op jit(solution)/shard_map/ppermute | solution.py:363
  108.2 18.2 %collective-permute-start.20 = (bf16[16,8,2560]{2,1,0:T(8,128)(2,1)S(1)}, bf16[16,8,2560]{2,1,0:T(8,128)(2,1)S(1)}, u32[]{:S(2)}, u32[]{:S(2)}) collective-permute-start(bf16[16,8,2560]{2,1,0:T(8,128)(2,1)S(1)} %get-tuple-element.90), channel_id=1, source_target_pairs={{0,2},{2,0},{4,6},{6,4},{8,10},{10,8},{12,14},{14,12},{16,18},{18,... | collective-permute-start | bytes 1966088 | tf_op jit(solution)/shard_map/ppermute | solution.py:363
  111.3 30.3 %collective-permute-start.3 = (bf16[16,8,2560]{2,1,0:T(8,128)(2,1)S(1)}, bf16[16,8,2560]{2,1,0:T(8,128)(2,1)S(1)}, u32[]{:S(2)}, u32[]{:S(2)}) collective-permute-start(bf16[16,8,2560]{2,1,0:T(8,128)(2,1)S(1)} %collective-permute-done.2.refs_1_.refs_13_), channel_id=1, source_target_pairs={{0,8},{2,10},{8,16},{10,18},{16,24},{18,26},{24,28},{26,30},{28,20... | collective-permute-start | bytes 1966088 | tf_op jit(solution)/shard_map/ppermute | solution.py:363
  112.1 29.5 %collective-permute-start.7 = (bf16[16,8,2560]{2,1,0:T(8,128)(2,1)S(1)}, bf16[16,8,2560]{2,1,0:T(8,128)(2,1)S(1)}, u32[]{:S(2)}, u32[]{:S(2)}) collective-permute-start(bf16[16,8,2560]{2,1,0:T(8,128)(2,1)S(1)} %collective-permute-done.6.refs_2_.refs_14_), channel_id=1, source_target_pairs={{0,4},{2,6},{8,0},{10,2},{16,8},{18,10},{24,16},{26,18},{28,24},{3... | collective-permute-start | bytes 1966088 | tf_op jit(solution)/shard_map/ppermute | solution.py:363
  115.2 11.3 %collective-permute-start.21 = (bf16[16,8,2560]{2,1,0:T(8,128)(2,1)S(1)}, bf16[16,8,2560]{2,1,0:T(8,128)(2,1)S(1)}, u32[]{:S(2)}, u32[]{:S(2)}) collective-permute-start(bf16[16,8,2560]{2,1,0:T(8,128)(2,1)S(1)} %get-tuple-element.95), channel_id=1, source_target_pairs={{0,2},{2,0},{4,6},{6,4},{8,10},{10,8},{12,14},{14,12},{16,18},{18,... | collective-permute-start | bytes 1966088 | tf_op jit(solution)/shard_map/ppermute | solution.py:363
  126.4 2.1 %collective-permute-start.22 = (bf16[16,8,2560]{2,1,0:T(8,128)(2,1)S(1)}, bf16[16,8,2560]{2,1,0:T(8,128)(2,1)S(1)}, u32[]{:S(2)}, u32[]{:S(2)}) collective-permute-start(bf16[16,8,2560]{2,1,0:T(8,128)(2,1)S(1)} %get-tuple-element.96), channel_id=1, source_target_pairs={{0,2},{2,0},{4,6},{6,4},{8,10},{10,8},{12,14},{14,12},{16,18},{18,... | collective-permute-start | bytes 1966088 | tf_op jit(solution)/shard_map/ppermute | solution.py:363
  143.1 1.9 %collective-permute-start.23 = (bf16[8,8,2560]{2,1,0:T(8,128)(2,1)S(1)}, bf16[8,8,2560]{2,1,0:T(8,128)(2,1)S(1)}, u32[]{:S(2)}, u32[]{:S(2)}) collective-permute-start(bf16[8,8,2560]{2,1,0:T(8,128)(2,1)S(1)} %get-tuple-element.103), channel_id=1, source_target_pairs={{0,2},{2,0},{4,6},{6,4},{8,10},{10,8},{12,14},{14,12},{16,18},{18,... | collective-permute-start | bytes 983048 | tf_op jit(solution)/shard_map/ppermute | solution.py:363
  143.3 2.0 %collective-permute-start.24 = (bf16[8,8,2560]{2,1,0:T(8,128)(2,1)S(1)}, bf16[8,8,2560]{2,1,0:T(8,128)(2,1)S(1)}, u32[]{:S(2)}, u32[]{:S(2)}) collective-permute-start(bf16[8,8,2560]{2,1,0:T(8,128)(2,1)S(1)} %get-tuple-element.104), channel_id=1, source_target_pairs={{0,2},{2,0},{4,6},{6,4},{8,10},{10,8},{12,14},{14,12},{16,18},{18,... | collective-permute-start | bytes 983048 | tf_op jit(solution)/shard_map/ppermute | solution.py:363

commit v10 on v8

--- a/solution.py
+++ b/solution.py
@@ -395,6 +395,10 @@
         if stage == 2:
             *pieces, late = lax.optimization_barrier((*pieces, segments[0][1][0]))
             segments[0] = ((), [late, segments[0][1][1]])
+        if stage == 3:
+            both = [array for piece in pieces for array in (piece, moved(piece, swap))]
+            bounds = my_first[2 * first : end + 1]
+            return far_part("far_3", bounds, my_block, 2 * limit, query_norm, sums, [(both, ())], live)
         theirs = their_first[middle : end + 1]
         picked = pick_part(f"pick_{stage}", theirs, their_block, limit, pieces[:size], pieces[size:])
         received = [moved(array, swap) for array in picked]
@@ -407,11 +411,8 @@
         if stage > 1:
             bounds = jnp.concatenate([*starts, my_first[end:][:1]])
             slots = min(request.shape[0], slots)
-            final = live if stage == 3 else None
-            beside = (spread(seen), right_keys, right_values) if stage == 2 else ()
-            sums = far_part(f"far_{stage}", bounds, my_block, slots, query_norm, sums, segments, final, beside)
-            segments, starts, slots = [], [], 0
-    return sums
+            beside = (spread(seen), right_keys, right_values)
+            sums = far_part("far_2", bounds, my_block, slots, query_norm, sums, segments, None, beside)
 
 
 def solution(mesh):

time: 138 us -> 138 us (level)
  Pallas kernels: 50.7 us -> 49 us
  waiting for transfers between devices: 30.9 us -> 32.5 us
    ppermute x22, waiting for transfers between devices: 30.9 us -> 32.5 us  [moved(): return lax.ppermute(piece, 'tile', pairs)]
    pallas_call x4 -> x3, Pallas kernels: 9.6 us -> 8.12 us  [pick_part(): pl.pallas_call(functools.partial(pick_kernel, groups, slots), in_specs=[p...]
  transfers between devices with their start and end apart: 25 -> 25, of which waited for: 9 -> 10; matrix products, arithmetic and copies ran while one was open for 8% -> 8% of each run, Pallas kernels for 31% -> 31%
where the time goes in v10:
time: 138 us; the launch traced here: 137 us
  Pallas kernels  49 us (36%)
  starting transfers between devices  34.6 us (25%)
  waiting for transfers between devices  32.5 us (24%)
  other arithmetic  7.74 us (6%)
  between operations  5.42 us (4%)
  blocking collectives  4.94 us (4%)
  local copies, waits for them, and re-layouts  3.04 us (2%)
    pallas_call x3, Pallas kernels, far_part(): pl.pallas_call(functools.partial(far_kernel, sizes, live is not None, len...  34.5 us
    ppermute x22, waiting for transfers between devices, moved(): return lax.ppermute(piece, 'tile', pairs)  32.5 us
    ppermute x22, starting transfers between devices, moved(): return lax.ppermute(piece, 'tile', pairs)  31.6 us
    pallas_call x3, Pallas kernels, pick_part(): pl.pallas_call(functools.partial(pick_kernel, groups, slots), in_specs=[p...  8.12 us
    pallas_call x1, Pallas kernels, near_part(): pl.pallas_call(near_kernel, in_specs=[IN_VMEM] * 6, out_specs=[IN_VMEM] *...  6.4 us
    psum x1, blocking collectives, per_device(): lax.psum((row_squares(query_rows), row_squares(key_rows)), 'head')  4.94 us
    ppermute x2, starting transfers between devices, passed_along(): lax.ppermute(value, axis, [(source, source + steps) for source in range(f...  3.08 us
  transfers between devices with their start and end apart: 25, of which 10 were waited for; matrix products, arithmetic and copies ran while one was open for 8% of the time, Pallas kernels for 31%

profile of v10, /device:TPU:0, one launch (start us, length us, event | category | flops | bytes accessed | tf_op | source)
XLA Modules:
  0.0 137.3 jit_solution(15034041904612675541)
XLA Ops:
  0.0 3.0 %collective-permute-start.11 = (bf16[16,8,2560]{2,1,0:T(8,128)(2,1)}, bf16[16,8,2560]{2,1,0:T(8,128)(2,1)S(1)}, u32[]{:S(2)}, u32[]{:S(2)}) collective-permute-start(bf16[16,8,2560]{2,1,0:T(8,128)(2,1)} %refs_10_), channel_id=1, source_target_pairs={{0,8},{2,10},{8,16},{10,18},{16,24},{18,26},{24,28},{26,30},{28,20... | collective-permute-start | bytes 1966088 | tf_op jit(solution)/shard_map/ppermute | solution.py:363
  4.9 2.0 %fusion = f32[384]{0:T(512)S(1)} fusion(bf16[384,2560]{1,0:T(8,128)(2,1)} %param.11), kind=kLoop, calls=%fused_computation.4 | loop fusion | flops 2948736 | bytes 1967616 | tf_op jit(solution)/shard_map/reduce_sum | solution.py:27
  7.4 4.9 %all-reduce.9 = (f32[384]{0:T(512)S(1)}, f32[384]{0:T(512)S(1)}) all-reduce(f32[384]{0:T(512)S(1)} %fusion, f32[384]{0:T(512)S(1)} %fusion.3), channel_id=1, replica_groups=mesh['tile'=16,'head'=2] {'head'}, use_global_device_ids=true, to_apply=%region_4.5 | all-reduce | flops 768 | bytes 6144 | tf_op jit(solution)/shard_map/psum | solution.py:333
  13.0 2.1 %fusion.5.k_ref = bf16[384,2560]{1,0:T(8,128)(2,1)S(1)} fusion(bf16[384,2560]{1,0:T(8,128)(2,1)} %param.12, f32[2560]{0:T(1024)S(1)} %copy-done.6, f32[384]{0:T(512)S(1)} %add_rsqrt_fusion), kind=kLoop, calls=%fused_computation.9 | loop fusion | flops 3932160 | bytes 3943936 | tf_op jit(solution)/shard_map/convert_element_type | solution.py:33
  15.1 1.4 %fusion.23 = (bf16[64,2560]{1,0:T(8,128)(2,1)S(1)}, bf16[64,2560]{1,0:T(8,128)(2,1)S(1)}, bf16[64,2560]{1,0:T(8,128)(2,1)S(1)}, bf16[64,2560]{1,0:T(8,128)(2,1)S(1)}) fusion(bf16[384,2560]{1,0:T(8,128)(2,1)S(1)} %fusion.5.k_ref, s32[]{:T(128)S(6)} %select_n.170, bf16[384,2560]{1,0:T(8,128)(2,1)} %v_ref.1), kind=kLoop, calls=%fused_computation.79 | loop fusion | bytes 5898244 | tf_op jit(solution)/shard_map/slice | solution.py:350
  16.7 1.8 %collective-permute-start.14 = (bf16[144,2560]{1,0:T(8,128)(2,1)S(1)}, bf16[144,2560]{1,0:T(8,128)(2,1)S(1)}, u32[]{:S(2)}, u32[]{:S(2)}) collective-permute-start(bf16[144,2560]{1,0:T(8,128)(2,1)S(1)} %fusion.8), channel_id=1, source_target_pairs={{0,2},{2,4},{4,6},{6,8},{8,10},{10,12},{12,14},{14,16},{16,18},{18... | collective-permute-start | bytes 2211848 | tf_op jit(solution)/shard_map/ppermute | solution.py:22
  18.5 2.2 %collective-permute-start = (bf16[16,8,2560]{2,1,0:T(8,128)(2,1)S(1)}, bf16[16,8,2560]{2,1,0:T(8,128)(2,1)S(1)}, u32[]{:S(2)}, u32[]{:S(2)}) collective-permute-start(bf16[16,8,2560]{2,1,0:T(8,128)(2,1)S(1)} %copy-done.1), channel_id=1, source_target_pairs={{0,8},{2,10},{8,16},{10,18},{16,24},{18,26},{24,28},{26,30},{28,20... | collective-permute-start | bytes 1966088 | tf_op jit(solution)/shard_map/ppermute | solution.py:363
  23.4 2.0 %collective-permute-start.12 = (bf16[16,8,2560]{2,1,0:T(8,128)(2,1)S(1)}, bf16[16,8,2560]{2,1,0:T(8,128)(2,1)S(1)}, u32[]{:S(2)}, u32[]{:S(2)}) collective-permute-start(bf16[16,8,2560]{2,1,0:T(8,128)(2,1)S(1)} %collective-permute-done.11.refs_5_.refs_12_), channel_id=1, source_target_pairs={{0,8},{2,10},{8,16},{10,18},{16,24},{18,26},{24,28},{26,30},{28,20... | collective-permute-start | bytes 1966088 | tf_op jit(solution)/shard_map/ppermute | solution.py:363
  25.7 6.4 %near_part.1 = (f32[20,8,384]{2,1,0:T(8,128)S(1)}, f32[20,8,384]{2,1,0:T(8,128)S(1)}, f32[2560,384]{1,0:T(8,128)S(1)}) custom-call(f32[448,128]{1,0:T(8,128)S(1)} %broadcast_in_dim.130.bias_ref, bf16[384,2560]{1,0:T(8,128)(2,1)S(1)} %fusion.2.q_ref.refs_3_, bf16[384,2560]{1,0:T(8,128)(2,1)S(1)} %fusion.5.k_ref, bf16[384,2560]{1,0:T(8,128)(2,1)S(1)} %copy-done, ...), custom_call_target="tpu_custom_call" | custom-call | flops 1761607680 | bytes 9830400 | tf_op jit(solution)/shard_map/near_part/pallas_call | solution.py:133
  32.1 3.2 %collective-permute-done.refs_2_.refs_9_ = bf16[16,8,2560]{2,1,0:T(8,128)(2,1)S(1)} collective-permute-done((bf16[16,8,2560]{2,1,0:T(8,128)(2,1)S(1)}, bf16[16,8,2560]{2,1,0:T(8,128)(2,1)S(1)}, u32[]{:S(2)}, u32[]{:S(2)}) %collective-permute-start) | collective-permute-done | bytes 655392 | tf_op jit(solution)/shard_map/ppermute | solution.py:363
  35.3 5.3 %collective-permute-done.8.refs_1_.refs_8_ = bf16[16,8,2560]{2,1,0:T(8,128)(2,1)S(1)} collective-permute-done((bf16[16,8,2560]{2,1,0:T(8,128)(2,1)S(1)}, bf16[16,8,2560]{2,1,0:T(8,128)(2,1)S(1)}, u32[]{:S(2)}, u32[]{:S(2)}) %collective-permute-start.8) | collective-permute-done | bytes 655392 | tf_op jit(solution)/shard_map/ppermute | solution.py:363
  40.6 3.3 %pick_0.1 = (bf16[24,8,2560]{2,1,0:T(8,128)(2,1)S(1)}, bf16[24,8,2560]{2,1,0:T(8,128)(2,1)S(1)}) custom-call(s32[4]{0:T(128)S(1)} %slice.84.first_ref, s32[88]{0:T(128)S(1)} %concatenate.55.block_ref, bf16[16,8,2560]{2,1,0:T(8,128)(2,1)S(1)} %copy-done.1, bf16[16,8,2560]{2,1,0:T(8,128)(2,1)S(1)} %collective-permute-done.8.refs_1_.refs_8_, ...), custom_call_target="tpu_custom_call" | custom-call | bytes 3932160 | tf_op jit(solution)/shard_map/pick_0/pallas_call | solution.py:169
  43.9 7.1 %collective-permute-start.16 = (bf16[24,8,2560]{2,1,0:T(8,128)(2,1)S(1)}, bf16[24,8,2560]{2,1,0:T(8,128)(2,1)S(1)}, u32[]{:S(2)}, u32[]{:S(2)}) collective-permute-start(bf16[24,8,2560]{2,1,0:T(8,128)(2,1)S(1)} %get-tuple-element.69), channel_id=1, source_target_pairs={{0,2},{2,0},{4,6},{6,4},{8,10},{10,8},{12,14},{14,12},{16,18},{18,... | collective-permute-start | bytes 2949128 | tf_op jit(solution)/shard_map/ppermute | solution.py:363
  51.2 2.5 %collective-permute-start.9 = (bf16[16,8,2560]{2,1,0:T(8,128)(2,1)S(1)}, bf16[16,8,2560]{2,1,0:T(8,128)(2,1)S(1)}, u32[]{:S(2)}, u32[]{:S(2)}) collective-permute-start(bf16[16,8,2560]{2,1,0:T(8,128)(2,1)S(1)} %collective-permute-done.8.refs_1_.refs_8_), channel_id=1, source_target_pairs={{0,4},{2,6},{8,0},{10,2},{16,8},{18,10},{24,16},{26,18},{28,24},{3... | collective-permute-start | bytes 1966088 | tf_op jit(solution)/shard_map/ppermute | solution.py:363
  54.6 1.1 collective-permute-start.6
  55.9 13.1 %collective-permute-done.1.refs_16_.refs_1_ = bf16[16,8,2560]{2,1,0:T(8,128)(2,1)S(1)} collective-permute-done((bf16[16,8,2560]{2,1,0:T(8,128)(2,1)S(1)}, bf16[16,8,2560]{2,1,0:T(8,128)(2,1)S(1)}, u32[]{:S(2)}, u32[]{:S(2)}) %collective-permute-start.1) | collective-permute-done | bytes 655392 | tf_op jit(solution)/shard_map/ppermute | solution.py:363
  69.0 5.0 %collective-permute-start.13 = (bf16[16,8,2560]{2,1,0:T(8,128)(2,1)S(1)}, bf16[16,8,2560]{2,1,0:T(8,128)(2,1)S(1)}, u32[]{:S(2)}, u32[]{:S(2)}) collective-permute-start(bf16[16,8,2560]{2,1,0:T(8,128)(2,1)S(1)} %collective-permute-done.12.refs_18_.refs_3_), channel_id=1, source_target_pairs={{0,8},{2,10},{8,16},{10,18},{16,24},{18,26},{24,28},{26,30},{28,20... | collective-permute-start | bytes 1966088 | tf_op jit(solution)/shard_map/ppermute | solution.py:363
  73.9 2.3 %collective-permute-start.2 = (bf16[16,8,2560]{2,1,0:T(8,128)(2,1)S(1)}, bf16[16,8,2560]{2,1,0:T(8,128)(2,1)S(1)}, u32[]{:S(2)}, u32[]{:S(2)}) collective-permute-start(bf16[16,8,2560]{2,1,0:T(8,128)(2,1)S(1)} %collective-permute-done.1.refs_16_.refs_1_), channel_id=1, source_target_pairs={{0,8},{2,10},{8,16},{10,18},{16,24},{18,26},{24,28},{26,30},{28,20... | collective-permute-start | bytes 1966088 | tf_op jit(solution)/shard_map/ppermute | solution.py:363
  76.2 1.3 collective-permute-start.18
  77.6 14.8 %far_1.1 = (f32[20,8,384]{2,1,0:T(8,128)S(1)}, f32[20,8,384]{2,1,0:T(8,128)S(1)}, f32[2560,384]{1,0:T(8,128)S(1)}) custom-call(s32[7]{0:T(128)S(1)} %pad_add_fusion.1.refs_0_, s32[128]{0:T(128)S(1)} %concatenate.52.refs_1_, f32[512,128]{1,0:T(8,128)S(1)} %broadcast_in_dim.133.refs_2_, ...), custom_call_target="tpu_custom_call", output_to_operand_aliasing={{0}: (4, {}), {1}: (5, {}), {2}: (6, {})} | custom-call | flops 2013265920 | bytes 9830400 | tf_op jit(solution)/shard_map/far_1/pallas_call | solution.py:259
  92.5 2.4 %pick_1.1 = (bf16[16,8,2560]{2,1,0:T(8,128)(2,1)S(1)}, bf16[16,8,2560]{2,1,0:T(8,128)(2,1)S(1)}) custom-call(s32[3]{0:T(128)S(1)} %get-tuple-element.115.first_ref, s32[80]{0:T(128)S(1)} %concatenate.56.block_ref, bf16[16,8,2560]{2,1,0:T(8,128)(2,1)S(1)} %collective-permute-done.9.refs_15_.refs_0_, ...), custom_call_target="tpu_custom_call" | custom-call | bytes 2621440 | tf_op jit(solution)/shard_map/pick_1/pallas_call | solution.py:169
  94.9 1.2 collective-permute-start.19
  97.3 1.3 pad_add_fusion.refs_0_
  98.6 3.2 %collective-permute-done.2.refs_1_.refs_13_ = bf16[16,8,2560]{2,1,0:T(8,128)(2,1)S(1)} collective-permute-done((bf16[16,8,2560]{2,1,0:T(8,128)(2,1)S(1)}, bf16[16,8,2560]{2,1,0:T(8,128)(2,1)S(1)}, u32[]{:S(2)}, u32[]{:S(2)}) %collective-permute-start.2) | collective-permute-done | bytes 655392 | tf_op jit(solution)/shard_map/ppermute | solution.py:363
  101.8 3.0 %collective-permute-done.10.refs_0_.refs_12_ = bf16[16,8,2560]{2,1,0:T(8,128)(2,1)S(1)} collective-permute-done((bf16[16,8,2560]{2,1,0:T(8,128)(2,1)S(1)}, bf16[16,8,2560]{2,1,0:T(8,128)(2,1)S(1)}, u32[]{:S(2)}, u32[]{:S(2)}) %collective-permute-start.10) | collective-permute-done | bytes 655392 | tf_op jit(solution)/shard_map/ppermute | solution.py:363
  104.9 2.5 %collective-permute-start.7 = (bf16[16,8,2560]{2,1,0:T(8,128)(2,1)S(1)}, bf16[16,8,2560]{2,1,0:T(8,128)(2,1)S(1)}, u32[]{:S(2)}, u32[]{:S(2)}) collective-permute-start(bf16[16,8,2560]{2,1,0:T(8,128)(2,1)S(1)} %collective-permute-done.6.refs_2_.refs_14_), channel_id=1, source_target_pairs={{0,4},{2,6},{8,0},{10,2},{16,8},{18,10},{24,16},{26,18},{28,24},{3... | collective-permute-start | bytes 1966088 | tf_op jit(solution)/shard_map/ppermute | solution.py:363
  107.4 2.4 %pick_2.1 = (bf16[16,8,2560]{2,1,0:T(8,128)(2,1)S(1)}, bf16[16,8,2560]{2,1,0:T(8,128)(2,1)S(1)}) custom-call(s32[3]{0:T(128)S(1)} %get-tuple-element.114.first_ref, s32[80]{0:T(128)S(1)} %concatenate.56.block_ref, bf16[16,8,2560]{2,1,0:T(8,128)(2,1)S(1)} %collective-permute-done.10.refs_0_.refs_12_, ...), custom_call_target="tpu_custom_call" | custom-call | bytes 2621440 | tf_op jit(solution)/shard_map/pick_2/pallas_call | solution.py:169
  109.8 1.8 %collective-permute-start.21 = (bf16[16,8,2560]{2,1,0:T(8,128)(2,1)S(1)}, bf16[16,8,2560]{2,1,0:T(8,128)(2,1)S(1)}, u32[]{:S(2)}, u32[]{:S(2)}) collective-permute-start(bf16[16,8,2560]{2,1,0:T(8,128)(2,1)S(1)} %get-tuple-element.93), channel_id=1, source_target_pairs={{0,2},{2,0},{4,6},{6,4},{8,10},{10,8},{12,14},{14,12},{16,18},{18,... | collective-permute-start | bytes 1966088 | tf_op jit(solution)/shard_map/ppermute | solution.py:363
  111.7 1.6 %collective-permute-done.21.refs_16_ = bf16[16,8,2560]{2,1,0:T(8,128)(2,1)S(1)} collective-permute-done((bf16[16,8,2560]{2,1,0:T(8,128)(2,1)S(1)}, bf16[16,8,2560]{2,1,0:T(8,128)(2,1)S(1)}, u32[]{:S(2)}, u32[]{:S(2)}) %collective-permute-start.21) | collective-permute-done | bytes 655392 | tf_op jit(solution)/shard_map/ppermute | solution.py:363
  113.3 0.9 collective-permute-done.22.refs_17_
  114.4 12.9 %far_2.1 = (f32[20,8,384]{2,1,0:T(8,128)S(1)}, f32[20,8,384]{2,1,0:T(8,128)S(1)}, f32[2560,384]{1,0:T(8,128)S(1)}) custom-call(s32[5]{0:T(128)S(1)} %pad_add_fusion.refs_0_, s32[112]{0:T(128)S(1)} %concatenate.46.refs_1_, f32[384,128]{1,0:T(8,128)S(1)} %broadcast_in_dim.125.refs_2_, ...), custom_call_target="tpu_custom_call", output_to_operand_aliasing={{0}: (4, {}), {1}: (5, {}), {2}: (6, {})} | custom-call | flops 1509949440 | bytes 9830400 | tf_op jit(solution)/shard_map/far_2/pallas_call | solution.py:259
  130.5 6.8 %far_3.1 = bf16[384,2560]{1,0:T(8,128)(2,1)} custom-call(s32[3]{0:T(128)S(1)} %get-tuple-element.122.refs_0_, s32[80]{0:T(128)S(1)} %concatenate.44.refs_1_, f32[128,128]{1,0:T(8,128)S(1)} %broadcast_in_dim.122.refs_2_, bf16[384,2560]{1,0:T(8,128)(2,1)S(1)} %fusion.2.q_ref.refs_3_, f32[20,8,384]{2,1,0:T(8,128)S(1)} %get-tuple-element.96.refs_4_, ...), custom_call_target="tpu_custom_call" | custom-call | flops 503316480 | bytes 9830400 | tf_op jit(solution)/shard_map/far_3/pallas_call | solution.py:259
  (84 shorter events, 7.0 us)
Async XLA Ops:
  0.0 6.9 %copy-start.3 = (bf16[384,2560]{1,0:T(8,128)(2,1)S(1)}, bf16[384,2560]{1,0:T(8,128)(2,1)}, u32[]{:S(2)}) copy-start(bf16[384,2560]{1,0:T(8,128)(2,1)} %param.12) | copy-start | bytes 5898244
  0.0 23.4 %collective-permute-start.11 = (bf16[16,8,2560]{2,1,0:T(8,128)(2,1)}, bf16[16,8,2560]{2,1,0:T(8,128)(2,1)S(1)}, u32[]{:S(2)}, u32[]{:S(2)}) collective-permute-start(bf16[16,8,2560]{2,1,0:T(8,128)(2,1)} %refs_10_), channel_id=1, source_target_pairs={{0,8},{2,10},{8,16},{10,18},{16,24},{18,26},{24,28},{26,30},{28,20... | collective-permute-start | bytes 1966088 | tf_op jit(solution)/shard_map/ppermute | solution.py:363
  3.0 22.4 %collective-permute-start.4 = (bf16[16,8,2560]{2,1,0:T(8,128)(2,1)}, bf16[16,8,2560]{2,1,0:T(8,128)(2,1)S(1)}, u32[]{:S(2)}, u32[]{:S(2)}) collective-permute-start(bf16[16,8,2560]{2,1,0:T(8,128)(2,1)} %refs_10_), channel_id=1, source_target_pairs={{0,4},{2,6},{8,0},{10,2},{16,8},{18,10},{24,16},{26,18},{28,24},{3... | collective-permute-start | bytes 1966088 | tf_op jit(solution)/shard_map/ppermute | solution.py:363
  4.2 19.0 %collective-permute-start.15 = (s32[81]{0:T(128)S(1)}, s32[81]{0:T(128)S(1)}, u32[]{:S(2)}, u32[]{:S(2)}) collective-permute-start(s32[81]{0:T(128)S(1)} %pad_add_fusion.2), channel_id=1, source_target_pairs={{0,2},{2,0},{4,6},{6,4},{8,10},{10,8},{12,14},{14,12},{16,18},{18,... | collective-permute-start | bytes 980 | tf_op jit(solution)/shard_map/ppermute | solution.py:329
  4.9 8.1 %copy-start.6 = (f32[2560]{0:T(1024)S(1)}, f32[2560]{0:T(1024)}, u32[]{:S(2)}) copy-start(f32[2560]{0:T(1024)} %param.15) | copy-start | bytes 30724
  15.1 3.3 %copy-start.1 = (bf16[16,8,2560]{2,1,0:T(8,128)(2,1)S(1)}, bf16[16,8,2560]{2,1,0:T(8,128)(2,1)}, u32[]{:S(2)}) copy-start(bf16[16,8,2560]{2,1,0:T(8,128)(2,1)} %refs_7_) | copy-start | bytes 1966084
  15.1 6.3 %copy-start.5 = (f32[2560]{0:T(1024)S(1)}, f32[2560]{0:T(1024)}, u32[]{:S(2)}) copy-start(f32[2560]{0:T(1024)} %param.14) | copy-start | bytes 30724
  15.1 7.5 %copy-start.4 = (bf16[384,2560]{1,0:T(8,128)(2,1)S(1)}, bf16[384,2560]{1,0:T(8,128)(2,1)}, u32[]{:S(2)}) copy-start(bf16[384,2560]{1,0:T(8,128)(2,1)} %param.11) | copy-start | bytes 5898244
  16.7 8.8 %collective-permute-start.14 = (bf16[144,2560]{1,0:T(8,128)(2,1)S(1)}, bf16[144,2560]{1,0:T(8,128)(2,1)S(1)}, u32[]{:S(2)}, u32[]{:S(2)}) collective-permute-start(bf16[144,2560]{1,0:T(8,128)(2,1)S(1)} %fusion.8), channel_id=1, source_target_pairs={{0,2},{2,4},{4,6},{6,8},{8,10},{10,12},{12,14},{14,16},{16,18},{18... | collective-permute-start | bytes 2211848 | tf_op jit(solution)/shard_map/ppermute | solution.py:22
  18.5 16.8 %collective-permute-start = (bf16[16,8,2560]{2,1,0:T(8,128)(2,1)S(1)}, bf16[16,8,2560]{2,1,0:T(8,128)(2,1)S(1)}, u32[]{:S(2)}, u32[]{:S(2)}) collective-permute-start(bf16[16,8,2560]{2,1,0:T(8,128)(2,1)S(1)} %copy-done.1), channel_id=1, source_target_pairs={{0,8},{2,10},{8,16},{10,18},{16,24},{18,26},{24,28},{26,30},{28,20... | collective-permute-start | bytes 1966088 | tf_op jit(solution)/shard_map/ppermute | solution.py:363
  22.6 3.0 %copy-start = (bf16[384,2560]{1,0:T(8,128)(2,1)S(1)}, bf16[384,2560]{1,0:T(8,128)(2,1)}, u32[]{:S(2)}) copy-start(bf16[384,2560]{1,0:T(8,128)(2,1)} %v_ref.1) | copy-start | bytes 5898244
  23.2 17.4 %collective-permute-start.8 = (bf16[16,8,2560]{2,1,0:T(8,128)(2,1)S(1)}, bf16[16,8,2560]{2,1,0:T(8,128)(2,1)S(1)}, u32[]{:S(2)}, u32[]{:S(2)}) collective-permute-start(bf16[16,8,2560]{2,1,0:T(8,128)(2,1)S(1)} %copy-done.1), channel_id=1, source_target_pairs={{0,4},{2,6},{8,0},{10,2},{16,8},{18,10},{24,16},{26,18},{28,24},{3... | collective-permute-start | bytes 1966088 | tf_op jit(solution)/shard_map/ppermute | solution.py:363
  23.4 27.7 %collective-permute-start.12 = (bf16[16,8,2560]{2,1,0:T(8,128)(2,1)S(1)}, bf16[16,8,2560]{2,1,0:T(8,128)(2,1)S(1)}, u32[]{:S(2)}, u32[]{:S(2)}) collective-permute-start(bf16[16,8,2560]{2,1,0:T(8,128)(2,1)S(1)} %collective-permute-done.11.refs_5_.refs_12_), channel_id=1, source_target_pairs={{0,8},{2,10},{8,16},{10,18},{16,24},{18,26},{24,28},{26,30},{28,20... | collective-permute-start | bytes 1966088 | tf_op jit(solution)/shard_map/ppermute | solution.py:363
  25.4 29.2 %collective-permute-start.5 = (bf16[16,8,2560]{2,1,0:T(8,128)(2,1)S(1)}, bf16[16,8,2560]{2,1,0:T(8,128)(2,1)S(1)}, u32[]{:S(2)}, u32[]{:S(2)}) collective-permute-start(bf16[16,8,2560]{2,1,0:T(8,128)(2,1)S(1)} %collective-permute-done.4.refs_4_.refs_11_), channel_id=1, source_target_pairs={{0,4},{2,6},{8,0},{10,2},{16,8},{18,10},{24,16},{26,18},{28,24},{3... | collective-permute-start | bytes 1966088 | tf_op jit(solution)/shard_map/ppermute | solution.py:363
  25.7 14.9 %copy-start.2 = (bf16[16,8,2560]{2,1,0:T(8,128)(2,1)S(1)}, bf16[16,8,2560]{2,1,0:T(8,128)(2,1)}, u32[]{:S(2)}) copy-start(bf16[16,8,2560]{2,1,0:T(8,128)(2,1)} %refs_10_) | copy-start | bytes 1966084
  43.9 32.3 %collective-permute-start.16 = (bf16[24,8,2560]{2,1,0:T(8,128)(2,1)S(1)}, bf16[24,8,2560]{2,1,0:T(8,128)(2,1)S(1)}, u32[]{:S(2)}, u32[]{:S(2)}) collective-permute-start(bf16[24,8,2560]{2,1,0:T(8,128)(2,1)S(1)} %get-tuple-element.69), channel_id=1, source_target_pairs={{0,2},{2,0},{4,6},{6,4},{8,10},{10,8},{12,14},{14,12},{16,18},{18,... | collective-permute-start | bytes 2949128 | tf_op jit(solution)/shard_map/ppermute | solution.py:363
  51.0 25.2 %collective-permute-start.17 = (bf16[24,8,2560]{2,1,0:T(8,128)(2,1)S(1)}, bf16[24,8,2560]{2,1,0:T(8,128)(2,1)S(1)}, u32[]{:S(2)}, u32[]{:S(2)}) collective-permute-start(bf16[24,8,2560]{2,1,0:T(8,128)(2,1)S(1)} %get-tuple-element.71), channel_id=1, source_target_pairs={{0,2},{2,0},{4,6},{6,4},{8,10},{10,8},{12,14},{14,12},{16,18},{18,... | collective-permute-start | bytes 2949128 | tf_op jit(solution)/shard_map/ppermute | solution.py:363
  51.1 17.8 %collective-permute-start.1 = (bf16[16,8,2560]{2,1,0:T(8,128)(2,1)S(1)}, bf16[16,8,2560]{2,1,0:T(8,128)(2,1)S(1)}, u32[]{:S(2)}, u32[]{:S(2)}) collective-permute-start(bf16[16,8,2560]{2,1,0:T(8,128)(2,1)S(1)} %collective-permute-done.refs_2_.refs_9_), channel_id=1, source_target_pairs={{0,8},{2,10},{8,16},{10,18},{16,24},{18,26},{24,28},{26,30},{28,20... | collective-permute-start | bytes 1966088 | tf_op jit(solution)/shard_map/ppermute | solution.py:363
  51.2 17.8 %collective-permute-start.9 = (bf16[16,8,2560]{2,1,0:T(8,128)(2,1)S(1)}, bf16[16,8,2560]{2,1,0:T(8,128)(2,1)S(1)}, u32[]{:S(2)}, u32[]{:S(2)}) collective-permute-start(bf16[16,8,2560]{2,1,0:T(8,128)(2,1)S(1)} %collective-permute-done.8.refs_1_.refs_8_), channel_id=1, source_target_pairs={{0,4},{2,6},{8,0},{10,2},{16,8},{18,10},{24,16},{26,18},{28,24},{3... | collective-permute-start | bytes 1966088 | tf_op jit(solution)/shard_map/ppermute | solution.py:363
  54.6 40.2 %collective-permute-start.6 = (bf16[16,8,2560]{2,1,0:T(8,128)(2,1)S(1)}, bf16[16,8,2560]{2,1,0:T(8,128)(2,1)S(1)}, u32[]{:S(2)}, u32[]{:S(2)}) collective-permute-start(bf16[16,8,2560]{2,1,0:T(8,128)(2,1)S(1)} %collective-permute-done.5.refs_17_.refs_2_), channel_id=1, source_target_pairs={{0,4},{2,6},{8,0},{10,2},{16,8},{18,10},{24,16},{26,18},{28,24},{3... | collective-permute-start | bytes 1966088 | tf_op jit(solution)/shard_map/ppermute | solution.py:363
  69.0 29.6 %collective-permute-start.13 = (bf16[16,8,2560]{2,1,0:T(8,128)(2,1)S(1)}, bf16[16,8,2560]{2,1,0:T(8,128)(2,1)S(1)}, u32[]{:S(2)}, u32[]{:S(2)}) collective-permute-start(bf16[16,8,2560]{2,1,0:T(8,128)(2,1)S(1)} %collective-permute-done.12.refs_18_.refs_3_), channel_id=1, source_target_pairs={{0,8},{2,10},{8,16},{10,18},{16,24},{18,26},{24,28},{26,30},{28,20... | collective-permute-start | bytes 1966088 | tf_op jit(solution)/shard_map/ppermute | solution.py:363
  73.9 27.9 %collective-permute-start.2 = (bf16[16,8,2560]{2,1,0:T(8,128)(2,1)S(1)}, bf16[16,8,2560]{2,1,0:T(8,128)(2,1)S(1)}, u32[]{:S(2)}, u32[]{:S(2)}) collective-permute-start(bf16[16,8,2560]{2,1,0:T(8,128)(2,1)S(1)} %collective-permute-done.1.refs_16_.refs_1_), channel_id=1, source_target_pairs={{0,8},{2,10},{8,16},{10,18},{16,24},{18,26},{24,28},{26,30},{28,20... | collective-permute-start | bytes 1966088 | tf_op jit(solution)/shard_map/ppermute | solution.py:363
  76.2 28.7 %collective-permute-start.10 = (bf16[16,8,2560]{2,1,0:T(8,128)(2,1)S(1)}, bf16[16,8,2560]{2,1,0:T(8,128)(2,1)S(1)}, u32[]{:S(2)}, u32[]{:S(2)}) collective-permute-start(bf16[16,8,2560]{2,1,0:T(8,128)(2,1)S(1)} %collective-permute-done.9.refs_15_.refs_0_), channel_id=1, source_target_pairs={{0,4},{2,6},{8,0},{10,2},{16,8},{18,10},{24,16},{26,18},{28,24},{3... | collective-permute-start | bytes 1966088 | tf_op jit(solution)/shard_map/ppermute | solution.py:363
  76.2 35.3 %collective-permute-start.18 = (bf16[144,2560]{1,0:T(8,128)(2,1)S(1)}, bf16[144,2560]{1,0:T(8,128)(2,1)S(1)}, u32[]{:S(2)}, u32[]{:S(2)}) collective-permute-start(bf16[144,2560]{1,0:T(8,128)(2,1)S(1)} %fusion.9), channel_id=1, source_target_pairs={{2,0},{4,2},{6,4},{8,6},{10,8},{12,10},{14,12},{16,14},{18,16},{20... | collective-permute-start | bytes 2211848 | tf_op jit(solution)/shard_map/ppermute | solution.py:22
  94.9 12.5 %collective-permute-start.19 = (bf16[16,8,2560]{2,1,0:T(8,128)(2,1)S(1)}, bf16[16,8,2560]{2,1,0:T(8,128)(2,1)S(1)}, u32[]{:S(2)}, u32[]{:S(2)}) collective-permute-start(bf16[16,8,2560]{2,1,0:T(8,128)(2,1)S(1)} %get-tuple-element.86), channel_id=1, source_target_pairs={{0,2},{2,0},{4,6},{6,4},{8,10},{10,8},{12,14},{14,12},{16,18},{18,... | collective-permute-start | bytes 1966088 | tf_op jit(solution)/shard_map/ppermute | solution.py:363
  98.5 13.1 %collective-permute-start.20 = (bf16[16,8,2560]{2,1,0:T(8,128)(2,1)S(1)}, bf16[16,8,2560]{2,1,0:T(8,128)(2,1)S(1)}, u32[]{:S(2)}, u32[]{:S(2)}) collective-permute-start(bf16[16,8,2560]{2,1,0:T(8,128)(2,1)S(1)} %get-tuple-element.88), channel_id=1, source_target_pairs={{0,2},{2,0},{4,6},{6,4},{8,10},{10,8},{12,14},{14,12},{16,18},{18,... | collective-permute-start | bytes 1966088 | tf_op jit(solution)/shard_map/ppermute | solution.py:363
  104.9 22.4 %collective-permute-start.7 = (bf16[16,8,2560]{2,1,0:T(8,128)(2,1)S(1)}, bf16[16,8,2560]{2,1,0:T(8,128)(2,1)S(1)}, u32[]{:S(2)}, u32[]{:S(2)}) collective-permute-start(bf16[16,8,2560]{2,1,0:T(8,128)(2,1)S(1)} %collective-permute-done.6.refs_2_.refs_14_), channel_id=1, source_target_pairs={{0,4},{2,6},{8,0},{10,2},{16,8},{18,10},{24,16},{26,18},{28,24},{3... | collective-permute-start | bytes 1966088 | tf_op jit(solution)/shard_map/ppermute | solution.py:363
  107.4 19.9 %collective-permute-start.3 = (bf16[16,8,2560]{2,1,0:T(8,128)(2,1)S(1)}, bf16[16,8,2560]{2,1,0:T(8,128)(2,1)S(1)}, u32[]{:S(2)}, u32[]{:S(2)}) collective-permute-start(bf16[16,8,2560]{2,1,0:T(8,128)(2,1)S(1)} %collective-permute-done.2.refs_1_.refs_13_), channel_id=1, source_target_pairs={{0,8},{2,10},{8,16},{10,18},{16,24},{18,26},{24,28},{26,30},{28,20... | collective-permute-start | bytes 1966088 | tf_op jit(solution)/shard_map/ppermute | solution.py:363
  109.8 3.5 %collective-permute-start.21 = (bf16[16,8,2560]{2,1,0:T(8,128)(2,1)S(1)}, bf16[16,8,2560]{2,1,0:T(8,128)(2,1)S(1)}, u32[]{:S(2)}, u32[]{:S(2)}) collective-permute-start(bf16[16,8,2560]{2,1,0:T(8,128)(2,1)S(1)} %get-tuple-element.93), channel_id=1, source_target_pairs={{0,2},{2,0},{4,6},{6,4},{8,10},{10,8},{12,14},{14,12},{16,18},{18,... | collective-permute-start | bytes 1966088 | tf_op jit(solution)/shard_map/ppermute | solution.py:363
  111.5 2.7 %collective-permute-start.22 = (bf16[16,8,2560]{2,1,0:T(8,128)(2,1)S(1)}, bf16[16,8,2560]{2,1,0:T(8,128)(2,1)S(1)}, u32[]{:S(2)}, u32[]{:S(2)}) collective-permute-start(bf16[16,8,2560]{2,1,0:T(8,128)(2,1)S(1)} %get-tuple-element.94), channel_id=1, source_target_pairs={{0,2},{2,0},{4,6},{6,4},{8,10},{10,8},{12,14},{14,12},{16,18},{18,... | collective-permute-start | bytes 1966088 | tf_op jit(solution)/shard_map/ppermute | solution.py:363
  127.3 2.2 %collective-permute-start.23 = (bf16[16,8,2560]{2,1,0:T(8,128)(2,1)S(1)}, bf16[16,8,2560]{2,1,0:T(8,128)(2,1)S(1)}, u32[]{:S(2)}, u32[]{:S(2)}) collective-permute-start(bf16[16,8,2560]{2,1,0:T(8,128)(2,1)S(1)} %collective-permute-done.3.refs_8_), channel_id=1, source_target_pairs={{0,2},{2,0},{4,6},{6,4},{8,10},{10,8},{12,14},{14,12},{16,18},{18,... | collective-permute-start | bytes 1966088 | tf_op jit(solution)/shard_map/ppermute | solution.py:363
  127.7 2.7 %collective-permute-start.24 = (bf16[16,8,2560]{2,1,0:T(8,128)(2,1)S(1)}, bf16[16,8,2560]{2,1,0:T(8,128)(2,1)S(1)}, u32[]{:S(2)}, u32[]{:S(2)}) collective-permute-start(bf16[16,8,2560]{2,1,0:T(8,128)(2,1)S(1)} %collective-permute-done.7.refs_10_), channel_id=1, source_target_pairs={{0,2},{2,0},{4,6},{6,4},{8,10},{10,8},{12,14},{14,12},{16,18},{18,... | collective-permute-start | bytes 1966088 | tf_op jit(solution)/shard_map/ppermute | solution.py:363
